TPU v7x, 32 devices: a whole 2x2x4 slice. The times are simulated.
32 devices in a mesh: groups: 1, ep: 16 (over z, y, x), sub: 2 (over core).
Axes of the slice: x: 2, y: 2, z: 4, core: 2. Of those that a mesh axis runs over, the one named last changes fastest.
Arguments:
- hidden_in: bfloat16 [256, 3584], P(('groups', 'ep', 'sub')), may hold values from -6 to 6
- expert_routes: int32 [256, 8], P(('groups', 'ep', 'sub')), may hold values from 0 to 15, all different within a row; in each aligned block of 8 rows (0 to 7, 8 to 15, ...) at most 8 rows name the same one
- route_scores: float32 [256, 8], P(('groups', 'ep', 'sub')), may hold values from 0.1 to 1
- expert_gate: bfloat16 [16, 3584, 1024], P('ep', None, 'sub'), may hold values from -0.09375 to 0.09375
- expert_up: bfloat16 [16, 3584, 1024], P('ep', None, 'sub'), may hold values from -0.09375 to 0.09375
- expert_down: bfloat16 [16, 1024, 3584], P('ep', 'sub'), may hold values from -0.1875 to 0.1875
- query_latent: bfloat16 [128, 128, 576], P(('groups', 'ep', 'sub')), may hold values from -49 to 49
- latent_cache: bfloat16 [128, 256, 576], P(('groups', 'ep', 'sub')), may hold values from -8 to 8
- cache_lengths: int32 [128], P(('groups', 'ep', 'sub')), may hold values from 2 to 256, as said below
Outputs:
- moe_output: bfloat16 [256, 3584], P(('groups', 'ep', 'sub'))
- attention_latent: bfloat16 [128, 128, 512], P(('groups', 'ep', 'sub'))
Inputs may be any that keep to these rules, and one draw needn't show every extreme that they name: `expert_routes`: each row names 8 different experts. Among the 8 rows of one device (aligned blocks), no expert is named more than 8 times, a bound that some block reaches. `cache_lengths`: some row has length 256.
All inputs are finite; a program needn't handle non-finite values.
Results may differ from a plain program's by a relative error of at most 0.0085.
Values may be sent and summed in bfloat16 or wider, within the bound.
No kernel may reach another device: no remote copies, remote signals or barrier semaphores. Data moves between devices by JAX's collectives and lax.ppermute only.
A program may use at most 64 MiB of HBM per device.

v0:
```python
import jax
import jax.numpy as jnp
from jax import lax
from jax.sharding import PartitionSpec as P

LATENT = 512


SOFTMAX_SCALE = 192.0 ** (-0.5)
ROUTE_SCALE = 2.5


def attend(query_latent, latent_cache, cache_lengths):
    scores = (
        jnp.einsum("rhc,rtc->rht", query_latent, latent_cache, preferred_element_type=jnp.float32)
        * SOFTMAX_SCALE
    )
    positions = jnp.arange(latent_cache.shape[1], dtype=jnp.int32)
    visible = positions[None, None, :] < cache_lengths[:, None, None]
    scores = jnp.where(visible, scores, jnp.float32(-1e30))
    largest = jnp.max(scores, axis=2, keepdims=True)
    powered = jnp.where(visible, jnp.exp(scores - largest), jnp.float32(0.0))
    probability = (powered / jnp.sum(powered, axis=2, keepdims=True)).astype(jnp.bfloat16)
    values = latent_cache[:, :, :LATENT]
    mixed = jnp.einsum("rht,rtc->rhc", probability, values, preferred_element_type=jnp.float32)
    return mixed.astype(jnp.bfloat16)


def expert_block(expert_rows, expert_gate, expert_up, expert_down):
    gate_value = jnp.einsum(
        "erd,edf->erf", expert_rows, expert_gate, preferred_element_type=jnp.float32
    )
    up_value = jnp.einsum(
        "erd,edf->erf", expert_rows, expert_up, preferred_element_type=jnp.float32
    )
    hidden = (jax.nn.silu(gate_value) * up_value).astype(jnp.bfloat16)
    return jnp.einsum("erf,efd->erd", hidden, expert_down, preferred_element_type=jnp.float32)


def per_device(
    hidden_in,
    expert_routes,
    route_scores,
    expert_gate,
    expert_up,
    expert_down,
    query_latent,
    latent_cache,
    cache_lengths,
):
    tok_rows, model_width = hidden_in.shape
    top_count = expert_routes.shape[1]
    local_experts = expert_gate.shape[0]
    ep_count = lax.axis_size("ep")
    experts = local_experts * ep_count
    capacity = min(tok_rows, max(2, 2 * tok_rows * top_count // experts))
    flat_routes = expert_routes.reshape(-1)
    onehot_table = (flat_routes[:, None] == jnp.arange(experts, dtype=jnp.int32)[None, :]).astype(
        jnp.int32
    )
    earlier = jnp.cumsum(onehot_table, axis=0) - onehot_table
    slot_index = jnp.sum(earlier * onehot_table, axis=1)
    destination = flat_routes * capacity + slot_index
    placing = (
        jnp.arange(experts * capacity, dtype=jnp.int32)[:, None] == destination[None, :]
    ).astype(jnp.bfloat16)
    owner_table = (
        jnp.arange(flat_routes.shape[0], dtype=jnp.int32)[:, None] // top_count
        == jnp.arange(tok_rows, dtype=jnp.int32)[None, :]
    ).astype(jnp.bfloat16)
    dispatch_map = jnp.dot(placing, owner_table, preferred_element_type=jnp.float32).astype(
        jnp.bfloat16
    )
    outgoing = jnp.dot(dispatch_map, hidden_in, preferred_element_type=jnp.float32).astype(
        jnp.bfloat16
    )
    outgoing = outgoing.reshape(experts, capacity, model_width)
    arrived = lax.all_to_all(outgoing, "ep", split_axis=0, concat_axis=1, tiled=True)
    both_cores = lax.all_gather(arrived, "sub", axis=1, tiled=True)
    partial_value = expert_block(both_cores, expert_gate, expert_up, expert_down)
    own_sums = lax.psum_scatter(
        partial_value.astype(jnp.bfloat16), "sub", scatter_dimension=1, tiled=True
    )
    returned = lax.all_to_all(own_sums, "ep", split_axis=1, concat_axis=0, tiled=True)
    returned = returned.reshape(experts * capacity, model_width)
    picked = (
        jnp.take(returned, destination, axis=0)
        .astype(jnp.float32)
        .reshape(tok_rows, top_count, model_width)
    )
    weights = ROUTE_SCALE * route_scores / jnp.sum(route_scores, axis=1, keepdims=True)
    moe_output = jnp.sum(picked * weights[:, :, None], axis=1).astype(jnp.bfloat16)
    attention_latent = attend(query_latent, latent_cache, cache_lengths)
    return (moe_output, attention_latent)


def solution(mesh):
    placed = (
        P(("groups", "ep", "sub"), None),
        P(("groups", "ep", "sub"), None),
        P(("groups", "ep", "sub"), None),
        P("ep", None, "sub"),
        P("ep", None, "sub"),
        P("ep", "sub", None),
        P(("groups", "ep", "sub"), None, None),
        P(("groups", "ep", "sub"), None, None),
        P(("groups", "ep", "sub")),
    )
    return jax.shard_map(
        per_device,
        mesh=mesh,
        in_specs=placed,
        out_specs=(P(("groups", "ep", "sub"), None), P(("groups", "ep", "sub"), None, None)),
        check_vma=False,
    )
```

profile of v0, /device:TPU:0, one launch (start us, length us, event | category | flops | bytes accessed | tf_op | source)
XLA Modules:
  0.0 121.1 jit_solution(3382688786674027176)
XLA Ops:
  7.2 0.0 copy-start
  7.2 0.0 all-gather.2.cloned.1.call-start
  7.2 0.8 reshape.159
  8.0 0.1 fusion.38
  8.1 0.1 reduce_window_sum.11
  8.2 0.2 select_reduce_fusion
  8.4 1.5 %fusion.2 = bf16[16,8,3584]{2,1,0:T(8,128)(2,1)S(1)} fusion(bf16[8,3584]{1,0:T(8,128)(2,1)} %param.9, s32[64]{0:T(128)S(1)} %get-tuple-element.3, s32[64]{0:T(128)S(1)} %get-tuple-element.2), kind=kOutput, calls=%fused_computation.5 | convolution fusion | flops 7939584 | bytes 975360 | tf_op jit(solution)/shard_map/dot_general | solution.py:74
  9.9 32.0 %all_to_all.21 = bf16[16,8,3584]{2,1,0:T(8,128)(2,1)} all-to-all(bf16[16,8,3584]{2,1,0:T(8,128)(2,1)S(1)} %fusion.2), channel_id=1, replica_groups=mesh['groups'=1,'ep'=16,'sub'=2] {'ep'}, dimensions={0} | all-to-all | bytes 1835008 | tf_op jit(solution)/shard_map/all_to_all | solution.py:78
  42.0 0.0 all-gather.2.cloned.1.call-update
  42.0 0.0 reduce-scatter.2.cloned.1.call-start
  42.1 8.3 %all-gather.2.cloned.1.call-done = bf16[1,256,3584]{2,1,0:T(8,128)(2,1)} async-done(((bf16[1,128,3584]{2,1,0:T(8,128)(2,1)}), bf16[1,256,3584]{2,1,0:T(8,128)(2,1)}) %all-gather.2.cloned.1.call-update) | async-done | bytes 1835024 | tf_op jit(solution)/shard_map/all_gather | solution.py:79
  50.4 0.0 copy-start.4
  50.4 3.8 %fusion.6 = f32[256,512]{1,0:T(8,128)S(1)} fusion(bf16[1,3584,512]{2,1,0:T(8,128)(2,1)} %param.12, bf16[1,256,3584]{2,1,0:T(8,128)(2,1)} %all-gather.2.cloned.1.call-done), kind=kOutput, calls=%fused_computation.9 | convolution fusion | flops 939524096 | bytes 6029312 | tf_op jit(solution)/shard_map/erd,edf->erf/dot_general | solution.py:30
  54.2 0.0 copy-done.4
  54.2 6.6 %fusion.1 = bf16[1,256,3584]{2,1,0:T(8,128)(2,1)} fusion(bf16[1,512,3584]{2,1,0:T(8,128)(2,1)} %param.14, bf16[1,3584,512]{2,1,0:T(8,128)(2,1)} %param.13, bf16[1,256,3584]{2,1,0:T(8,128)(2,1)S(1)} %copy-done.4, f32[256,512]{1,0:T(8,128)S(1)} %fusion.6), kind=kOutput, calls=%fused_computation.3 | convolution fusion | flops 1880752128 | bytes 11534336 | tf_op jit(solution)/shard_map/erf,efd->erd/dot_general | solution.py:37
  60.8 0.0 reduce-scatter.2.cloned.1.call-update
  60.8 10.7 %reduce-scatter.2.cloned.1.call-done = bf16[1,128,3584]{2,1,0:T(8,128)(2,1)} async-done(((bf16[1,256,3584]{2,1,0:T(8,128)(2,1)}), bf16[1,128,3584]{2,1,0:T(8,128)(2,1)}) %reduce-scatter.2.cloned.1.call-update) | async-done | bytes 917520 | tf_op jit(solution)/shard_map/reduce_scatter | solution.py:81
  71.5 2.6 %copy.21 = bf16[1,128,3584]{2,0,1:T(2,128)(2,1)S(1)} copy(bf16[1,128,3584]{2,1,0:T(8,128)(2,1)} %reduce-scatter.2.cloned.1.call-done) | data formatting | bytes 1835008 | tf_op jit(solution)/shard_map/reduce_scatter | solution.py:81
  74.1 0.5 broadcast.113
  74.6 6.2 %reduce = bf16[128,3584]{1,0:T(8,128)(2,1)S(1)} reduce(bf16[128,1,3584]{2,1,0:T(2,128)(2,1)S(1)} %bitcast.54, bf16[]{:T(256)} %broadcast.113), dimensions={1}, to_apply=%bitcast.52.reduce_sub_computation | reduce | bytes 1835010
  80.8 0.0 copy-start.2
  80.8 0.0 copy-start.3
  80.8 0.0 copy-start.5
  80.9 1.3 %reshape.174 = bf16[16,2,14336]{2,1,0:T(2,128)(2,1)} reshape(bf16[128,3584]{1,0:T(8,128)(2,1)S(1)} %reduce) | data formatting | bytes 1835008
  82.1 0.0 copy-start.1
  82.1 6.9 %all-to-all-start.1 = ((bf16[16,2,14336]{2,1,0:T(2,128)(2,1)}), bf16[16,2,14336]{2,1,0:T(2,128)(2,1)S(1)}, u32[]{:S(2)}, u32[]{:S(2)}) async-start(bf16[16,2,14336]{2,1,0:T(2,128)(2,1)} %reshape.174), calls=%async_computation.2 | async-start | bytes 1835008 | tf_op jit(solution)/shard_map/all_to_all | solution.py:84
  89.0 0.0 copy-done.2
  89.1 0.1 reduce_sum.41
  89.1 0.1 mul.66
  89.2 0.0 copy-done.3
  89.2 0.1 reduce_sum.43
  89.4 0.0 copy-done.5
  89.4 0.1 iota_compare_fusion.7
  89.4 0.0 copy-done
  89.4 0.0 copy-done.1
  89.4 0.4 fusion.18
  89.9 0.2 fusion.45
  90.1 0.1 multiply_divide_fusion
  90.2 1.8 %convolution_convert_fusion.2 = bf16[4,128,512]{2,1,0:T(8,128)(2,1)} fusion(bf16[4,256,576]{1,2,0:T(8,128)(2,1)S(1)} %copy-done.1, f32[4,128]{1,0:T(4,128)S(1)} %fusion.45, f32[4,128,256]{2,1,0:T(8,128)S(1)} %fusion.18, pred[4,256]{1,0:T(4,128)(4,1)S(1)} %iota_compare_fusion.7), kind=kOutput, calls=%fused_computation.13 | convolution fusion | flops 135004928 | bytes 2624512 | tf_op jit(solution)/shard_map/rht,rtc->rhc/dot_general | solution.py:25
  92.0 19.4 %all-to-all-done.1 = bf16[16,2,14336]{2,1,0:T(2,128)(2,1)S(1)} async-done(((bf16[16,2,14336]{2,1,0:T(2,128)(2,1)}), bf16[16,2,14336]{2,1,0:T(2,128)(2,1)S(1)}, u32[]{:S(2)}, u32[]{:S(2)}) %all-to-all-start.1) | async-done | bytes 917536 | tf_op jit(solution)/shard_map/all_to_all | solution.py:84
  111.4 0.9 reshape.175
  112.3 0.1 copy.20
  112.5 0.8 gather_fusion
  113.3 1.0 multiply_reduce_fusion
  (5 shorter events, 0.0 us)
Async XLA Ops:
  7.2 82.3 %copy-start = (bf16[4,128,576]{1,2,0:T(8,128)(2,1)S(1)}, bf16[4,128,576]{1,2,0:T(8,128)(2,1)}, u32[]{:S(2)}) copy-start(bf16[4,128,576]{1,2,0:T(8,128)(2,1)} %param.15) | copy-start | bytes 1769476
  7.2 43.2 %all-gather.2.cloned.1.call-start = ((), (), s32[]{:S(2)}) async-start(), calls=%async_computation.3 | async-start | bytes 2752512 | tf_op jit(solution)/shard_map/all_gather | solution.py:79
  42.0 29.5 %reduce-scatter.2.cloned.1.call-start = ((), (), s32[]{:S(2)}) async-start(), calls=%async_computation.4 | async-start | bytes 2752512 | tf_op jit(solution)/shard_map/reduce_scatter | solution.py:81
  50.4 3.8 %copy-start.4 = (bf16[1,256,3584]{2,1,0:T(8,128)(2,1)S(1)}, bf16[1,256,3584]{2,1,0:T(8,128)(2,1)}, u32[]{:S(2)}) copy-start(bf16[1,256,3584]{2,1,0:T(8,128)(2,1)} %all-gather.2.cloned.1.call-done) | copy-start | bytes 5505028
  80.8 8.2 %copy-start.2 = (s32[8,8]{1,0:T(8,128)S(1)}, s32[8,8]{1,0:T(8,128)}, u32[]{:S(2)}) copy-start(s32[8,8]{1,0:T(8,128)} %param.10) | copy-start | bytes 772
  80.8 8.4 %copy-start.3 = (f32[8,8]{1,0:T(8,128)S(1)}, f32[8,8]{1,0:T(8,128)}, u32[]{:S(2)}) copy-start(f32[8,8]{1,0:T(8,128)} %param.11) | copy-start | bytes 772
  80.8 8.5 %copy-start.5 = (s32[4]{0:T(128)S(1)}, s32[4]{0:T(128)}, u32[]{:S(2)}) copy-start(s32[4]{0:T(128)} %param.17) | copy-start | bytes 52
  82.1 7.3 %copy-start.1 = (bf16[4,256,576]{1,2,0:T(8,128)(2,1)S(1)}, bf16[4,256,576]{1,2,0:T(8,128)(2,1)}, u32[]{:S(2)}) copy-start(bf16[4,256,576]{1,2,0:T(8,128)(2,1)} %param.16) | copy-start | bytes 3538948
  82.1 29.3 %all-to-all-start.1 = ((bf16[16,2,14336]{2,1,0:T(2,128)(2,1)}), bf16[16,2,14336]{2,1,0:T(2,128)(2,1)S(1)}, u32[]{:S(2)}, u32[]{:S(2)}) async-start(bf16[16,2,14336]{2,1,0:T(2,128)(2,1)} %reshape.174), calls=%async_computation.2 | async-start | bytes 1835008 | tf_op jit(solution)/shard_map/all_to_all | solution.py:84
Sparse Core Ops, SparseCore 0:
  42.1 8.1 all-gather.1
  60.9 10.5 reduce-scatter.1
where the time goes:
time: 121 us
  waiting for transfers between devices  38.4 us (32%)
  blocking collectives  32 us (26%)
  matrix products  14.2 us (12%)
  between operations  14.2 us (12%)
  other arithmetic  8.1 us (7%)
  local copies, waits for them, and re-layouts  7.25 us (6%)
  starting transfers between devices  6.97 us (6%)
    all_to_all x1, blocking collectives, per_device(): lax.all_to_all(outgoing, 'ep', split_axis=0, concat_axis=1, tiled=True)  32 us
    all_to_all x1, waiting for transfers between devices, per_device(): lax.all_to_all(own_sums, 'ep', split_axis=1, concat_axis=0, tiled=True)  19.4 us
    reduce_scatter x1, waiting for transfers between devices, per_device(): lax.psum_scatter(partial_value.astype(jnp.bfloat16), 'sub', scatter_dimen...  10.7 us
    all_gather x1, waiting for transfers between devices, per_device(): both_cores = lax.all_gather(arrived, 'sub', axis=1, tiled=True)  8.31 us
    all_to_all x1, starting transfers between devices, per_device(): lax.all_to_all(own_sums, 'ep', split_axis=1, concat_axis=0, tiled=True)  6.89 us
    dot_general x1, matrix products, expert_block(): jnp.einsum('erf,efd->erd', hidden, expert_down, preferred_element_type=jn...  6.56 us
    unnamed x1, other arithmetic  6.21 us
    dot_general x1, matrix products, expert_block(): jnp.einsum('erd,edf->erf', expert_rows, expert_gate, preferred_element_ty...  3.83 us
  transfers between devices with their start and end apart: 3, of which 3 were waited for; matrix products, arithmetic and copies ran while one was open for 2% of the time, Pallas kernels for 0%

commit v1 on v0

v1 whole, which is shorter than its diff:
```python
import jax
import jax.numpy as jnp
from jax import lax
from jax.sharding import PartitionSpec as P

LATENT = 512


SOFTMAX_SCALE = 192.0 ** (-0.5)
ROUTE_SCALE = 2.5
LANES = 128


def attend(query_latent, latent_cache, cache_lengths):
    scores = (
        jnp.einsum("rhc,rtc->rht", query_latent, latent_cache, preferred_element_type=jnp.float32)
        * SOFTMAX_SCALE
    )
    positions = jnp.arange(latent_cache.shape[1], dtype=jnp.int32)
    visible = positions[None, None, :] < cache_lengths[:, None, None]
    scores = jnp.where(visible, scores, jnp.float32(-1e30))
    largest = jnp.max(scores, axis=2, keepdims=True)
    powered = jnp.where(visible, jnp.exp(scores - largest), jnp.float32(0.0))
    probability = (powered / jnp.sum(powered, axis=2, keepdims=True)).astype(jnp.bfloat16)
    values = latent_cache[:, :, :LATENT]
    mixed = jnp.einsum("rht,rtc->rhc", probability, values, preferred_element_type=jnp.float32)
    return mixed.astype(jnp.bfloat16)


def swap(value, axis, mask):
    count = lax.axis_size(axis)
    return lax.ppermute(value, axis, [(i, i ^ mask) for i in range(count)])


def per_device(
    hidden_in,
    expert_routes,
    route_scores,
    expert_gate,
    expert_up,
    expert_down,
    query_latent,
    latent_cache,
    cache_lengths,
):
    tok_rows, model_width = hidden_in.shape
    ep_count = lax.axis_size("ep")
    inner = 4 if ep_count % 4 == 0 else 1
    outer = ep_count // inner
    experts = ep_count

    weights = ROUTE_SCALE * route_scores / jnp.sum(route_scores, axis=1, keepdims=True)
    chosen = expert_routes[:, :, None] == jnp.arange(experts, dtype=jnp.int32)[None, None, :]
    dense = jnp.sum(jnp.where(chosen, weights[:, :, None], 0.0), axis=1)
    high = lax.reduce_precision(dense, 8, 7)
    low = dense - high
    coded = jnp.concatenate([high, low], axis=1).astype(jnp.bfloat16)
    pad = -coded.shape[1] % LANES
    coded = jnp.pad(coded, ((0, 0), (0, pad)))
    own = jnp.concatenate([hidden_in, coded], axis=1)

    column = jnp.concatenate([own] + [swap(own, "ep", inner * k) for k in range(1, outer)], axis=0)
    core = jnp.concatenate([column] + [swap(column, "ep", k) for k in range(1, inner)], axis=0)
    rows = jnp.concatenate([core, swap(core, "sub", 1)], axis=0)
    half = core.shape[0]

    expert_rows, tail = rows[:, :model_width], rows[:, model_width:].astype(jnp.float32)
    me = lax.axis_index("ep")
    lane = jnp.arange(tail.shape[1], dtype=jnp.int32)
    mine = (lane == me) | (lane == me + experts)
    weight = jnp.sum(jnp.where(mine[None, :], tail, 0.0), axis=1, keepdims=True)

    gate_value = jnp.dot(expert_rows, expert_gate[0], preferred_element_type=jnp.float32)
    up_value = jnp.dot(expert_rows, expert_up[0], preferred_element_type=jnp.float32)
    hidden = (jax.nn.silu(gate_value) * up_value * weight).astype(jnp.bfloat16)
    partial = jnp.dot(hidden, expert_down[0], preferred_element_type=jnp.float32)

    other = swap(partial[half:].astype(jnp.bfloat16), "sub", 1)
    both = (partial[:half] + other.astype(jnp.float32)).astype(jnp.bfloat16)
    block = outer * tok_rows
    pieces = [both[:block]] + [swap(both[k * block : (k + 1) * block], "ep", k) for k in range(1, inner)]
    total = sum(p.astype(jnp.float32) for p in pieces).astype(jnp.bfloat16)
    pieces = [total[:tok_rows]] + [
        swap(total[k * tok_rows : (k + 1) * tok_rows], "ep", inner * k) for k in range(1, outer)
    ]
    moe_output = sum(p.astype(jnp.float32) for p in pieces).astype(jnp.bfloat16)
    attention_latent = attend(query_latent, latent_cache, cache_lengths)
    return (moe_output, attention_latent)


def solution(mesh):
    placed = (
        P(("groups", "ep", "sub"), None),
        P(("groups", "ep", "sub"), None),
        P(("groups", "ep", "sub"), None),
        P("ep", None, "sub"),
        P("ep", None, "sub"),
        P("ep", "sub", None),
        P(("groups", "ep", "sub"), None, None),
        P(("groups", "ep", "sub"), None, None),
        P(("groups", "ep", "sub")),
    )
    return jax.shard_map(
        per_device,
        mesh=mesh,
        in_specs=placed,
        out_specs=(P(("groups", "ep", "sub"), None), P(("groups", "ep", "sub"), None, None)),
        check_vma=False,
    )
```

time: 121 us -> 72.8 us (0.60)
  blocking collectives: 32 us -> 0 us
  between operations: 14.2 us -> 0.74 us
  starting transfers between devices: 6.97 us -> 17.4 us
  waiting for transfers between devices: 38.4 us -> 28.3 us
  matrix products: 14.2 us -> 12.6 us
  local copies, waits for them, and re-layouts: 7.25 us -> 5.82 us
    all_to_all x1 -> x0, blocking collectives: 32 us -> none  [per_device(): lax.all_to_all(outgoing, 'ep', split_axis=0, concat_axis=1, tiled=True)]
    ppermute x0 -> x14, waiting for transfers between devices: none -> 28.3 us  [swap(): return lax.ppermute(value, axis, [(i, i ^ mask) for i in range(count)])]
    all_to_all x1 -> x0, waiting for transfers between devices: 19.4 us -> none  [per_device(): lax.all_to_all(own_sums, 'ep', split_axis=1, concat_axis=0, tiled=True)]
    ppermute x0 -> x14, starting transfers between devices: none -> 17.4 us  [swap(): return lax.ppermute(value, axis, [(i, i ^ mask) for i in range(count)])]
    reduce_scatter x1 -> x0, waiting for transfers between devices: 10.7 us -> none  [per_device(): lax.psum_scatter(partial_value.astype(jnp.bfloat16), 'sub', scatter_dimen...]
    all_gather x1 -> x0, waiting for transfers between devices: 8.31 us -> none  [per_device(): both_cores = lax.all_gather(arrived, 'sub', axis=1, tiled=True)]
    all_to_all x1 -> x0, starting transfers between devices: 6.89 us -> none  [per_device(): lax.all_to_all(own_sums, 'ep', split_axis=1, concat_axis=0, tiled=True)]
    unnamed x1, other arithmetic: 6.21 us -> 1.45 us
  transfers between devices with their start and end apart: 3 -> 14, of which waited for: 3 -> 9; matrix products, arithmetic and copies ran while one was open for 2% -> 8% of each run, Pallas kernels for 0% -> 0%
where the time goes in v1:
time: 72.8 us; the launch traced here: 72.5 us
  waiting for transfers between devices  28.3 us (39%)
  starting transfers between devices  17.4 us (24%)
  matrix products  12.6 us (17%)
  other arithmetic  7.68 us (11%)
  local copies, waits for them, and re-layouts  5.82 us (8%)
  between operations  0.74 us (1%)
    ppermute x14, waiting for transfers between devices, swap(): return lax.ppermute(value, axis, [(i, i ^ mask) for i in range(count)])  28.3 us
    ppermute x14, starting transfers between devices, swap(): return lax.ppermute(value, axis, [(i, i ^ mask) for i in range(count)])  17.4 us
    dot_general x1, matrix products, per_device(): jnp.dot(hidden, expert_down[0], preferred_element_type=jnp.float32)  7.18 us
    unnamed x11, local copies, waits for them, and re-layouts  3.33 us
    dot_general x1, matrix products, per_device(): jnp.dot(expert_rows, expert_up[0], preferred_element_type=jnp.float32)  3.14 us
    dot_general x1, matrix products, attend(): jnp.einsum('rht,rtc->rhc', probability, values, preferred_element_type=jn...  1.82 us
    convert_element_type x1, other arithmetic, per_device(): both = (partial[:half] + other.astype(jnp.float32)).astype(jnp.bfloat16)  1.7 us
    slice x1, local copies, waits for them, and re-layouts, per_device(): other = swap(partial[half:].astype(jnp.bfloat16), 'sub', 1)  1.59 us
  transfers between devices with their start and end apart: 14, of which 9 were waited for; matrix products, arithmetic and copies ran while one was open for 8% of the time, Pallas kernels for 0%

profile of v1, /device:TPU:0, one launch (start us, length us, event | category | flops | bytes accessed | tf_op | source)
XLA Modules:
  0.0 72.5 jit_solution(6333144880082332974)
XLA Ops:
  0.6 0.0 copy-start
  0.6 0.9 %reduce_sum.36 = f32[8]{0:T(128)S(1)} reduce(f32[8,8]{1,0:T(8,128)} %param.11, f32[]{:T(128)} %constant.5.clone.1), dimensions={1}, to_apply=%region_0.0 | reduce | flops 56 | bytes 292 | tf_op jit(solution)/shard_map/reduce_sum | solution.py:52
  1.5 0.8 %multiply_divide_fusion = f32[8,8]{1,0:T(8,128)S(1)} fusion(f32[8,8]{1,0:T(8,128)} %param.11, f32[8]{0:T(128)S(1)} %reduce_sum.36), kind=kLoop, calls=%fused_computation.53 | loop fusion | flops 128 | bytes 544 | tf_op jit(solution)/shard_map/div | solution.py:52
  2.3 0.8 %select_reduce_fusion.1 = f32[8,16]{1,0:T(8,128)S(1)} fusion(f32[8,8]{1,0:T(8,128)S(1)} %multiply_divide_fusion, s32[8,8]{1,0:T(8,128)} %param.10), kind=kLoop, calls=%fused_computation.44 | loop fusion | flops 2944 | bytes 1024 | tf_op jit(solution)/shard_map/reduce_sum | solution.py:54
  3.1 0.1 fusion.29
  3.1 1.4 %constant_dynamic-update-slice_fusion.6 = (bf16[128,3712]{1,0:T(8,128)(2,1)}, bf16[256,3712]{1,0:T(8,128)(2,1)S(1)}, bf16[8,3712]{1,0:T(8,128)(2,1)S(1)}) fusion(bf16[8,128]{1,0:T(8,128)(2,1)S(1)} %fusion.29, bf16[8,3584]{1,0:T(8,128)(2,1)} %param.9), kind=kLoop, calls=%fused_computation.35 | loop fusion | flops 118782 | bytes 237568
  4.6 3.0 %collective-permute-start = (bf16[8,3712]{1,0:T(8,128)(2,1)S(1)}, bf16[8,3712]{1,0:T(8,128)(2,1)S(1)}, u32[]{:S(2)}, u32[]{:S(2)}) collective-permute-start(bf16[8,3712]{1,0:T(8,128)(2,1)S(1)} %get-tuple-element.22), channel_id=1, source_target_pairs={{0,8},{2,10},{4,12},{6,14},{8,0},{10,2},{12,4},{14,6},{16,24},{18,... | collective-permute-start | bytes 178184 | tf_op jit(solution)/shard_map/ppermute | solution.py:32
  7.6 2.6 %collective-permute-start.1 = (bf16[8,3712]{1,0:T(8,128)(2,1)S(1)}, bf16[8,3712]{1,0:T(8,128)(2,1)S(1)}, u32[]{:S(2)}, u32[]{:S(2)}) collective-permute-start(bf16[8,3712]{1,0:T(8,128)(2,1)S(1)} %get-tuple-element.22), channel_id=1, source_target_pairs={{0,16},{2,18},{4,20},{6,22},{8,24},{10,26},{12,28},{14,30},{16,0},... | collective-permute-start | bytes 178184 | tf_op jit(solution)/shard_map/ppermute | solution.py:32
  10.2 0.0 collective-permute-start.2
  10.2 0.0 collective-permute-done
  10.2 3.7 %collective-permute-done.1 = bf16[8,3712]{1,0:T(8,128)(2,1)S(1)} collective-permute-done((bf16[8,3712]{1,0:T(8,128)(2,1)S(1)}, bf16[8,3712]{1,0:T(8,128)(2,1)S(1)}, u32[]{:S(2)}, u32[]{:S(2)}) %collective-permute-start.1) | collective-permute-done | bytes 59424 | tf_op jit(solution)/shard_map/ppermute | solution.py:32
  13.9 2.3 %collective-permute-done.2 = bf16[8,3712]{1,0:T(8,128)(2,1)S(1)} collective-permute-done((bf16[8,3712]{1,0:T(8,128)(2,1)S(1)}, bf16[8,3712]{1,0:T(8,128)(2,1)S(1)}, u32[]{:S(2)}, u32[]{:S(2)}) %collective-permute-start.2) | collective-permute-done | bytes 59424 | tf_op jit(solution)/shard_map/ppermute | solution.py:32
  16.2 0.8 %pad_maximum_fusion = bf16[32,3712]{1,0:T(8,128)(2,1)S(1)} fusion(bf16[8,3712]{1,0:T(8,128)(2,1)S(1)} %collective-permute-done.2, bf16[8,3712]{1,0:T(8,128)(2,1)S(1)} %collective-permute-done.1, bf16[8,3712]{1,0:T(8,128)(2,1)S(1)} %collective-permute-done, bf16[8,128]{1,0:T(8,128)(2,1)S(1)} %fusion.29, bf16[8,3584]{1,0:T(8,128)(2,1)} %param.9), kind=kLoop, calls=%fused_computation.25 | loop fusion | flops 1187840 | bytes 475136 | tf_op jit(solution)/shard_map/concatenate | solution.py:62
  17.1 1.6 %collective-permute-start.3 = (bf16[32,3712]{1,0:T(8,128)(2,1)S(1)}, bf16[32,3712]{1,0:T(8,128)(2,1)S(1)}, u32[]{:S(2)}, u32[]{:S(2)}) collective-permute-start(bf16[32,3712]{1,0:T(8,128)(2,1)S(1)} %pad_maximum_fusion), channel_id=1, source_target_pairs={{0,2},{2,0},{4,6},{6,4},{8,10},{10,8},{12,14},{14,12},{16,18},{18,... | collective-permute-start | bytes 712712 | tf_op jit(solution)/shard_map/ppermute | solution.py:32
  18.6 1.5 %collective-permute-start.4 = (bf16[32,3712]{1,0:T(8,128)(2,1)S(1)}, bf16[32,3712]{1,0:T(8,128)(2,1)S(1)}, u32[]{:S(2)}, u32[]{:S(2)}) collective-permute-start(bf16[32,3712]{1,0:T(8,128)(2,1)S(1)} %pad_maximum_fusion), channel_id=1, source_target_pairs={{0,4},{2,6},{4,0},{6,2},{8,12},{10,14},{12,8},{14,10},{16,20},{18,... | collective-permute-start | bytes 712712 | tf_op jit(solution)/shard_map/ppermute | solution.py:32
  20.1 0.5 collective-permute-start.5
  20.6 0.6 constant_dynamic-update-slice_fusion.5
  21.2 0.6 constant_dynamic-update-slice_fusion.4
  21.9 0.6 constant_dynamic-update-slice_fusion.3
  22.5 3.1 %collective-permute-done.3 = bf16[32,3712]{1,0:T(8,128)(2,1)S(1)} collective-permute-done((bf16[32,3712]{1,0:T(8,128)(2,1)S(1)}, bf16[32,3712]{1,0:T(8,128)(2,1)S(1)}, u32[]{:S(2)}, u32[]{:S(2)}) %collective-permute-start.3) | collective-permute-done | bytes 237600 | tf_op jit(solution)/shard_map/ppermute | solution.py:32
  25.6 0.7 constant_dynamic-update-slice_fusion.2
  26.3 3.0 %collective-permute-done.4 = bf16[32,3712]{1,0:T(8,128)(2,1)S(1)} collective-permute-done((bf16[32,3712]{1,0:T(8,128)(2,1)S(1)}, bf16[32,3712]{1,0:T(8,128)(2,1)S(1)}, u32[]{:S(2)}, u32[]{:S(2)}) %collective-permute-start.4) | collective-permute-done | bytes 237600 | tf_op jit(solution)/shard_map/ppermute | solution.py:32
  29.3 0.7 constant_dynamic-update-slice_fusion.1
  30.1 0.0 collective-permute-done.5
  30.1 0.7 constant_dynamic-update-slice_fusion
  30.8 0.0 collective-permute-start.6
  30.8 2.7 %collective-permute-done.6 = bf16[128,3712]{1,0:T(8,128)(2,1)S(1)} collective-permute-done((bf16[128,3712]{1,0:T(8,128)(2,1)}, bf16[128,3712]{1,0:T(8,128)(2,1)S(1)}, u32[]{:S(2)}, u32[]{:S(2)}) %collective-permute-start.6) | collective-permute-done | bytes 950304 | tf_op jit(solution)/shard_map/ppermute | solution.py:32
  33.5 0.1 constant_dynamic-update-slice_fusion.7
  33.6 3.1 %fusion.3 = f32[256,512]{1,0:T(8,128)S(1)} fusion(bf16[1,3584,512]{2,1,0:T(8,128)(2,1)} %param.13, bf16[256,3712]{1,0:T(8,128)(2,1)S(1)} %constant_dynamic-update-slice_fusion.7), kind=kOutput, calls=%fused_computation.3 | convolution fusion | flops 939524096 | bytes 6029312 | tf_op jit(solution)/shard_map/dot_general | solution.py:74
  36.8 0.1 select_reduce_fusion
  36.9 0.0 copy-start.2
  36.9 7.2 %fusion.1 = f32[256,3584]{1,0:T(8,128)} fusion(bf16[1,512,3584]{2,1,0:T(8,128)(2,1)} %param.14, f32[256,512]{1,0:T(8,128)S(1)} %fusion.3, bf16[1,3584,512]{2,1,0:T(8,128)(2,1)} %param.12, bf16[256,3712]{1,0:T(8,128)(2,1)S(1)} %constant_dynamic-update-slice_fusion.7, f32[256]{0:T(256)S(1)} %select_reduce_fusion), kind=kOutput, calls=%fused_computation.1 | convolution fusion | flops 1879965696 | bytes 13370368 | tf_op jit(solution)/shard_map/dot_general | solution.py:76
  44.1 1.6 %slice.82 = bf16[128,3584]{1,0:T(8,128)(2,1)S(1)} slice(f32[256,3584]{1,0:T(8,128)} %fusion.1), slice={[128:256], [0:3584]} | slice | bytes 1835008 | tf_op jit(solution)/shard_map/slice | solution.py:78
  45.7 0.2 collective-permute-start.7
  45.9 0.0 copy-done.2
  45.9 0.1 iota_compare_fusion.2
  46.0 0.0 copy-start.1
  46.0 2.3 %collective-permute-done.7 = bf16[128,3584]{1,0:T(8,128)(2,1)S(1)} collective-permute-done((bf16[128,3584]{1,0:T(8,128)(2,1)S(1)}, bf16[128,3584]{1,0:T(8,128)(2,1)S(1)}, u32[]{:S(2)}, u32[]{:S(2)}) %collective-permute-start.7) | collective-permute-done | bytes 917536 | tf_op jit(solution)/shard_map/ppermute | solution.py:32
  48.2 1.7 %fusion.7 = bf16[128,3584]{1,0:T(8,128)(2,1)S(1)} fusion(f32[256,3584]{1,0:T(8,128)} %fusion.1, bf16[128,3584]{1,0:T(8,128)(2,1)S(1)} %collective-permute-done.7), kind=kLoop, calls=%fused_computation.9 | loop fusion | flops 1376256 | bytes 3670016 | tf_op jit(solution)/shard_map/convert_element_type | solution.py:79
  50.0 1.5 %collective-permute-start.10 = (bf16[32,3584]{1,0:T(8,128)(2,1)S(1)}, bf16[32,3584]{1,0:T(8,128)(2,1)S(1)}, u32[]{:S(2)}, u32[]{:S(2)}) collective-permute-start(bf16[32,3584]{1,0:T(8,128)(2,1)S(1)} %get-tuple-element.3), channel_id=1, source_target_pairs={{0,6},{2,4},{4,2},{6,0},{8,14},{10,12},{12,10},{14,8},{16,22},{18,... | collective-permute-start | bytes 688136 | tf_op jit(solution)/shard_map/ppermute | solution.py:32
  51.5 1.5 %collective-permute-start.8 = (bf16[32,3584]{1,0:T(8,128)(2,1)S(1)}, bf16[32,3584]{1,0:T(8,128)(2,1)S(1)}, u32[]{:S(2)}, u32[]{:S(2)}) collective-permute-start(bf16[32,3584]{1,0:T(8,128)(2,1)S(1)} %get-tuple-element.2), channel_id=1, source_target_pairs={{0,2},{2,0},{4,6},{6,4},{8,10},{10,8},{12,14},{14,12},{16,18},{18,... | collective-permute-start | bytes 688136 | tf_op jit(solution)/shard_map/ppermute | solution.py:32
  53.0 0.5 collective-permute-start.9
  53.5 0.0 copy-done
  53.5 0.0 copy-done.1
  53.5 0.4 fusion.13
  54.0 0.2 fusion.35
  54.2 5.2 %collective-permute-done.10 = bf16[32,3584]{1,0:T(8,128)(2,1)S(1)} collective-permute-done((bf16[32,3584]{1,0:T(8,128)(2,1)S(1)}, bf16[32,3584]{1,0:T(8,128)(2,1)S(1)}, u32[]{:S(2)}, u32[]{:S(2)}) %collective-permute-start.10) | collective-permute-done | bytes 229408 | tf_op jit(solution)/shard_map/ppermute | solution.py:32
  59.4 4.2 %collective-permute-done.8 = bf16[32,3584]{1,0:T(8,128)(2,1)S(1)} collective-permute-done((bf16[32,3584]{1,0:T(8,128)(2,1)S(1)}, bf16[32,3584]{1,0:T(8,128)(2,1)S(1)}, u32[]{:S(2)}, u32[]{:S(2)}) %collective-permute-start.8) | collective-permute-done | bytes 229408 | tf_op jit(solution)/shard_map/ppermute | solution.py:32
  63.6 0.0 collective-permute-done.9
  63.6 0.1 add_convert_fusion
  63.7 0.1 collective-permute-start.11
  63.8 1.6 %collective-permute-start.12 = (bf16[8,3584]{1,0:T(8,128)(2,1)S(1)}, bf16[8,3584]{1,0:T(8,128)(2,1)S(1)}, u32[]{:S(2)}, u32[]{:S(2)}) collective-permute-start(bf16[8,3584]{1,0:T(8,128)(2,1)S(1)} %get-tuple-element.13), channel_id=1, source_target_pairs={{0,16},{2,18},{4,20},{6,22},{8,24},{10,26},{12,28},{14,30},{16,0},... | collective-permute-start | bytes 172040 | tf_op jit(solution)/shard_map/ppermute | solution.py:32
  65.4 2.8 %collective-permute-start.13 = (bf16[8,3584]{1,0:T(8,128)(2,1)S(1)}, bf16[8,3584]{1,0:T(8,128)(2,1)S(1)}, u32[]{:S(2)}, u32[]{:S(2)}) collective-permute-start(bf16[8,3584]{1,0:T(8,128)(2,1)S(1)} %get-tuple-element.12), channel_id=1, source_target_pairs={{0,24},{2,26},{4,28},{6,30},{8,16},{10,18},{12,20},{14,22},{16,8},... | collective-permute-start | bytes 172040 | tf_op jit(solution)/shard_map/ppermute | solution.py:32
  68.2 1.8 %convolution_convert_fusion = bf16[4,128,512]{2,1,0:T(8,128)(2,1)} fusion(bf16[4,256,576]{1,2,0:T(8,128)(2,1)S(1)} %copy-done.1, f32[4,128]{1,0:T(4,128)S(1)} %fusion.35, f32[4,128,256]{2,1,0:T(8,128)S(1)} %fusion.13, pred[4,256]{1,0:T(4,128)(4,1)S(1)} %iota_compare_fusion.2), kind=kOutput, calls=%fused_computation.12 | convolution fusion | flops 135004928 | bytes 2624512 | tf_op jit(solution)/shard_map/rht,rtc->rhc/dot_general | solution.py:26
  70.0 0.0 collective-permute-done.11
  70.0 1.8 %collective-permute-done.12 = bf16[8,3584]{1,0:T(8,128)(2,1)S(1)} collective-permute-done((bf16[8,3584]{1,0:T(8,128)(2,1)S(1)}, bf16[8,3584]{1,0:T(8,128)(2,1)S(1)}, u32[]{:S(2)}, u32[]{:S(2)}) %collective-permute-start.12) | collective-permute-done | bytes 57376 | tf_op jit(solution)/shard_map/ppermute | solution.py:32
  71.8 0.0 collective-permute-done.13
  71.8 0.7 add_convert_fusion.1
  (4 shorter events, 0.1 us)
Async XLA Ops:
  0.6 52.9 %copy-start = (bf16[4,128,576]{1,2,0:T(8,128)(2,1)S(1)}, bf16[4,128,576]{1,2,0:T(8,128)(2,1)}, u32[]{:S(2)}) copy-start(bf16[4,128,576]{1,2,0:T(8,128)(2,1)} %param.15) | copy-start | bytes 1769476
  4.6 5.6 %collective-permute-start = (bf16[8,3712]{1,0:T(8,128)(2,1)S(1)}, bf16[8,3712]{1,0:T(8,128)(2,1)S(1)}, u32[]{:S(2)}, u32[]{:S(2)}) collective-permute-start(bf16[8,3712]{1,0:T(8,128)(2,1)S(1)} %get-tuple-element.22), channel_id=1, source_target_pairs={{0,8},{2,10},{4,12},{6,14},{8,0},{10,2},{12,4},{14,6},{16,24},{18,... | collective-permute-start | bytes 178184 | tf_op jit(solution)/shard_map/ppermute | solution.py:32
  7.6 6.3 %collective-permute-start.1 = (bf16[8,3712]{1,0:T(8,128)(2,1)S(1)}, bf16[8,3712]{1,0:T(8,128)(2,1)S(1)}, u32[]{:S(2)}, u32[]{:S(2)}) collective-permute-start(bf16[8,3712]{1,0:T(8,128)(2,1)S(1)} %get-tuple-element.22), channel_id=1, source_target_pairs={{0,16},{2,18},{4,20},{6,22},{8,24},{10,26},{12,28},{14,30},{16,0},... | collective-permute-start | bytes 178184 | tf_op jit(solution)/shard_map/ppermute | solution.py:32
  10.2 6.0 %collective-permute-start.2 = (bf16[8,3712]{1,0:T(8,128)(2,1)S(1)}, bf16[8,3712]{1,0:T(8,128)(2,1)S(1)}, u32[]{:S(2)}, u32[]{:S(2)}) collective-permute-start(bf16[8,3712]{1,0:T(8,128)(2,1)S(1)} %get-tuple-element.22), channel_id=1, source_target_pairs={{0,24},{2,26},{4,28},{6,30},{8,16},{10,18},{12,20},{14,22},{16,8},... | collective-permute-start | bytes 178184 | tf_op jit(solution)/shard_map/ppermute | solution.py:32
  17.1 8.5 %collective-permute-start.3 = (bf16[32,3712]{1,0:T(8,128)(2,1)S(1)}, bf16[32,3712]{1,0:T(8,128)(2,1)S(1)}, u32[]{:S(2)}, u32[]{:S(2)}) collective-permute-start(bf16[32,3712]{1,0:T(8,128)(2,1)S(1)} %pad_maximum_fusion), channel_id=1, source_target_pairs={{0,2},{2,0},{4,6},{6,4},{8,10},{10,8},{12,14},{14,12},{16,18},{18,... | collective-permute-start | bytes 712712 | tf_op jit(solution)/shard_map/ppermute | solution.py:32
  18.6 10.7 %collective-permute-start.4 = (bf16[32,3712]{1,0:T(8,128)(2,1)S(1)}, bf16[32,3712]{1,0:T(8,128)(2,1)S(1)}, u32[]{:S(2)}, u32[]{:S(2)}) collective-permute-start(bf16[32,3712]{1,0:T(8,128)(2,1)S(1)} %pad_maximum_fusion), channel_id=1, source_target_pairs={{0,4},{2,6},{4,0},{6,2},{8,12},{10,14},{12,8},{14,10},{16,20},{18,... | collective-permute-start | bytes 712712 | tf_op jit(solution)/shard_map/ppermute | solution.py:32
  20.1 9.9 %collective-permute-start.5 = (bf16[32,3712]{1,0:T(8,128)(2,1)S(1)}, bf16[32,3712]{1,0:T(8,128)(2,1)S(1)}, u32[]{:S(2)}, u32[]{:S(2)}) collective-permute-start(bf16[32,3712]{1,0:T(8,128)(2,1)S(1)} %pad_maximum_fusion), channel_id=1, source_target_pairs={{0,6},{2,4},{4,2},{6,0},{8,14},{10,12},{12,10},{14,8},{16,22},{18,... | collective-permute-start | bytes 712712 | tf_op jit(solution)/shard_map/ppermute | solution.py:32
  30.8 2.7 %collective-permute-start.6 = (bf16[128,3712]{1,0:T(8,128)(2,1)}, bf16[128,3712]{1,0:T(8,128)(2,1)S(1)}, u32[]{:S(2)}, u32[]{:S(2)}) collective-permute-start(bf16[128,3712]{1,0:T(8,128)(2,1)} %get-tuple-element.5), channel_id=1, source_target_pairs={{0,1},{1,0},{2,3},{3,2},{4,5},{5,4},{6,7},{7,6},{8,9},{9,8},{10,11... | collective-permute-start | bytes 2850824 | tf_op jit(solution)/shard_map/ppermute | solution.py:32
  36.9 9.0 %copy-start.2 = (s32[4]{0:T(128)S(1)}, s32[4]{0:T(128)}, u32[]{:S(2)}) copy-start(s32[4]{0:T(128)} %param.17) | copy-start | bytes 52
  45.7 2.5 %collective-permute-start.7 = (bf16[128,3584]{1,0:T(8,128)(2,1)S(1)}, bf16[128,3584]{1,0:T(8,128)(2,1)S(1)}, u32[]{:S(2)}, u32[]{:S(2)}) collective-permute-start(bf16[128,3584]{1,0:T(8,128)(2,1)S(1)} %slice.82), channel_id=1, source_target_pairs={{0,1},{1,0},{2,3},{3,2},{4,5},{5,4},{6,7},{7,6},{8,9},{9,8},{10,11... | collective-permute-start | bytes 2752520 | tf_op jit(solution)/shard_map/ppermute | solution.py:32
  46.0 7.6 %copy-start.1 = (bf16[4,256,576]{1,2,0:T(8,128)(2,1)S(1)}, bf16[4,256,576]{1,2,0:T(8,128)(2,1)}, u32[]{:S(2)}) copy-start(bf16[4,256,576]{1,2,0:T(8,128)(2,1)} %param.16) | copy-start | bytes 3538948
  50.0 9.5 %collective-permute-start.10 = (bf16[32,3584]{1,0:T(8,128)(2,1)S(1)}, bf16[32,3584]{1,0:T(8,128)(2,1)S(1)}, u32[]{:S(2)}, u32[]{:S(2)}) collective-permute-start(bf16[32,3584]{1,0:T(8,128)(2,1)S(1)} %get-tuple-element.3), channel_id=1, source_target_pairs={{0,6},{2,4},{4,2},{6,0},{8,14},{10,12},{12,10},{14,8},{16,22},{18,... | collective-permute-start | bytes 688136 | tf_op jit(solution)/shard_map/ppermute | solution.py:32
  51.5 12.1 %collective-permute-start.8 = (bf16[32,3584]{1,0:T(8,128)(2,1)S(1)}, bf16[32,3584]{1,0:T(8,128)(2,1)S(1)}, u32[]{:S(2)}, u32[]{:S(2)}) collective-permute-start(bf16[32,3584]{1,0:T(8,128)(2,1)S(1)} %get-tuple-element.2), channel_id=1, source_target_pairs={{0,2},{2,0},{4,6},{6,4},{8,10},{10,8},{12,14},{14,12},{16,18},{18,... | collective-permute-start | bytes 688136 | tf_op jit(solution)/shard_map/ppermute | solution.py:32
  53.0 10.6 %collective-permute-start.9 = (bf16[32,3584]{1,0:T(8,128)(2,1)S(1)}, bf16[32,3584]{1,0:T(8,128)(2,1)S(1)}, u32[]{:S(2)}, u32[]{:S(2)}) collective-permute-start(bf16[32,3584]{1,0:T(8,128)(2,1)S(1)} %get-tuple-element.4), channel_id=1, source_target_pairs={{0,4},{2,6},{4,0},{6,2},{8,12},{10,14},{12,8},{14,10},{16,20},{18,... | collective-permute-start | bytes 688136 | tf_op jit(solution)/shard_map/ppermute | solution.py:32
  63.7 6.3 %collective-permute-start.11 = (bf16[8,3584]{1,0:T(8,128)(2,1)S(1)}, bf16[8,3584]{1,0:T(8,128)(2,1)S(1)}, u32[]{:S(2)}, u32[]{:S(2)}) collective-permute-start(bf16[8,3584]{1,0:T(8,128)(2,1)S(1)} %get-tuple-element.11), channel_id=1, source_target_pairs={{0,8},{2,10},{4,12},{6,14},{8,0},{10,2},{12,4},{14,6},{16,24},{18,... | collective-permute-start | bytes 172040 | tf_op jit(solution)/shard_map/ppermute | solution.py:32
  63.8 8.0 %collective-permute-start.12 = (bf16[8,3584]{1,0:T(8,128)(2,1)S(1)}, bf16[8,3584]{1,0:T(8,128)(2,1)S(1)}, u32[]{:S(2)}, u32[]{:S(2)}) collective-permute-start(bf16[8,3584]{1,0:T(8,128)(2,1)S(1)} %get-tuple-element.13), channel_id=1, source_target_pairs={{0,16},{2,18},{4,20},{6,22},{8,24},{10,26},{12,28},{14,30},{16,0},... | collective-permute-start | bytes 172040 | tf_op jit(solution)/shard_map/ppermute | solution.py:32
  65.4 6.4 %collective-permute-start.13 = (bf16[8,3584]{1,0:T(8,128)(2,1)S(1)}, bf16[8,3584]{1,0:T(8,128)(2,1)S(1)}, u32[]{:S(2)}, u32[]{:S(2)}) collective-permute-start(bf16[8,3584]{1,0:T(8,128)(2,1)S(1)} %get-tuple-element.12), channel_id=1, source_target_pairs={{0,24},{2,26},{4,28},{6,30},{8,16},{10,18},{12,20},{14,22},{16,8},... | collective-permute-start | bytes 172040 | tf_op jit(solution)/shard_map/ppermute | solution.py:32

commit v2 on v1

v2 whole, which is shorter than its diff:
```python
import jax
import jax.numpy as jnp
from jax import lax
from jax.experimental import pallas as pl
from jax.experimental.pallas import tpu as pltpu
from jax.sharding import PartitionSpec as P

LATENT = 512


SOFTMAX_SCALE = 192.0 ** (-0.5)
ROUTE_SCALE = 2.5
LANES = 128


def attend(query_latent, latent_cache, cache_lengths):
    scores = (
        jnp.einsum("rhc,rtc->rht", query_latent, latent_cache, preferred_element_type=jnp.float32)
        * SOFTMAX_SCALE
    )
    positions = jnp.arange(latent_cache.shape[1], dtype=jnp.int32)
    visible = positions[None, None, :] < cache_lengths[:, None, None]
    scores = jnp.where(visible, scores, jnp.float32(-1e30))
    largest = jnp.max(scores, axis=2, keepdims=True)
    powered = jnp.where(visible, jnp.exp(scores - largest), jnp.float32(0.0))
    probability = (powered / jnp.sum(powered, axis=2, keepdims=True)).astype(jnp.bfloat16)
    values = latent_cache[:, :, :LATENT]
    mixed = jnp.einsum("rht,rtc->rhc", probability, values, preferred_element_type=jnp.float32)
    return mixed.astype(jnp.bfloat16)


def rounds_up(value, step):
    return -(-value // step) * step


def pack_kernel(hidden_ref, routes_ref, scores_ref, out_ref):
    rows, model_width = hidden_ref.shape
    scores = scores_ref[...]
    routes = routes_ref[...]
    weights = ROUTE_SCALE * scores / jnp.sum(scores, axis=1, keepdims=True)
    lanes = out_ref.shape[1] - model_width
    lane = lax.broadcasted_iota(jnp.int32, (rows, lanes), 1)
    experts = lanes // 2
    dense = jnp.zeros((rows, lanes), jnp.float32)
    for k in range(routes.shape[1]):
        named = routes[:, k : k + 1]
        dense += jnp.where((lane == named) | (lane == named + experts), weights[:, k : k + 1], 0.0)
    high = dense.astype(jnp.bfloat16)
    low = (dense - high.astype(jnp.float32)).astype(jnp.bfloat16)
    out_ref[:, :model_width] = hidden_ref[...]
    out_ref[:, model_width:] = jnp.where(lane < experts, high.astype(jnp.float32), low.astype(jnp.float32)).astype(
        jnp.bfloat16
    )


def pack(hidden_in, expert_routes, route_scores, experts):
    rows, model_width = hidden_in.shape
    lanes = rounds_up(2 * experts, LANES)
    return pl.pallas_call(
        pack_kernel,
        out_shape=jax.ShapeDtypeStruct((rows, model_width + lanes), jnp.bfloat16),
        compiler_params=pltpu.CompilerParams(vmem_limit_bytes=2 << 20),
        cost_estimate=pl.CostEstimate(flops=1 << 16, bytes_accessed=4 * rows * model_width, transcendentals=0),
    )(hidden_in, expert_routes, route_scores)


def expert_kernel(me_ref, rows_ref, gate_ref, up_ref, down_ref, mine_ref, other_ref, hidden_ref):
    total, _ = rows_ref.shape
    model_width, units = gate_ref.shape
    lanes = rows_ref.shape[1] - model_width
    half = total // 2
    me = me_ref[0]
    block = min(total, 256)
    chunk = 256

    @pl.loop(0, total // block)
    def _(i):
        here = pl.ds(pl.multiple_of(i * block, block), block)
        tail = rows_ref[here, model_width:].astype(jnp.float32)
        lane = lax.broadcasted_iota(jnp.int32, (block, lanes), 1)
        taken = (lane == me) | (lane == me + lanes // 2)
        weight = jnp.sum(jnp.where(taken, tail, 0.0), axis=1, keepdims=True)
        for c in range(units // chunk):
            cols = slice(c * chunk, (c + 1) * chunk)
            x = rows_ref[here, :model_width]
            gate_value = jnp.dot(x, gate_ref[:, cols], preferred_element_type=jnp.float32)
            up_value = jnp.dot(x, up_ref[:, cols], preferred_element_type=jnp.float32)
            value = gate_value / (1.0 + jnp.exp(-gate_value)) * up_value * weight
            hidden_ref[here, cols] = value.astype(jnp.bfloat16)

    step = 512

    @pl.loop(0, model_width // step)
    def _(c):
        cols = pl.ds(pl.multiple_of(c * step, step), step)
        for i in range(total // block):
            value = jnp.dot(
                hidden_ref[i * block : (i + 1) * block, :], down_ref[:, cols], preferred_element_type=jnp.float32
            ).astype(jnp.bfloat16)
            low, high = i * block, (i + 1) * block
            if high <= half:
                mine_ref[low:high, cols] = value
            elif low >= half:
                other_ref[low - half : high - half, cols] = value
            else:
                mine_ref[low:half, cols] = value[: half - low]
                other_ref[: high - half, cols] = value[half - low :]


def expert_block(rows, expert_gate, expert_up, expert_down, me):
    total, width = rows.shape
    model_width, units = expert_gate.shape
    half = total // 2
    vmem = pl.BlockSpec(memory_space=pltpu.VMEM)
    out = jax.ShapeDtypeStruct((half, model_width), jnp.bfloat16)
    weights = [pltpu.with_memory_space_constraint(w, pltpu.VMEM) for w in (expert_gate, expert_up, expert_down)]
    return pl.pallas_call(
        expert_kernel,
        out_shape=(out, out),
        in_specs=[pl.BlockSpec(memory_space=pltpu.SMEM), vmem, vmem, vmem, vmem],
        out_specs=(vmem, vmem),
        scratch_shapes=[pltpu.VMEM((total, units), jnp.bfloat16)],
        compiler_params=pltpu.CompilerParams(vmem_limit_bytes=(16 << 20) + 8 * total * width),
        cost_estimate=pl.CostEstimate(
            flops=6 * total * model_width * units,
            bytes_accessed=6 * model_width * units + 4 * total * width,
            transcendentals=total * units,
        ),
    )(me.reshape(1), rows, *weights)


def per_device(
    hidden_in,
    expert_routes,
    route_scores,
    expert_gate,
    expert_up,
    expert_down,
    query_latent,
    latent_cache,
    cache_lengths,
):
    tok_rows, model_width = hidden_in.shape
    ep_count, sub_count = lax.axis_size("ep"), lax.axis_size("sub")
    inner = 4 if ep_count % 4 == 0 else 1
    outer = ep_count // inner

    def swap(value, even, odd):
        pairs = [
            (i * sub_count + s, (i ^ (odd if s else even)) * sub_count + s)
            for i in range(ep_count)
            for s in range(sub_count)
        ]
        return lax.ppermute(value, ("ep", "sub"), pairs)

    def first(value, k):
        return swap(value, inner * k, k if inner == outer else inner * k)

    def second(value, k):
        return swap(value, k, inner * k if inner == outer else k)

    def over_cores(value):
        return lax.ppermute(value, "sub", [(i, i ^ 1) for i in range(sub_count)])

    def order(count):
        return list(range(1, count))[::-1]

    own = pack(hidden_in, expert_routes, route_scores, ep_count)
    near = {k: first(own, k) for k in order(outer)}
    side = {k: second(own, k) for k in order(inner)}
    column = jnp.concatenate([near[k] for k in range(1, outer)], axis=0)
    far = {k: second(column, k) for k in (order(inner)[1:] + order(inner)[:1])}
    core = jnp.concatenate(
        [own, column] + [side[k] for k in range(1, inner)] + [far[k] for k in range(1, inner)], axis=0
    )
    rows = jnp.concatenate([core, over_cores(core)], axis=0)

    mine, other = expert_block(rows, expert_gate[0], expert_up[0], expert_down[0], lax.axis_index("ep"))

    both = (mine.astype(jnp.float32) + over_cores(other).astype(jnp.float32)).astype(jnp.bfloat16)
    place = {}
    at = outer * tok_rows
    for k in range(1, inner):
        place["side", k] = both[at : at + tok_rows]
        at += tok_rows
    for k in range(1, inner):
        place["far", k] = both[at : at + (outer - 1) * tok_rows]
        at += (outer - 1) * tok_rows
    far = [second(place["far", k], k) for k in order(inner)]
    side = [second(place["side", k], k) for k in order(inner)]
    column = (
        both[tok_rows : outer * tok_rows].astype(jnp.float32) + sum(p.astype(jnp.float32) for p in far)
    ).astype(jnp.bfloat16)
    near = [first(column[(k - 1) * tok_rows : k * tok_rows], k) for k in order(outer)]
    moe_output = (
        both[:tok_rows].astype(jnp.float32) + sum(p.astype(jnp.float32) for p in side + near)
    ).astype(jnp.bfloat16)
    attention_latent = attend(query_latent, latent_cache, cache_lengths)
    return (moe_output, attention_latent)


def solution(mesh):
    placed = (
        P(("groups", "ep", "sub"), None),
        P(("groups", "ep", "sub"), None),
        P(("groups", "ep", "sub"), None),
        P("ep", None, "sub"),
        P("ep", None, "sub"),
        P("ep", "sub", None),
        P(("groups", "ep", "sub"), None, None),
        P(("groups", "ep", "sub"), None, None),
        P(("groups", "ep", "sub")),
    )
    return jax.shard_map(
        per_device,
        mesh=mesh,
        in_specs=placed,
        out_specs=(P(("groups", "ep", "sub"), None), P(("groups", "ep", "sub"), None, None)),
        check_vma=False,
    )
```

time: 72.8 us -> 60.3 us (0.83)
  waiting for transfers between devices: 28.3 us -> 9.42 us
  local copies, waits for them, and re-layouts: 5.82 us -> 16.4 us
  matrix products: 12.6 us -> 2.92 us
  starting transfers between devices: 17.4 us -> 24.2 us
  other arithmetic: 7.68 us -> 1.88 us
  Pallas kernels: 0 us -> 4.44 us
    ppermute x14 -> x20, waiting for transfers between devices: 28.3 us -> 9.42 us  [the longest x18 5.7 us: swap(): return lax.ppermute(value, ('ep', 'sub'), pairs)]
    unnamed x11 -> x31, local copies, waits for them, and re-layouts: 3.33 us -> 14.2 us
    dot_general x2 -> x0, matrix products: 10.3 us -> none  [the longest x1 7.18 us: per_device(): jnp.dot(hidden, expert_down[0], preferred_element_type=jnp.float32)]
    ppermute x14 -> x20, starting transfers between devices: 17.4 us -> 24.2 us  [the longest x18 24 us: swap(): return lax.ppermute(value, ('ep', 'sub'), pairs)]
    pallas_call x0 -> x2, Pallas kernels: none -> 4.44 us  [the longest x1 4.26 us: expert_block(): pl.pallas_call(expert_kernel, out_shape=(out, out), in_specs=[pl.BlockSpe...]
    reduce_sum x3 -> x0, other arithmetic: 1.75 us -> none  [the longest x1 0.87 us: per_device(): jnp.sum(route_scores, axis=1, keepdims=True)]
    convert_element_type x3, other arithmetic: 2.47 us -> 0.98 us  [the longest x1 0.68 us: per_device(): moe_output = (both[:tok_rows].astype(jnp.float32) + sum((p.astype(jnp.flo...]
    unnamed x1 -> x0, other arithmetic: 1.45 us -> none
  transfers between devices with their start and end apart: 14 -> 20, of which waited for: 9 -> 10; matrix products, arithmetic and copies ran while one was open for 8% -> 18% of each run, Pallas kernels for 0% -> 0%
where the time goes in v2:
time: 60.3 us; the launch traced here: 60 us
  starting transfers between devices  24.2 us (40%)
  local copies, waits for them, and re-layouts  16.4 us (27%)
  waiting for transfers between devices  9.42 us (16%)
  Pallas kernels  4.44 us (7%)
  matrix products  2.92 us (5%)
  other arithmetic  1.88 us (3%)
  between operations  0.75 us (1%)
    ppermute x18, starting transfers between devices, swap(): return lax.ppermute(value, ('ep', 'sub'), pairs)  24 us
    unnamed x31, local copies, waits for them, and re-layouts  14.2 us
    ppermute x18, waiting for transfers between devices, swap(): return lax.ppermute(value, ('ep', 'sub'), pairs)  5.7 us
    pallas_call x1, Pallas kernels, expert_block(): pl.pallas_call(expert_kernel, out_shape=(out, out), in_specs=[pl.BlockSpe...  4.26 us
    ppermute x2, waiting for transfers between devices, over_cores(): return lax.ppermute(value, 'sub', [(i, i ^ 1) for i in range(sub_count)])  3.71 us
    dot_general x1, matrix products, attend(): jnp.einsum('rht,rtc->rhc', probability, values, preferred_element_type=jn...  2.49 us
  transfers between devices with their start and end apart: 20, of which 10 were waited for; matrix products, arithmetic and copies ran while one was open for 18% of the time, Pallas kernels for 0%

profile of v2, /device:TPU:0, one launch (start us, length us, event | category | flops | bytes accessed | tf_op | source)
XLA Modules:
  0.0 60.0 jit_solution(10222968623766498982)
XLA Ops:
  0.6 0.0 copy-start
  0.7 0.9 %copy-done.4 = bf16[8,3584]{1,0:T(8,128)(2,1)S(1)} copy-done((bf16[8,3584]{1,0:T(8,128)(2,1)S(1)}, bf16[8,3584]{1,0:T(8,128)(2,1)}, u32[]{:S(2)}) %copy-start.4) | copy-done | bytes 57368
  1.5 0.7 %copy-done.5 = s32[8,8]{1,0:T(8,128)S(1)} copy-done((s32[8,8]{1,0:T(8,128)S(1)}, s32[8,8]{1,0:T(8,128)}, u32[]{:S(2)}) %copy-start.5) | copy-done | bytes 280
  2.2 0.7 %copy-done.6 = f32[8,8]{1,0:T(8,128)S(1)} copy-done((f32[8,8]{1,0:T(8,128)S(1)}, f32[8,8]{1,0:T(8,128)}, u32[]{:S(2)}) %copy-start.6) | copy-done | bytes 280
  2.9 0.2 shard_map.104
  3.1 3.1 %collective-permute-start = (bf16[8,3712]{1,0:T(8,128)(2,1)S(1)}, bf16[8,3712]{1,0:T(8,128)(2,1)S(1)}, u32[]{:S(2)}, u32[]{:S(2)}) collective-permute-start(bf16[8,3712]{1,0:T(8,128)(2,1)S(1)} %shard_map.104), channel_id=1, source_target_pairs={{0,8},{1,3},{2,10},{3,1},{4,12},{5,7},{6,14},{7,5},{8,0},{9,11},{1... | collective-permute-start | bytes 178184 | tf_op jit(solution)/shard_map/ppermute | solution.py:154
  6.2 2.6 %collective-permute-start.1 = (bf16[8,3712]{1,0:T(8,128)(2,1)S(1)}, bf16[8,3712]{1,0:T(8,128)(2,1)S(1)}, u32[]{:S(2)}, u32[]{:S(2)}) collective-permute-start(bf16[8,3712]{1,0:T(8,128)(2,1)S(1)} %shard_map.104), channel_id=1, source_target_pairs={{0,16},{1,5},{2,18},{3,7},{4,20},{5,1},{6,22},{7,3},{8,24},{9,13},... | collective-permute-start | bytes 178184 | tf_op jit(solution)/shard_map/ppermute | solution.py:154
  8.8 0.0 collective-permute-start.2
  8.8 1.7 %collective-permute-start.3 = (bf16[8,3712]{1,0:T(8,128)(2,1)S(1)}, bf16[8,3712]{1,0:T(8,128)(2,1)S(1)}, u32[]{:S(2)}, u32[]{:S(2)}) collective-permute-start(bf16[8,3712]{1,0:T(8,128)(2,1)S(1)} %shard_map.104), channel_id=1, source_target_pairs={{0,2},{1,9},{2,0},{3,11},{4,6},{5,13},{6,4},{7,15},{8,10},{9,1},{1... | collective-permute-start | bytes 178184 | tf_op jit(solution)/shard_map/ppermute | solution.py:154
  10.5 1.5 %collective-permute-start.4 = (bf16[8,3712]{1,0:T(8,128)(2,1)S(1)}, bf16[8,3712]{1,0:T(8,128)(2,1)S(1)}, u32[]{:S(2)}, u32[]{:S(2)}) collective-permute-start(bf16[8,3712]{1,0:T(8,128)(2,1)S(1)} %shard_map.104), channel_id=1, source_target_pairs={{0,4},{1,17},{2,6},{3,19},{4,0},{5,21},{6,2},{7,23},{8,12},{9,25},... | collective-permute-start | bytes 178184 | tf_op jit(solution)/shard_map/ppermute | solution.py:154
  12.0 0.6 %constant_dynamic-update-slice_fusion.12 = (bf16[128,3712]{1,0:T(8,128)(2,1)}, bf16[256,3712]{1,0:T(8,128)(2,1)S(1)}) fusion(bf16[8,3712]{1,0:T(8,128)(2,1)S(1)} %shard_map.104), kind=kLoop, calls=%fused_computation.25 | loop fusion | bytes 178176
  12.6 0.0 collective-permute-done
  12.6 0.3 collective-permute-start.5
  12.9 0.6 %constant_dynamic-update-slice_fusion.11 = (bf16[128,3712]{1,0:T(8,128)(2,1)}, bf16[256,3712]{1,0:T(8,128)(2,1)S(1)}, bf16[24,3712]{1,0:T(8,128)(2,1)S(1)}) fusion(bf16[128,3712]{1,0:T(8,128)(2,1)} %get-tuple-element.36, bf16[8,3712]{1,0:T(8,128)(2,1)S(1)} %collective-permute-done, bf16[256,3712]{1,0:T(8,128)(2,1)S(1)} %get-tuple-element.37), kind=kLoop, calls=%fused_computation.24 | loop fusion | bytes 237568
  13.5 0.0 collective-permute-done.1
  13.5 0.6 %constant_dynamic-update-slice_fusion.10 = (bf16[128,3712]{1,0:T(8,128)(2,1)}, bf16[256,3712]{1,0:T(8,128)(2,1)S(1)}, bf16[24,3712]{1,0:T(8,128)(2,1)S(1)}) fusion(bf16[128,3712]{1,0:T(8,128)(2,1)} %get-tuple-element.33, bf16[8,3712]{1,0:T(8,128)(2,1)S(1)} %collective-permute-done.1, bf16[256,3712]{1,0:T(8,128)(2,1)S(1)} %get-tuple-element.34, ...), kind=kLoop, calls=%fused_computation.23 | loop fusion | bytes 237568
  14.2 0.7 %collective-permute-done.2 = bf16[8,3712]{1,0:T(8,128)(2,1)S(1)} collective-permute-done((bf16[8,3712]{1,0:T(8,128)(2,1)S(1)}, bf16[8,3712]{1,0:T(8,128)(2,1)S(1)}, u32[]{:S(2)}, u32[]{:S(2)}) %collective-permute-start.2) | collective-permute-done | bytes 59424 | tf_op jit(solution)/shard_map/ppermute | solution.py:154
  14.9 0.6 %constant_dynamic-update-slice_fusion.9 = (bf16[128,3712]{1,0:T(8,128)(2,1)}, bf16[256,3712]{1,0:T(8,128)(2,1)S(1)}, bf16[24,3712]{1,0:T(8,128)(2,1)S(1)}) fusion(bf16[128,3712]{1,0:T(8,128)(2,1)} %get-tuple-element.30, bf16[8,3712]{1,0:T(8,128)(2,1)S(1)} %collective-permute-done.2, bf16[256,3712]{1,0:T(8,128)(2,1)S(1)} %get-tuple-element.31, ...), kind=kLoop, calls=%fused_computation.22 | loop fusion | bytes 237568
  15.5 1.5 %collective-permute-start.6 = (bf16[24,3712]{1,0:T(8,128)(2,1)S(1)}, bf16[24,3712]{1,0:T(8,128)(2,1)S(1)}, u32[]{:S(2)}, u32[]{:S(2)}) collective-permute-start(bf16[24,3712]{1,0:T(8,128)(2,1)S(1)} %get-tuple-element.29), channel_id=1, source_target_pairs={{0,2},{1,9},{2,0},{3,11},{4,6},{5,13},{6,4},{7,15},{8,10},{9,1},{1... | collective-permute-start | bytes 534536 | tf_op jit(solution)/shard_map/ppermute | solution.py:154
  17.0 1.5 %collective-permute-start.7 = (bf16[24,3712]{1,0:T(8,128)(2,1)S(1)}, bf16[24,3712]{1,0:T(8,128)(2,1)S(1)}, u32[]{:S(2)}, u32[]{:S(2)}) collective-permute-start(bf16[24,3712]{1,0:T(8,128)(2,1)S(1)} %get-tuple-element.29), channel_id=1, source_target_pairs={{0,4},{1,17},{2,6},{3,19},{4,0},{5,21},{6,2},{7,23},{8,12},{9,25},... | collective-permute-start | bytes 534536 | tf_op jit(solution)/shard_map/ppermute | solution.py:154
  18.5 0.0 collective-permute-done.3
  18.5 0.5 collective-permute-start.8
  19.0 0.6 %constant_dynamic-update-slice_fusion.8 = (bf16[128,3712]{1,0:T(8,128)(2,1)}, bf16[256,3712]{1,0:T(8,128)(2,1)S(1)}) fusion(bf16[128,3712]{1,0:T(8,128)(2,1)} %get-tuple-element.27, bf16[8,3712]{1,0:T(8,128)(2,1)S(1)} %collective-permute-done.3, bf16[256,3712]{1,0:T(8,128)(2,1)S(1)} %get-tuple-element.28), kind=kLoop, calls=%fused_computation.21 | loop fusion | bytes 178176
  19.6 0.6 %constant_dynamic-update-slice_fusion.7 = (bf16[128,3712]{1,0:T(8,128)(2,1)}, bf16[256,3712]{1,0:T(8,128)(2,1)S(1)}) fusion(bf16[128,3712]{1,0:T(8,128)(2,1)} %get-tuple-element.25, bf16[8,3712]{1,0:T(8,128)(2,1)S(1)} %collective-permute-done.4, bf16[256,3712]{1,0:T(8,128)(2,1)S(1)} %get-tuple-element.26), kind=kLoop, calls=%fused_computation.20 | loop fusion | bytes 178176
  20.3 0.6 %constant_dynamic-update-slice_fusion.6 = (bf16[128,3712]{1,0:T(8,128)(2,1)}, bf16[256,3712]{1,0:T(8,128)(2,1)S(1)}) fusion(bf16[128,3712]{1,0:T(8,128)(2,1)} %get-tuple-element.23, bf16[8,3712]{1,0:T(8,128)(2,1)S(1)} %collective-permute-done.5, bf16[256,3712]{1,0:T(8,128)(2,1)S(1)} %get-tuple-element.24), kind=kLoop, calls=%fused_computation.19 | loop fusion | bytes 178176
  20.9 0.1 collective-permute-done.6
  21.0 0.7 %constant_dynamic-update-slice_fusion.5 = (bf16[128,3712]{1,0:T(8,128)(2,1)}, bf16[256,3712]{1,0:T(8,128)(2,1)S(1)}) fusion(bf16[128,3712]{1,0:T(8,128)(2,1)} %get-tuple-element.21, bf16[24,3712]{1,0:T(8,128)(2,1)S(1)} %collective-permute-done.6, bf16[256,3712]{1,0:T(8,128)(2,1)S(1)} %get-tuple-element.22), kind=kLoop, calls=%fused_computation.18 | loop fusion | bytes 534528
  21.7 1.8 %collective-permute-done.7 = bf16[24,3712]{1,0:T(8,128)(2,1)S(1)} collective-permute-done((bf16[24,3712]{1,0:T(8,128)(2,1)S(1)}, bf16[24,3712]{1,0:T(8,128)(2,1)S(1)}, u32[]{:S(2)}, u32[]{:S(2)}) %collective-permute-start.7) | collective-permute-done | bytes 178208 | tf_op jit(solution)/shard_map/ppermute | solution.py:154
  23.4 0.7 %constant_dynamic-update-slice_fusion.4 = (bf16[128,3712]{1,0:T(8,128)(2,1)}, bf16[256,3712]{1,0:T(8,128)(2,1)S(1)}) fusion(bf16[128,3712]{1,0:T(8,128)(2,1)} %get-tuple-element.16, bf16[24,3712]{1,0:T(8,128)(2,1)S(1)} %collective-permute-done.7, bf16[256,3712]{1,0:T(8,128)(2,1)S(1)} %get-tuple-element.17), kind=kLoop, calls=%fused_computation.17 | loop fusion | bytes 534528
  24.1 0.8 %collective-permute-done.8 = bf16[24,3712]{1,0:T(8,128)(2,1)S(1)} collective-permute-done((bf16[24,3712]{1,0:T(8,128)(2,1)S(1)}, bf16[24,3712]{1,0:T(8,128)(2,1)S(1)}, u32[]{:S(2)}, u32[]{:S(2)}) %collective-permute-start.8) | collective-permute-done | bytes 178208 | tf_op jit(solution)/shard_map/ppermute | solution.py:154
  24.9 0.7 %constant_dynamic-update-slice_fusion.3 = (bf16[128,3712]{1,0:T(8,128)(2,1)}, bf16[256,3712]{1,0:T(8,128)(2,1)S(1)}) fusion(bf16[128,3712]{1,0:T(8,128)(2,1)} %get-tuple-element.14, bf16[24,3712]{1,0:T(8,128)(2,1)S(1)} %collective-permute-done.8, bf16[256,3712]{1,0:T(8,128)(2,1)S(1)} %get-tuple-element.15), kind=kLoop, calls=%fused_computation.16 | loop fusion | bytes 534528 | tf_op jit(solution)/shard_map/concatenate | solution.py:173
  25.6 0.0 collective-permute-start.9
  25.6 2.7 %collective-permute-done.9 = bf16[128,3712]{1,0:T(8,128)(2,1)S(1)} collective-permute-done((bf16[128,3712]{1,0:T(8,128)(2,1)}, bf16[128,3712]{1,0:T(8,128)(2,1)S(1)}, u32[]{:S(2)}, u32[]{:S(2)}) %collective-permute-start.9) | collective-permute-done | bytes 950304 | tf_op jit(solution)/shard_map/ppermute | solution.py:163
  28.3 0.1 constant_dynamic-update-slice_fusion.13.rows_ref
  28.4 0.0 copy-start.1
  28.5 2.0 %copy-done.1 = bf16[1,3584,512]{2,1,0:T(8,128)(2,1)S(1)} copy-done((bf16[1,3584,512]{2,1,0:T(8,128)(2,1)S(1)}, bf16[1,3584,512]{2,1,0:T(8,128)(2,1)}, u32[]{:S(2)}) %copy-start.1) | copy-done | bytes 3670040
  30.5 2.0 %copy-done.2 = bf16[1,3584,512]{2,1,0:T(8,128)(2,1)S(1)} copy-done((bf16[1,3584,512]{2,1,0:T(8,128)(2,1)S(1)}, bf16[1,3584,512]{2,1,0:T(8,128)(2,1)}, u32[]{:S(2)}) %copy-start.2) | copy-done | bytes 3670040
  32.5 2.0 %copy-done.3 = bf16[1,512,3584]{2,1,0:T(8,128)(2,1)S(1)} copy-done((bf16[1,512,3584]{2,1,0:T(8,128)(2,1)S(1)}, bf16[1,512,3584]{2,1,0:T(8,128)(2,1)}, u32[]{:S(2)}) %copy-start.3) | copy-done | bytes 3670040
  34.6 4.3 %shard_map.105 = (bf16[128,3584]{1,0:T(8,128)(2,1)S(1)}, bf16[128,3584]{1,0:T(8,128)(2,1)S(1)}) custom-call(s32[1]{0:T(128)} %bitcast.me_ref, bf16[256,3712]{1,0:T(8,128)(2,1)S(1)} %constant_dynamic-update-slice_fusion.13.rows_ref, bf16[3584,512]{1,0:T(8,128)(2,1)S(1)} %bitcast.8, bf16[3584,512]{1,0:T(8,128)(2,1)S(1)} %bitcast.9, bf16[512,3584]{1,0:T(8,128)(2,1)S(1)} %bitcast.10), custom_call_target="tpu_custom_call" | custom-call | flops 2818572288 | bytes 14811136 | tf_op jit(solution)/shard_map/pallas_call | solution.py:117
  38.8 0.2 collective-permute-start.10
  39.0 0.1 iota_compare_fusion
  39.1 0.4 fusion.4
  39.6 0.8 %fusion.12 = f32[4,128]{1,0:T(4,128)} fusion(f32[4,128,256]{2,1,0:T(8,128)S(1)} %fusion.4, pred[4,256]{1,0:T(4,128)(4,1)S(1)} %iota_compare_fusion), kind=kOutput, calls=%fused_computation.43 | output fusion | flops 393471 | bytes 527360 | tf_op jit(solution)/shard_map/sub | solution.py:25
  40.4 1.0 %collective-permute-done.10 = bf16[128,3584]{1,0:T(8,128)(2,1)S(1)} collective-permute-done((bf16[128,3584]{1,0:T(8,128)(2,1)S(1)}, bf16[128,3584]{1,0:T(8,128)(2,1)S(1)}, u32[]{:S(2)}, u32[]{:S(2)}) %collective-permute-start.10) | collective-permute-done | bytes 917536 | tf_op jit(solution)/shard_map/ppermute | solution.py:163
  41.4 0.2 add_convert_fusion
  41.6 0.0 copy-start.8
  41.6 1.7 %collective-permute-start.14 = (bf16[24,3584]{1,0:T(8,128)(2,1)S(1)}, bf16[24,3584]{1,0:T(8,128)(2,1)S(1)}, u32[]{:S(2)}, u32[]{:S(2)}) collective-permute-start(bf16[24,3584]{1,0:T(8,128)(2,1)S(1)} %get-tuple-element.9), channel_id=1, source_target_pairs={{0,6},{1,25},{2,4},{3,27},{4,2},{5,29},{6,0},{7,31},{8,14},{9,17},... | collective-permute-start | bytes 516104 | tf_op jit(solution)/shard_map/ppermute | solution.py:154
  43.4 0.5 collective-permute-start.15
  43.9 1.3 %collective-permute-start.16 = (bf16[24,3584]{1,0:T(8,128)(2,1)S(1)}, bf16[24,3584]{1,0:T(8,128)(2,1)S(1)}, u32[]{:S(2)}, u32[]{:S(2)}) collective-permute-start(bf16[24,3584]{1,0:T(8,128)(2,1)S(1)} %get-tuple-element.10), channel_id=1, source_target_pairs={{0,2},{1,9},{2,0},{3,11},{4,6},{5,13},{6,4},{7,15},{8,10},{9,1},{1... | collective-permute-start | bytes 516104 | tf_op jit(solution)/shard_map/ppermute | solution.py:154
  45.2 0.7 %fusion.9 = (bf16[8,3584]{1,0:T(8,128)(2,1)S(1)}, bf16[8,3584]{1,0:T(8,128)(2,1)}, bf16[8,3584]{1,0:T(8,128)(2,1)}) fusion(bf16[128,3584]{1,0:T(8,128)(2,1)S(1)} %add_convert_fusion), kind=kLoop, calls=%fused_computation.40 | loop fusion | bytes 344064 | tf_op jit(solution)/shard_map/slice | solution.py:184
  45.9 1.7 %collective-permute-start.11 = (bf16[8,3584]{1,0:T(8,128)(2,1)S(1)}, bf16[8,3584]{1,0:T(8,128)(2,1)S(1)}, u32[]{:S(2)}, u32[]{:S(2)}) collective-permute-start(bf16[8,3584]{1,0:T(8,128)(2,1)S(1)} %get-tuple-element.6), channel_id=1, source_target_pairs={{0,6},{1,25},{2,4},{3,27},{4,2},{5,29},{6,0},{7,31},{8,14},{9,17},... | collective-permute-start | bytes 172040 | tf_op jit(solution)/shard_map/ppermute | solution.py:154
  47.5 0.5 collective-permute-start.12
  48.0 0.1 collective-permute-done.14
  48.1 1.2 %collective-permute-start.13 = (bf16[8,3584]{1,0:T(8,128)(2,1)}, bf16[8,3584]{1,0:T(8,128)(2,1)S(1)}, u32[]{:S(2)}, u32[]{:S(2)}) collective-permute-start(bf16[8,3584]{1,0:T(8,128)(2,1)} %get-tuple-element.7), channel_id=1, source_target_pairs={{0,2},{1,9},{2,0},{3,11},{4,6},{5,13},{6,4},{7,15},{8,10},{9,1},{1... | collective-permute-start | bytes 172040 | tf_op jit(solution)/shard_map/ppermute | solution.py:154
  49.4 0.5 collective-permute-done.15
  49.9 0.3 collective-permute-done.16
  50.1 0.1 add_convert_fusion.1
  50.2 0.7 %fusion.11 = (bf16[8,3584]{1,0:T(8,128)(2,1)}, bf16[8,3584]{1,0:T(8,128)(2,1)}, bf16[8,3584]{1,0:T(8,128)(2,1)}) fusion(bf16[24,3584]{1,0:T(8,128)(2,1)S(1)} %add_convert_fusion.1), kind=kLoop, calls=%fused_computation.42 | loop fusion | bytes 344064 | tf_op jit(solution)/shard_map/slice | solution.py:194
  50.9 3.1 %collective-permute-start.17 = (bf16[8,3584]{1,0:T(8,128)(2,1)}, bf16[8,3584]{1,0:T(8,128)(2,1)S(1)}, u32[]{:S(2)}, u32[]{:S(2)}) collective-permute-start(bf16[8,3584]{1,0:T(8,128)(2,1)} %get-tuple-element.18), channel_id=1, source_target_pairs={{0,24},{1,7},{2,26},{3,5},{4,28},{5,3},{6,30},{7,1},{8,16},{9,15},... | collective-permute-start | bytes 172040 | tf_op jit(solution)/shard_map/ppermute | solution.py:154
  54.0 0.0 collective-permute-start.18
  54.0 1.3 %collective-permute-start.19 = (bf16[8,3584]{1,0:T(8,128)(2,1)}, bf16[8,3584]{1,0:T(8,128)(2,1)S(1)}, u32[]{:S(2)}, u32[]{:S(2)}) collective-permute-start(bf16[8,3584]{1,0:T(8,128)(2,1)} %get-tuple-element.19), channel_id=1, source_target_pairs={{0,8},{1,3},{2,10},{3,1},{4,12},{5,7},{6,14},{7,5},{8,0},{9,11},{1... | collective-permute-start | bytes 172040 | tf_op jit(solution)/shard_map/ppermute | solution.py:154
  55.3 2.5 %convolution_convert_fusion = bf16[4,128,512]{2,1,0:T(8,128)(2,1)} fusion(bf16[4,256,576]{1,2,0:T(8,128)(2,1)S(1)} %copy-done.8, f32[4,128]{1,0:T(4,128)} %fusion.12, f32[4,128,256]{2,1,0:T(8,128)S(1)} %fusion.4, pred[4,256]{1,0:T(4,128)(4,1)} %copy-done.9), kind=kOutput, calls=%fused_computation.2 | convolution fusion | flops 135004928 | bytes 2624512 | tf_op jit(solution)/shard_map/rht,rtc->rhc/dot_general | solution.py:28
  57.8 1.5 %collective-permute-done.18 = bf16[8,3584]{1,0:T(8,128)(2,1)S(1)} collective-permute-done((bf16[8,3584]{1,0:T(8,128)(2,1)}, bf16[8,3584]{1,0:T(8,128)(2,1)S(1)}, u32[]{:S(2)}, u32[]{:S(2)}) %collective-permute-start.18) | collective-permute-done | bytes 57376 | tf_op jit(solution)/shard_map/ppermute | solution.py:154
  59.3 0.7 %add_convert_fusion.2 = bf16[8,3584]{1,0:T(8,128)(2,1)} fusion(bf16[8,3584]{1,0:T(8,128)(2,1)S(1)} %collective-permute-done.19, bf16[8,3584]{1,0:T(8,128)(2,1)S(1)} %collective-permute-done.18, bf16[8,3584]{1,0:T(8,128)(2,1)S(1)} %collective-permute-done.17, bf16[8,3584]{1,0:T(8,128)(2,1)S(1)} %collective-permute-done.13, ...), kind=kLoop, calls=%fused_computation.12 | loop fusion | flops 401408 | bytes 458752 | tf_op jit(solution)/shard_map/convert_element_type | solution.py:197
  (21 shorter events, 0.1 us)
Async XLA Ops:
  0.6 38.5 %copy-start = (bf16[4,128,576]{1,2,0:T(8,128)(2,1)S(1)}, bf16[4,128,576]{1,2,0:T(8,128)(2,1)}, u32[]{:S(2)}) copy-start(bf16[4,128,576]{1,2,0:T(8,128)(2,1)} %param.15) | copy-start | bytes 1769476
  0.6 0.9 %copy-start.4 = (bf16[8,3584]{1,0:T(8,128)(2,1)S(1)}, bf16[8,3584]{1,0:T(8,128)(2,1)}, u32[]{:S(2)}) copy-start(bf16[8,3584]{1,0:T(8,128)(2,1)} %hidden_ref.1) | copy-start | bytes 172036
  1.5 0.7 %copy-start.5 = (s32[8,8]{1,0:T(8,128)S(1)}, s32[8,8]{1,0:T(8,128)}, u32[]{:S(2)}) copy-start(s32[8,8]{1,0:T(8,128)} %routes_ref.1) | copy-start | bytes 772
  2.2 0.7 %copy-start.6 = (f32[8,8]{1,0:T(8,128)S(1)}, f32[8,8]{1,0:T(8,128)}, u32[]{:S(2)}) copy-start(f32[8,8]{1,0:T(8,128)} %scores_ref.1) | copy-start | bytes 772
  3.1 9.5 %collective-permute-start = (bf16[8,3712]{1,0:T(8,128)(2,1)S(1)}, bf16[8,3712]{1,0:T(8,128)(2,1)S(1)}, u32[]{:S(2)}, u32[]{:S(2)}) collective-permute-start(bf16[8,3712]{1,0:T(8,128)(2,1)S(1)} %shard_map.104), channel_id=1, source_target_pairs={{0,8},{1,3},{2,10},{3,1},{4,12},{5,7},{6,14},{7,5},{8,0},{9,11},{1... | collective-permute-start | bytes 178184 | tf_op jit(solution)/shard_map/ppermute | solution.py:154
  6.2 7.3 %collective-permute-start.1 = (bf16[8,3712]{1,0:T(8,128)(2,1)S(1)}, bf16[8,3712]{1,0:T(8,128)(2,1)S(1)}, u32[]{:S(2)}, u32[]{:S(2)}) collective-permute-start(bf16[8,3712]{1,0:T(8,128)(2,1)S(1)} %shard_map.104), channel_id=1, source_target_pairs={{0,16},{1,5},{2,18},{3,7},{4,20},{5,1},{6,22},{7,3},{8,24},{9,13},... | collective-permute-start | bytes 178184 | tf_op jit(solution)/shard_map/ppermute | solution.py:154
  8.8 6.1 %collective-permute-start.2 = (bf16[8,3712]{1,0:T(8,128)(2,1)S(1)}, bf16[8,3712]{1,0:T(8,128)(2,1)S(1)}, u32[]{:S(2)}, u32[]{:S(2)}) collective-permute-start(bf16[8,3712]{1,0:T(8,128)(2,1)S(1)} %shard_map.104), channel_id=1, source_target_pairs={{0,24},{1,7},{2,26},{3,5},{4,28},{5,3},{6,30},{7,1},{8,16},{9,15},... | collective-permute-start | bytes 178184 | tf_op jit(solution)/shard_map/ppermute | solution.py:154
  8.8 9.7 %collective-permute-start.3 = (bf16[8,3712]{1,0:T(8,128)(2,1)S(1)}, bf16[8,3712]{1,0:T(8,128)(2,1)S(1)}, u32[]{:S(2)}, u32[]{:S(2)}) collective-permute-start(bf16[8,3712]{1,0:T(8,128)(2,1)S(1)} %shard_map.104), channel_id=1, source_target_pairs={{0,2},{1,9},{2,0},{3,11},{4,6},{5,13},{6,4},{7,15},{8,10},{9,1},{1... | collective-permute-start | bytes 178184 | tf_op jit(solution)/shard_map/ppermute | solution.py:154
  10.5 9.2 %collective-permute-start.4 = (bf16[8,3712]{1,0:T(8,128)(2,1)S(1)}, bf16[8,3712]{1,0:T(8,128)(2,1)S(1)}, u32[]{:S(2)}, u32[]{:S(2)}) collective-permute-start(bf16[8,3712]{1,0:T(8,128)(2,1)S(1)} %shard_map.104), channel_id=1, source_target_pairs={{0,4},{1,17},{2,6},{3,19},{4,0},{5,21},{6,2},{7,23},{8,12},{9,25},... | collective-permute-start | bytes 178184 | tf_op jit(solution)/shard_map/ppermute | solution.py:154
  12.6 7.6 %collective-permute-start.5 = (bf16[8,3712]{1,0:T(8,128)(2,1)S(1)}, bf16[8,3712]{1,0:T(8,128)(2,1)S(1)}, u32[]{:S(2)}, u32[]{:S(2)}) collective-permute-start(bf16[8,3712]{1,0:T(8,128)(2,1)S(1)} %shard_map.104), channel_id=1, source_target_pairs={{0,6},{1,25},{2,4},{3,27},{4,2},{5,29},{6,0},{7,31},{8,14},{9,17},... | collective-permute-start | bytes 178184 | tf_op jit(solution)/shard_map/ppermute | solution.py:154
  15.5 5.5 %collective-permute-start.6 = (bf16[24,3712]{1,0:T(8,128)(2,1)S(1)}, bf16[24,3712]{1,0:T(8,128)(2,1)S(1)}, u32[]{:S(2)}, u32[]{:S(2)}) collective-permute-start(bf16[24,3712]{1,0:T(8,128)(2,1)S(1)} %get-tuple-element.29), channel_id=1, source_target_pairs={{0,2},{1,9},{2,0},{3,11},{4,6},{5,13},{6,4},{7,15},{8,10},{9,1},{1... | collective-permute-start | bytes 534536 | tf_op jit(solution)/shard_map/ppermute | solution.py:154
  17.0 6.5 %collective-permute-start.7 = (bf16[24,3712]{1,0:T(8,128)(2,1)S(1)}, bf16[24,3712]{1,0:T(8,128)(2,1)S(1)}, u32[]{:S(2)}, u32[]{:S(2)}) collective-permute-start(bf16[24,3712]{1,0:T(8,128)(2,1)S(1)} %get-tuple-element.29), channel_id=1, source_target_pairs={{0,4},{1,17},{2,6},{3,19},{4,0},{5,21},{6,2},{7,23},{8,12},{9,25},... | collective-permute-start | bytes 534536 | tf_op jit(solution)/shard_map/ppermute | solution.py:154
  18.5 6.4 %collective-permute-start.8 = (bf16[24,3712]{1,0:T(8,128)(2,1)S(1)}, bf16[24,3712]{1,0:T(8,128)(2,1)S(1)}, u32[]{:S(2)}, u32[]{:S(2)}) collective-permute-start(bf16[24,3712]{1,0:T(8,128)(2,1)S(1)} %get-tuple-element.29), channel_id=1, source_target_pairs={{0,6},{1,25},{2,4},{3,27},{4,2},{5,29},{6,0},{7,31},{8,14},{9,17},... | collective-permute-start | bytes 534536 | tf_op jit(solution)/shard_map/ppermute | solution.py:154
  25.6 2.7 %collective-permute-start.9 = (bf16[128,3712]{1,0:T(8,128)(2,1)}, bf16[128,3712]{1,0:T(8,128)(2,1)S(1)}, u32[]{:S(2)}, u32[]{:S(2)}) collective-permute-start(bf16[128,3712]{1,0:T(8,128)(2,1)} %get-tuple-element.12), channel_id=1, source_target_pairs={{0,1},{1,0},{2,3},{3,2},{4,5},{5,4},{6,7},{7,6},{8,9},{9,8},{10,11... | collective-permute-start | bytes 2850824 | tf_op jit(solution)/shard_map/ppermute | solution.py:163
  28.4 2.0 %copy-start.1 = (bf16[1,3584,512]{2,1,0:T(8,128)(2,1)S(1)}, bf16[1,3584,512]{2,1,0:T(8,128)(2,1)}, u32[]{:S(2)}) copy-start(bf16[1,3584,512]{2,1,0:T(8,128)(2,1)} %param.12) | copy-start | bytes 11010052
  30.5 2.0 %copy-start.2 = (bf16[1,3584,512]{2,1,0:T(8,128)(2,1)S(1)}, bf16[1,3584,512]{2,1,0:T(8,128)(2,1)}, u32[]{:S(2)}) copy-start(bf16[1,3584,512]{2,1,0:T(8,128)(2,1)} %param.13) | copy-start | bytes 11010052
  32.5 2.0 %copy-start.3 = (bf16[1,512,3584]{2,1,0:T(8,128)(2,1)S(1)}, bf16[1,512,3584]{2,1,0:T(8,128)(2,1)}, u32[]{:S(2)}) copy-start(bf16[1,512,3584]{2,1,0:T(8,128)(2,1)} %param.14) | copy-start | bytes 11010052
  34.6 4.5 %copy-start.10 = (s32[4]{0:T(128)S(1)}, s32[4]{0:T(128)}, u32[]{:S(2)}) copy-start(s32[4]{0:T(128)} %param.17) | copy-start | bytes 52
  34.6 4.6 %copy-start.7 = (bf16[4,256,576]{1,2,0:T(8,128)(2,1)S(1)}, bf16[4,256,576]{1,2,0:T(8,128)(2,1)}, u32[]{:S(2)}) copy-start(bf16[4,256,576]{1,2,0:T(8,128)(2,1)} %param.16) | copy-start | bytes 3538948
  38.8 2.5 %collective-permute-start.10 = (bf16[128,3584]{1,0:T(8,128)(2,1)S(1)}, bf16[128,3584]{1,0:T(8,128)(2,1)S(1)}, u32[]{:S(2)}, u32[]{:S(2)}) collective-permute-start(bf16[128,3584]{1,0:T(8,128)(2,1)S(1)} %get-tuple-element.5), channel_id=1, source_target_pairs={{0,1},{1,0},{2,3},{3,2},{4,5},{5,4},{6,7},{7,6},{8,9},{9,8},{10,11... | collective-permute-start | bytes 2752520 | tf_op jit(solution)/shard_map/ppermute | solution.py:163
  39.1 2.3 %copy-start.9 = (pred[4,256]{1,0:T(4,128)(4,1)}, pred[4,256]{1,0:T(4,128)(4,1)S(1)}, u32[]{:S(2)}) copy-start(pred[4,256]{1,0:T(4,128)(4,1)S(1)} %iota_compare_fusion) | copy-start | bytes 3076
  41.6 13.7 %copy-start.8 = (bf16[4,256,576]{1,2,0:T(8,128)(2,1)S(1)}, bf16[4,256,576]{1,2,0:T(8,128)(2,1)}, u32[]{:S(2)}) copy-start(bf16[4,256,576]{1,2,0:T(8,128)(2,1)} %param.16) | copy-start | bytes 3538948
  41.6 6.5 %collective-permute-start.14 = (bf16[24,3584]{1,0:T(8,128)(2,1)S(1)}, bf16[24,3584]{1,0:T(8,128)(2,1)S(1)}, u32[]{:S(2)}, u32[]{:S(2)}) collective-permute-start(bf16[24,3584]{1,0:T(8,128)(2,1)S(1)} %get-tuple-element.9), channel_id=1, source_target_pairs={{0,6},{1,25},{2,4},{3,27},{4,2},{5,29},{6,0},{7,31},{8,14},{9,17},... | collective-permute-start | bytes 516104 | tf_op jit(solution)/shard_map/ppermute | solution.py:154
  43.4 6.5 %collective-permute-start.15 = (bf16[24,3584]{1,0:T(8,128)(2,1)S(1)}, bf16[24,3584]{1,0:T(8,128)(2,1)S(1)}, u32[]{:S(2)}, u32[]{:S(2)}) collective-permute-start(bf16[24,3584]{1,0:T(8,128)(2,1)S(1)} %get-tuple-element.11), channel_id=1, source_target_pairs={{0,4},{1,17},{2,6},{3,19},{4,0},{5,21},{6,2},{7,23},{8,12},{9,25},... | collective-permute-start | bytes 516104 | tf_op jit(solution)/shard_map/ppermute | solution.py:154
  43.9 6.3 %collective-permute-start.16 = (bf16[24,3584]{1,0:T(8,128)(2,1)S(1)}, bf16[24,3584]{1,0:T(8,128)(2,1)S(1)}, u32[]{:S(2)}, u32[]{:S(2)}) collective-permute-start(bf16[24,3584]{1,0:T(8,128)(2,1)S(1)} %get-tuple-element.10), channel_id=1, source_target_pairs={{0,2},{1,9},{2,0},{3,11},{4,6},{5,13},{6,4},{7,15},{8,10},{9,1},{1... | collective-permute-start | bytes 516104 | tf_op jit(solution)/shard_map/ppermute | solution.py:154
  45.9 8.1 %collective-permute-start.11 = (bf16[8,3584]{1,0:T(8,128)(2,1)S(1)}, bf16[8,3584]{1,0:T(8,128)(2,1)S(1)}, u32[]{:S(2)}, u32[]{:S(2)}) collective-permute-start(bf16[8,3584]{1,0:T(8,128)(2,1)S(1)} %get-tuple-element.6), channel_id=1, source_target_pairs={{0,6},{1,25},{2,4},{3,27},{4,2},{5,29},{6,0},{7,31},{8,14},{9,17},... | collective-permute-start | bytes 172040 | tf_op jit(solution)/shard_map/ppermute | solution.py:154
  47.5 10.2 %collective-permute-start.12 = (bf16[8,3584]{1,0:T(8,128)(2,1)}, bf16[8,3584]{1,0:T(8,128)(2,1)S(1)}, u32[]{:S(2)}, u32[]{:S(2)}) collective-permute-start(bf16[8,3584]{1,0:T(8,128)(2,1)} %get-tuple-element.8), channel_id=1, source_target_pairs={{0,4},{1,17},{2,6},{3,19},{4,0},{5,21},{6,2},{7,23},{8,12},{9,25},... | collective-permute-start | bytes 172040 | tf_op jit(solution)/shard_map/ppermute | solution.py:154
  48.1 9.7 %collective-permute-start.13 = (bf16[8,3584]{1,0:T(8,128)(2,1)}, bf16[8,3584]{1,0:T(8,128)(2,1)S(1)}, u32[]{:S(2)}, u32[]{:S(2)}) collective-permute-start(bf16[8,3584]{1,0:T(8,128)(2,1)} %get-tuple-element.7), channel_id=1, source_target_pairs={{0,2},{1,9},{2,0},{3,11},{4,6},{5,13},{6,4},{7,15},{8,10},{9,1},{1... | collective-permute-start | bytes 172040 | tf_op jit(solution)/shard_map/ppermute | solution.py:154
  50.9 6.9 %collective-permute-start.17 = (bf16[8,3584]{1,0:T(8,128)(2,1)}, bf16[8,3584]{1,0:T(8,128)(2,1)S(1)}, u32[]{:S(2)}, u32[]{:S(2)}) collective-permute-start(bf16[8,3584]{1,0:T(8,128)(2,1)} %get-tuple-element.18), channel_id=1, source_target_pairs={{0,24},{1,7},{2,26},{3,5},{4,28},{5,3},{6,30},{7,1},{8,16},{9,15},... | collective-permute-start | bytes 172040 | tf_op jit(solution)/shard_map/ppermute | solution.py:154
  54.0 5.3 %collective-permute-start.18 = (bf16[8,3584]{1,0:T(8,128)(2,1)}, bf16[8,3584]{1,0:T(8,128)(2,1)S(1)}, u32[]{:S(2)}, u32[]{:S(2)}) collective-permute-start(bf16[8,3584]{1,0:T(8,128)(2,1)} %get-tuple-element.20), channel_id=1, source_target_pairs={{0,16},{1,5},{2,18},{3,7},{4,20},{5,1},{6,22},{7,3},{8,24},{9,13},... | collective-permute-start | bytes 172040 | tf_op jit(solution)/shard_map/ppermute | solution.py:154
  54.0 5.3 %collective-permute-start.19 = (bf16[8,3584]{1,0:T(8,128)(2,1)}, bf16[8,3584]{1,0:T(8,128)(2,1)S(1)}, u32[]{:S(2)}, u32[]{:S(2)}) collective-permute-start(bf16[8,3584]{1,0:T(8,128)(2,1)} %get-tuple-element.19), channel_id=1, source_target_pairs={{0,8},{1,3},{2,10},{3,1},{4,12},{5,7},{6,14},{7,5},{8,0},{9,11},{1... | collective-permute-start | bytes 172040 | tf_op jit(solution)/shard_map/ppermute | solution.py:154

commit v3 on v2

--- a/solution.py
+++ b/solution.py
@@ -1,3 +1,5 @@
+import functools
+
 import jax
 import jax.numpy as jnp
 from jax import lax
@@ -13,30 +15,88 @@
 LANES = 128
 
 
-def attend(query_latent, latent_cache, cache_lengths):
-    scores = (
-        jnp.einsum("rhc,rtc->rht", query_latent, latent_cache, preferred_element_type=jnp.float32)
-        * SOFTMAX_SCALE
-    )
-    positions = jnp.arange(latent_cache.shape[1], dtype=jnp.int32)
-    visible = positions[None, None, :] < cache_lengths[:, None, None]
-    scores = jnp.where(visible, scores, jnp.float32(-1e30))
-    largest = jnp.max(scores, axis=2, keepdims=True)
-    powered = jnp.where(visible, jnp.exp(scores - largest), jnp.float32(0.0))
-    probability = (powered / jnp.sum(powered, axis=2, keepdims=True)).astype(jnp.bfloat16)
-    values = latent_cache[:, :, :LATENT]
-    mixed = jnp.einsum("rht,rtc->rhc", probability, values, preferred_element_type=jnp.float32)
-    return mixed.astype(jnp.bfloat16)
+VMEM = pl.BlockSpec(memory_space=pltpu.VMEM)
+SMEM = pl.BlockSpec(memory_space=pltpu.SMEM)
+ANY = pl.BlockSpec(memory_space=pl.ANY)
+HBM = pl.BlockSpec(memory_space=pltpu.HBM)
+
+
+def in_vmem(shape, dtype):
+    return pltpu.VMEM(shape, dtype)
+
+
+def stored(value):
+    return pltpu.with_memory_space_constraint(value, pltpu.HBM)
+
+
+def held(value):
+    return pltpu.with_memory_space_constraint(value, pltpu.VMEM)
+
+
+def attend_kernel(lengths_ref, query_ref, cache_ref, gate_ref, up_ref, down_ref, after_ref, out_ref, *rest):
+    copies = [
+        pltpu.make_async_copy(source, target, rest[3].at[i])
+        for i, (source, target) in enumerate(zip((gate_ref, up_ref, down_ref), rest[:3], strict=True))
+    ]
+    for copy in copies:
+        copy.start()
+    latent = out_ref.shape[2]
+    for r in range(query_ref.shape[0]):
+        query, cache = query_ref[r], cache_ref[r]
+        scores = SOFTMAX_SCALE * lax.dot_general(
+            query, cache, (((0,), (0,)), ((), ())), preferred_element_type=jnp.float32
+        )
+        visible = lax.broadcasted_iota(jnp.int32, scores.shape, 1) < lengths_ref[r]
+        scores = jnp.where(visible, scores, -1e30)
+        largest = jnp.max(scores, axis=1, keepdims=True)
+        powered = jnp.where(visible, jnp.exp(scores - largest), 0.0)
+        probability = (powered / jnp.sum(powered, axis=1, keepdims=True)).astype(jnp.bfloat16)
+        out_ref[r] = lax.dot_general(
+            probability, cache[:latent], (((1,), (1,)), ((), ())), preferred_element_type=jnp.float32
+        ).astype(jnp.bfloat16)
+    for copy in copies:
+        copy.wait()
+
+
+def attend(query_latent, latent_cache, cache_lengths, weights, after):
+    rows, heads, entries = query_latent.shape
+    positions = latent_cache.shape[1]
+    return pl.pallas_call(
+        attend_kernel,
+        out_shape=(
+            jax.ShapeDtypeStruct((rows, heads, LATENT), jnp.bfloat16),
+            *(in_vmem(w.shape, w.dtype) for w in weights),
+        ),
+        in_specs=[SMEM, VMEM, VMEM, HBM, HBM, HBM, ANY],
+        out_specs=(VMEM,) * 4,
+        scratch_shapes=[pltpu.SemaphoreType.DMA((3,))],
+        compiler_params=pltpu.CompilerParams(vmem_limit_bytes=8 << 20),
+        cost_estimate=pl.CostEstimate(
+            flops=4 * rows * heads * positions * entries,
+            bytes_accessed=2 * sum(w.size for w in weights),
+            transcendentals=rows * heads * positions,
+        ),
+    )(cache_lengths, jnp.swapaxes(query_latent, 1, 2), jnp.swapaxes(latent_cache, 1, 2), *(stored(w) for w in weights), after)
 
 
 def rounds_up(value, step):
     return -(-value // step) * step
 
 
-def pack_kernel(hidden_ref, routes_ref, scores_ref, out_ref):
+def pack_kernel(hidden_ref, routes_ref, scores_ref, out_ref, rows_ref, named_ref, affinity_ref, sems):
     rows, model_width = hidden_ref.shape
-    scores = scores_ref[...]
-    routes = routes_ref[...]
+    copies = [
+        pltpu.make_async_copy(source, target, sems.at[i])
+        for i, (source, target) in enumerate(
+            ((routes_ref, named_ref), (scores_ref, affinity_ref), (hidden_ref, rows_ref))
+        )
+    ]
+    for copy in copies:
+        copy.start()
+    copies[0].wait()
+    copies[1].wait()
+    scores = affinity_ref[...]
+    routes = named_ref[...]
     weights = ROUTE_SCALE * scores / jnp.sum(scores, axis=1, keepdims=True)
     lanes = out_ref.shape[1] - model_width
     lane = lax.broadcasted_iota(jnp.int32, (rows, lanes), 1)
@@ -45,12 +105,10 @@
     for k in range(routes.shape[1]):
         named = routes[:, k : k + 1]
         dense += jnp.where((lane == named) | (lane == named + experts), weights[:, k : k + 1], 0.0)
-    high = dense.astype(jnp.bfloat16)
-    low = (dense - high.astype(jnp.float32)).astype(jnp.bfloat16)
-    out_ref[:, :model_width] = hidden_ref[...]
-    out_ref[:, model_width:] = jnp.where(lane < experts, high.astype(jnp.float32), low.astype(jnp.float32)).astype(
-        jnp.bfloat16
-    )
+    high = dense.astype(jnp.bfloat16).astype(jnp.float32)
+    out_ref[:, model_width:] = jnp.where(lane < experts, high, dense - high).astype(jnp.bfloat16)
+    copies[2].wait()
+    out_ref[:, :model_width] = rows_ref[...]
 
 
 def pack(hidden_in, expert_routes, route_scores, experts):
@@ -58,10 +116,18 @@
     lanes = rounds_up(2 * experts, LANES)
     return pl.pallas_call(
         pack_kernel,
-        out_shape=jax.ShapeDtypeStruct((rows, model_width + lanes), jnp.bfloat16),
-        compiler_params=pltpu.CompilerParams(vmem_limit_bytes=2 << 20),
+        out_shape=in_vmem((rows, model_width + lanes), jnp.bfloat16),
+        in_specs=[HBM] * 3,
+        out_specs=VMEM,
+        scratch_shapes=[
+            pltpu.VMEM(hidden_in.shape, hidden_in.dtype),
+            pltpu.VMEM(expert_routes.shape, expert_routes.dtype),
+            pltpu.VMEM(route_scores.shape, route_scores.dtype),
+            pltpu.SemaphoreType.DMA((3,)),
+        ],
+        compiler_params=pltpu.CompilerParams(vmem_limit_bytes=4 << 20),
         cost_estimate=pl.CostEstimate(flops=1 << 16, bytes_accessed=4 * rows * model_width, transcendentals=0),
-    )(hidden_in, expert_routes, route_scores)
+    )(stored(hidden_in), stored(expert_routes), stored(route_scores))
 
 
 def expert_kernel(me_ref, rows_ref, gate_ref, up_ref, down_ref, mine_ref, other_ref, hidden_ref):
@@ -110,23 +176,48 @@
 def expert_block(rows, expert_gate, expert_up, expert_down, me):
     total, width = rows.shape
     model_width, units = expert_gate.shape
-    half = total // 2
-    vmem = pl.BlockSpec(memory_space=pltpu.VMEM)
-    out = jax.ShapeDtypeStruct((half, model_width), jnp.bfloat16)
-    weights = [pltpu.with_memory_space_constraint(w, pltpu.VMEM) for w in (expert_gate, expert_up, expert_down)]
+    out = in_vmem((total // 2, model_width), jnp.bfloat16)
     return pl.pallas_call(
         expert_kernel,
         out_shape=(out, out),
-        in_specs=[pl.BlockSpec(memory_space=pltpu.SMEM), vmem, vmem, vmem, vmem],
-        out_specs=(vmem, vmem),
+        in_specs=[SMEM] + [VMEM] * 4,
+        out_specs=(VMEM, VMEM),
         scratch_shapes=[pltpu.VMEM((total, units), jnp.bfloat16)],
-        compiler_params=pltpu.CompilerParams(vmem_limit_bytes=(16 << 20) + 8 * total * width),
+        compiler_params=pltpu.CompilerParams(vmem_limit_bytes=(8 << 20) + 4 * total * units),
         cost_estimate=pl.CostEstimate(
             flops=6 * total * model_width * units,
-            bytes_accessed=6 * model_width * units + 4 * total * width,
+            bytes_accessed=4 * total * width,
             transcendentals=total * units,
         ),
-    )(me.reshape(1), rows, *weights)
+    )(me.reshape(1), held(rows), *(held(w) for w in (expert_gate, expert_up, expert_down)))
+
+
+def add_kernel(base_count, sizes, *refs):
+    values = [ref[...].astype(jnp.float32) for ref in refs[:base_count]]
+    total = values[0]
+    for value in values[1:]:
+        total += value
+    low = 0
+    for out_ref, size in zip(refs[base_count:], sizes, strict=True):
+        out_ref[...] = total[low : low + size].astype(jnp.bfloat16)
+        low += size
+
+
+def add(values, sizes, last=False):
+    rows, width = values[0].shape
+    shape = jax.ShapeDtypeStruct if last else in_vmem
+    return pl.pallas_call(
+        functools.partial(add_kernel, len(values), sizes),
+        out_shape=tuple(shape((size, width), jnp.bfloat16) for size in sizes),
+        in_specs=[VMEM] * len(values),
+        out_specs=(VMEM,) * len(sizes),
+        compiler_params=pltpu.CompilerParams(vmem_limit_bytes=(4 << 20) + 8 * rows * width),
+        cost_estimate=pl.CostEstimate(
+            flops=len(values) * rows * width,
+            bytes_accessed=2 * len(values) * rows * width,
+            transcendentals=0,
+        ),
+    )(*(held(v) for v in values))
 
 
 def per_device(
@@ -170,32 +261,27 @@
     side = {k: second(own, k) for k in order(inner)}
     column = jnp.concatenate([near[k] for k in range(1, outer)], axis=0)
     far = {k: second(column, k) for k in (order(inner)[1:] + order(inner)[:1])}
-    core = jnp.concatenate(
-        [own, column] + [side[k] for k in range(1, inner)] + [far[k] for k in range(1, inner)], axis=0
+    attention_latent, *weights = attend(
+        query_latent,
+        latent_cache,
+        cache_lengths,
+        (expert_gate[0], expert_up[0], expert_down[0]),
+        column,
     )
-    rows = jnp.concatenate([core, over_cores(core)], axis=0)
-
-    mine, other = expert_block(rows, expert_gate[0], expert_up[0], expert_down[0], lax.axis_index("ep"))
-
-    both = (mine.astype(jnp.float32) + over_cores(other).astype(jnp.float32)).astype(jnp.bfloat16)
-    place = {}
-    at = outer * tok_rows
-    for k in range(1, inner):
-        place["side", k] = both[at : at + tok_rows]
-        at += tok_rows
-    for k in range(1, inner):
-        place["far", k] = both[at : at + (outer - 1) * tok_rows]
-        at += (outer - 1) * tok_rows
-    far = [second(place["far", k], k) for k in order(inner)]
-    side = [second(place["side", k], k) for k in order(inner)]
-    column = (
-        both[tok_rows : outer * tok_rows].astype(jnp.float32) + sum(p.astype(jnp.float32) for p in far)
-    ).astype(jnp.bfloat16)
-    near = [first(column[(k - 1) * tok_rows : k * tok_rows], k) for k in order(outer)]
-    moe_output = (
-        both[:tok_rows].astype(jnp.float32) + sum(p.astype(jnp.float32) for p in side + near)
-    ).astype(jnp.bfloat16)
-    attention_latent = attend(query_latent, latent_cache, cache_lengths)
+    early = jnp.concatenate([own, column] + [side[k] for k in range(1, inner)], axis=0)
+    pieces = [early] + [far[k] for k in range(1, inner)]
+    rows = jnp.concatenate(pieces + [over_cores(p) for p in pieces], axis=0)
+
+    mine, other = expert_block(rows, *weights, lax.axis_index("ep"))
+
+    step = (outer - 1) * tok_rows
+    sizes = [tok_rows, step] + [tok_rows] * (inner - 1) + [step] * (inner - 1)
+    kept, column, *parts = add([mine, over_cores(other)], sizes)
+    far = [second(parts[inner - 1 + k - 1], k) for k in order(inner)]
+    side = [second(parts[k - 1], k) for k in order(inner)]
+    near = add([column, *far], [tok_rows] * (outer - 1))
+    near = [first(near[k - 1], k) for k in order(outer)]
+    (moe_output,) = add([kept, *side, *near], [tok_rows], last=True)
     return (moe_output, attention_latent)
 
 

time: 60.3 us -> 63.9 us (1.060)
  local copies, waits for them, and re-layouts: 16.4 us -> 6.3 us
  Pallas kernels: 4.44 us -> 11.8 us
  waiting for transfers between devices: 9.42 us -> 16.6 us
  starting transfers between devices: 24.2 us -> 28.3 us
  matrix products: 2.92 us -> 0 us
  other arithmetic: 1.88 us -> 0 us
    unnamed x31 -> x18, local copies, waits for them, and re-layouts: 14.2 us -> 5.64 us
    ppermute x18, waiting for transfers between devices: 5.7 us -> 13.3 us  [swap(): return lax.ppermute(value, ('ep', 'sub'), pairs)]
    pallas_call x2 -> x6, Pallas kernels: 4.44 us -> 11.8 us  [the longest x1 5.56 us: attend(): pl.pallas_call(attend_kernel, out_shape=(jax.ShapeDtypeStruct((rows, head...]
    dot_general x2 -> x0, matrix products: 2.92 us -> none  [the longest x1 2.49 us: attend(): jnp.einsum('rht,rtc->rhc', probability, values, preferred_element_type=jn...]
    ppermute x18, starting transfers between devices: 24 us -> 26.8 us  [swap(): return lax.ppermute(value, ('ep', 'sub'), pairs)]
    slice x3 -> x0, local copies, waits for them, and re-layouts: 1.36 us -> none  [the longest x1 0.66 us: per_device(): place['side', k] = both[at:at + tok_rows]]
    ppermute x2 -> x5, starting transfers between devices: 0.21 us -> 1.41 us  [over_cores(): return lax.ppermute(value, 'sub', [(i, i ^ 1) for i in range(sub_count)])]
    convert_element_type x3 -> x0, other arithmetic: 0.98 us -> none  [the longest x1 0.68 us: per_device(): moe_output = (both[:tok_rows].astype(jnp.float32) + sum((p.astype(jnp.flo...]
  transfers between devices with their start and end apart: 20 -> 23, of which waited for: 10 -> 9; matrix products, arithmetic and copies ran while one was open for 18% -> 7% of each run, Pallas kernels for 0% -> 9%
where the time goes in v3:
time: 63.9 us; the launch traced here: 63.7 us
  starting transfers between devices  28.3 us (44%)
  waiting for transfers between devices  16.6 us (26%)
  Pallas kernels  11.8 us (18%)
  local copies, waits for them, and re-layouts  6.3 us (10%)
  between operations  0.76 us (1%)
    ppermute x18, starting transfers between devices, swap(): return lax.ppermute(value, ('ep', 'sub'), pairs)  26.8 us
    ppermute x18, waiting for transfers between devices, swap(): return lax.ppermute(value, ('ep', 'sub'), pairs)  13.3 us
    unnamed x18, local copies, waits for them, and re-layouts  5.64 us
    pallas_call x1, Pallas kernels, attend(): pl.pallas_call(attend_kernel, out_shape=(jax.ShapeDtypeStruct((rows, head...  5.56 us
    pallas_call x1, Pallas kernels, expert_block(): pl.pallas_call(expert_kernel, out_shape=(out, out), in_specs=[SMEM] + [VM...  4.27 us
    ppermute x5, waiting for transfers between devices, over_cores(): return lax.ppermute(value, 'sub', [(i, i ^ 1) for i in range(sub_count)])  3.26 us
    ppermute x5, starting transfers between devices, over_cores(): return lax.ppermute(value, 'sub', [(i, i ^ 1) for i in range(sub_count)])  1.41 us
  transfers between devices with their start and end apart: 23, of which 9 were waited for; matrix products, arithmetic and copies ran while one was open for 7% of the time, Pallas kernels for 9%

profile of v3, /device:TPU:0, one launch (start us, length us, event | category | flops | bytes accessed | tf_op | source)
XLA Modules:
  0.0 63.7 jit_solution(12137016816538073434)
XLA Ops:
  0.6 0.0 copy-start
  0.6 1.0 %shard_map.104 = bf16[8,3712]{1,0:T(8,128)(2,1)S(1)} custom-call(bf16[8,3584]{1,0:T(8,128)(2,1)} %hidden_ref.1, s32[8,8]{1,0:T(8,128)} %routes_ref.1, f32[8,8]{1,0:T(8,128)} %scores_ref.1), custom_call_target="tpu_custom_call" | custom-call | flops 65536 | bytes 114688 | tf_op jit(solution)/shard_map/pallas_call | solution.py:117
  1.7 4.0 %collective-permute-start.5 = (bf16[8,3712]{1,0:T(8,128)(2,1)S(1)}, bf16[8,3712]{1,0:T(8,128)(2,1)S(1)}, u32[]{:S(2)}, u32[]{:S(2)}) collective-permute-start(bf16[8,3712]{1,0:T(8,128)(2,1)S(1)} %shard_map.104), channel_id=1, source_target_pairs={{0,6},{1,25},{2,4},{3,27},{4,2},{5,29},{6,0},{7,31},{8,14},{9,17},... | collective-permute-start | bytes 178184 | tf_op jit(solution)/shard_map/ppermute | solution.py:245
  5.6 0.5 collective-permute-start.4
  6.1 0.1 collective-permute-start.3
  6.3 4.0 %collective-permute-start.2 = (bf16[8,3712]{1,0:T(8,128)(2,1)S(1)}, bf16[8,3712]{1,0:T(8,128)(2,1)S(1)}, u32[]{:S(2)}, u32[]{:S(2)}) collective-permute-start(bf16[8,3712]{1,0:T(8,128)(2,1)S(1)} %shard_map.104), channel_id=1, source_target_pairs={{0,24},{1,7},{2,26},{3,5},{4,28},{5,3},{6,30},{7,1},{8,16},{9,15},... | collective-permute-start | bytes 178184 | tf_op jit(solution)/shard_map/ppermute | solution.py:245
  10.3 0.0 collective-permute-start
  10.3 0.6 constant_dynamic-update-slice_fusion.9
  10.9 3.6 %collective-permute-done = bf16[8,3712]{1,0:T(8,128)(2,1)S(1)} collective-permute-done((bf16[8,3712]{1,0:T(8,128)(2,1)S(1)}, bf16[8,3712]{1,0:T(8,128)(2,1)S(1)}, u32[]{:S(2)}, u32[]{:S(2)}) %collective-permute-start) | collective-permute-done | bytes 59424 | tf_op jit(solution)/shard_map/ppermute | solution.py:245
  14.5 0.0 collective-permute-start.1
  14.5 0.6 constant_dynamic-update-slice_fusion.8
  15.1 5.6 %collective-permute-done.1 = bf16[8,3712]{1,0:T(8,128)(2,1)S(1)} collective-permute-done((bf16[8,3712]{1,0:T(8,128)(2,1)S(1)}, bf16[8,3712]{1,0:T(8,128)(2,1)S(1)}, u32[]{:S(2)}, u32[]{:S(2)}) %collective-permute-start.1) | collective-permute-done | bytes 59424 | tf_op jit(solution)/shard_map/ppermute | solution.py:245
  20.7 0.6 constant_dynamic-update-slice_fusion.7
  21.3 0.0 collective-permute-done.2
  21.3 0.6 constant_dynamic-update-slice_fusion.6
  21.9 6.4 %collective-permute-start.8 = (bf16[24,3712]{1,0:T(8,128)(2,1)S(1)}, bf16[24,3712]{1,0:T(8,128)(2,1)S(1)}, u32[]{:S(2)}, u32[]{:S(2)}) collective-permute-start(bf16[24,3712]{1,0:T(8,128)(2,1)S(1)} %get-tuple-element.44.after_ref), channel_id=1, source_target_pairs={{0,6},{1,25},{2,4},{3,27},{4,2},{5,29},{6,0},{7,31},{8,14},{9,17},... | collective-permute-start | bytes 534536 | tf_op jit(solution)/shard_map/ppermute | solution.py:245
  28.4 0.4 collective-permute-start.7
  28.7 0.0 collective-permute-done.3
  28.7 0.2 collective-permute-start.6
  28.9 0.6 constant_dynamic-update-slice_fusion.5
  29.6 0.0 collective-permute-done.4
  29.6 0.6 constant_dynamic-update-slice_fusion.4
  30.2 0.0 collective-permute-done.5
  30.2 0.6 %constant_dynamic-update-slice_fusion.3 = (bf16[56,3712]{1,0:T(8,128)(2,1)}, bf16[256,3712]{1,0:T(8,128)(2,1)S(1)}) fusion(bf16[56,3712]{1,0:T(8,128)(2,1)} %get-tuple-element.38, bf16[8,3712]{1,0:T(8,128)(2,1)S(1)} %collective-permute-done.5, bf16[256,3712]{1,0:T(8,128)(2,1)S(1)} %get-tuple-element.39), kind=kLoop, calls=%fused_computation.3 | loop fusion | bytes 178176 | tf_op jit(solution)/shard_map/concatenate | solution.py:271
  30.8 0.0 collective-permute-start.9
  30.9 0.0 copy-done
  30.9 0.0 copy-start.1
  30.9 1.1 %copy-done.1 = bf16[4,128,576]{1,2,0:T(8,128)(2,1)S(1)} copy-done((bf16[4,128,576]{1,2,0:T(8,128)(2,1)S(1)}, bf16[4,128,576]{1,2,0:T(8,128)(2,1)}, u32[]{:S(2)}) %copy-start.1) | copy-done | bytes 589848
  31.9 0.7 %copy-done.2 = s32[4]{0:T(128)S(1)} copy-done((s32[4]{0:T(128)S(1)}, s32[4]{0:T(128)}, u32[]{:S(2)}) %copy-start.2) | copy-done | bytes 40
  32.6 5.6 %shard_map.105 = (bf16[4,128,512]{2,1,0:T(8,128)(2,1)}, bf16[3584,512]{1,0:T(8,128)(2,1)S(1)}, bf16[3584,512]{1,0:T(8,128)(2,1)S(1)}, bf16[512,3584]{1,0:T(8,128)(2,1)S(1)}) custom-call(s32[4]{0:T(128)S(1)} %copy-done.2, bf16[4,576,128]{2,1,0:T(8,128)(2,1)S(1)} %bitcast.7, bf16[4,576,256]{2,1,0:T(8,128)(2,1)S(1)} %bitcast.6, bf16[3584,512]{1,0:T(8,128)(2,1)} %bitcast.8, ...), custom_call_target="tpu_custom_call" | custom-call | flops 301989888 | bytes 11010048 | tf_op jit(solution)/shard_map/pallas_call | solution.py:64
  38.1 0.0 collective-permute-done.8
  38.2 0.6 collective-permute-start.12
  38.7 0.0 collective-permute-done.7
  38.7 0.1 collective-permute-start.11
  38.8 0.0 collective-permute-done.6
  38.8 0.4 collective-permute-start.10
  39.3 0.0 collective-permute-done.9
  39.4 1.0 %collective-permute-done.10 = bf16[24,3712]{1,0:T(8,128)(2,1)S(1)} collective-permute-done((bf16[24,3712]{1,0:T(8,128)(2,1)S(1)}, bf16[24,3712]{1,0:T(8,128)(2,1)S(1)}, u32[]{:S(2)}, u32[]{:S(2)}) %collective-permute-start.10) | collective-permute-done | bytes 178208 | tf_op jit(solution)/shard_map/ppermute | solution.py:254
  40.4 0.0 collective-permute-done.11
  40.5 0.0 collective-permute-done.12
  40.5 4.3 %shard_map.106 = (bf16[128,3584]{1,0:T(8,128)(2,1)S(1)}, bf16[128,3584]{1,0:T(8,128)(2,1)S(1)}) custom-call(s32[1]{0:T(128)} %bitcast.me_ref, bf16[256,3712]{1,0:T(8,128)(2,1)S(1)} %constant_dynamic-update-slice_fusion.10.rows_ref, bf16[3584,512]{1,0:T(8,128)(2,1)S(1)} %get-tuple-element.19.gate_ref, bf16[3584,512]{1,0:T(8,128)(2,1)S(1)} %get-tuple-element.20.up_ref, ...), custom_call_target="tpu_custom_call" | custom-call | flops 2818572288 | bytes 3801088 | tf_op jit(solution)/shard_map/pallas_call | solution.py:180
  44.8 0.3 collective-permute-start.13
  45.1 2.2 %collective-permute-done.13.refs_1_ = bf16[128,3584]{1,0:T(8,128)(2,1)S(1)} collective-permute-done((bf16[128,3584]{1,0:T(8,128)(2,1)S(1)}, bf16[128,3584]{1,0:T(8,128)(2,1)S(1)}, u32[]{:S(2)}, u32[]{:S(2)}) %collective-permute-start.13) | collective-permute-done | bytes 917536 | tf_op jit(solution)/shard_map/ppermute | solution.py:254
  47.3 0.2 shard_map.107
  47.5 3.0 %collective-permute-start.17 = (bf16[24,3584]{1,0:T(8,128)(2,1)S(1)}, bf16[24,3584]{1,0:T(8,128)(2,1)S(1)}, u32[]{:S(2)}, u32[]{:S(2)}) collective-permute-start(bf16[24,3584]{1,0:T(8,128)(2,1)S(1)} %get-tuple-element.29), channel_id=1, source_target_pairs={{0,6},{1,25},{2,4},{3,27},{4,2},{5,29},{6,0},{7,31},{8,14},{9,17},... | collective-permute-start | bytes 516104 | tf_op jit(solution)/shard_map/ppermute | solution.py:245
  50.5 0.4 collective-permute-start.18
  50.9 0.3 collective-permute-start.19
  51.1 2.8 %collective-permute-start.14 = (bf16[8,3584]{1,0:T(8,128)(2,1)S(1)}, bf16[8,3584]{1,0:T(8,128)(2,1)S(1)}, u32[]{:S(2)}, u32[]{:S(2)}) collective-permute-start(bf16[8,3584]{1,0:T(8,128)(2,1)S(1)} %get-tuple-element.25), channel_id=1, source_target_pairs={{0,6},{1,25},{2,4},{3,27},{4,2},{5,29},{6,0},{7,31},{8,14},{9,17},... | collective-permute-start | bytes 172040 | tf_op jit(solution)/shard_map/ppermute | solution.py:245
  54.0 0.4 collective-permute-start.15
  54.4 0.0 collective-permute-done.17.refs_1_
  54.4 1.5 %collective-permute-start.16 = (bf16[8,3584]{1,0:T(8,128)(2,1)S(1)}, bf16[8,3584]{1,0:T(8,128)(2,1)S(1)}, u32[]{:S(2)}, u32[]{:S(2)}) collective-permute-start(bf16[8,3584]{1,0:T(8,128)(2,1)S(1)} %get-tuple-element.27), channel_id=1, source_target_pairs={{0,2},{1,9},{2,0},{3,11},{4,6},{5,13},{6,4},{7,15},{8,10},{9,1},{1... | collective-permute-start | bytes 172040 | tf_op jit(solution)/shard_map/ppermute | solution.py:245
  55.8 0.1 collective-permute-done.18.refs_2_
  55.9 0.4 collective-permute-done.19.refs_3_
  56.3 0.1 shard_map.108
  56.4 0.1 collective-permute-start.20
  56.4 0.1 collective-permute-start.21
  56.5 1.5 %collective-permute-done.14.refs_1_ = bf16[8,3584]{1,0:T(8,128)(2,1)S(1)} collective-permute-done((bf16[8,3584]{1,0:T(8,128)(2,1)S(1)}, bf16[8,3584]{1,0:T(8,128)(2,1)S(1)}, u32[]{:S(2)}, u32[]{:S(2)}) %collective-permute-start.14) | collective-permute-done | bytes 57376 | tf_op jit(solution)/shard_map/ppermute | solution.py:245
  58.0 2.8 %collective-permute-start.22 = (bf16[8,3584]{1,0:T(8,128)(2,1)S(1)}, bf16[8,3584]{1,0:T(8,128)(2,1)S(1)}, u32[]{:S(2)}, u32[]{:S(2)}) collective-permute-start(bf16[8,3584]{1,0:T(8,128)(2,1)S(1)} %get-tuple-element.34), channel_id=1, source_target_pairs={{0,8},{1,3},{2,10},{3,1},{4,12},{5,7},{6,14},{7,5},{8,0},{9,11},{1... | collective-permute-start | bytes 172040 | tf_op jit(solution)/shard_map/ppermute | solution.py:245
  60.8 0.0 collective-permute-done.15.refs_2_
  60.8 0.0 collective-permute-done.16.refs_3_
  60.8 1.6 %collective-permute-done.20.refs_4_ = bf16[8,3584]{1,0:T(8,128)(2,1)S(1)} collective-permute-done((bf16[8,3584]{1,0:T(8,128)(2,1)S(1)}, bf16[8,3584]{1,0:T(8,128)(2,1)S(1)}, u32[]{:S(2)}, u32[]{:S(2)}) %collective-permute-start.20) | collective-permute-done | bytes 57376 | tf_op jit(solution)/shard_map/ppermute | solution.py:245
  62.4 0.0 collective-permute-done.21.refs_5_
  62.4 0.6 collective-permute-done.22.refs_6_
  63.0 0.7 %shard_map.109 = bf16[8,3584]{1,0:T(8,128)(2,1)} custom-call(bf16[8,3584]{1,0:T(8,128)(2,1)S(1)} %get-tuple-element.24.refs_0_, bf16[8,3584]{1,0:T(8,128)(2,1)S(1)} %collective-permute-done.14.refs_1_, bf16[8,3584]{1,0:T(8,128)(2,1)S(1)} %collective-permute-done.15.refs_2_, bf16[8,3584]{1,0:T(8,128)(2,1)S(1)} %collective-permute-done.16.refs_3_, ...), custom_call_target="tpu_custom_call" | custom-call | flops 200704 | bytes 401408 | tf_op jit(solution)/shard_map/pallas_call | solution.py:209
  (8 shorter events, 0.2 us)
Async XLA Ops:
  0.6 30.2 %copy-start = (bf16[4,256,576]{1,2,0:T(8,128)(2,1)S(1)}, bf16[4,256,576]{1,2,0:T(8,128)(2,1)}, u32[]{:S(2)}) copy-start(bf16[4,256,576]{1,2,0:T(8,128)(2,1)} %param.16) | copy-start | bytes 3538948
  1.7 28.5 %collective-permute-start.5 = (bf16[8,3712]{1,0:T(8,128)(2,1)S(1)}, bf16[8,3712]{1,0:T(8,128)(2,1)S(1)}, u32[]{:S(2)}, u32[]{:S(2)}) collective-permute-start(bf16[8,3712]{1,0:T(8,128)(2,1)S(1)} %shard_map.104), channel_id=1, source_target_pairs={{0,6},{1,25},{2,4},{3,27},{4,2},{5,29},{6,0},{7,31},{8,14},{9,17},... | collective-permute-start | bytes 178184 | tf_op jit(solution)/shard_map/ppermute | solution.py:245
  5.6 23.9 %collective-permute-start.4 = (bf16[8,3712]{1,0:T(8,128)(2,1)S(1)}, bf16[8,3712]{1,0:T(8,128)(2,1)S(1)}, u32[]{:S(2)}, u32[]{:S(2)}) collective-permute-start(bf16[8,3712]{1,0:T(8,128)(2,1)S(1)} %shard_map.104), channel_id=1, source_target_pairs={{0,4},{1,17},{2,6},{3,19},{4,0},{5,21},{6,2},{7,23},{8,12},{9,25},... | collective-permute-start | bytes 178184 | tf_op jit(solution)/shard_map/ppermute | solution.py:245
  6.1 22.6 %collective-permute-start.3 = (bf16[8,3712]{1,0:T(8,128)(2,1)S(1)}, bf16[8,3712]{1,0:T(8,128)(2,1)S(1)}, u32[]{:S(2)}, u32[]{:S(2)}) collective-permute-start(bf16[8,3712]{1,0:T(8,128)(2,1)S(1)} %shard_map.104), channel_id=1, source_target_pairs={{0,2},{1,9},{2,0},{3,11},{4,6},{5,13},{6,4},{7,15},{8,10},{9,1},{1... | collective-permute-start | bytes 178184 | tf_op jit(solution)/shard_map/ppermute | solution.py:245
  6.3 15.0 %collective-permute-start.2 = (bf16[8,3712]{1,0:T(8,128)(2,1)S(1)}, bf16[8,3712]{1,0:T(8,128)(2,1)S(1)}, u32[]{:S(2)}, u32[]{:S(2)}) collective-permute-start(bf16[8,3712]{1,0:T(8,128)(2,1)S(1)} %shard_map.104), channel_id=1, source_target_pairs={{0,24},{1,7},{2,26},{3,5},{4,28},{5,3},{6,30},{7,1},{8,16},{9,15},... | collective-permute-start | bytes 178184 | tf_op jit(solution)/shard_map/ppermute | solution.py:245
  10.3 4.2 %collective-permute-start = (bf16[8,3712]{1,0:T(8,128)(2,1)S(1)}, bf16[8,3712]{1,0:T(8,128)(2,1)S(1)}, u32[]{:S(2)}, u32[]{:S(2)}) collective-permute-start(bf16[8,3712]{1,0:T(8,128)(2,1)S(1)} %shard_map.104), channel_id=1, source_target_pairs={{0,8},{1,3},{2,10},{3,1},{4,12},{5,7},{6,14},{7,5},{8,0},{9,11},{1... | collective-permute-start | bytes 178184 | tf_op jit(solution)/shard_map/ppermute | solution.py:245
  14.5 6.2 %collective-permute-start.1 = (bf16[8,3712]{1,0:T(8,128)(2,1)S(1)}, bf16[8,3712]{1,0:T(8,128)(2,1)S(1)}, u32[]{:S(2)}, u32[]{:S(2)}) collective-permute-start(bf16[8,3712]{1,0:T(8,128)(2,1)S(1)} %shard_map.104), channel_id=1, source_target_pairs={{0,16},{1,5},{2,18},{3,7},{4,20},{5,1},{6,22},{7,3},{8,24},{9,13},... | collective-permute-start | bytes 178184 | tf_op jit(solution)/shard_map/ppermute | solution.py:245
  21.9 16.2 %collective-permute-start.8 = (bf16[24,3712]{1,0:T(8,128)(2,1)S(1)}, bf16[24,3712]{1,0:T(8,128)(2,1)S(1)}, u32[]{:S(2)}, u32[]{:S(2)}) collective-permute-start(bf16[24,3712]{1,0:T(8,128)(2,1)S(1)} %get-tuple-element.44.after_ref), channel_id=1, source_target_pairs={{0,6},{1,25},{2,4},{3,27},{4,2},{5,29},{6,0},{7,31},{8,14},{9,17},... | collective-permute-start | bytes 534536 | tf_op jit(solution)/shard_map/ppermute | solution.py:245
  28.4 10.4 %collective-permute-start.7 = (bf16[24,3712]{1,0:T(8,128)(2,1)S(1)}, bf16[24,3712]{1,0:T(8,128)(2,1)S(1)}, u32[]{:S(2)}, u32[]{:S(2)}) collective-permute-start(bf16[24,3712]{1,0:T(8,128)(2,1)S(1)} %get-tuple-element.44.after_ref), channel_id=1, source_target_pairs={{0,4},{1,17},{2,6},{3,19},{4,0},{5,21},{6,2},{7,23},{8,12},{9,25},... | collective-permute-start | bytes 534536 | tf_op jit(solution)/shard_map/ppermute | solution.py:245
  28.7 10.1 %collective-permute-start.6 = (bf16[24,3712]{1,0:T(8,128)(2,1)S(1)}, bf16[24,3712]{1,0:T(8,128)(2,1)S(1)}, u32[]{:S(2)}, u32[]{:S(2)}) collective-permute-start(bf16[24,3712]{1,0:T(8,128)(2,1)S(1)} %get-tuple-element.44.after_ref), channel_id=1, source_target_pairs={{0,2},{1,9},{2,0},{3,11},{4,6},{5,13},{6,4},{7,15},{8,10},{9,1},{1... | collective-permute-start | bytes 534536 | tf_op jit(solution)/shard_map/ppermute | solution.py:245
  30.8 8.5 %collective-permute-start.9 = (bf16[56,3712]{1,0:T(8,128)(2,1)}, bf16[56,3712]{1,0:T(8,128)(2,1)S(1)}, u32[]{:S(2)}, u32[]{:S(2)}) collective-permute-start(bf16[56,3712]{1,0:T(8,128)(2,1)} %get-tuple-element.36), channel_id=1, source_target_pairs={{0,1},{1,0},{2,3},{3,2},{4,5},{5,4},{6,7},{7,6},{8,9},{9,8},{10,11... | collective-permute-start | bytes 1247240 | tf_op jit(solution)/shard_map/ppermute | solution.py:254
  30.9 1.1 %copy-start.1 = (bf16[4,128,576]{1,2,0:T(8,128)(2,1)S(1)}, bf16[4,128,576]{1,2,0:T(8,128)(2,1)}, u32[]{:S(2)}) copy-start(bf16[4,128,576]{1,2,0:T(8,128)(2,1)} %param.15) | copy-start | bytes 1769476
  31.9 0.7 %copy-start.2 = (s32[4]{0:T(128)S(1)}, s32[4]{0:T(128)}, u32[]{:S(2)}) copy-start(s32[4]{0:T(128)} %lengths_ref.1) | copy-start | bytes 52
  38.2 2.3 %collective-permute-start.12 = (bf16[24,3712]{1,0:T(8,128)(2,1)S(1)}, bf16[24,3712]{1,0:T(8,128)(2,1)S(1)}, u32[]{:S(2)}, u32[]{:S(2)}) collective-permute-start(bf16[24,3712]{1,0:T(8,128)(2,1)S(1)} %collective-permute-done.8), channel_id=1, source_target_pairs={{0,1},{1,0},{2,3},{3,2},{4,5},{5,4},{6,7},{7,6},{8,9},{9,8},{10,11... | collective-permute-start | bytes 534536 | tf_op jit(solution)/shard_map/ppermute | solution.py:254
  38.7 1.7 %collective-permute-start.11 = (bf16[24,3712]{1,0:T(8,128)(2,1)S(1)}, bf16[24,3712]{1,0:T(8,128)(2,1)S(1)}, u32[]{:S(2)}, u32[]{:S(2)}) collective-permute-start(bf16[24,3712]{1,0:T(8,128)(2,1)S(1)} %collective-permute-done.7), channel_id=1, source_target_pairs={{0,1},{1,0},{2,3},{3,2},{4,5},{5,4},{6,7},{7,6},{8,9},{9,8},{10,11... | collective-permute-start | bytes 534536 | tf_op jit(solution)/shard_map/ppermute | solution.py:254
  38.8 1.6 %collective-permute-start.10 = (bf16[24,3712]{1,0:T(8,128)(2,1)S(1)}, bf16[24,3712]{1,0:T(8,128)(2,1)S(1)}, u32[]{:S(2)}, u32[]{:S(2)}) collective-permute-start(bf16[24,3712]{1,0:T(8,128)(2,1)S(1)} %collective-permute-done.6), channel_id=1, source_target_pairs={{0,1},{1,0},{2,3},{3,2},{4,5},{5,4},{6,7},{7,6},{8,9},{9,8},{10,11... | collective-permute-start | bytes 534536 | tf_op jit(solution)/shard_map/ppermute | solution.py:254
  44.8 2.5 %collective-permute-start.13 = (bf16[128,3584]{1,0:T(8,128)(2,1)S(1)}, bf16[128,3584]{1,0:T(8,128)(2,1)S(1)}, u32[]{:S(2)}, u32[]{:S(2)}) collective-permute-start(bf16[128,3584]{1,0:T(8,128)(2,1)S(1)} %get-tuple-element.23), channel_id=1, source_target_pairs={{0,1},{1,0},{2,3},{3,2},{4,5},{5,4},{6,7},{7,6},{8,9},{9,8},{10,11... | collective-permute-start | bytes 2752520 | tf_op jit(solution)/shard_map/ppermute | solution.py:254
  47.5 6.8 %collective-permute-start.17 = (bf16[24,3584]{1,0:T(8,128)(2,1)S(1)}, bf16[24,3584]{1,0:T(8,128)(2,1)S(1)}, u32[]{:S(2)}, u32[]{:S(2)}) collective-permute-start(bf16[24,3584]{1,0:T(8,128)(2,1)S(1)} %get-tuple-element.29), channel_id=1, source_target_pairs={{0,6},{1,25},{2,4},{3,27},{4,2},{5,29},{6,0},{7,31},{8,14},{9,17},... | collective-permute-start | bytes 516104 | tf_op jit(solution)/shard_map/ppermute | solution.py:245
  50.5 5.4 %collective-permute-start.18 = (bf16[24,3584]{1,0:T(8,128)(2,1)S(1)}, bf16[24,3584]{1,0:T(8,128)(2,1)S(1)}, u32[]{:S(2)}, u32[]{:S(2)}) collective-permute-start(bf16[24,3584]{1,0:T(8,128)(2,1)S(1)} %get-tuple-element.30), channel_id=1, source_target_pairs={{0,4},{1,17},{2,6},{3,19},{4,0},{5,21},{6,2},{7,23},{8,12},{9,25},... | collective-permute-start | bytes 516104 | tf_op jit(solution)/shard_map/ppermute | solution.py:245
  50.9 5.4 %collective-permute-start.19 = (bf16[24,3584]{1,0:T(8,128)(2,1)S(1)}, bf16[24,3584]{1,0:T(8,128)(2,1)S(1)}, u32[]{:S(2)}, u32[]{:S(2)}) collective-permute-start(bf16[24,3584]{1,0:T(8,128)(2,1)S(1)} %get-tuple-element.31), channel_id=1, source_target_pairs={{0,2},{1,9},{2,0},{3,11},{4,6},{5,13},{6,4},{7,15},{8,10},{9,1},{1... | collective-permute-start | bytes 516104 | tf_op jit(solution)/shard_map/ppermute | solution.py:245
  51.1 6.9 %collective-permute-start.14 = (bf16[8,3584]{1,0:T(8,128)(2,1)S(1)}, bf16[8,3584]{1,0:T(8,128)(2,1)S(1)}, u32[]{:S(2)}, u32[]{:S(2)}) collective-permute-start(bf16[8,3584]{1,0:T(8,128)(2,1)S(1)} %get-tuple-element.25), channel_id=1, source_target_pairs={{0,6},{1,25},{2,4},{3,27},{4,2},{5,29},{6,0},{7,31},{8,14},{9,17},... | collective-permute-start | bytes 172040 | tf_op jit(solution)/shard_map/ppermute | solution.py:245
  54.0 6.8 %collective-permute-start.15 = (bf16[8,3584]{1,0:T(8,128)(2,1)S(1)}, bf16[8,3584]{1,0:T(8,128)(2,1)S(1)}, u32[]{:S(2)}, u32[]{:S(2)}) collective-permute-start(bf16[8,3584]{1,0:T(8,128)(2,1)S(1)} %get-tuple-element.26), channel_id=1, source_target_pairs={{0,4},{1,17},{2,6},{3,19},{4,0},{5,21},{6,2},{7,23},{8,12},{9,25},... | collective-permute-start | bytes 172040 | tf_op jit(solution)/shard_map/ppermute | solution.py:245
  54.4 6.5 %collective-permute-start.16 = (bf16[8,3584]{1,0:T(8,128)(2,1)S(1)}, bf16[8,3584]{1,0:T(8,128)(2,1)S(1)}, u32[]{:S(2)}, u32[]{:S(2)}) collective-permute-start(bf16[8,3584]{1,0:T(8,128)(2,1)S(1)} %get-tuple-element.27), channel_id=1, source_target_pairs={{0,2},{1,9},{2,0},{3,11},{4,6},{5,13},{6,4},{7,15},{8,10},{9,1},{1... | collective-permute-start | bytes 172040 | tf_op jit(solution)/shard_map/ppermute | solution.py:245
  56.4 6.0 %collective-permute-start.20 = (bf16[8,3584]{1,0:T(8,128)(2,1)S(1)}, bf16[8,3584]{1,0:T(8,128)(2,1)S(1)}, u32[]{:S(2)}, u32[]{:S(2)}) collective-permute-start(bf16[8,3584]{1,0:T(8,128)(2,1)S(1)} %get-tuple-element.32), channel_id=1, source_target_pairs={{0,24},{1,7},{2,26},{3,5},{4,28},{5,3},{6,30},{7,1},{8,16},{9,15},... | collective-permute-start | bytes 172040 | tf_op jit(solution)/shard_map/ppermute | solution.py:245
  56.4 6.0 %collective-permute-start.21 = (bf16[8,3584]{1,0:T(8,128)(2,1)S(1)}, bf16[8,3584]{1,0:T(8,128)(2,1)S(1)}, u32[]{:S(2)}, u32[]{:S(2)}) collective-permute-start(bf16[8,3584]{1,0:T(8,128)(2,1)S(1)} %get-tuple-element.33), channel_id=1, source_target_pairs={{0,16},{1,5},{2,18},{3,7},{4,20},{5,1},{6,22},{7,3},{8,24},{9,13},... | collective-permute-start | bytes 172040 | tf_op jit(solution)/shard_map/ppermute | solution.py:245
  58.0 5.0 %collective-permute-start.22 = (bf16[8,3584]{1,0:T(8,128)(2,1)S(1)}, bf16[8,3584]{1,0:T(8,128)(2,1)S(1)}, u32[]{:S(2)}, u32[]{:S(2)}) collective-permute-start(bf16[8,3584]{1,0:T(8,128)(2,1)S(1)} %get-tuple-element.34), channel_id=1, source_target_pairs={{0,8},{1,3},{2,10},{3,1},{4,12},{5,7},{6,14},{7,5},{8,0},{9,11},{1... | collective-permute-start | bytes 172040 | tf_op jit(solution)/shard_map/ppermute | solution.py:245

commit v4 on v3

--- a/solution.py
+++ b/solution.py
@@ -13,6 +13,7 @@
 SOFTMAX_SCALE = 192.0 ** (-0.5)
 ROUTE_SCALE = 2.5
 LANES = 128
+FETCHES = 2
 
 
 VMEM = pl.BlockSpec(memory_space=pltpu.VMEM)
@@ -33,13 +34,19 @@
     return pltpu.with_memory_space_constraint(value, pltpu.VMEM)
 
 
-def attend_kernel(lengths_ref, query_ref, cache_ref, gate_ref, up_ref, down_ref, after_ref, out_ref, *rest):
-    copies = [
-        pltpu.make_async_copy(source, target, rest[3].at[i])
-        for i, (source, target) in enumerate(zip((gate_ref, up_ref, down_ref), rest[:3], strict=True))
-    ]
+def attend_kernel(
+    lengths_hbm, query_hbm, cache_hbm, gate_hbm, up_hbm, down_hbm, after_ref,
+    out_ref, gate_ref, up_ref, down_ref, token_ref, lengths_ref, query_ref, cache_ref, sems,
+):
+    pairs = [(lengths_hbm, lengths_ref), (query_hbm, query_ref), (cache_hbm, cache_ref)]
+    for source, target in ((gate_hbm, gate_ref), (up_hbm, up_ref), (down_hbm, down_ref)):
+        rows = source.shape[0] // FETCHES
+        pairs += [(source.at[pl.ds(i * rows, rows)], target.at[pl.ds(i * rows, rows)]) for i in range(FETCHES)]
+    copies = [pltpu.make_async_copy(s, t, sems.at[i]) for i, (s, t) in enumerate(pairs)]
     for copy in copies:
         copy.start()
+    for copy in copies[:3]:
+        copy.wait()
     latent = out_ref.shape[2]
     for r in range(query_ref.shape[0]):
         query, cache = query_ref[r], cache_ref[r]
@@ -54,29 +61,38 @@
         out_ref[r] = lax.dot_general(
             probability, cache[:latent], (((1,), (1,)), ((), ())), preferred_element_type=jnp.float32
         ).astype(jnp.bfloat16)
-    for copy in copies:
+    token_ref[...] = jnp.zeros_like(token_ref)
+    for copy in copies[3:]:
         copy.wait()
 
 
 def attend(query_latent, latent_cache, cache_lengths, weights, after):
     rows, heads, entries = query_latent.shape
     positions = latent_cache.shape[1]
+    query, cache = jnp.swapaxes(query_latent, 1, 2), jnp.swapaxes(latent_cache, 1, 2)
+    operands = (cache_lengths, query, cache, *weights)
     return pl.pallas_call(
         attend_kernel,
         out_shape=(
             jax.ShapeDtypeStruct((rows, heads, LATENT), jnp.bfloat16),
             *(in_vmem(w.shape, w.dtype) for w in weights),
+            in_vmem((8, LANES), jnp.float32),
         ),
-        in_specs=[SMEM, VMEM, VMEM, HBM, HBM, HBM, ANY],
-        out_specs=(VMEM,) * 4,
-        scratch_shapes=[pltpu.SemaphoreType.DMA((3,))],
-        compiler_params=pltpu.CompilerParams(vmem_limit_bytes=8 << 20),
+        in_specs=[HBM] * 6 + [ANY],
+        out_specs=(VMEM,) * 5,
+        scratch_shapes=[
+            pltpu.SMEM(cache_lengths.shape, jnp.int32),
+            pltpu.VMEM(query.shape, query.dtype),
+            pltpu.VMEM(cache.shape, cache.dtype),
+            pltpu.SemaphoreType.DMA((3 + 3 * FETCHES,)),
+        ],
+        compiler_params=pltpu.CompilerParams(vmem_limit_bytes=12 << 20),
         cost_estimate=pl.CostEstimate(
             flops=4 * rows * heads * positions * entries,
             bytes_accessed=2 * sum(w.size for w in weights),
             transcendentals=rows * heads * positions,
         ),
-    )(cache_lengths, jnp.swapaxes(query_latent, 1, 2), jnp.swapaxes(latent_cache, 1, 2), *(stored(w) for w in weights), after)
+    )(*(stored(v) for v in operands), after)
 
 
 def rounds_up(value, step):
@@ -130,14 +146,54 @@
     )(stored(hidden_in), stored(expert_routes), stored(route_scores))
 
 
-def expert_kernel(me_ref, rows_ref, gate_ref, up_ref, down_ref, mine_ref, other_ref, hidden_ref):
+def join_kernel(*refs):
+    value = jnp.concatenate([ref[...].astype(jnp.float32) for ref in refs[:-1]], axis=0)
+    refs[-1][...] = value.astype(jnp.bfloat16)
+
+
+def join(pieces):
+    total, width = sum(p.shape[0] for p in pieces), pieces[0].shape[1]
+    return pl.pallas_call(
+        join_kernel,
+        out_shape=in_vmem((total, width), jnp.bfloat16),
+        in_specs=[VMEM] * len(pieces),
+        out_specs=VMEM,
+        compiler_params=pltpu.CompilerParams(vmem_limit_bytes=(2 << 20) + 8 * total * width),
+        cost_estimate=pl.CostEstimate(flops=total * width, bytes_accessed=4 * total * width, transcendentals=0),
+    )(*(held(p) for p in pieces))
+
+
+def tie_kernel(value_ref, after_ref, out_ref):
+    pass
+
+
+def tie(value, after):
+    return pl.pallas_call(
+        tie_kernel,
+        out_shape=in_vmem(value.shape, value.dtype),
+        in_specs=[VMEM, VMEM],
+        out_specs=VMEM,
+        input_output_aliases={0: 0},
+        compiler_params=pltpu.CompilerParams(vmem_limit_bytes=1 << 20),
+        cost_estimate=pl.CostEstimate(flops=0, bytes_accessed=0, transcendentals=0),
+    )(held(value), held(after))
+
+
+def expert_kernel(count, *refs):
+    pieces = refs[:count]
+    gate_ref, up_ref, down_ref, mine_ref, other_ref, rows_ref, hidden_ref = refs[count:]
     total, _ = rows_ref.shape
     model_width, units = gate_ref.shape
     lanes = rows_ref.shape[1] - model_width
     half = total // 2
-    me = me_ref[0]
+    me = lax.axis_index("ep")
     block = min(total, 256)
     chunk = 256
+
+    low = 0
+    for piece in pieces:
+        rows_ref[low : low + piece.shape[0], :] = piece[...]
+        low += piece.shape[0]
 
     @pl.loop(0, total // block)
     def _(i):
@@ -173,50 +229,47 @@
                 other_ref[: high - half, cols] = value[half - low :]
 
 
-def expert_block(rows, expert_gate, expert_up, expert_down, me):
-    total, width = rows.shape
+def expert_block(pieces, expert_gate, expert_up, expert_down):
+    total, width = sum(p.shape[0] for p in pieces), pieces[0].shape[1]
     model_width, units = expert_gate.shape
     out = in_vmem((total // 2, model_width), jnp.bfloat16)
     return pl.pallas_call(
-        expert_kernel,
+        functools.partial(expert_kernel, len(pieces)),
         out_shape=(out, out),
-        in_specs=[SMEM] + [VMEM] * 4,
+        in_specs=[VMEM] * (len(pieces) + 3),
         out_specs=(VMEM, VMEM),
-        scratch_shapes=[pltpu.VMEM((total, units), jnp.bfloat16)],
-        compiler_params=pltpu.CompilerParams(vmem_limit_bytes=(8 << 20) + 4 * total * units),
+        scratch_shapes=[pltpu.VMEM((total, width), jnp.bfloat16), pltpu.VMEM((total, units), jnp.bfloat16)],
+        compiler_params=pltpu.CompilerParams(vmem_limit_bytes=(8 << 20) + 4 * total * units + 2 * total * width),
         cost_estimate=pl.CostEstimate(
             flops=6 * total * model_width * units,
             bytes_accessed=4 * total * width,
             transcendentals=total * units,
         ),
-    )(me.reshape(1), held(rows), *(held(w) for w in (expert_gate, expert_up, expert_down)))
-
-
-def add_kernel(base_count, sizes, *refs):
-    values = [ref[...].astype(jnp.float32) for ref in refs[:base_count]]
-    total = values[0]
-    for value in values[1:]:
-        total += value
+    )(*(held(p) for p in pieces), *(held(w) for w in (expert_gate, expert_up, expert_down)))
+
+
+def add_kernel(count, rows, sizes, *refs):
+    total = None
+    for ref, (low, high) in zip(refs[:count], rows, strict=True):
+        value = ref[...].astype(jnp.float32)[low:high]
+        total = value if total is None else total + value
     low = 0
-    for out_ref, size in zip(refs[base_count:], sizes, strict=True):
+    for out_ref, size in zip(refs[count:], sizes, strict=True):
         out_ref[...] = total[low : low + size].astype(jnp.bfloat16)
         low += size
 
 
-def add(values, sizes, last=False):
-    rows, width = values[0].shape
+def add(values, rows, sizes, last=False):
+    width = values[0].shape[1]
     shape = jax.ShapeDtypeStruct if last else in_vmem
-    return pl.pallas_call(
-        functools.partial(add_kernel, len(values), sizes),
+    elements = sum(v.size for v in values)
+    return pl.pallas_call(
+        functools.partial(add_kernel, len(values), rows, sizes),
         out_shape=tuple(shape((size, width), jnp.bfloat16) for size in sizes),
         in_specs=[VMEM] * len(values),
         out_specs=(VMEM,) * len(sizes),
-        compiler_params=pltpu.CompilerParams(vmem_limit_bytes=(4 << 20) + 8 * rows * width),
-        cost_estimate=pl.CostEstimate(
-            flops=len(values) * rows * width,
-            bytes_accessed=2 * len(values) * rows * width,
-            transcendentals=0,
-        ),
+        compiler_params=pltpu.CompilerParams(vmem_limit_bytes=(4 << 20) + 8 * values[0].size),
+        cost_estimate=pl.CostEstimate(flops=elements, bytes_accessed=2 * elements, transcendentals=0),
     )(*(held(v) for v in values))
 
 
@@ -233,7 +286,7 @@
 ):
     tok_rows, model_width = hidden_in.shape
     ep_count, sub_count = lax.axis_size("ep"), lax.axis_size("sub")
-    inner = 4 if ep_count % 4 == 0 else 1
+    inner = 4
     outer = ep_count // inner
 
     def swap(value, even, odd):
@@ -253,35 +306,32 @@
     def over_cores(value):
         return lax.ppermute(value, "sub", [(i, i ^ 1) for i in range(sub_count)])
 
-    def order(count):
-        return list(range(1, count))[::-1]
-
     own = pack(hidden_in, expert_routes, route_scores, ep_count)
-    near = {k: first(own, k) for k in order(outer)}
-    side = {k: second(own, k) for k in order(inner)}
-    column = jnp.concatenate([near[k] for k in range(1, outer)], axis=0)
-    far = {k: second(column, k) for k in (order(inner)[1:] + order(inner)[:1])}
-    attention_latent, *weights = attend(
+    near = {k: first(own, k) for k in range(outer - 1, 0, -1)}
+    block = join([own] + [near[k] for k in range(1, outer)])
+    steps = [*range(inner - 2, 0, -1), inner - 1]
+    far = {k: second(block, k) for k in steps}
+    attention_latent, *weights, token = attend(
         query_latent,
         latent_cache,
         cache_lengths,
         (expert_gate[0], expert_up[0], expert_down[0]),
-        column,
-    )
-    early = jnp.concatenate([own, column] + [side[k] for k in range(1, inner)], axis=0)
-    pieces = [early] + [far[k] for k in range(1, inner)]
-    rows = jnp.concatenate(pieces + [over_cores(p) for p in pieces], axis=0)
-
-    mine, other = expert_block(rows, *weights, lax.axis_index("ep"))
-
-    step = (outer - 1) * tok_rows
-    sizes = [tok_rows, step] + [tok_rows] * (inner - 1) + [step] * (inner - 1)
-    kept, column, *parts = add([mine, over_cores(other)], sizes)
-    far = [second(parts[inner - 1 + k - 1], k) for k in order(inner)]
-    side = [second(parts[k - 1], k) for k in order(inner)]
-    near = add([column, *far], [tok_rows] * (outer - 1))
-    near = [first(near[k - 1], k) for k in order(outer)]
-    (moe_output,) = add([kept, *side, *near], [tok_rows], last=True)
+        block,
+    )
+    pieces = [block] + [tie(far[k], token) for k in range(1, inner)]
+    pieces += [over_cores(p) for p in pieces]
+    mine, other = expert_block(pieces, *weights)
+
+    size = outer * tok_rows
+    kept, column, *parts = add(
+        [mine, over_cores(other)], [(0, size * inner)] * 2, [tok_rows, size - tok_rows] + [size] * (inner - 1)
+    )
+    far = [second(parts[k - 1], k) for k in steps]
+    near = add(
+        [column, *far], [(0, size - tok_rows)] + [(tok_rows, size)] * len(far), [tok_rows] * (outer - 1)
+    )
+    near = [first(near[k - 1], k) for k in range(outer - 1, 0, -1)]
+    (moe_output,) = add([kept, *far, *near], [(0, tok_rows)] * (1 + len(far) + len(near)), [tok_rows], last=True)
     return (moe_output, attention_latent)
 
 

time: 63.9 us -> 49.4 us (0.77)
  starting transfers between devices: 28.3 us -> 18.6 us
  local copies, waits for them, and re-layouts: 6.3 us -> 0 us
  waiting for transfers between devices: 16.6 us -> 18.2 us
    ppermute x18 -> x12, starting transfers between devices: 26.8 us -> 17.3 us  [swap(): return lax.ppermute(value, ('ep', 'sub'), pairs)]
    unnamed x18 -> x0, local copies, waits for them, and re-layouts: 5.64 us -> none
    ppermute x18 -> x12, waiting for transfers between devices: 13.3 us -> 14.6 us  [swap(): return lax.ppermute(value, ('ep', 'sub'), pairs)]
    concatenate x2 -> x0, local copies, waits for them, and re-layouts: 0.66 us -> none  [the longest x1 0.64 us: per_device(): jnp.concatenate([own, column] + [side[k] for k in range(1, inner)], axis=0)]
    pallas_call x4 -> x8, Pallas kernels: 5.24 us -> 5.22 us  [the longest x1 4.21 us: expert_block(): pl.pallas_call(functools.partial(expert_kernel, len(pieces)), out_shape=(...]
  transfers between devices with their start and end apart: 23 -> 17, of which waited for: 9 -> 12; matrix products, arithmetic and copies ran while one was open for 7% -> 0% of each run, Pallas kernels for 9% -> 11%
where the time goes in v4:
time: 49.4 us; the launch traced here: 49.3 us
  starting transfers between devices  18.6 us (38%)
  waiting for transfers between devices  18.2 us (37%)
  Pallas kernels  11.7 us (24%)
  between operations  0.7 us (1%)
    ppermute x12, starting transfers between devices, swap(): return lax.ppermute(value, ('ep', 'sub'), pairs)  17.3 us
    ppermute x12, waiting for transfers between devices, swap(): return lax.ppermute(value, ('ep', 'sub'), pairs)  14.6 us
    pallas_call x1, Pallas kernels, attend(): pl.pallas_call(attend_kernel, out_shape=(jax.ShapeDtypeStruct((rows, head...  5.58 us
    pallas_call x1, Pallas kernels, expert_block(): pl.pallas_call(functools.partial(expert_kernel, len(pieces)), out_shape=(...  4.21 us
    ppermute x5, waiting for transfers between devices, over_cores(): return lax.ppermute(value, 'sub', [(i, i ^ 1) for i in range(sub_count)])  3.62 us
    ppermute x5, starting transfers between devices, over_cores(): return lax.ppermute(value, 'sub', [(i, i ^ 1) for i in range(sub_count)])  1.32 us
  transfers between devices with their start and end apart: 17, of which 12 were waited for; matrix products, arithmetic and copies ran while one was open for 0% of the time, Pallas kernels for 11%

profile of v4, /device:TPU:0, one launch (start us, length us, event | category | flops | bytes accessed | tf_op | source)
XLA Modules:
  0.0 49.3 jit_solution(13547186231907906035)
XLA Ops:
  0.6 0.9 %shard_map.104.refs_0_ = bf16[8,3712]{1,0:T(8,128)(2,1)S(1)} custom-call(bf16[8,3584]{1,0:T(8,128)(2,1)} %hidden_ref.1, s32[8,8]{1,0:T(8,128)} %routes_ref.1, f32[8,8]{1,0:T(8,128)} %scores_ref.1), custom_call_target="tpu_custom_call" | custom-call | flops 65536 | bytes 114688 | tf_op jit(solution)/shard_map/pallas_call | solution.py:133
  1.6 5.1 %collective-permute-start.2 = (bf16[8,3712]{1,0:T(8,128)(2,1)S(1)}, bf16[8,3712]{1,0:T(8,128)(2,1)S(1)}, u32[]{:S(2)}, u32[]{:S(2)}) collective-permute-start(bf16[8,3712]{1,0:T(8,128)(2,1)S(1)} %shard_map.104.refs_0_), channel_id=1, source_target_pairs={{0,24},{1,7},{2,26},{3,5},{4,28},{5,3},{6,30},{7,1},{8,16},{9,15},... | collective-permute-start | bytes 178184 | tf_op jit(solution)/shard_map/ppermute | solution.py:298
  6.7 0.0 collective-permute-start.1
  6.7 0.6 %collective-permute-start = (bf16[8,3712]{1,0:T(8,128)(2,1)S(1)}, bf16[8,3712]{1,0:T(8,128)(2,1)S(1)}, u32[]{:S(2)}, u32[]{:S(2)}) collective-permute-start(bf16[8,3712]{1,0:T(8,128)(2,1)S(1)} %shard_map.104.refs_0_), channel_id=1, source_target_pairs={{0,8},{1,3},{2,10},{3,1},{4,12},{5,7},{6,14},{7,5},{8,0},{9,11},{1... | collective-permute-start | bytes 178184 | tf_op jit(solution)/shard_map/ppermute | solution.py:298
  7.3 1.6 %collective-permute-done.2.refs_3_ = bf16[8,3712]{1,0:T(8,128)(2,1)S(1)} collective-permute-done((bf16[8,3712]{1,0:T(8,128)(2,1)S(1)}, bf16[8,3712]{1,0:T(8,128)(2,1)S(1)}, u32[]{:S(2)}, u32[]{:S(2)}) %collective-permute-start.2) | collective-permute-done | bytes 59424 | tf_op jit(solution)/shard_map/ppermute | solution.py:298
  8.9 2.9 %collective-permute-done.1.refs_2_ = bf16[8,3712]{1,0:T(8,128)(2,1)S(1)} collective-permute-done((bf16[8,3712]{1,0:T(8,128)(2,1)S(1)}, bf16[8,3712]{1,0:T(8,128)(2,1)S(1)}, u32[]{:S(2)}, u32[]{:S(2)}) %collective-permute-start.1) | collective-permute-done | bytes 59424 | tf_op jit(solution)/shard_map/ppermute | solution.py:298
  11.8 0.0 collective-permute-done.refs_1_
  11.8 1.9 %collective-permute-start.3 = (bf16[32,3712]{1,0:T(8,128)(2,1)S(1)}, bf16[32,3712]{1,0:T(8,128)(2,1)S(1)}, u32[]{:S(2)}, u32[]{:S(2)}) collective-permute-start(bf16[32,3712]{1,0:T(8,128)(2,1)S(1)} %shard_map.105.after_ref.refs_0_), channel_id=1, source_target_pairs={{0,2},{1,9},{2,0},{3,11},{4,6},{5,13},{6,4},{7,15},{8,10},{9,1},{1... | collective-permute-start | bytes 712712 | tf_op jit(solution)/shard_map/ppermute | solution.py:298
  13.7 1.5 %collective-permute-start.4 = (bf16[32,3712]{1,0:T(8,128)(2,1)S(1)}, bf16[32,3712]{1,0:T(8,128)(2,1)S(1)}, u32[]{:S(2)}, u32[]{:S(2)}) collective-permute-start(bf16[32,3712]{1,0:T(8,128)(2,1)S(1)} %shard_map.105.after_ref.refs_0_), channel_id=1, source_target_pairs={{0,4},{1,17},{2,6},{3,19},{4,0},{5,21},{6,2},{7,23},{8,12},{9,25},... | collective-permute-start | bytes 712712 | tf_op jit(solution)/shard_map/ppermute | solution.py:298
  15.3 0.1 collective-permute-start.5
  15.4 0.0 collective-permute-start.6
  15.4 5.6 %shard_map.106 = (bf16[4,128,512]{2,1,0:T(8,128)(2,1)}, bf16[3584,512]{1,0:T(8,128)(2,1)S(1)}, bf16[3584,512]{1,0:T(8,128)(2,1)S(1)}, bf16[512,3584]{1,0:T(8,128)(2,1)S(1)}, f32[8,128]{1,0:T(8,128)S(1)}) custom-call(s32[4]{0:T(128)} %lengths_hbm.1, bf16[4,576,128]{2,1,0:T(8,128)(2,1)} %bitcast.9, bf16[4,576,256]{2,1,0:T(8,128)(2,1)} %bitcast.8, ...), custom_call_target="tpu_custom_call" | custom-call | flops 301989888 | bytes 11010048 | tf_op jit(solution)/shard_map/pallas_call | solution.py:74
  21.0 0.0 collective-permute-done.3.value_ref
  21.0 0.6 %collective-permute-start.7 = (bf16[32,3712]{1,0:T(8,128)(2,1)S(1)}, bf16[32,3712]{1,0:T(8,128)(2,1)S(1)}, u32[]{:S(2)}, u32[]{:S(2)}) collective-permute-start(bf16[32,3712]{1,0:T(8,128)(2,1)S(1)} %shard_map.107.refs_1_), channel_id=1, source_target_pairs={{0,1},{1,0},{2,3},{3,2},{4,5},{5,4},{6,7},{7,6},{8,9},{9,8},{10,11... | collective-permute-start | bytes 712712 | tf_op jit(solution)/shard_map/ppermute | solution.py:307
  21.6 0.8 %collective-permute-done.4.value_ref = bf16[32,3712]{1,0:T(8,128)(2,1)S(1)} collective-permute-done((bf16[32,3712]{1,0:T(8,128)(2,1)S(1)}, bf16[32,3712]{1,0:T(8,128)(2,1)S(1)}, u32[]{:S(2)}, u32[]{:S(2)}) %collective-permute-start.4) | collective-permute-done | bytes 237600 | tf_op jit(solution)/shard_map/ppermute | solution.py:298
  22.4 0.0 collective-permute-start.8
  22.4 0.0 collective-permute-done.5.value_ref
  22.4 0.5 %collective-permute-start.9 = (bf16[32,3712]{1,0:T(8,128)(2,1)S(1)}, bf16[32,3712]{1,0:T(8,128)(2,1)S(1)}, u32[]{:S(2)}, u32[]{:S(2)}) collective-permute-start(bf16[32,3712]{1,0:T(8,128)(2,1)S(1)} %shard_map.109.refs_3_), channel_id=1, source_target_pairs={{0,1},{1,0},{2,3},{3,2},{4,5},{5,4},{6,7},{7,6},{8,9},{9,8},{10,11... | collective-permute-start | bytes 712712 | tf_op jit(solution)/shard_map/ppermute | solution.py:307
  22.9 0.0 collective-permute-done.6.refs_4_
  22.9 0.0 collective-permute-done.7.refs_5_
  22.9 1.0 %collective-permute-done.8.refs_6_ = bf16[32,3712]{1,0:T(8,128)(2,1)S(1)} collective-permute-done((bf16[32,3712]{1,0:T(8,128)(2,1)S(1)}, bf16[32,3712]{1,0:T(8,128)(2,1)S(1)}, u32[]{:S(2)}, u32[]{:S(2)}) %collective-permute-start.8) | collective-permute-done | bytes 237600 | tf_op jit(solution)/shard_map/ppermute | solution.py:307
  23.9 0.3 collective-permute-done.9.refs_7_
  24.2 4.2 %shard_map.110 = (bf16[128,3584]{1,0:T(8,128)(2,1)S(1)}, bf16[128,3584]{1,0:T(8,128)(2,1)S(1)}) custom-call(bf16[32,3712]{1,0:T(8,128)(2,1)S(1)} %shard_map.105.after_ref.refs_0_, bf16[32,3712]{1,0:T(8,128)(2,1)S(1)} %shard_map.107.refs_1_, bf16[32,3712]{1,0:T(8,128)(2,1)S(1)} %shard_map.108.refs_2_, bf16[32,3712]{1,0:T(8,128)(2,1)S(1)} %shard_map.109.refs_3_, ...), custom_call_target="tpu_custom_call" | custom-call | flops 2818572288 | bytes 3801088 | tf_op jit(solution)/shard_map/pallas_call | solution.py:236
  28.4 0.2 collective-permute-start.10
  28.7 2.3 %collective-permute-done.10.refs_1_ = bf16[128,3584]{1,0:T(8,128)(2,1)S(1)} collective-permute-done((bf16[128,3584]{1,0:T(8,128)(2,1)S(1)}, bf16[128,3584]{1,0:T(8,128)(2,1)S(1)}, u32[]{:S(2)}, u32[]{:S(2)}) %collective-permute-start.10) | collective-permute-done | bytes 917536 | tf_op jit(solution)/shard_map/ppermute | solution.py:307
  31.0 0.2 shard_map.111
  31.2 1.6 %collective-permute-start.11 = (bf16[32,3584]{1,0:T(8,128)(2,1)S(1)}, bf16[32,3584]{1,0:T(8,128)(2,1)S(1)}, u32[]{:S(2)}, u32[]{:S(2)}) collective-permute-start(bf16[32,3584]{1,0:T(8,128)(2,1)S(1)} %get-tuple-element.24), channel_id=1, source_target_pairs={{0,4},{1,17},{2,6},{3,19},{4,0},{5,21},{6,2},{7,23},{8,12},{9,25},... | collective-permute-start | bytes 688136 | tf_op jit(solution)/shard_map/ppermute | solution.py:298
  32.8 1.0 %collective-permute-start.12 = (bf16[32,3584]{1,0:T(8,128)(2,1)S(1)}, bf16[32,3584]{1,0:T(8,128)(2,1)S(1)}, u32[]{:S(2)}, u32[]{:S(2)}) collective-permute-start(bf16[32,3584]{1,0:T(8,128)(2,1)S(1)} %get-tuple-element.25), channel_id=1, source_target_pairs={{0,2},{1,9},{2,0},{3,11},{4,6},{5,13},{6,4},{7,15},{8,10},{9,1},{1... | collective-permute-start | bytes 688136 | tf_op jit(solution)/shard_map/ppermute | solution.py:298
  33.8 0.9 %collective-permute-start.13 = (bf16[32,3584]{1,0:T(8,128)(2,1)S(1)}, bf16[32,3584]{1,0:T(8,128)(2,1)S(1)}, u32[]{:S(2)}, u32[]{:S(2)}) collective-permute-start(bf16[32,3584]{1,0:T(8,128)(2,1)S(1)} %get-tuple-element.26), channel_id=1, source_target_pairs={{0,6},{1,25},{2,4},{3,27},{4,2},{5,29},{6,0},{7,31},{8,14},{9,17},... | collective-permute-start | bytes 688136 | tf_op jit(solution)/shard_map/ppermute | solution.py:298
  34.8 2.5 %collective-permute-done.11.refs_1_ = bf16[32,3584]{1,0:T(8,128)(2,1)S(1)} collective-permute-done((bf16[32,3584]{1,0:T(8,128)(2,1)S(1)}, bf16[32,3584]{1,0:T(8,128)(2,1)S(1)}, u32[]{:S(2)}, u32[]{:S(2)}) %collective-permute-start.11) | collective-permute-done | bytes 229408 | tf_op jit(solution)/shard_map/ppermute | solution.py:298
  37.3 1.5 %collective-permute-done.12.refs_2_ = bf16[32,3584]{1,0:T(8,128)(2,1)S(1)} collective-permute-done((bf16[32,3584]{1,0:T(8,128)(2,1)S(1)}, bf16[32,3584]{1,0:T(8,128)(2,1)S(1)}, u32[]{:S(2)}, u32[]{:S(2)}) %collective-permute-start.12) | collective-permute-done | bytes 229408 | tf_op jit(solution)/shard_map/ppermute | solution.py:298
  38.8 2.4 %collective-permute-done.13.refs_3_ = bf16[32,3584]{1,0:T(8,128)(2,1)S(1)} collective-permute-done((bf16[32,3584]{1,0:T(8,128)(2,1)S(1)}, bf16[32,3584]{1,0:T(8,128)(2,1)S(1)}, u32[]{:S(2)}, u32[]{:S(2)}) %collective-permute-start.13) | collective-permute-done | bytes 229408 | tf_op jit(solution)/shard_map/ppermute | solution.py:298
  41.2 0.1 shard_map.112
  41.3 1.3 %collective-permute-start.14 = (bf16[8,3584]{1,0:T(8,128)(2,1)S(1)}, bf16[8,3584]{1,0:T(8,128)(2,1)S(1)}, u32[]{:S(2)}, u32[]{:S(2)}) collective-permute-start(bf16[8,3584]{1,0:T(8,128)(2,1)S(1)} %get-tuple-element.28), channel_id=1, source_target_pairs={{0,24},{1,7},{2,26},{3,5},{4,28},{5,3},{6,30},{7,1},{8,16},{9,15},... | collective-permute-start | bytes 172040 | tf_op jit(solution)/shard_map/ppermute | solution.py:298
  42.6 1.2 %collective-permute-start.15 = (bf16[8,3584]{1,0:T(8,128)(2,1)S(1)}, bf16[8,3584]{1,0:T(8,128)(2,1)S(1)}, u32[]{:S(2)}, u32[]{:S(2)}) collective-permute-start(bf16[8,3584]{1,0:T(8,128)(2,1)S(1)} %get-tuple-element.29), channel_id=1, source_target_pairs={{0,16},{1,5},{2,18},{3,7},{4,20},{5,1},{6,22},{7,3},{8,24},{9,13},... | collective-permute-start | bytes 172040 | tf_op jit(solution)/shard_map/ppermute | solution.py:298
  43.8 1.9 %collective-permute-start.16 = (bf16[8,3584]{1,0:T(8,128)(2,1)S(1)}, bf16[8,3584]{1,0:T(8,128)(2,1)S(1)}, u32[]{:S(2)}, u32[]{:S(2)}) collective-permute-start(bf16[8,3584]{1,0:T(8,128)(2,1)S(1)} %get-tuple-element.30), channel_id=1, source_target_pairs={{0,8},{1,3},{2,10},{3,1},{4,12},{5,7},{6,14},{7,5},{8,0},{9,11},{1... | collective-permute-start | bytes 172040 | tf_op jit(solution)/shard_map/ppermute | solution.py:298
  45.8 1.6 %collective-permute-done.14.refs_4_ = bf16[8,3584]{1,0:T(8,128)(2,1)S(1)} collective-permute-done((bf16[8,3584]{1,0:T(8,128)(2,1)S(1)}, bf16[8,3584]{1,0:T(8,128)(2,1)S(1)}, u32[]{:S(2)}, u32[]{:S(2)}) %collective-permute-start.14) | collective-permute-done | bytes 57376 | tf_op jit(solution)/shard_map/ppermute | solution.py:298
  47.4 0.7 %collective-permute-done.15.refs_5_ = bf16[8,3584]{1,0:T(8,128)(2,1)S(1)} collective-permute-done((bf16[8,3584]{1,0:T(8,128)(2,1)S(1)}, bf16[8,3584]{1,0:T(8,128)(2,1)S(1)}, u32[]{:S(2)}, u32[]{:S(2)}) %collective-permute-start.15) | collective-permute-done | bytes 57376 | tf_op jit(solution)/shard_map/ppermute | solution.py:298
  48.0 0.6 %collective-permute-done.16.refs_6_ = bf16[8,3584]{1,0:T(8,128)(2,1)S(1)} collective-permute-done((bf16[8,3584]{1,0:T(8,128)(2,1)S(1)}, bf16[8,3584]{1,0:T(8,128)(2,1)S(1)}, u32[]{:S(2)}, u32[]{:S(2)}) %collective-permute-start.16) | collective-permute-done | bytes 57376 | tf_op jit(solution)/shard_map/ppermute | solution.py:298
  48.6 0.7 %shard_map.113 = bf16[8,3584]{1,0:T(8,128)(2,1)} custom-call(bf16[8,3584]{1,0:T(8,128)(2,1)S(1)} %get-tuple-element.23.refs_0_, bf16[32,3584]{1,0:T(8,128)(2,1)S(1)} %collective-permute-done.11.refs_1_, bf16[32,3584]{1,0:T(8,128)(2,1)S(1)} %collective-permute-done.12.refs_2_, bf16[32,3584]{1,0:T(8,128)(2,1)S(1)} %collective-permute-done.13.refs_3_, ...), custom_call_target="tpu_custom_call" | custom-call | flops 458752 | bytes 917504 | tf_op jit(solution)/shard_map/pallas_call | solution.py:266
  (4 shorter events, 0.0 us)
Async XLA Ops:
  1.6 7.4 %collective-permute-start.2 = (bf16[8,3712]{1,0:T(8,128)(2,1)S(1)}, bf16[8,3712]{1,0:T(8,128)(2,1)S(1)}, u32[]{:S(2)}, u32[]{:S(2)}) collective-permute-start(bf16[8,3712]{1,0:T(8,128)(2,1)S(1)} %shard_map.104.refs_0_), channel_id=1, source_target_pairs={{0,24},{1,7},{2,26},{3,5},{4,28},{5,3},{6,30},{7,1},{8,16},{9,15},... | collective-permute-start | bytes 178184 | tf_op jit(solution)/shard_map/ppermute | solution.py:298
  6.7 5.1 %collective-permute-start.1 = (bf16[8,3712]{1,0:T(8,128)(2,1)S(1)}, bf16[8,3712]{1,0:T(8,128)(2,1)S(1)}, u32[]{:S(2)}, u32[]{:S(2)}) collective-permute-start(bf16[8,3712]{1,0:T(8,128)(2,1)S(1)} %shard_map.104.refs_0_), channel_id=1, source_target_pairs={{0,16},{1,5},{2,18},{3,7},{4,20},{5,1},{6,22},{7,3},{8,24},{9,13},... | collective-permute-start | bytes 178184 | tf_op jit(solution)/shard_map/ppermute | solution.py:298
  6.7 5.1 %collective-permute-start = (bf16[8,3712]{1,0:T(8,128)(2,1)S(1)}, bf16[8,3712]{1,0:T(8,128)(2,1)S(1)}, u32[]{:S(2)}, u32[]{:S(2)}) collective-permute-start(bf16[8,3712]{1,0:T(8,128)(2,1)S(1)} %shard_map.104.refs_0_), channel_id=1, source_target_pairs={{0,8},{1,3},{2,10},{3,1},{4,12},{5,7},{6,14},{7,5},{8,0},{9,11},{1... | collective-permute-start | bytes 178184 | tf_op jit(solution)/shard_map/ppermute | solution.py:298
  11.8 9.2 %collective-permute-start.3 = (bf16[32,3712]{1,0:T(8,128)(2,1)S(1)}, bf16[32,3712]{1,0:T(8,128)(2,1)S(1)}, u32[]{:S(2)}, u32[]{:S(2)}) collective-permute-start(bf16[32,3712]{1,0:T(8,128)(2,1)S(1)} %shard_map.105.after_ref.refs_0_), channel_id=1, source_target_pairs={{0,2},{1,9},{2,0},{3,11},{4,6},{5,13},{6,4},{7,15},{8,10},{9,1},{1... | collective-permute-start | bytes 712712 | tf_op jit(solution)/shard_map/ppermute | solution.py:298
  13.7 8.7 %collective-permute-start.4 = (bf16[32,3712]{1,0:T(8,128)(2,1)S(1)}, bf16[32,3712]{1,0:T(8,128)(2,1)S(1)}, u32[]{:S(2)}, u32[]{:S(2)}) collective-permute-start(bf16[32,3712]{1,0:T(8,128)(2,1)S(1)} %shard_map.105.after_ref.refs_0_), channel_id=1, source_target_pairs={{0,4},{1,17},{2,6},{3,19},{4,0},{5,21},{6,2},{7,23},{8,12},{9,25},... | collective-permute-start | bytes 712712 | tf_op jit(solution)/shard_map/ppermute | solution.py:298
  15.3 7.1 %collective-permute-start.5 = (bf16[32,3712]{1,0:T(8,128)(2,1)S(1)}, bf16[32,3712]{1,0:T(8,128)(2,1)S(1)}, u32[]{:S(2)}, u32[]{:S(2)}) collective-permute-start(bf16[32,3712]{1,0:T(8,128)(2,1)S(1)} %shard_map.105.after_ref.refs_0_), channel_id=1, source_target_pairs={{0,6},{1,25},{2,4},{3,27},{4,2},{5,29},{6,0},{7,31},{8,14},{9,17},... | collective-permute-start | bytes 712712 | tf_op jit(solution)/shard_map/ppermute | solution.py:298
  15.4 7.5 %collective-permute-start.6 = (bf16[32,3712]{1,0:T(8,128)(2,1)S(1)}, bf16[32,3712]{1,0:T(8,128)(2,1)S(1)}, u32[]{:S(2)}, u32[]{:S(2)}) collective-permute-start(bf16[32,3712]{1,0:T(8,128)(2,1)S(1)} %shard_map.105.after_ref.refs_0_), channel_id=1, source_target_pairs={{0,1},{1,0},{2,3},{3,2},{4,5},{5,4},{6,7},{7,6},{8,9},{9,8},{10,11... | collective-permute-start | bytes 712712 | tf_op jit(solution)/shard_map/ppermute | solution.py:307
  21.0 1.9 %collective-permute-start.7 = (bf16[32,3712]{1,0:T(8,128)(2,1)S(1)}, bf16[32,3712]{1,0:T(8,128)(2,1)S(1)}, u32[]{:S(2)}, u32[]{:S(2)}) collective-permute-start(bf16[32,3712]{1,0:T(8,128)(2,1)S(1)} %shard_map.107.refs_1_), channel_id=1, source_target_pairs={{0,1},{1,0},{2,3},{3,2},{4,5},{5,4},{6,7},{7,6},{8,9},{9,8},{10,11... | collective-permute-start | bytes 712712 | tf_op jit(solution)/shard_map/ppermute | solution.py:307
  22.4 1.5 %collective-permute-start.8 = (bf16[32,3712]{1,0:T(8,128)(2,1)S(1)}, bf16[32,3712]{1,0:T(8,128)(2,1)S(1)}, u32[]{:S(2)}, u32[]{:S(2)}) collective-permute-start(bf16[32,3712]{1,0:T(8,128)(2,1)S(1)} %shard_map.108.refs_2_), channel_id=1, source_target_pairs={{0,1},{1,0},{2,3},{3,2},{4,5},{5,4},{6,7},{7,6},{8,9},{9,8},{10,11... | collective-permute-start | bytes 712712 | tf_op jit(solution)/shard_map/ppermute | solution.py:307
  22.4 1.8 %collective-permute-start.9 = (bf16[32,3712]{1,0:T(8,128)(2,1)S(1)}, bf16[32,3712]{1,0:T(8,128)(2,1)S(1)}, u32[]{:S(2)}, u32[]{:S(2)}) collective-permute-start(bf16[32,3712]{1,0:T(8,128)(2,1)S(1)} %shard_map.109.refs_3_), channel_id=1, source_target_pairs={{0,1},{1,0},{2,3},{3,2},{4,5},{5,4},{6,7},{7,6},{8,9},{9,8},{10,11... | collective-permute-start | bytes 712712 | tf_op jit(solution)/shard_map/ppermute | solution.py:307
  28.4 2.5 %collective-permute-start.10 = (bf16[128,3584]{1,0:T(8,128)(2,1)S(1)}, bf16[128,3584]{1,0:T(8,128)(2,1)S(1)}, u32[]{:S(2)}, u32[]{:S(2)}) collective-permute-start(bf16[128,3584]{1,0:T(8,128)(2,1)S(1)} %get-tuple-element.22), channel_id=1, source_target_pairs={{0,1},{1,0},{2,3},{3,2},{4,5},{5,4},{6,7},{7,6},{8,9},{9,8},{10,11... | collective-permute-start | bytes 2752520 | tf_op jit(solution)/shard_map/ppermute | solution.py:307
  31.2 6.1 %collective-permute-start.11 = (bf16[32,3584]{1,0:T(8,128)(2,1)S(1)}, bf16[32,3584]{1,0:T(8,128)(2,1)S(1)}, u32[]{:S(2)}, u32[]{:S(2)}) collective-permute-start(bf16[32,3584]{1,0:T(8,128)(2,1)S(1)} %get-tuple-element.24), channel_id=1, source_target_pairs={{0,4},{1,17},{2,6},{3,19},{4,0},{5,21},{6,2},{7,23},{8,12},{9,25},... | collective-permute-start | bytes 688136 | tf_op jit(solution)/shard_map/ppermute | solution.py:298
  32.8 6.0 %collective-permute-start.12 = (bf16[32,3584]{1,0:T(8,128)(2,1)S(1)}, bf16[32,3584]{1,0:T(8,128)(2,1)S(1)}, u32[]{:S(2)}, u32[]{:S(2)}) collective-permute-start(bf16[32,3584]{1,0:T(8,128)(2,1)S(1)} %get-tuple-element.25), channel_id=1, source_target_pairs={{0,2},{1,9},{2,0},{3,11},{4,6},{5,13},{6,4},{7,15},{8,10},{9,1},{1... | collective-permute-start | bytes 688136 | tf_op jit(solution)/shard_map/ppermute | solution.py:298
  33.8 7.4 %collective-permute-start.13 = (bf16[32,3584]{1,0:T(8,128)(2,1)S(1)}, bf16[32,3584]{1,0:T(8,128)(2,1)S(1)}, u32[]{:S(2)}, u32[]{:S(2)}) collective-permute-start(bf16[32,3584]{1,0:T(8,128)(2,1)S(1)} %get-tuple-element.26), channel_id=1, source_target_pairs={{0,6},{1,25},{2,4},{3,27},{4,2},{5,29},{6,0},{7,31},{8,14},{9,17},... | collective-permute-start | bytes 688136 | tf_op jit(solution)/shard_map/ppermute | solution.py:298
  41.3 6.1 %collective-permute-start.14 = (bf16[8,3584]{1,0:T(8,128)(2,1)S(1)}, bf16[8,3584]{1,0:T(8,128)(2,1)S(1)}, u32[]{:S(2)}, u32[]{:S(2)}) collective-permute-start(bf16[8,3584]{1,0:T(8,128)(2,1)S(1)} %get-tuple-element.28), channel_id=1, source_target_pairs={{0,24},{1,7},{2,26},{3,5},{4,28},{5,3},{6,30},{7,1},{8,16},{9,15},... | collective-permute-start | bytes 172040 | tf_op jit(solution)/shard_map/ppermute | solution.py:298
  42.6 5.4 %collective-permute-start.15 = (bf16[8,3584]{1,0:T(8,128)(2,1)S(1)}, bf16[8,3584]{1,0:T(8,128)(2,1)S(1)}, u32[]{:S(2)}, u32[]{:S(2)}) collective-permute-start(bf16[8,3584]{1,0:T(8,128)(2,1)S(1)} %get-tuple-element.29), channel_id=1, source_target_pairs={{0,16},{1,5},{2,18},{3,7},{4,20},{5,1},{6,22},{7,3},{8,24},{9,13},... | collective-permute-start | bytes 172040 | tf_op jit(solution)/shard_map/ppermute | solution.py:298
  43.8 4.8 %collective-permute-start.16 = (bf16[8,3584]{1,0:T(8,128)(2,1)S(1)}, bf16[8,3584]{1,0:T(8,128)(2,1)S(1)}, u32[]{:S(2)}, u32[]{:S(2)}) collective-permute-start(bf16[8,3584]{1,0:T(8,128)(2,1)S(1)} %get-tuple-element.30), channel_id=1, source_target_pairs={{0,8},{1,3},{2,10},{3,1},{4,12},{5,7},{6,14},{7,5},{8,0},{9,11},{1... | collective-permute-start | bytes 172040 | tf_op jit(solution)/shard_map/ppermute | solution.py:298

commit v5 on v4

--- a/solution.py
+++ b/solution.py
@@ -195,9 +195,7 @@
         rows_ref[low : low + piece.shape[0], :] = piece[...]
         low += piece.shape[0]
 
-    @pl.loop(0, total // block)
-    def _(i):
-        here = pl.ds(pl.multiple_of(i * block, block), block)
+    def units_of(here):
         tail = rows_ref[here, model_width:].astype(jnp.float32)
         lane = lax.broadcasted_iota(jnp.int32, (block, lanes), 1)
         taken = (lane == me) | (lane == me + lanes // 2)
@@ -210,16 +208,11 @@
             value = gate_value / (1.0 + jnp.exp(-gate_value)) * up_value * weight
             hidden_ref[here, cols] = value.astype(jnp.bfloat16)
 
-    step = 512
-
-    @pl.loop(0, model_width // step)
-    def _(c):
-        cols = pl.ds(pl.multiple_of(c * step, step), step)
+    def results_of(cols):
         for i in range(total // block):
-            value = jnp.dot(
-                hidden_ref[i * block : (i + 1) * block, :], down_ref[:, cols], preferred_element_type=jnp.float32
-            ).astype(jnp.bfloat16)
             low, high = i * block, (i + 1) * block
+            value = jnp.dot(hidden_ref[low:high, :], down_ref[:, cols], preferred_element_type=jnp.float32)
+            value = value.astype(jnp.bfloat16)
             if high <= half:
                 mine_ref[low:high, cols] = value
             elif low >= half:
@@ -227,6 +220,15 @@
             else:
                 mine_ref[low:half, cols] = value[: half - low]
                 other_ref[: high - half, cols] = value[half - low :]
+
+    step = 512
+    if total == block:
+        units_of(slice(0, block))
+        for c in range(model_width // step):
+            results_of(slice(c * step, (c + 1) * step))
+    else:
+        pl.loop(0, total // block)(lambda i: units_of(pl.ds(pl.multiple_of(i * block, block), block)))
+        pl.loop(0, model_width // step)(lambda c: results_of(pl.ds(pl.multiple_of(c * step, step), step)))
 
 
 def expert_block(pieces, expert_gate, expert_up, expert_down):
@@ -322,16 +324,13 @@
     pieces += [over_cores(p) for p in pieces]
     mine, other = expert_block(pieces, *weights)
 
-    size = outer * tok_rows
-    kept, column, *parts = add(
-        [mine, over_cores(other)], [(0, size * inner)] * 2, [tok_rows, size - tok_rows] + [size] * (inner - 1)
-    )
-    far = [second(parts[k - 1], k) for k in steps]
-    near = add(
-        [column, *far], [(0, size - tok_rows)] + [(tok_rows, size)] * len(far), [tok_rows] * (outer - 1)
-    )
+    size = (outer - 1) * tok_rows
+    kept, column, *parts = add([mine, over_cores(other)], [(0, mine.shape[0])] * 2, [tok_rows, size] * inner)
+    far = [second(parts[2 * k - 1], k) for k in steps]
+    side = [second(parts[2 * k - 2], k) for k in steps]
+    near = add([column, *far], [(0, size)] * inner, [tok_rows] * (outer - 1))
     near = [first(near[k - 1], k) for k in range(outer - 1, 0, -1)]
-    (moe_output,) = add([kept, *far, *near], [(0, tok_rows)] * (1 + len(far) + len(near)), [tok_rows], last=True)
+    (moe_output,) = add([kept, *side, *near], [(0, tok_rows)] * (1 + len(side) + len(near)), [tok_rows], last=True)
     return (moe_output, attention_latent)
 
 

time: 49.4 us -> 47.3 us (0.957)
  waiting for transfers between devices: 18.2 us -> 13.3 us
  starting transfers between devices: 18.6 us -> 22.5 us
  Pallas kernels: 11.7 us -> 10.5 us
    ppermute x12 -> x15, waiting for transfers between devices: 14.6 us -> 9.68 us  [swap(): return lax.ppermute(value, ('ep', 'sub'), pairs)]
    ppermute x12 -> x15, starting transfers between devices: 17.3 us -> 21.2 us  [swap(): return lax.ppermute(value, ('ep', 'sub'), pairs)]
    pallas_call x1, Pallas kernels: 4.21 us -> 3.03 us  [expert_block(): pl.pallas_call(functools.partial(expert_kernel, len(pieces)), out_shape=(...]
  transfers between devices with their start and end apart: 17 -> 20, of which waited for: 12 -> 10; matrix products, arithmetic and copies ran while one was open for 0% -> 0% of each run, Pallas kernels for 11% -> 12%
where the time goes in v5:
time: 47.3 us; the launch traced here: 47.1 us
  starting transfers between devices  22.5 us (48%)
  waiting for transfers between devices  13.3 us (28%)
  Pallas kernels  10.5 us (22%)
  between operations  0.71 us (2%)
    ppermute x15, starting transfers between devices, swap(): return lax.ppermute(value, ('ep', 'sub'), pairs)  21.2 us
    ppermute x15, waiting for transfers between devices, swap(): return lax.ppermute(value, ('ep', 'sub'), pairs)  9.68 us
    pallas_call x1, Pallas kernels, attend(): pl.pallas_call(attend_kernel, out_shape=(jax.ShapeDtypeStruct((rows, head...  5.58 us
    ppermute x5, waiting for transfers between devices, over_cores(): return lax.ppermute(value, 'sub', [(i, i ^ 1) for i in range(sub_count)])  3.62 us
    pallas_call x1, Pallas kernels, expert_block(): pl.pallas_call(functools.partial(expert_kernel, len(pieces)), out_shape=(...  3.03 us
    ppermute x5, starting transfers between devices, over_cores(): return lax.ppermute(value, 'sub', [(i, i ^ 1) for i in range(sub_count)])  1.32 us
    pallas_call x3, Pallas kernels, add(): pl.pallas_call(functools.partial(add_kernel, len(values), rows, sizes), o...  0.98 us
  transfers between devices with their start and end apart: 20, of which 10 were waited for; matrix products, arithmetic and copies ran while one was open for 0% of the time, Pallas kernels for 12%

profile of v5, /device:TPU:0, one launch (start us, length us, event | category | flops | bytes accessed | tf_op | source)
XLA Modules:
  0.0 47.1 jit_solution(12234373222047676244)
XLA Ops:
  0.6 0.9 %shard_map.104.refs_0_ = bf16[8,3712]{1,0:T(8,128)(2,1)S(1)} custom-call(bf16[8,3584]{1,0:T(8,128)(2,1)} %hidden_ref.1, s32[8,8]{1,0:T(8,128)} %routes_ref.1, f32[8,8]{1,0:T(8,128)} %scores_ref.1), custom_call_target="tpu_custom_call" | custom-call | flops 65536 | bytes 114688 | tf_op jit(solution)/shard_map/pallas_call | solution.py:133
  1.6 5.1 %collective-permute-start.2 = (bf16[8,3712]{1,0:T(8,128)(2,1)S(1)}, bf16[8,3712]{1,0:T(8,128)(2,1)S(1)}, u32[]{:S(2)}, u32[]{:S(2)}) collective-permute-start(bf16[8,3712]{1,0:T(8,128)(2,1)S(1)} %shard_map.104.refs_0_), channel_id=1, source_target_pairs={{0,24},{1,7},{2,26},{3,5},{4,28},{5,3},{6,30},{7,1},{8,16},{9,15},... | collective-permute-start | bytes 178184 | tf_op jit(solution)/shard_map/ppermute | solution.py:300
  6.7 0.0 collective-permute-start.1
  6.7 0.6 %collective-permute-start = (bf16[8,3712]{1,0:T(8,128)(2,1)S(1)}, bf16[8,3712]{1,0:T(8,128)(2,1)S(1)}, u32[]{:S(2)}, u32[]{:S(2)}) collective-permute-start(bf16[8,3712]{1,0:T(8,128)(2,1)S(1)} %shard_map.104.refs_0_), channel_id=1, source_target_pairs={{0,8},{1,3},{2,10},{3,1},{4,12},{5,7},{6,14},{7,5},{8,0},{9,11},{1... | collective-permute-start | bytes 178184 | tf_op jit(solution)/shard_map/ppermute | solution.py:300
  7.3 1.6 %collective-permute-done.2.refs_3_ = bf16[8,3712]{1,0:T(8,128)(2,1)S(1)} collective-permute-done((bf16[8,3712]{1,0:T(8,128)(2,1)S(1)}, bf16[8,3712]{1,0:T(8,128)(2,1)S(1)}, u32[]{:S(2)}, u32[]{:S(2)}) %collective-permute-start.2) | collective-permute-done | bytes 59424 | tf_op jit(solution)/shard_map/ppermute | solution.py:300
  8.9 2.9 %collective-permute-done.1.refs_2_ = bf16[8,3712]{1,0:T(8,128)(2,1)S(1)} collective-permute-done((bf16[8,3712]{1,0:T(8,128)(2,1)S(1)}, bf16[8,3712]{1,0:T(8,128)(2,1)S(1)}, u32[]{:S(2)}, u32[]{:S(2)}) %collective-permute-start.1) | collective-permute-done | bytes 59424 | tf_op jit(solution)/shard_map/ppermute | solution.py:300
  11.8 0.0 collective-permute-done.refs_1_
  11.8 1.9 %collective-permute-start.3 = (bf16[32,3712]{1,0:T(8,128)(2,1)S(1)}, bf16[32,3712]{1,0:T(8,128)(2,1)S(1)}, u32[]{:S(2)}, u32[]{:S(2)}) collective-permute-start(bf16[32,3712]{1,0:T(8,128)(2,1)S(1)} %shard_map.105.after_ref.refs_0_), channel_id=1, source_target_pairs={{0,2},{1,9},{2,0},{3,11},{4,6},{5,13},{6,4},{7,15},{8,10},{9,1},{1... | collective-permute-start | bytes 712712 | tf_op jit(solution)/shard_map/ppermute | solution.py:300
  13.7 1.5 %collective-permute-start.4 = (bf16[32,3712]{1,0:T(8,128)(2,1)S(1)}, bf16[32,3712]{1,0:T(8,128)(2,1)S(1)}, u32[]{:S(2)}, u32[]{:S(2)}) collective-permute-start(bf16[32,3712]{1,0:T(8,128)(2,1)S(1)} %shard_map.105.after_ref.refs_0_), channel_id=1, source_target_pairs={{0,4},{1,17},{2,6},{3,19},{4,0},{5,21},{6,2},{7,23},{8,12},{9,25},... | collective-permute-start | bytes 712712 | tf_op jit(solution)/shard_map/ppermute | solution.py:300
  15.3 0.1 collective-permute-start.5
  15.4 0.0 collective-permute-start.6
  15.4 5.6 %shard_map.106 = (bf16[4,128,512]{2,1,0:T(8,128)(2,1)}, bf16[3584,512]{1,0:T(8,128)(2,1)S(1)}, bf16[3584,512]{1,0:T(8,128)(2,1)S(1)}, bf16[512,3584]{1,0:T(8,128)(2,1)S(1)}, f32[8,128]{1,0:T(8,128)S(1)}) custom-call(s32[4]{0:T(128)} %lengths_hbm.1, bf16[4,576,128]{2,1,0:T(8,128)(2,1)} %bitcast.9, bf16[4,576,256]{2,1,0:T(8,128)(2,1)} %bitcast.8, ...), custom_call_target="tpu_custom_call" | custom-call | flops 301989888 | bytes 11010048 | tf_op jit(solution)/shard_map/pallas_call | solution.py:74
  21.0 0.0 collective-permute-done.3.value_ref
  21.0 0.6 %collective-permute-start.7 = (bf16[32,3712]{1,0:T(8,128)(2,1)S(1)}, bf16[32,3712]{1,0:T(8,128)(2,1)S(1)}, u32[]{:S(2)}, u32[]{:S(2)}) collective-permute-start(bf16[32,3712]{1,0:T(8,128)(2,1)S(1)} %shard_map.107.refs_1_), channel_id=1, source_target_pairs={{0,1},{1,0},{2,3},{3,2},{4,5},{5,4},{6,7},{7,6},{8,9},{9,8},{10,11... | collective-permute-start | bytes 712712 | tf_op jit(solution)/shard_map/ppermute | solution.py:309
  21.6 0.8 %collective-permute-done.4.value_ref = bf16[32,3712]{1,0:T(8,128)(2,1)S(1)} collective-permute-done((bf16[32,3712]{1,0:T(8,128)(2,1)S(1)}, bf16[32,3712]{1,0:T(8,128)(2,1)S(1)}, u32[]{:S(2)}, u32[]{:S(2)}) %collective-permute-start.4) | collective-permute-done | bytes 237600 | tf_op jit(solution)/shard_map/ppermute | solution.py:300
  22.4 0.0 collective-permute-start.8
  22.4 0.0 collective-permute-done.5.value_ref
  22.4 0.5 %collective-permute-start.9 = (bf16[32,3712]{1,0:T(8,128)(2,1)S(1)}, bf16[32,3712]{1,0:T(8,128)(2,1)S(1)}, u32[]{:S(2)}, u32[]{:S(2)}) collective-permute-start(bf16[32,3712]{1,0:T(8,128)(2,1)S(1)} %shard_map.109.refs_3_), channel_id=1, source_target_pairs={{0,1},{1,0},{2,3},{3,2},{4,5},{5,4},{6,7},{7,6},{8,9},{9,8},{10,11... | collective-permute-start | bytes 712712 | tf_op jit(solution)/shard_map/ppermute | solution.py:309
  22.9 0.0 collective-permute-done.6.refs_4_
  22.9 0.0 collective-permute-done.7.refs_5_
  22.9 1.0 %collective-permute-done.8.refs_6_ = bf16[32,3712]{1,0:T(8,128)(2,1)S(1)} collective-permute-done((bf16[32,3712]{1,0:T(8,128)(2,1)S(1)}, bf16[32,3712]{1,0:T(8,128)(2,1)S(1)}, u32[]{:S(2)}, u32[]{:S(2)}) %collective-permute-start.8) | collective-permute-done | bytes 237600 | tf_op jit(solution)/shard_map/ppermute | solution.py:309
  23.9 0.3 collective-permute-done.9.refs_7_
  24.2 3.0 %shard_map.110 = (bf16[128,3584]{1,0:T(8,128)(2,1)S(1)}, bf16[128,3584]{1,0:T(8,128)(2,1)S(1)}) custom-call(bf16[32,3712]{1,0:T(8,128)(2,1)S(1)} %shard_map.105.after_ref.refs_0_, bf16[32,3712]{1,0:T(8,128)(2,1)S(1)} %shard_map.107.refs_1_, bf16[32,3712]{1,0:T(8,128)(2,1)S(1)} %shard_map.108.refs_2_, bf16[32,3712]{1,0:T(8,128)(2,1)S(1)} %shard_map.109.refs_3_, ...), custom_call_target="tpu_custom_call" | custom-call | flops 2818572288 | bytes 3801088 | tf_op jit(solution)/shard_map/pallas_call | solution.py:238
  27.3 0.2 collective-permute-start.10
  27.5 2.3 %collective-permute-done.10.refs_1_ = bf16[128,3584]{1,0:T(8,128)(2,1)S(1)} collective-permute-done((bf16[128,3584]{1,0:T(8,128)(2,1)S(1)}, bf16[128,3584]{1,0:T(8,128)(2,1)S(1)}, u32[]{:S(2)}, u32[]{:S(2)}) %collective-permute-start.10) | collective-permute-done | bytes 917536 | tf_op jit(solution)/shard_map/ppermute | solution.py:309
  29.8 0.2 shard_map.111
  30.0 1.6 %collective-permute-start.14 = (bf16[24,3584]{1,0:T(8,128)(2,1)S(1)}, bf16[24,3584]{1,0:T(8,128)(2,1)S(1)}, u32[]{:S(2)}, u32[]{:S(2)}) collective-permute-start(bf16[24,3584]{1,0:T(8,128)(2,1)S(1)} %get-tuple-element.31), channel_id=1, source_target_pairs={{0,4},{1,17},{2,6},{3,19},{4,0},{5,21},{6,2},{7,23},{8,12},{9,25},... | collective-permute-start | bytes 516104 | tf_op jit(solution)/shard_map/ppermute | solution.py:300
  31.6 1.0 %collective-permute-start.15 = (bf16[24,3584]{1,0:T(8,128)(2,1)S(1)}, bf16[24,3584]{1,0:T(8,128)(2,1)S(1)}, u32[]{:S(2)}, u32[]{:S(2)}) collective-permute-start(bf16[24,3584]{1,0:T(8,128)(2,1)S(1)} %get-tuple-element.32), channel_id=1, source_target_pairs={{0,2},{1,9},{2,0},{3,11},{4,6},{5,13},{6,4},{7,15},{8,10},{9,1},{1... | collective-permute-start | bytes 516104 | tf_op jit(solution)/shard_map/ppermute | solution.py:300
  32.6 0.9 %collective-permute-start.16 = (bf16[24,3584]{1,0:T(8,128)(2,1)S(1)}, bf16[24,3584]{1,0:T(8,128)(2,1)S(1)}, u32[]{:S(2)}, u32[]{:S(2)}) collective-permute-start(bf16[24,3584]{1,0:T(8,128)(2,1)S(1)} %get-tuple-element.33), channel_id=1, source_target_pairs={{0,6},{1,25},{2,4},{3,27},{4,2},{5,29},{6,0},{7,31},{8,14},{9,17},... | collective-permute-start | bytes 516104 | tf_op jit(solution)/shard_map/ppermute | solution.py:300
  33.6 1.5 %collective-permute-start.11 = (bf16[8,3584]{1,0:T(8,128)(2,1)S(1)}, bf16[8,3584]{1,0:T(8,128)(2,1)S(1)}, u32[]{:S(2)}, u32[]{:S(2)}) collective-permute-start(bf16[8,3584]{1,0:T(8,128)(2,1)S(1)} %get-tuple-element.27), channel_id=1, source_target_pairs={{0,4},{1,17},{2,6},{3,19},{4,0},{5,21},{6,2},{7,23},{8,12},{9,25},... | collective-permute-start | bytes 172040 | tf_op jit(solution)/shard_map/ppermute | solution.py:300
  35.1 1.0 %collective-permute-start.12 = (bf16[8,3584]{1,0:T(8,128)(2,1)S(1)}, bf16[8,3584]{1,0:T(8,128)(2,1)S(1)}, u32[]{:S(2)}, u32[]{:S(2)}) collective-permute-start(bf16[8,3584]{1,0:T(8,128)(2,1)S(1)} %get-tuple-element.28), channel_id=1, source_target_pairs={{0,2},{1,9},{2,0},{3,11},{4,6},{5,13},{6,4},{7,15},{8,10},{9,1},{1... | collective-permute-start | bytes 172040 | tf_op jit(solution)/shard_map/ppermute | solution.py:300
  36.1 0.0 collective-permute-done.14.refs_1_
  36.1 1.3 %collective-permute-start.13 = (bf16[8,3584]{1,0:T(8,128)(2,1)S(1)}, bf16[8,3584]{1,0:T(8,128)(2,1)S(1)}, u32[]{:S(2)}, u32[]{:S(2)}) collective-permute-start(bf16[8,3584]{1,0:T(8,128)(2,1)S(1)} %get-tuple-element.29), channel_id=1, source_target_pairs={{0,6},{1,25},{2,4},{3,27},{4,2},{5,29},{6,0},{7,31},{8,14},{9,17},... | collective-permute-start | bytes 172040 | tf_op jit(solution)/shard_map/ppermute | solution.py:300
  37.5 0.0 collective-permute-done.15.refs_2_
  37.5 1.6 %collective-permute-done.16.refs_3_ = bf16[24,3584]{1,0:T(8,128)(2,1)S(1)} collective-permute-done((bf16[24,3584]{1,0:T(8,128)(2,1)S(1)}, bf16[24,3584]{1,0:T(8,128)(2,1)S(1)}, u32[]{:S(2)}, u32[]{:S(2)}) %collective-permute-start.16) | collective-permute-done | bytes 172064 | tf_op jit(solution)/shard_map/ppermute | solution.py:300
  39.0 0.1 shard_map.112
  39.1 1.3 %collective-permute-start.17 = (bf16[8,3584]{1,0:T(8,128)(2,1)S(1)}, bf16[8,3584]{1,0:T(8,128)(2,1)S(1)}, u32[]{:S(2)}, u32[]{:S(2)}) collective-permute-start(bf16[8,3584]{1,0:T(8,128)(2,1)S(1)} %get-tuple-element.34), channel_id=1, source_target_pairs={{0,24},{1,7},{2,26},{3,5},{4,28},{5,3},{6,30},{7,1},{8,16},{9,15},... | collective-permute-start | bytes 172040 | tf_op jit(solution)/shard_map/ppermute | solution.py:300
  40.4 1.1 %collective-permute-start.18 = (bf16[8,3584]{1,0:T(8,128)(2,1)S(1)}, bf16[8,3584]{1,0:T(8,128)(2,1)S(1)}, u32[]{:S(2)}, u32[]{:S(2)}) collective-permute-start(bf16[8,3584]{1,0:T(8,128)(2,1)S(1)} %get-tuple-element.35), channel_id=1, source_target_pairs={{0,16},{1,5},{2,18},{3,7},{4,20},{5,1},{6,22},{7,3},{8,24},{9,13},... | collective-permute-start | bytes 172040 | tf_op jit(solution)/shard_map/ppermute | solution.py:300
  41.5 0.0 collective-permute-done.11.refs_1_
  41.5 2.1 %collective-permute-start.19 = (bf16[8,3584]{1,0:T(8,128)(2,1)S(1)}, bf16[8,3584]{1,0:T(8,128)(2,1)S(1)}, u32[]{:S(2)}, u32[]{:S(2)}) collective-permute-start(bf16[8,3584]{1,0:T(8,128)(2,1)S(1)} %get-tuple-element.36), channel_id=1, source_target_pairs={{0,8},{1,3},{2,10},{3,1},{4,12},{5,7},{6,14},{7,5},{8,0},{9,11},{1... | collective-permute-start | bytes 172040 | tf_op jit(solution)/shard_map/ppermute | solution.py:300
  43.6 0.0 collective-permute-done.12.refs_2_
  43.6 0.0 collective-permute-done.13.refs_3_
  43.6 1.6 %collective-permute-done.17.refs_4_ = bf16[8,3584]{1,0:T(8,128)(2,1)S(1)} collective-permute-done((bf16[8,3584]{1,0:T(8,128)(2,1)S(1)}, bf16[8,3584]{1,0:T(8,128)(2,1)S(1)}, u32[]{:S(2)}, u32[]{:S(2)}) %collective-permute-start.17) | collective-permute-done | bytes 57376 | tf_op jit(solution)/shard_map/ppermute | solution.py:300
  45.2 0.6 %collective-permute-done.18.refs_5_ = bf16[8,3584]{1,0:T(8,128)(2,1)S(1)} collective-permute-done((bf16[8,3584]{1,0:T(8,128)(2,1)S(1)}, bf16[8,3584]{1,0:T(8,128)(2,1)S(1)}, u32[]{:S(2)}, u32[]{:S(2)}) %collective-permute-start.18) | collective-permute-done | bytes 57376 | tf_op jit(solution)/shard_map/ppermute | solution.py:300
  45.9 0.5 %collective-permute-done.19.refs_6_ = bf16[8,3584]{1,0:T(8,128)(2,1)S(1)} collective-permute-done((bf16[8,3584]{1,0:T(8,128)(2,1)S(1)}, bf16[8,3584]{1,0:T(8,128)(2,1)S(1)}, u32[]{:S(2)}, u32[]{:S(2)}) %collective-permute-start.19) | collective-permute-done | bytes 57376 | tf_op jit(solution)/shard_map/ppermute | solution.py:300
  46.4 0.7 %shard_map.113 = bf16[8,3584]{1,0:T(8,128)(2,1)} custom-call(bf16[8,3584]{1,0:T(8,128)(2,1)S(1)} %get-tuple-element.26.refs_0_, bf16[8,3584]{1,0:T(8,128)(2,1)S(1)} %collective-permute-done.11.refs_1_, bf16[8,3584]{1,0:T(8,128)(2,1)S(1)} %collective-permute-done.12.refs_2_, bf16[8,3584]{1,0:T(8,128)(2,1)S(1)} %collective-permute-done.13.refs_3_, ...), custom_call_target="tpu_custom_call" | custom-call | flops 200704 | bytes 401408 | tf_op jit(solution)/shard_map/pallas_call | solution.py:268
  (4 shorter events, 0.0 us)
Async XLA Ops:
  1.6 7.4 %collective-permute-start.2 = (bf16[8,3712]{1,0:T(8,128)(2,1)S(1)}, bf16[8,3712]{1,0:T(8,128)(2,1)S(1)}, u32[]{:S(2)}, u32[]{:S(2)}) collective-permute-start(bf16[8,3712]{1,0:T(8,128)(2,1)S(1)} %shard_map.104.refs_0_), channel_id=1, source_target_pairs={{0,24},{1,7},{2,26},{3,5},{4,28},{5,3},{6,30},{7,1},{8,16},{9,15},... | collective-permute-start | bytes 178184 | tf_op jit(solution)/shard_map/ppermute | solution.py:300
  6.7 5.1 %collective-permute-start.1 = (bf16[8,3712]{1,0:T(8,128)(2,1)S(1)}, bf16[8,3712]{1,0:T(8,128)(2,1)S(1)}, u32[]{:S(2)}, u32[]{:S(2)}) collective-permute-start(bf16[8,3712]{1,0:T(8,128)(2,1)S(1)} %shard_map.104.refs_0_), channel_id=1, source_target_pairs={{0,16},{1,5},{2,18},{3,7},{4,20},{5,1},{6,22},{7,3},{8,24},{9,13},... | collective-permute-start | bytes 178184 | tf_op jit(solution)/shard_map/ppermute | solution.py:300
  6.7 5.1 %collective-permute-start = (bf16[8,3712]{1,0:T(8,128)(2,1)S(1)}, bf16[8,3712]{1,0:T(8,128)(2,1)S(1)}, u32[]{:S(2)}, u32[]{:S(2)}) collective-permute-start(bf16[8,3712]{1,0:T(8,128)(2,1)S(1)} %shard_map.104.refs_0_), channel_id=1, source_target_pairs={{0,8},{1,3},{2,10},{3,1},{4,12},{5,7},{6,14},{7,5},{8,0},{9,11},{1... | collective-permute-start | bytes 178184 | tf_op jit(solution)/shard_map/ppermute | solution.py:300
  11.8 9.2 %collective-permute-start.3 = (bf16[32,3712]{1,0:T(8,128)(2,1)S(1)}, bf16[32,3712]{1,0:T(8,128)(2,1)S(1)}, u32[]{:S(2)}, u32[]{:S(2)}) collective-permute-start(bf16[32,3712]{1,0:T(8,128)(2,1)S(1)} %shard_map.105.after_ref.refs_0_), channel_id=1, source_target_pairs={{0,2},{1,9},{2,0},{3,11},{4,6},{5,13},{6,4},{7,15},{8,10},{9,1},{1... | collective-permute-start | bytes 712712 | tf_op jit(solution)/shard_map/ppermute | solution.py:300
  13.7 8.7 %collective-permute-start.4 = (bf16[32,3712]{1,0:T(8,128)(2,1)S(1)}, bf16[32,3712]{1,0:T(8,128)(2,1)S(1)}, u32[]{:S(2)}, u32[]{:S(2)}) collective-permute-start(bf16[32,3712]{1,0:T(8,128)(2,1)S(1)} %shard_map.105.after_ref.refs_0_), channel_id=1, source_target_pairs={{0,4},{1,17},{2,6},{3,19},{4,0},{5,21},{6,2},{7,23},{8,12},{9,25},... | collective-permute-start | bytes 712712 | tf_op jit(solution)/shard_map/ppermute | solution.py:300
  15.3 7.1 %collective-permute-start.5 = (bf16[32,3712]{1,0:T(8,128)(2,1)S(1)}, bf16[32,3712]{1,0:T(8,128)(2,1)S(1)}, u32[]{:S(2)}, u32[]{:S(2)}) collective-permute-start(bf16[32,3712]{1,0:T(8,128)(2,1)S(1)} %shard_map.105.after_ref.refs_0_), channel_id=1, source_target_pairs={{0,6},{1,25},{2,4},{3,27},{4,2},{5,29},{6,0},{7,31},{8,14},{9,17},... | collective-permute-start | bytes 712712 | tf_op jit(solution)/shard_map/ppermute | solution.py:300
  15.4 7.5 %collective-permute-start.6 = (bf16[32,3712]{1,0:T(8,128)(2,1)S(1)}, bf16[32,3712]{1,0:T(8,128)(2,1)S(1)}, u32[]{:S(2)}, u32[]{:S(2)}) collective-permute-start(bf16[32,3712]{1,0:T(8,128)(2,1)S(1)} %shard_map.105.after_ref.refs_0_), channel_id=1, source_target_pairs={{0,1},{1,0},{2,3},{3,2},{4,5},{5,4},{6,7},{7,6},{8,9},{9,8},{10,11... | collective-permute-start | bytes 712712 | tf_op jit(solution)/shard_map/ppermute | solution.py:309
  21.0 1.9 %collective-permute-start.7 = (bf16[32,3712]{1,0:T(8,128)(2,1)S(1)}, bf16[32,3712]{1,0:T(8,128)(2,1)S(1)}, u32[]{:S(2)}, u32[]{:S(2)}) collective-permute-start(bf16[32,3712]{1,0:T(8,128)(2,1)S(1)} %shard_map.107.refs_1_), channel_id=1, source_target_pairs={{0,1},{1,0},{2,3},{3,2},{4,5},{5,4},{6,7},{7,6},{8,9},{9,8},{10,11... | collective-permute-start | bytes 712712 | tf_op jit(solution)/shard_map/ppermute | solution.py:309
  22.4 1.5 %collective-permute-start.8 = (bf16[32,3712]{1,0:T(8,128)(2,1)S(1)}, bf16[32,3712]{1,0:T(8,128)(2,1)S(1)}, u32[]{:S(2)}, u32[]{:S(2)}) collective-permute-start(bf16[32,3712]{1,0:T(8,128)(2,1)S(1)} %shard_map.108.refs_2_), channel_id=1, source_target_pairs={{0,1},{1,0},{2,3},{3,2},{4,5},{5,4},{6,7},{7,6},{8,9},{9,8},{10,11... | collective-permute-start | bytes 712712 | tf_op jit(solution)/shard_map/ppermute | solution.py:309
  22.4 1.8 %collective-permute-start.9 = (bf16[32,3712]{1,0:T(8,128)(2,1)S(1)}, bf16[32,3712]{1,0:T(8,128)(2,1)S(1)}, u32[]{:S(2)}, u32[]{:S(2)}) collective-permute-start(bf16[32,3712]{1,0:T(8,128)(2,1)S(1)} %shard_map.109.refs_3_), channel_id=1, source_target_pairs={{0,1},{1,0},{2,3},{3,2},{4,5},{5,4},{6,7},{7,6},{8,9},{9,8},{10,11... | collective-permute-start | bytes 712712 | tf_op jit(solution)/shard_map/ppermute | solution.py:309
  27.3 2.5 %collective-permute-start.10 = (bf16[128,3584]{1,0:T(8,128)(2,1)S(1)}, bf16[128,3584]{1,0:T(8,128)(2,1)S(1)}, u32[]{:S(2)}, u32[]{:S(2)}) collective-permute-start(bf16[128,3584]{1,0:T(8,128)(2,1)S(1)} %get-tuple-element.25), channel_id=1, source_target_pairs={{0,1},{1,0},{2,3},{3,2},{4,5},{5,4},{6,7},{7,6},{8,9},{9,8},{10,11... | collective-permute-start | bytes 2752520 | tf_op jit(solution)/shard_map/ppermute | solution.py:309
  30.0 6.1 %collective-permute-start.14 = (bf16[24,3584]{1,0:T(8,128)(2,1)S(1)}, bf16[24,3584]{1,0:T(8,128)(2,1)S(1)}, u32[]{:S(2)}, u32[]{:S(2)}) collective-permute-start(bf16[24,3584]{1,0:T(8,128)(2,1)S(1)} %get-tuple-element.31), channel_id=1, source_target_pairs={{0,4},{1,17},{2,6},{3,19},{4,0},{5,21},{6,2},{7,23},{8,12},{9,25},... | collective-permute-start | bytes 516104 | tf_op jit(solution)/shard_map/ppermute | solution.py:300
  31.6 5.9 %collective-permute-start.15 = (bf16[24,3584]{1,0:T(8,128)(2,1)S(1)}, bf16[24,3584]{1,0:T(8,128)(2,1)S(1)}, u32[]{:S(2)}, u32[]{:S(2)}) collective-permute-start(bf16[24,3584]{1,0:T(8,128)(2,1)S(1)} %get-tuple-element.32), channel_id=1, source_target_pairs={{0,2},{1,9},{2,0},{3,11},{4,6},{5,13},{6,4},{7,15},{8,10},{9,1},{1... | collective-permute-start | bytes 516104 | tf_op jit(solution)/shard_map/ppermute | solution.py:300
  32.6 6.4 %collective-permute-start.16 = (bf16[24,3584]{1,0:T(8,128)(2,1)S(1)}, bf16[24,3584]{1,0:T(8,128)(2,1)S(1)}, u32[]{:S(2)}, u32[]{:S(2)}) collective-permute-start(bf16[24,3584]{1,0:T(8,128)(2,1)S(1)} %get-tuple-element.33), channel_id=1, source_target_pairs={{0,6},{1,25},{2,4},{3,27},{4,2},{5,29},{6,0},{7,31},{8,14},{9,17},... | collective-permute-start | bytes 516104 | tf_op jit(solution)/shard_map/ppermute | solution.py:300
  33.6 7.9 %collective-permute-start.11 = (bf16[8,3584]{1,0:T(8,128)(2,1)S(1)}, bf16[8,3584]{1,0:T(8,128)(2,1)S(1)}, u32[]{:S(2)}, u32[]{:S(2)}) collective-permute-start(bf16[8,3584]{1,0:T(8,128)(2,1)S(1)} %get-tuple-element.27), channel_id=1, source_target_pairs={{0,4},{1,17},{2,6},{3,19},{4,0},{5,21},{6,2},{7,23},{8,12},{9,25},... | collective-permute-start | bytes 172040 | tf_op jit(solution)/shard_map/ppermute | solution.py:300
  35.1 8.5 %collective-permute-start.12 = (bf16[8,3584]{1,0:T(8,128)(2,1)S(1)}, bf16[8,3584]{1,0:T(8,128)(2,1)S(1)}, u32[]{:S(2)}, u32[]{:S(2)}) collective-permute-start(bf16[8,3584]{1,0:T(8,128)(2,1)S(1)} %get-tuple-element.28), channel_id=1, source_target_pairs={{0,2},{1,9},{2,0},{3,11},{4,6},{5,13},{6,4},{7,15},{8,10},{9,1},{1... | collective-permute-start | bytes 172040 | tf_op jit(solution)/shard_map/ppermute | solution.py:300
  36.1 7.5 %collective-permute-start.13 = (bf16[8,3584]{1,0:T(8,128)(2,1)S(1)}, bf16[8,3584]{1,0:T(8,128)(2,1)S(1)}, u32[]{:S(2)}, u32[]{:S(2)}) collective-permute-start(bf16[8,3584]{1,0:T(8,128)(2,1)S(1)} %get-tuple-element.29), channel_id=1, source_target_pairs={{0,6},{1,25},{2,4},{3,27},{4,2},{5,29},{6,0},{7,31},{8,14},{9,17},... | collective-permute-start | bytes 172040 | tf_op jit(solution)/shard_map/ppermute | solution.py:300
  39.1 6.1 %collective-permute-start.17 = (bf16[8,3584]{1,0:T(8,128)(2,1)S(1)}, bf16[8,3584]{1,0:T(8,128)(2,1)S(1)}, u32[]{:S(2)}, u32[]{:S(2)}) collective-permute-start(bf16[8,3584]{1,0:T(8,128)(2,1)S(1)} %get-tuple-element.34), channel_id=1, source_target_pairs={{0,24},{1,7},{2,26},{3,5},{4,28},{5,3},{6,30},{7,1},{8,16},{9,15},... | collective-permute-start | bytes 172040 | tf_op jit(solution)/shard_map/ppermute | solution.py:300
  40.4 5.5 %collective-permute-start.18 = (bf16[8,3584]{1,0:T(8,128)(2,1)S(1)}, bf16[8,3584]{1,0:T(8,128)(2,1)S(1)}, u32[]{:S(2)}, u32[]{:S(2)}) collective-permute-start(bf16[8,3584]{1,0:T(8,128)(2,1)S(1)} %get-tuple-element.35), channel_id=1, source_target_pairs={{0,16},{1,5},{2,18},{3,7},{4,20},{5,1},{6,22},{7,3},{8,24},{9,13},... | collective-permute-start | bytes 172040 | tf_op jit(solution)/shard_map/ppermute | solution.py:300
  41.5 4.9 %collective-permute-start.19 = (bf16[8,3584]{1,0:T(8,128)(2,1)S(1)}, bf16[8,3584]{1,0:T(8,128)(2,1)S(1)}, u32[]{:S(2)}, u32[]{:S(2)}) collective-permute-start(bf16[8,3584]{1,0:T(8,128)(2,1)S(1)} %get-tuple-element.36), channel_id=1, source_target_pairs={{0,8},{1,3},{2,10},{3,1},{4,12},{5,7},{6,14},{7,5},{8,0},{9,11},{1... | collective-permute-start | bytes 172040 | tf_op jit(solution)/shard_map/ppermute | solution.py:300

commit v6 on v5

--- a/solution.py
+++ b/solution.py
@@ -146,21 +146,22 @@
     )(stored(hidden_in), stored(expert_routes), stored(route_scores))
 
 
-def join_kernel(*refs):
-    value = jnp.concatenate([ref[...].astype(jnp.float32) for ref in refs[:-1]], axis=0)
+def join_kernel(count, *refs):
+    value = jnp.concatenate([ref[...].astype(jnp.float32) for ref in refs[:count]], axis=0)
     refs[-1][...] = value.astype(jnp.bfloat16)
 
 
-def join(pieces):
+def join(pieces, after=()):
     total, width = sum(p.shape[0] for p in pieces), pieces[0].shape[1]
-    return pl.pallas_call(
-        join_kernel,
+    operands = [*pieces, *after]
+    return pl.pallas_call(
+        functools.partial(join_kernel, len(pieces)),
         out_shape=in_vmem((total, width), jnp.bfloat16),
-        in_specs=[VMEM] * len(pieces),
+        in_specs=[VMEM] * len(operands),
         out_specs=VMEM,
         compiler_params=pltpu.CompilerParams(vmem_limit_bytes=(2 << 20) + 8 * total * width),
         cost_estimate=pl.CostEstimate(flops=total * width, bytes_accessed=4 * total * width, transcendentals=0),
-    )(*(held(p) for p in pieces))
+    )(*(held(p) for p in operands))
 
 
 def tie_kernel(value_ref, after_ref, out_ref):
@@ -310,9 +311,12 @@
 
     own = pack(hidden_in, expert_routes, route_scores, ep_count)
     near = {k: first(own, k) for k in range(outer - 1, 0, -1)}
-    block = join([own] + [near[k] for k in range(1, outer)])
-    steps = [*range(inner - 2, 0, -1), inner - 1]
-    far = {k: second(block, k) for k in steps}
+    last = inner - 1
+    ahead = second(own, last)
+    received = [near[k] for k in range(1, outer)]
+    block, column = join([own, *received]), join(received, [ahead])
+    steps = [*range(last - 1, 0, -1), last]
+    far = {k: second(column if k == last else block, k) for k in steps}
     attention_latent, *weights, token = attend(
         query_latent,
         latent_cache,
@@ -320,7 +324,8 @@
         (expert_gate[0], expert_up[0], expert_down[0]),
         block,
     )
-    pieces = [block] + [tie(far[k], token) for k in range(1, inner)]
+    pieces = [block] + [tie(far[k], token) for k in range(1, last)]
+    pieces += [join([ahead, far[last]], pieces)]
     pieces += [over_cores(p) for p in pieces]
     mine, other = expert_block(pieces, *weights)
 

time: 47.3 us -> 51.8 us (1.095)
  starting transfers between devices: 22.5 us -> 26 us
  waiting for transfers between devices: 13.3 us -> 14.2 us
    ppermute x15 -> x16, starting transfers between devices: 21.2 us -> 24.5 us  [swap(): return lax.ppermute(value, ('ep', 'sub'), pairs)]
    ppermute x15 -> x16, waiting for transfers between devices: 9.68 us -> 10.8 us  [swap(): return lax.ppermute(value, ('ep', 'sub'), pairs)]
  transfers between devices with their start and end apart: 20 -> 21, of which waited for: 10 -> 12; matrix products, arithmetic and copies ran while one was open for 0% -> 0% of each run, Pallas kernels for 12% -> 11%
where the time goes in v6:
time: 51.8 us; the launch traced here: 51.6 us
  starting transfers between devices  26 us (50%)
  waiting for transfers between devices  14.2 us (27%)
  Pallas kernels  10.6 us (20%)
  between operations  0.74 us (1%)
    ppermute x16, starting transfers between devices, swap(): return lax.ppermute(value, ('ep', 'sub'), pairs)  24.5 us
    ppermute x16, waiting for transfers between devices, swap(): return lax.ppermute(value, ('ep', 'sub'), pairs)  10.8 us
    pallas_call x1, Pallas kernels, attend(): pl.pallas_call(attend_kernel, out_shape=(jax.ShapeDtypeStruct((rows, head...  5.58 us
    ppermute x5, waiting for transfers between devices, over_cores(): return lax.ppermute(value, 'sub', [(i, i ^ 1) for i in range(sub_count)])  3.46 us
    pallas_call x1, Pallas kernels, expert_block(): pl.pallas_call(functools.partial(expert_kernel, len(pieces)), out_shape=(...  3.03 us
    ppermute x5, starting transfers between devices, over_cores(): return lax.ppermute(value, 'sub', [(i, i ^ 1) for i in range(sub_count)])  1.49 us
  transfers between devices with their start and end apart: 21, of which 12 were waited for; matrix products, arithmetic and copies ran while one was open for 0% of the time, Pallas kernels for 11%

profile of v6, /device:TPU:0, one launch (start us, length us, event | category | flops | bytes accessed | tf_op | source)
XLA Modules:
  0.0 51.6 jit_solution(1548061615148481432)
XLA Ops:
  0.6 0.9 %shard_map.104.refs_0_ = bf16[8,3712]{1,0:T(8,128)(2,1)S(1)} custom-call(bf16[8,3584]{1,0:T(8,128)(2,1)} %hidden_ref.1, s32[8,8]{1,0:T(8,128)} %routes_ref.1, f32[8,8]{1,0:T(8,128)} %scores_ref.1), custom_call_target="tpu_custom_call" | custom-call | flops 65536 | bytes 114688 | tf_op jit(solution)/shard_map/pallas_call | solution.py:133
  1.6 5.1 %collective-permute-start.2 = (bf16[8,3712]{1,0:T(8,128)(2,1)S(1)}, bf16[8,3712]{1,0:T(8,128)(2,1)S(1)}, u32[]{:S(2)}, u32[]{:S(2)}) collective-permute-start(bf16[8,3712]{1,0:T(8,128)(2,1)S(1)} %shard_map.104.refs_0_), channel_id=1, source_target_pairs={{0,24},{1,7},{2,26},{3,5},{4,28},{5,3},{6,30},{7,1},{8,16},{9,15},... | collective-permute-start | bytes 178184 | tf_op jit(solution)/shard_map/ppermute | solution.py:301
  6.7 0.0 collective-permute-start.1
  6.7 0.6 %collective-permute-start = (bf16[8,3712]{1,0:T(8,128)(2,1)S(1)}, bf16[8,3712]{1,0:T(8,128)(2,1)S(1)}, u32[]{:S(2)}, u32[]{:S(2)}) collective-permute-start(bf16[8,3712]{1,0:T(8,128)(2,1)S(1)} %shard_map.104.refs_0_), channel_id=1, source_target_pairs={{0,8},{1,3},{2,10},{3,1},{4,12},{5,7},{6,14},{7,5},{8,0},{9,11},{1... | collective-permute-start | bytes 178184 | tf_op jit(solution)/shard_map/ppermute | solution.py:301
  7.3 1.6 %collective-permute-done.2.refs_3_.refs_2_ = bf16[8,3712]{1,0:T(8,128)(2,1)S(1)} collective-permute-done((bf16[8,3712]{1,0:T(8,128)(2,1)S(1)}, bf16[8,3712]{1,0:T(8,128)(2,1)S(1)}, u32[]{:S(2)}, u32[]{:S(2)}) %collective-permute-start.2) | collective-permute-done | bytes 59424 | tf_op jit(solution)/shard_map/ppermute | solution.py:301
  8.9 2.9 %collective-permute-done.1.refs_2_.refs_1_ = bf16[8,3712]{1,0:T(8,128)(2,1)S(1)} collective-permute-done((bf16[8,3712]{1,0:T(8,128)(2,1)S(1)}, bf16[8,3712]{1,0:T(8,128)(2,1)S(1)}, u32[]{:S(2)}, u32[]{:S(2)}) %collective-permute-start.1) | collective-permute-done | bytes 59424 | tf_op jit(solution)/shard_map/ppermute | solution.py:301
  11.8 0.0 collective-permute-done.refs_1_.refs_0_
  11.8 1.6 %collective-permute-start.4 = (bf16[32,3712]{1,0:T(8,128)(2,1)S(1)}, bf16[32,3712]{1,0:T(8,128)(2,1)S(1)}, u32[]{:S(2)}, u32[]{:S(2)}) collective-permute-start(bf16[32,3712]{1,0:T(8,128)(2,1)S(1)} %shard_map.105.after_ref.refs_2_.refs_0_), channel_id=1, source_target_pairs={{0,4},{1,17},{2,6},{3,19},{4,0},{5,21},{6,2},{7,23},{8,12},{9,25},... | collective-permute-start | bytes 712712 | tf_op jit(solution)/shard_map/ppermute | solution.py:301
  13.4 2.7 %collective-permute-start.5 = (bf16[8,3712]{1,0:T(8,128)(2,1)S(1)}, bf16[8,3712]{1,0:T(8,128)(2,1)S(1)}, u32[]{:S(2)}, u32[]{:S(2)}) collective-permute-start(bf16[8,3712]{1,0:T(8,128)(2,1)S(1)} %shard_map.104.refs_0_), channel_id=1, source_target_pairs={{0,6},{1,25},{2,4},{3,27},{4,2},{5,29},{6,0},{7,31},{8,14},{9,17},... | collective-permute-start | bytes 178184 | tf_op jit(solution)/shard_map/ppermute | solution.py:301
  16.1 0.4 collective-permute-start.3
  16.5 2.1 %collective-permute-done.5.refs_3_.refs_0_ = bf16[8,3712]{1,0:T(8,128)(2,1)S(1)} collective-permute-done((bf16[8,3712]{1,0:T(8,128)(2,1)S(1)}, bf16[8,3712]{1,0:T(8,128)(2,1)S(1)}, u32[]{:S(2)}, u32[]{:S(2)}) %collective-permute-start.5) | collective-permute-done | bytes 59424 | tf_op jit(solution)/shard_map/ppermute | solution.py:301
  18.6 2.8 %collective-permute-start.6 = (bf16[24,3712]{1,0:T(8,128)(2,1)S(1)}, bf16[24,3712]{1,0:T(8,128)(2,1)S(1)}, u32[]{:S(2)}, u32[]{:S(2)}) collective-permute-start(bf16[24,3712]{1,0:T(8,128)(2,1)S(1)} %shard_map.109), channel_id=1, source_target_pairs={{0,6},{1,25},{2,4},{3,27},{4,2},{5,29},{6,0},{7,31},{8,14},{9,17},... | collective-permute-start | bytes 534536 | tf_op jit(solution)/shard_map/ppermute | solution.py:301
  21.4 0.0 collective-permute-start.7
  21.4 5.6 %shard_map.106 = (bf16[4,128,512]{2,1,0:T(8,128)(2,1)}, bf16[3584,512]{1,0:T(8,128)(2,1)S(1)}, bf16[3584,512]{1,0:T(8,128)(2,1)S(1)}, bf16[512,3584]{1,0:T(8,128)(2,1)S(1)}, f32[8,128]{1,0:T(8,128)S(1)}) custom-call(s32[4]{0:T(128)} %lengths_hbm.1, bf16[4,576,128]{2,1,0:T(8,128)(2,1)} %bitcast.9, bf16[4,576,256]{2,1,0:T(8,128)(2,1)} %bitcast.8, ...), custom_call_target="tpu_custom_call" | custom-call | flops 301989888 | bytes 11010048 | tf_op jit(solution)/shard_map/pallas_call | solution.py:74
  27.0 0.0 collective-permute-done.4.value_ref
  27.0 0.0 collective-permute-done.3.value_ref
  27.0 0.0 collective-permute-done.6.refs_1_
  27.1 0.6 %collective-permute-start.10 = (bf16[32,3712]{1,0:T(8,128)(2,1)S(1)}, bf16[32,3712]{1,0:T(8,128)(2,1)S(1)}, u32[]{:S(2)}, u32[]{:S(2)}) collective-permute-start(bf16[32,3712]{1,0:T(8,128)(2,1)S(1)} %shard_map.110.refs_3_), channel_id=1, source_target_pairs={{0,1},{1,0},{2,3},{3,2},{4,5},{5,4},{6,7},{7,6},{8,9},{9,8},{10,11... | collective-permute-start | bytes 712712 | tf_op jit(solution)/shard_map/ppermute | solution.py:310
  27.6 0.1 collective-permute-start.8
  27.7 0.4 collective-permute-start.9
  28.1 0.0 collective-permute-done.7.refs_4_
  28.1 0.6 %collective-permute-done.10.refs_7_ = bf16[32,3712]{1,0:T(8,128)(2,1)S(1)} collective-permute-done((bf16[32,3712]{1,0:T(8,128)(2,1)S(1)}, bf16[32,3712]{1,0:T(8,128)(2,1)S(1)}, u32[]{:S(2)}, u32[]{:S(2)}) %collective-permute-start.10) | collective-permute-done | bytes 237600 | tf_op jit(solution)/shard_map/ppermute | solution.py:310
  28.8 0.4 collective-permute-done.8.refs_5_
  29.1 0.3 collective-permute-done.9.refs_6_
  29.5 3.0 %shard_map.111 = (bf16[128,3584]{1,0:T(8,128)(2,1)S(1)}, bf16[128,3584]{1,0:T(8,128)(2,1)S(1)}) custom-call(bf16[32,3712]{1,0:T(8,128)(2,1)S(1)} %shard_map.105.after_ref.refs_2_.refs_0_, bf16[32,3712]{1,0:T(8,128)(2,1)S(1)} %shard_map.107.refs_3_.refs_1_, bf16[32,3712]{1,0:T(8,128)(2,1)S(1)} %shard_map.108.refs_4_.refs_2_, ...), custom_call_target="tpu_custom_call" | custom-call | flops 2818572288 | bytes 3801088 | tf_op jit(solution)/shard_map/pallas_call | solution.py:239
  32.5 0.4 collective-permute-start.11
  32.9 2.1 %collective-permute-done.11.refs_1_ = bf16[128,3584]{1,0:T(8,128)(2,1)S(1)} collective-permute-done((bf16[128,3584]{1,0:T(8,128)(2,1)S(1)}, bf16[128,3584]{1,0:T(8,128)(2,1)S(1)}, u32[]{:S(2)}, u32[]{:S(2)}) %collective-permute-start.11) | collective-permute-done | bytes 917536 | tf_op jit(solution)/shard_map/ppermute | solution.py:310
  35.1 0.2 shard_map.112
  35.3 1.8 %collective-permute-start.15 = (bf16[24,3584]{1,0:T(8,128)(2,1)S(1)}, bf16[24,3584]{1,0:T(8,128)(2,1)S(1)}, u32[]{:S(2)}, u32[]{:S(2)}) collective-permute-start(bf16[24,3584]{1,0:T(8,128)(2,1)S(1)} %get-tuple-element.31), channel_id=1, source_target_pairs={{0,4},{1,17},{2,6},{3,19},{4,0},{5,21},{6,2},{7,23},{8,12},{9,25},... | collective-permute-start | bytes 516104 | tf_op jit(solution)/shard_map/ppermute | solution.py:301
  37.1 0.0 collective-permute-start.16
  37.1 1.7 %collective-permute-start.17 = (bf16[24,3584]{1,0:T(8,128)(2,1)S(1)}, bf16[24,3584]{1,0:T(8,128)(2,1)S(1)}, u32[]{:S(2)}, u32[]{:S(2)}) collective-permute-start(bf16[24,3584]{1,0:T(8,128)(2,1)S(1)} %get-tuple-element.33), channel_id=1, source_target_pairs={{0,6},{1,25},{2,4},{3,27},{4,2},{5,29},{6,0},{7,31},{8,14},{9,17},... | collective-permute-start | bytes 516104 | tf_op jit(solution)/shard_map/ppermute | solution.py:301
  38.8 1.7 %collective-permute-start.12 = (bf16[8,3584]{1,0:T(8,128)(2,1)S(1)}, bf16[8,3584]{1,0:T(8,128)(2,1)S(1)}, u32[]{:S(2)}, u32[]{:S(2)}) collective-permute-start(bf16[8,3584]{1,0:T(8,128)(2,1)S(1)} %get-tuple-element.27), channel_id=1, source_target_pairs={{0,4},{1,17},{2,6},{3,19},{4,0},{5,21},{6,2},{7,23},{8,12},{9,25},... | collective-permute-start | bytes 172040 | tf_op jit(solution)/shard_map/ppermute | solution.py:301
  40.6 0.0 collective-permute-start.13
  40.6 0.2 collective-permute-done.15.refs_1_
  40.7 1.6 %collective-permute-start.14 = (bf16[8,3584]{1,0:T(8,128)(2,1)S(1)}, bf16[8,3584]{1,0:T(8,128)(2,1)S(1)}, u32[]{:S(2)}, u32[]{:S(2)}) collective-permute-start(bf16[8,3584]{1,0:T(8,128)(2,1)S(1)} %get-tuple-element.29), channel_id=1, source_target_pairs={{0,6},{1,25},{2,4},{3,27},{4,2},{5,29},{6,0},{7,31},{8,14},{9,17},... | collective-permute-start | bytes 172040 | tf_op jit(solution)/shard_map/ppermute | solution.py:301
  42.3 0.2 collective-permute-done.16.refs_2_
  42.5 1.7 %collective-permute-done.17.refs_3_ = bf16[24,3584]{1,0:T(8,128)(2,1)S(1)} collective-permute-done((bf16[24,3584]{1,0:T(8,128)(2,1)S(1)}, bf16[24,3584]{1,0:T(8,128)(2,1)S(1)}, u32[]{:S(2)}, u32[]{:S(2)}) %collective-permute-start.17) | collective-permute-done | bytes 172064 | tf_op jit(solution)/shard_map/ppermute | solution.py:301
  44.2 0.1 shard_map.113
  44.2 0.3 collective-permute-start.18
  44.6 1.1 %collective-permute-start.19 = (bf16[8,3584]{1,0:T(8,128)(2,1)S(1)}, bf16[8,3584]{1,0:T(8,128)(2,1)S(1)}, u32[]{:S(2)}, u32[]{:S(2)}) collective-permute-start(bf16[8,3584]{1,0:T(8,128)(2,1)S(1)} %get-tuple-element.35), channel_id=1, source_target_pairs={{0,16},{1,5},{2,18},{3,7},{4,20},{5,1},{6,22},{7,3},{8,24},{9,13},... | collective-permute-start | bytes 172040 | tf_op jit(solution)/shard_map/ppermute | solution.py:301
  45.7 0.0 collective-permute-done.12.refs_1_
  45.7 3.0 %collective-permute-start.20 = (bf16[8,3584]{1,0:T(8,128)(2,1)S(1)}, bf16[8,3584]{1,0:T(8,128)(2,1)S(1)}, u32[]{:S(2)}, u32[]{:S(2)}) collective-permute-start(bf16[8,3584]{1,0:T(8,128)(2,1)S(1)} %get-tuple-element.36), channel_id=1, source_target_pairs={{0,8},{1,3},{2,10},{3,1},{4,12},{5,7},{6,14},{7,5},{8,0},{9,11},{1... | collective-permute-start | bytes 172040 | tf_op jit(solution)/shard_map/ppermute | solution.py:301
  48.7 0.0 collective-permute-done.13.refs_2_
  48.7 0.0 collective-permute-done.14.refs_3_
  48.7 1.6 %collective-permute-done.18.refs_4_ = bf16[8,3584]{1,0:T(8,128)(2,1)S(1)} collective-permute-done((bf16[8,3584]{1,0:T(8,128)(2,1)S(1)}, bf16[8,3584]{1,0:T(8,128)(2,1)S(1)}, u32[]{:S(2)}, u32[]{:S(2)}) %collective-permute-start.18) | collective-permute-done | bytes 57376 | tf_op jit(solution)/shard_map/ppermute | solution.py:301
  50.3 0.0 collective-permute-done.19.refs_5_
  50.3 0.6 %collective-permute-done.20.refs_6_ = bf16[8,3584]{1,0:T(8,128)(2,1)S(1)} collective-permute-done((bf16[8,3584]{1,0:T(8,128)(2,1)S(1)}, bf16[8,3584]{1,0:T(8,128)(2,1)S(1)}, u32[]{:S(2)}, u32[]{:S(2)}) %collective-permute-start.20) | collective-permute-done | bytes 57376 | tf_op jit(solution)/shard_map/ppermute | solution.py:301
  50.9 0.7 %shard_map.114 = bf16[8,3584]{1,0:T(8,128)(2,1)} custom-call(bf16[8,3584]{1,0:T(8,128)(2,1)S(1)} %get-tuple-element.26.refs_0_, bf16[8,3584]{1,0:T(8,128)(2,1)S(1)} %collective-permute-done.12.refs_1_, bf16[8,3584]{1,0:T(8,128)(2,1)S(1)} %collective-permute-done.13.refs_2_, bf16[8,3584]{1,0:T(8,128)(2,1)S(1)} %collective-permute-done.14.refs_3_, ...), custom_call_target="tpu_custom_call" | custom-call | flops 200704 | bytes 401408 | tf_op jit(solution)/shard_map/pallas_call | solution.py:269
  (5 shorter events, 0.1 us)
Async XLA Ops:
  1.6 7.4 %collective-permute-start.2 = (bf16[8,3712]{1,0:T(8,128)(2,1)S(1)}, bf16[8,3712]{1,0:T(8,128)(2,1)S(1)}, u32[]{:S(2)}, u32[]{:S(2)}) collective-permute-start(bf16[8,3712]{1,0:T(8,128)(2,1)S(1)} %shard_map.104.refs_0_), channel_id=1, source_target_pairs={{0,24},{1,7},{2,26},{3,5},{4,28},{5,3},{6,30},{7,1},{8,16},{9,15},... | collective-permute-start | bytes 178184 | tf_op jit(solution)/shard_map/ppermute | solution.py:301
  6.7 5.1 %collective-permute-start.1 = (bf16[8,3712]{1,0:T(8,128)(2,1)S(1)}, bf16[8,3712]{1,0:T(8,128)(2,1)S(1)}, u32[]{:S(2)}, u32[]{:S(2)}) collective-permute-start(bf16[8,3712]{1,0:T(8,128)(2,1)S(1)} %shard_map.104.refs_0_), channel_id=1, source_target_pairs={{0,16},{1,5},{2,18},{3,7},{4,20},{5,1},{6,22},{7,3},{8,24},{9,13},... | collective-permute-start | bytes 178184 | tf_op jit(solution)/shard_map/ppermute | solution.py:301
  6.7 5.1 %collective-permute-start = (bf16[8,3712]{1,0:T(8,128)(2,1)S(1)}, bf16[8,3712]{1,0:T(8,128)(2,1)S(1)}, u32[]{:S(2)}, u32[]{:S(2)}) collective-permute-start(bf16[8,3712]{1,0:T(8,128)(2,1)S(1)} %shard_map.104.refs_0_), channel_id=1, source_target_pairs={{0,8},{1,3},{2,10},{3,1},{4,12},{5,7},{6,14},{7,5},{8,0},{9,11},{1... | collective-permute-start | bytes 178184 | tf_op jit(solution)/shard_map/ppermute | solution.py:301
  11.8 15.2 %collective-permute-start.4 = (bf16[32,3712]{1,0:T(8,128)(2,1)S(1)}, bf16[32,3712]{1,0:T(8,128)(2,1)S(1)}, u32[]{:S(2)}, u32[]{:S(2)}) collective-permute-start(bf16[32,3712]{1,0:T(8,128)(2,1)S(1)} %shard_map.105.after_ref.refs_2_.refs_0_), channel_id=1, source_target_pairs={{0,4},{1,17},{2,6},{3,19},{4,0},{5,21},{6,2},{7,23},{8,12},{9,25},... | collective-permute-start | bytes 712712 | tf_op jit(solution)/shard_map/ppermute | solution.py:301
  13.4 5.2 %collective-permute-start.5 = (bf16[8,3712]{1,0:T(8,128)(2,1)S(1)}, bf16[8,3712]{1,0:T(8,128)(2,1)S(1)}, u32[]{:S(2)}, u32[]{:S(2)}) collective-permute-start(bf16[8,3712]{1,0:T(8,128)(2,1)S(1)} %shard_map.104.refs_0_), channel_id=1, source_target_pairs={{0,6},{1,25},{2,4},{3,27},{4,2},{5,29},{6,0},{7,31},{8,14},{9,17},... | collective-permute-start | bytes 178184 | tf_op jit(solution)/shard_map/ppermute | solution.py:301
  16.1 10.9 %collective-permute-start.3 = (bf16[32,3712]{1,0:T(8,128)(2,1)S(1)}, bf16[32,3712]{1,0:T(8,128)(2,1)S(1)}, u32[]{:S(2)}, u32[]{:S(2)}) collective-permute-start(bf16[32,3712]{1,0:T(8,128)(2,1)S(1)} %shard_map.105.after_ref.refs_2_.refs_0_), channel_id=1, source_target_pairs={{0,2},{1,9},{2,0},{3,11},{4,6},{5,13},{6,4},{7,15},{8,10},{9,1},{1... | collective-permute-start | bytes 712712 | tf_op jit(solution)/shard_map/ppermute | solution.py:301
  18.6 8.4 %collective-permute-start.6 = (bf16[24,3712]{1,0:T(8,128)(2,1)S(1)}, bf16[24,3712]{1,0:T(8,128)(2,1)S(1)}, u32[]{:S(2)}, u32[]{:S(2)}) collective-permute-start(bf16[24,3712]{1,0:T(8,128)(2,1)S(1)} %shard_map.109), channel_id=1, source_target_pairs={{0,6},{1,25},{2,4},{3,27},{4,2},{5,29},{6,0},{7,31},{8,14},{9,17},... | collective-permute-start | bytes 534536 | tf_op jit(solution)/shard_map/ppermute | solution.py:301
  21.4 6.8 %collective-permute-start.7 = (bf16[32,3712]{1,0:T(8,128)(2,1)S(1)}, bf16[32,3712]{1,0:T(8,128)(2,1)S(1)}, u32[]{:S(2)}, u32[]{:S(2)}) collective-permute-start(bf16[32,3712]{1,0:T(8,128)(2,1)S(1)} %shard_map.105.after_ref.refs_2_.refs_0_), channel_id=1, source_target_pairs={{0,1},{1,0},{2,3},{3,2},{4,5},{5,4},{6,7},{7,6},{8,9},{9,8},{10,11... | collective-permute-start | bytes 712712 | tf_op jit(solution)/shard_map/ppermute | solution.py:310
  27.1 1.7 %collective-permute-start.10 = (bf16[32,3712]{1,0:T(8,128)(2,1)S(1)}, bf16[32,3712]{1,0:T(8,128)(2,1)S(1)}, u32[]{:S(2)}, u32[]{:S(2)}) collective-permute-start(bf16[32,3712]{1,0:T(8,128)(2,1)S(1)} %shard_map.110.refs_3_), channel_id=1, source_target_pairs={{0,1},{1,0},{2,3},{3,2},{4,5},{5,4},{6,7},{7,6},{8,9},{9,8},{10,11... | collective-permute-start | bytes 712712 | tf_op jit(solution)/shard_map/ppermute | solution.py:310
  27.6 1.5 %collective-permute-start.8 = (bf16[32,3712]{1,0:T(8,128)(2,1)S(1)}, bf16[32,3712]{1,0:T(8,128)(2,1)S(1)}, u32[]{:S(2)}, u32[]{:S(2)}) collective-permute-start(bf16[32,3712]{1,0:T(8,128)(2,1)S(1)} %shard_map.107.refs_3_.refs_1_), channel_id=1, source_target_pairs={{0,1},{1,0},{2,3},{3,2},{4,5},{5,4},{6,7},{7,6},{8,9},{9,8},{10,11... | collective-permute-start | bytes 712712 | tf_op jit(solution)/shard_map/ppermute | solution.py:310
  27.7 1.8 %collective-permute-start.9 = (bf16[32,3712]{1,0:T(8,128)(2,1)S(1)}, bf16[32,3712]{1,0:T(8,128)(2,1)S(1)}, u32[]{:S(2)}, u32[]{:S(2)}) collective-permute-start(bf16[32,3712]{1,0:T(8,128)(2,1)S(1)} %shard_map.108.refs_4_.refs_2_), channel_id=1, source_target_pairs={{0,1},{1,0},{2,3},{3,2},{4,5},{5,4},{6,7},{7,6},{8,9},{9,8},{10,11... | collective-permute-start | bytes 712712 | tf_op jit(solution)/shard_map/ppermute | solution.py:310
  32.5 2.5 %collective-permute-start.11 = (bf16[128,3584]{1,0:T(8,128)(2,1)S(1)}, bf16[128,3584]{1,0:T(8,128)(2,1)S(1)}, u32[]{:S(2)}, u32[]{:S(2)}) collective-permute-start(bf16[128,3584]{1,0:T(8,128)(2,1)S(1)} %get-tuple-element.25), channel_id=1, source_target_pairs={{0,1},{1,0},{2,3},{3,2},{4,5},{5,4},{6,7},{7,6},{8,9},{9,8},{10,11... | collective-permute-start | bytes 2752520 | tf_op jit(solution)/shard_map/ppermute | solution.py:310
  35.3 5.5 %collective-permute-start.15 = (bf16[24,3584]{1,0:T(8,128)(2,1)S(1)}, bf16[24,3584]{1,0:T(8,128)(2,1)S(1)}, u32[]{:S(2)}, u32[]{:S(2)}) collective-permute-start(bf16[24,3584]{1,0:T(8,128)(2,1)S(1)} %get-tuple-element.31), channel_id=1, source_target_pairs={{0,4},{1,17},{2,6},{3,19},{4,0},{5,21},{6,2},{7,23},{8,12},{9,25},... | collective-permute-start | bytes 516104 | tf_op jit(solution)/shard_map/ppermute | solution.py:301
  37.1 5.4 %collective-permute-start.16 = (bf16[24,3584]{1,0:T(8,128)(2,1)S(1)}, bf16[24,3584]{1,0:T(8,128)(2,1)S(1)}, u32[]{:S(2)}, u32[]{:S(2)}) collective-permute-start(bf16[24,3584]{1,0:T(8,128)(2,1)S(1)} %get-tuple-element.32), channel_id=1, source_target_pairs={{0,2},{1,9},{2,0},{3,11},{4,6},{5,13},{6,4},{7,15},{8,10},{9,1},{1... | collective-permute-start | bytes 516104 | tf_op jit(solution)/shard_map/ppermute | solution.py:301
  37.1 7.1 %collective-permute-start.17 = (bf16[24,3584]{1,0:T(8,128)(2,1)S(1)}, bf16[24,3584]{1,0:T(8,128)(2,1)S(1)}, u32[]{:S(2)}, u32[]{:S(2)}) collective-permute-start(bf16[24,3584]{1,0:T(8,128)(2,1)S(1)} %get-tuple-element.33), channel_id=1, source_target_pairs={{0,6},{1,25},{2,4},{3,27},{4,2},{5,29},{6,0},{7,31},{8,14},{9,17},... | collective-permute-start | bytes 516104 | tf_op jit(solution)/shard_map/ppermute | solution.py:301
  38.8 6.9 %collective-permute-start.12 = (bf16[8,3584]{1,0:T(8,128)(2,1)S(1)}, bf16[8,3584]{1,0:T(8,128)(2,1)S(1)}, u32[]{:S(2)}, u32[]{:S(2)}) collective-permute-start(bf16[8,3584]{1,0:T(8,128)(2,1)S(1)} %get-tuple-element.27), channel_id=1, source_target_pairs={{0,4},{1,17},{2,6},{3,19},{4,0},{5,21},{6,2},{7,23},{8,12},{9,25},... | collective-permute-start | bytes 172040 | tf_op jit(solution)/shard_map/ppermute | solution.py:301
  40.6 8.1 %collective-permute-start.13 = (bf16[8,3584]{1,0:T(8,128)(2,1)S(1)}, bf16[8,3584]{1,0:T(8,128)(2,1)S(1)}, u32[]{:S(2)}, u32[]{:S(2)}) collective-permute-start(bf16[8,3584]{1,0:T(8,128)(2,1)S(1)} %get-tuple-element.28), channel_id=1, source_target_pairs={{0,2},{1,9},{2,0},{3,11},{4,6},{5,13},{6,4},{7,15},{8,10},{9,1},{1... | collective-permute-start | bytes 172040 | tf_op jit(solution)/shard_map/ppermute | solution.py:301
  40.7 8.0 %collective-permute-start.14 = (bf16[8,3584]{1,0:T(8,128)(2,1)S(1)}, bf16[8,3584]{1,0:T(8,128)(2,1)S(1)}, u32[]{:S(2)}, u32[]{:S(2)}) collective-permute-start(bf16[8,3584]{1,0:T(8,128)(2,1)S(1)} %get-tuple-element.29), channel_id=1, source_target_pairs={{0,6},{1,25},{2,4},{3,27},{4,2},{5,29},{6,0},{7,31},{8,14},{9,17},... | collective-permute-start | bytes 172040 | tf_op jit(solution)/shard_map/ppermute | solution.py:301
  44.2 6.0 %collective-permute-start.18 = (bf16[8,3584]{1,0:T(8,128)(2,1)S(1)}, bf16[8,3584]{1,0:T(8,128)(2,1)S(1)}, u32[]{:S(2)}, u32[]{:S(2)}) collective-permute-start(bf16[8,3584]{1,0:T(8,128)(2,1)S(1)} %get-tuple-element.34), channel_id=1, source_target_pairs={{0,24},{1,7},{2,26},{3,5},{4,28},{5,3},{6,30},{7,1},{8,16},{9,15},... | collective-permute-start | bytes 172040 | tf_op jit(solution)/shard_map/ppermute | solution.py:301
  44.6 5.7 %collective-permute-start.19 = (bf16[8,3584]{1,0:T(8,128)(2,1)S(1)}, bf16[8,3584]{1,0:T(8,128)(2,1)S(1)}, u32[]{:S(2)}, u32[]{:S(2)}) collective-permute-start(bf16[8,3584]{1,0:T(8,128)(2,1)S(1)} %get-tuple-element.35), channel_id=1, source_target_pairs={{0,16},{1,5},{2,18},{3,7},{4,20},{5,1},{6,22},{7,3},{8,24},{9,13},... | collective-permute-start | bytes 172040 | tf_op jit(solution)/shard_map/ppermute | solution.py:301
  45.7 5.2 %collective-permute-start.20 = (bf16[8,3584]{1,0:T(8,128)(2,1)S(1)}, bf16[8,3584]{1,0:T(8,128)(2,1)S(1)}, u32[]{:S(2)}, u32[]{:S(2)}) collective-permute-start(bf16[8,3584]{1,0:T(8,128)(2,1)S(1)} %get-tuple-element.36), channel_id=1, source_target_pairs={{0,8},{1,3},{2,10},{3,1},{4,12},{5,7},{6,14},{7,5},{8,0},{9,11},{1... | collective-permute-start | bytes 172040 | tf_op jit(solution)/shard_map/ppermute | solution.py:301

commit v7 on v6

--- a/solution.py
+++ b/solution.py
@@ -324,8 +324,7 @@
         (expert_gate[0], expert_up[0], expert_down[0]),
         block,
     )
-    pieces = [block] + [tie(far[k], token) for k in range(1, last)]
-    pieces += [join([ahead, far[last]], pieces)]
+    pieces = [block] + [tie(far[k], token) for k in range(1, last)] + [join([ahead, far[last]], [token])]
     pieces += [over_cores(p) for p in pieces]
     mine, other = expert_block(pieces, *weights)
 

time: 51.8 us -> 48.1 us (0.929)
  waiting for transfers between devices: 14.2 us -> 11.4 us
  starting transfers between devices: 26 us -> 25.2 us
    ppermute x16, waiting for transfers between devices: 10.8 us -> 7.67 us  [swap(): return lax.ppermute(value, ('ep', 'sub'), pairs)]
  transfers between devices with their start and end apart: 21 -> 21, of which waited for: 12 -> 9; matrix products, arithmetic and copies ran while one was open for 0% -> 0% of each run, Pallas kernels for 11% -> 12%
where the time goes in v7:
time: 48.1 us; the launch traced here: 47.9 us
  starting transfers between devices  25.2 us (52%)
  waiting for transfers between devices  11.4 us (24%)
  Pallas kernels  10.6 us (22%)
  between operations  0.69 us (1%)
    ppermute x16, starting transfers between devices, swap(): return lax.ppermute(value, ('ep', 'sub'), pairs)  24.2 us
    ppermute x16, waiting for transfers between devices, swap(): return lax.ppermute(value, ('ep', 'sub'), pairs)  7.67 us
    pallas_call x1, Pallas kernels, attend(): pl.pallas_call(attend_kernel, out_shape=(jax.ShapeDtypeStruct((rows, head...  5.58 us
    ppermute x5, waiting for transfers between devices, over_cores(): return lax.ppermute(value, 'sub', [(i, i ^ 1) for i in range(sub_count)])  3.76 us
    pallas_call x1, Pallas kernels, expert_block(): pl.pallas_call(functools.partial(expert_kernel, len(pieces)), out_shape=(...  3.03 us
    ppermute x5, starting transfers between devices, over_cores(): return lax.ppermute(value, 'sub', [(i, i ^ 1) for i in range(sub_count)])  1.01 us
    pallas_call x3, Pallas kernels, add(): pl.pallas_call(functools.partial(add_kernel, len(values), rows, sizes), o...  0.98 us
  transfers between devices with their start and end apart: 21, of which 9 were waited for; matrix products, arithmetic and copies ran while one was open for 0% of the time, Pallas kernels for 12%

profile of v7, /device:TPU:0, one launch (start us, length us, event | category | flops | bytes accessed | tf_op | source)
XLA Modules:
  0.0 47.9 jit_solution(8876418914468031170)
XLA Ops:
  0.6 0.9 %shard_map.104.refs_0_ = bf16[8,3712]{1,0:T(8,128)(2,1)S(1)} custom-call(bf16[8,3584]{1,0:T(8,128)(2,1)} %hidden_ref.1, s32[8,8]{1,0:T(8,128)} %routes_ref.1, f32[8,8]{1,0:T(8,128)} %scores_ref.1), custom_call_target="tpu_custom_call" | custom-call | flops 65536 | bytes 114688 | tf_op jit(solution)/shard_map/pallas_call | solution.py:133
  1.6 5.1 %collective-permute-start.2 = (bf16[8,3712]{1,0:T(8,128)(2,1)S(1)}, bf16[8,3712]{1,0:T(8,128)(2,1)S(1)}, u32[]{:S(2)}, u32[]{:S(2)}) collective-permute-start(bf16[8,3712]{1,0:T(8,128)(2,1)S(1)} %shard_map.104.refs_0_), channel_id=1, source_target_pairs={{0,24},{1,7},{2,26},{3,5},{4,28},{5,3},{6,30},{7,1},{8,16},{9,15},... | collective-permute-start | bytes 178184 | tf_op jit(solution)/shard_map/ppermute | solution.py:301
  6.7 0.0 collective-permute-start.1
  6.7 0.6 %collective-permute-start = (bf16[8,3712]{1,0:T(8,128)(2,1)S(1)}, bf16[8,3712]{1,0:T(8,128)(2,1)S(1)}, u32[]{:S(2)}, u32[]{:S(2)}) collective-permute-start(bf16[8,3712]{1,0:T(8,128)(2,1)S(1)} %shard_map.104.refs_0_), channel_id=1, source_target_pairs={{0,8},{1,3},{2,10},{3,1},{4,12},{5,7},{6,14},{7,5},{8,0},{9,11},{1... | collective-permute-start | bytes 178184 | tf_op jit(solution)/shard_map/ppermute | solution.py:301
  7.3 2.6 %collective-permute-start.5 = (bf16[8,3712]{1,0:T(8,128)(2,1)S(1)}, bf16[8,3712]{1,0:T(8,128)(2,1)S(1)}, u32[]{:S(2)}, u32[]{:S(2)}) collective-permute-start(bf16[8,3712]{1,0:T(8,128)(2,1)S(1)} %shard_map.104.refs_0_), channel_id=1, source_target_pairs={{0,6},{1,25},{2,4},{3,27},{4,2},{5,29},{6,0},{7,31},{8,14},{9,17},... | collective-permute-start | bytes 178184 | tf_op jit(solution)/shard_map/ppermute | solution.py:301
  9.9 0.0 collective-permute-done.2.refs_3_.refs_2_
  9.9 2.1 %collective-permute-done.1.refs_2_.refs_1_ = bf16[8,3712]{1,0:T(8,128)(2,1)S(1)} collective-permute-done((bf16[8,3712]{1,0:T(8,128)(2,1)S(1)}, bf16[8,3712]{1,0:T(8,128)(2,1)S(1)}, u32[]{:S(2)}, u32[]{:S(2)}) %collective-permute-start.1) | collective-permute-done | bytes 59424 | tf_op jit(solution)/shard_map/ppermute | solution.py:301
  12.0 0.0 collective-permute-done.refs_1_.refs_0_
  12.0 1.6 %collective-permute-start.3 = (bf16[32,3712]{1,0:T(8,128)(2,1)S(1)}, bf16[32,3712]{1,0:T(8,128)(2,1)S(1)}, u32[]{:S(2)}, u32[]{:S(2)}) collective-permute-start(bf16[32,3712]{1,0:T(8,128)(2,1)S(1)} %shard_map.105.after_ref.refs_0_), channel_id=1, source_target_pairs={{0,2},{1,9},{2,0},{3,11},{4,6},{5,13},{6,4},{7,15},{8,10},{9,1},{1... | collective-permute-start | bytes 712712 | tf_op jit(solution)/shard_map/ppermute | solution.py:301
  13.6 1.5 %collective-permute-start.4 = (bf16[32,3712]{1,0:T(8,128)(2,1)S(1)}, bf16[32,3712]{1,0:T(8,128)(2,1)S(1)}, u32[]{:S(2)}, u32[]{:S(2)}) collective-permute-start(bf16[32,3712]{1,0:T(8,128)(2,1)S(1)} %shard_map.105.after_ref.refs_0_), channel_id=1, source_target_pairs={{0,4},{1,17},{2,6},{3,19},{4,0},{5,21},{6,2},{7,23},{8,12},{9,25},... | collective-permute-start | bytes 712712 | tf_op jit(solution)/shard_map/ppermute | solution.py:301
  15.1 0.0 collective-permute-done.5.refs_3_.refs_0_
  15.1 0.5 %collective-permute-start.6 = (bf16[24,3712]{1,0:T(8,128)(2,1)S(1)}, bf16[24,3712]{1,0:T(8,128)(2,1)S(1)}, u32[]{:S(2)}, u32[]{:S(2)}) collective-permute-start(bf16[24,3712]{1,0:T(8,128)(2,1)S(1)} %shard_map.109), channel_id=1, source_target_pairs={{0,6},{1,25},{2,4},{3,27},{4,2},{5,29},{6,0},{7,31},{8,14},{9,17},... | collective-permute-start | bytes 534536 | tf_op jit(solution)/shard_map/ppermute | solution.py:301
  15.7 0.0 collective-permute-start.7
  15.7 5.6 %shard_map.106 = (bf16[4,128,512]{2,1,0:T(8,128)(2,1)}, bf16[3584,512]{1,0:T(8,128)(2,1)S(1)}, bf16[3584,512]{1,0:T(8,128)(2,1)S(1)}, bf16[512,3584]{1,0:T(8,128)(2,1)S(1)}, f32[8,128]{1,0:T(8,128)S(1)}) custom-call(s32[4]{0:T(128)} %lengths_hbm.1, bf16[4,576,128]{2,1,0:T(8,128)(2,1)} %bitcast.9, bf16[4,576,256]{2,1,0:T(8,128)(2,1)} %bitcast.8, ...), custom_call_target="tpu_custom_call" | custom-call | flops 301989888 | bytes 11010048 | tf_op jit(solution)/shard_map/pallas_call | solution.py:74
  21.3 0.3 collective-permute-done.6.refs_1_
  21.6 0.2 collective-permute-start.10
  21.9 0.0 collective-permute-done.3.value_ref
  21.9 0.3 collective-permute-start.8
  22.2 0.0 collective-permute-done.4.value_ref
  22.2 0.2 collective-permute-start.9
  22.4 0.0 collective-permute-done.7.refs_4_
  22.4 0.8 %collective-permute-done.10.refs_7_ = bf16[32,3712]{1,0:T(8,128)(2,1)S(1)} collective-permute-done((bf16[32,3712]{1,0:T(8,128)(2,1)S(1)}, bf16[32,3712]{1,0:T(8,128)(2,1)S(1)}, u32[]{:S(2)}, u32[]{:S(2)}) %collective-permute-start.10) | collective-permute-done | bytes 237600 | tf_op jit(solution)/shard_map/ppermute | solution.py:310
  23.2 0.3 collective-permute-done.8.refs_5_
  23.5 0.3 collective-permute-done.9.refs_6_
  23.9 3.0 %shard_map.111 = (bf16[128,3584]{1,0:T(8,128)(2,1)S(1)}, bf16[128,3584]{1,0:T(8,128)(2,1)S(1)}) custom-call(bf16[32,3712]{1,0:T(8,128)(2,1)S(1)} %shard_map.105.after_ref.refs_0_, bf16[32,3712]{1,0:T(8,128)(2,1)S(1)} %shard_map.107.refs_1_, bf16[32,3712]{1,0:T(8,128)(2,1)S(1)} %shard_map.108.refs_2_, bf16[32,3712]{1,0:T(8,128)(2,1)S(1)} %shard_map.110.refs_3_, ...), custom_call_target="tpu_custom_call" | custom-call | flops 2818572288 | bytes 3801088 | tf_op jit(solution)/shard_map/pallas_call | solution.py:239
  26.9 0.2 collective-permute-start.11
  27.2 2.3 %collective-permute-done.11.refs_1_ = bf16[128,3584]{1,0:T(8,128)(2,1)S(1)} collective-permute-done((bf16[128,3584]{1,0:T(8,128)(2,1)S(1)}, bf16[128,3584]{1,0:T(8,128)(2,1)S(1)}, u32[]{:S(2)}, u32[]{:S(2)}) %collective-permute-start.11) | collective-permute-done | bytes 917536 | tf_op jit(solution)/shard_map/ppermute | solution.py:310
  29.5 0.2 shard_map.112
  29.7 1.4 %collective-permute-start.15 = (bf16[24,3584]{1,0:T(8,128)(2,1)S(1)}, bf16[24,3584]{1,0:T(8,128)(2,1)S(1)}, u32[]{:S(2)}, u32[]{:S(2)}) collective-permute-start(bf16[24,3584]{1,0:T(8,128)(2,1)S(1)} %get-tuple-element.31), channel_id=1, source_target_pairs={{0,4},{1,17},{2,6},{3,19},{4,0},{5,21},{6,2},{7,23},{8,12},{9,25},... | collective-permute-start | bytes 516104 | tf_op jit(solution)/shard_map/ppermute | solution.py:301
  31.1 1.5 %collective-permute-start.16 = (bf16[24,3584]{1,0:T(8,128)(2,1)S(1)}, bf16[24,3584]{1,0:T(8,128)(2,1)S(1)}, u32[]{:S(2)}, u32[]{:S(2)}) collective-permute-start(bf16[24,3584]{1,0:T(8,128)(2,1)S(1)} %get-tuple-element.32), channel_id=1, source_target_pairs={{0,2},{1,9},{2,0},{3,11},{4,6},{5,13},{6,4},{7,15},{8,10},{9,1},{1... | collective-permute-start | bytes 516104 | tf_op jit(solution)/shard_map/ppermute | solution.py:301
  32.6 0.6 %collective-permute-start.17 = (bf16[24,3584]{1,0:T(8,128)(2,1)S(1)}, bf16[24,3584]{1,0:T(8,128)(2,1)S(1)}, u32[]{:S(2)}, u32[]{:S(2)}) collective-permute-start(bf16[24,3584]{1,0:T(8,128)(2,1)S(1)} %get-tuple-element.33), channel_id=1, source_target_pairs={{0,6},{1,25},{2,4},{3,27},{4,2},{5,29},{6,0},{7,31},{8,14},{9,17},... | collective-permute-start | bytes 516104 | tf_op jit(solution)/shard_map/ppermute | solution.py:301
  33.2 1.4 %collective-permute-start.12 = (bf16[8,3584]{1,0:T(8,128)(2,1)S(1)}, bf16[8,3584]{1,0:T(8,128)(2,1)S(1)}, u32[]{:S(2)}, u32[]{:S(2)}) collective-permute-start(bf16[8,3584]{1,0:T(8,128)(2,1)S(1)} %get-tuple-element.27), channel_id=1, source_target_pairs={{0,4},{1,17},{2,6},{3,19},{4,0},{5,21},{6,2},{7,23},{8,12},{9,25},... | collective-permute-start | bytes 172040 | tf_op jit(solution)/shard_map/ppermute | solution.py:301
  34.6 1.5 %collective-permute-start.13 = (bf16[8,3584]{1,0:T(8,128)(2,1)S(1)}, bf16[8,3584]{1,0:T(8,128)(2,1)S(1)}, u32[]{:S(2)}, u32[]{:S(2)}) collective-permute-start(bf16[8,3584]{1,0:T(8,128)(2,1)S(1)} %get-tuple-element.28), channel_id=1, source_target_pairs={{0,2},{1,9},{2,0},{3,11},{4,6},{5,13},{6,4},{7,15},{8,10},{9,1},{1... | collective-permute-start | bytes 172040 | tf_op jit(solution)/shard_map/ppermute | solution.py:301
  36.1 0.0 collective-permute-done.15.refs_1_
  36.1 1.3 %collective-permute-start.14 = (bf16[8,3584]{1,0:T(8,128)(2,1)S(1)}, bf16[8,3584]{1,0:T(8,128)(2,1)S(1)}, u32[]{:S(2)}, u32[]{:S(2)}) collective-permute-start(bf16[8,3584]{1,0:T(8,128)(2,1)S(1)} %get-tuple-element.29), channel_id=1, source_target_pairs={{0,6},{1,25},{2,4},{3,27},{4,2},{5,29},{6,0},{7,31},{8,14},{9,17},... | collective-permute-start | bytes 172040 | tf_op jit(solution)/shard_map/ppermute | solution.py:301
  37.5 0.0 collective-permute-done.16.refs_2_
  37.5 1.6 %collective-permute-done.17.refs_3_ = bf16[24,3584]{1,0:T(8,128)(2,1)S(1)} collective-permute-done((bf16[24,3584]{1,0:T(8,128)(2,1)S(1)}, bf16[24,3584]{1,0:T(8,128)(2,1)S(1)}, u32[]{:S(2)}, u32[]{:S(2)}) %collective-permute-start.17) | collective-permute-done | bytes 172064 | tf_op jit(solution)/shard_map/ppermute | solution.py:301
  39.0 0.1 shard_map.113
  39.1 2.5 %collective-permute-start.18 = (bf16[8,3584]{1,0:T(8,128)(2,1)S(1)}, bf16[8,3584]{1,0:T(8,128)(2,1)S(1)}, u32[]{:S(2)}, u32[]{:S(2)}) collective-permute-start(bf16[8,3584]{1,0:T(8,128)(2,1)S(1)} %get-tuple-element.34), channel_id=1, source_target_pairs={{0,24},{1,7},{2,26},{3,5},{4,28},{5,3},{6,30},{7,1},{8,16},{9,15},... | collective-permute-start | bytes 172040 | tf_op jit(solution)/shard_map/ppermute | solution.py:301
  41.6 0.0 collective-permute-start.19
  41.6 0.0 collective-permute-done.12.refs_1_
  41.6 2.0 %collective-permute-start.20 = (bf16[8,3584]{1,0:T(8,128)(2,1)S(1)}, bf16[8,3584]{1,0:T(8,128)(2,1)S(1)}, u32[]{:S(2)}, u32[]{:S(2)}) collective-permute-start(bf16[8,3584]{1,0:T(8,128)(2,1)S(1)} %get-tuple-element.36), channel_id=1, source_target_pairs={{0,8},{1,3},{2,10},{3,1},{4,12},{5,7},{6,14},{7,5},{8,0},{9,11},{1... | collective-permute-start | bytes 172040 | tf_op jit(solution)/shard_map/ppermute | solution.py:301
  43.6 0.0 collective-permute-done.13.refs_2_
  43.6 0.0 collective-permute-done.14.refs_3_
  43.6 1.6 %collective-permute-done.18.refs_4_ = bf16[8,3584]{1,0:T(8,128)(2,1)S(1)} collective-permute-done((bf16[8,3584]{1,0:T(8,128)(2,1)S(1)}, bf16[8,3584]{1,0:T(8,128)(2,1)S(1)}, u32[]{:S(2)}, u32[]{:S(2)}) %collective-permute-start.18) | collective-permute-done | bytes 57376 | tf_op jit(solution)/shard_map/ppermute | solution.py:301
  45.2 2.1 %collective-permute-done.19.refs_5_ = bf16[8,3584]{1,0:T(8,128)(2,1)S(1)} collective-permute-done((bf16[8,3584]{1,0:T(8,128)(2,1)S(1)}, bf16[8,3584]{1,0:T(8,128)(2,1)S(1)}, u32[]{:S(2)}, u32[]{:S(2)}) %collective-permute-start.19) | collective-permute-done | bytes 57376 | tf_op jit(solution)/shard_map/ppermute | solution.py:301
  47.2 0.0 collective-permute-done.20.refs_6_
  47.2 0.7 %shard_map.114 = bf16[8,3584]{1,0:T(8,128)(2,1)} custom-call(bf16[8,3584]{1,0:T(8,128)(2,1)S(1)} %get-tuple-element.26.refs_0_, bf16[8,3584]{1,0:T(8,128)(2,1)S(1)} %collective-permute-done.12.refs_1_, bf16[8,3584]{1,0:T(8,128)(2,1)S(1)} %collective-permute-done.13.refs_2_, bf16[8,3584]{1,0:T(8,128)(2,1)S(1)} %collective-permute-done.14.refs_3_, ...), custom_call_target="tpu_custom_call" | custom-call | flops 200704 | bytes 401408 | tf_op jit(solution)/shard_map/pallas_call | solution.py:269
  (5 shorter events, 0.0 us)
Async XLA Ops:
  1.6 8.4 %collective-permute-start.2 = (bf16[8,3712]{1,0:T(8,128)(2,1)S(1)}, bf16[8,3712]{1,0:T(8,128)(2,1)S(1)}, u32[]{:S(2)}, u32[]{:S(2)}) collective-permute-start(bf16[8,3712]{1,0:T(8,128)(2,1)S(1)} %shard_map.104.refs_0_), channel_id=1, source_target_pairs={{0,24},{1,7},{2,26},{3,5},{4,28},{5,3},{6,30},{7,1},{8,16},{9,15},... | collective-permute-start | bytes 178184 | tf_op jit(solution)/shard_map/ppermute | solution.py:301
  6.7 5.3 %collective-permute-start.1 = (bf16[8,3712]{1,0:T(8,128)(2,1)S(1)}, bf16[8,3712]{1,0:T(8,128)(2,1)S(1)}, u32[]{:S(2)}, u32[]{:S(2)}) collective-permute-start(bf16[8,3712]{1,0:T(8,128)(2,1)S(1)} %shard_map.104.refs_0_), channel_id=1, source_target_pairs={{0,16},{1,5},{2,18},{3,7},{4,20},{5,1},{6,22},{7,3},{8,24},{9,13},... | collective-permute-start | bytes 178184 | tf_op jit(solution)/shard_map/ppermute | solution.py:301
  6.7 5.3 %collective-permute-start = (bf16[8,3712]{1,0:T(8,128)(2,1)S(1)}, bf16[8,3712]{1,0:T(8,128)(2,1)S(1)}, u32[]{:S(2)}, u32[]{:S(2)}) collective-permute-start(bf16[8,3712]{1,0:T(8,128)(2,1)S(1)} %shard_map.104.refs_0_), channel_id=1, source_target_pairs={{0,8},{1,3},{2,10},{3,1},{4,12},{5,7},{6,14},{7,5},{8,0},{9,11},{1... | collective-permute-start | bytes 178184 | tf_op jit(solution)/shard_map/ppermute | solution.py:301
  7.3 7.8 %collective-permute-start.5 = (bf16[8,3712]{1,0:T(8,128)(2,1)S(1)}, bf16[8,3712]{1,0:T(8,128)(2,1)S(1)}, u32[]{:S(2)}, u32[]{:S(2)}) collective-permute-start(bf16[8,3712]{1,0:T(8,128)(2,1)S(1)} %shard_map.104.refs_0_), channel_id=1, source_target_pairs={{0,6},{1,25},{2,4},{3,27},{4,2},{5,29},{6,0},{7,31},{8,14},{9,17},... | collective-permute-start | bytes 178184 | tf_op jit(solution)/shard_map/ppermute | solution.py:301
  12.0 9.8 %collective-permute-start.3 = (bf16[32,3712]{1,0:T(8,128)(2,1)S(1)}, bf16[32,3712]{1,0:T(8,128)(2,1)S(1)}, u32[]{:S(2)}, u32[]{:S(2)}) collective-permute-start(bf16[32,3712]{1,0:T(8,128)(2,1)S(1)} %shard_map.105.after_ref.refs_0_), channel_id=1, source_target_pairs={{0,2},{1,9},{2,0},{3,11},{4,6},{5,13},{6,4},{7,15},{8,10},{9,1},{1... | collective-permute-start | bytes 712712 | tf_op jit(solution)/shard_map/ppermute | solution.py:301
  13.6 8.6 %collective-permute-start.4 = (bf16[32,3712]{1,0:T(8,128)(2,1)S(1)}, bf16[32,3712]{1,0:T(8,128)(2,1)S(1)}, u32[]{:S(2)}, u32[]{:S(2)}) collective-permute-start(bf16[32,3712]{1,0:T(8,128)(2,1)S(1)} %shard_map.105.after_ref.refs_0_), channel_id=1, source_target_pairs={{0,4},{1,17},{2,6},{3,19},{4,0},{5,21},{6,2},{7,23},{8,12},{9,25},... | collective-permute-start | bytes 712712 | tf_op jit(solution)/shard_map/ppermute | solution.py:301
  15.1 6.5 %collective-permute-start.6 = (bf16[24,3712]{1,0:T(8,128)(2,1)S(1)}, bf16[24,3712]{1,0:T(8,128)(2,1)S(1)}, u32[]{:S(2)}, u32[]{:S(2)}) collective-permute-start(bf16[24,3712]{1,0:T(8,128)(2,1)S(1)} %shard_map.109), channel_id=1, source_target_pairs={{0,6},{1,25},{2,4},{3,27},{4,2},{5,29},{6,0},{7,31},{8,14},{9,17},... | collective-permute-start | bytes 534536 | tf_op jit(solution)/shard_map/ppermute | solution.py:301
  15.7 6.7 %collective-permute-start.7 = (bf16[32,3712]{1,0:T(8,128)(2,1)S(1)}, bf16[32,3712]{1,0:T(8,128)(2,1)S(1)}, u32[]{:S(2)}, u32[]{:S(2)}) collective-permute-start(bf16[32,3712]{1,0:T(8,128)(2,1)S(1)} %shard_map.105.after_ref.refs_0_), channel_id=1, source_target_pairs={{0,1},{1,0},{2,3},{3,2},{4,5},{5,4},{6,7},{7,6},{8,9},{9,8},{10,11... | collective-permute-start | bytes 712712 | tf_op jit(solution)/shard_map/ppermute | solution.py:310
  21.6 1.6 %collective-permute-start.10 = (bf16[32,3712]{1,0:T(8,128)(2,1)S(1)}, bf16[32,3712]{1,0:T(8,128)(2,1)S(1)}, u32[]{:S(2)}, u32[]{:S(2)}) collective-permute-start(bf16[32,3712]{1,0:T(8,128)(2,1)S(1)} %shard_map.110.refs_3_), channel_id=1, source_target_pairs={{0,1},{1,0},{2,3},{3,2},{4,5},{5,4},{6,7},{7,6},{8,9},{9,8},{10,11... | collective-permute-start | bytes 712712 | tf_op jit(solution)/shard_map/ppermute | solution.py:310
  21.9 1.7 %collective-permute-start.8 = (bf16[32,3712]{1,0:T(8,128)(2,1)S(1)}, bf16[32,3712]{1,0:T(8,128)(2,1)S(1)}, u32[]{:S(2)}, u32[]{:S(2)}) collective-permute-start(bf16[32,3712]{1,0:T(8,128)(2,1)S(1)} %shard_map.107.refs_1_), channel_id=1, source_target_pairs={{0,1},{1,0},{2,3},{3,2},{4,5},{5,4},{6,7},{7,6},{8,9},{9,8},{10,11... | collective-permute-start | bytes 712712 | tf_op jit(solution)/shard_map/ppermute | solution.py:310
  22.2 1.7 %collective-permute-start.9 = (bf16[32,3712]{1,0:T(8,128)(2,1)S(1)}, bf16[32,3712]{1,0:T(8,128)(2,1)S(1)}, u32[]{:S(2)}, u32[]{:S(2)}) collective-permute-start(bf16[32,3712]{1,0:T(8,128)(2,1)S(1)} %shard_map.108.refs_2_), channel_id=1, source_target_pairs={{0,1},{1,0},{2,3},{3,2},{4,5},{5,4},{6,7},{7,6},{8,9},{9,8},{10,11... | collective-permute-start | bytes 712712 | tf_op jit(solution)/shard_map/ppermute | solution.py:310
  26.9 2.5 %collective-permute-start.11 = (bf16[128,3584]{1,0:T(8,128)(2,1)S(1)}, bf16[128,3584]{1,0:T(8,128)(2,1)S(1)}, u32[]{:S(2)}, u32[]{:S(2)}) collective-permute-start(bf16[128,3584]{1,0:T(8,128)(2,1)S(1)} %get-tuple-element.25), channel_id=1, source_target_pairs={{0,1},{1,0},{2,3},{3,2},{4,5},{5,4},{6,7},{7,6},{8,9},{9,8},{10,11... | collective-permute-start | bytes 2752520 | tf_op jit(solution)/shard_map/ppermute | solution.py:310
  29.7 6.4 %collective-permute-start.15 = (bf16[24,3584]{1,0:T(8,128)(2,1)S(1)}, bf16[24,3584]{1,0:T(8,128)(2,1)S(1)}, u32[]{:S(2)}, u32[]{:S(2)}) collective-permute-start(bf16[24,3584]{1,0:T(8,128)(2,1)S(1)} %get-tuple-element.31), channel_id=1, source_target_pairs={{0,4},{1,17},{2,6},{3,19},{4,0},{5,21},{6,2},{7,23},{8,12},{9,25},... | collective-permute-start | bytes 516104 | tf_op jit(solution)/shard_map/ppermute | solution.py:301
  31.1 6.3 %collective-permute-start.16 = (bf16[24,3584]{1,0:T(8,128)(2,1)S(1)}, bf16[24,3584]{1,0:T(8,128)(2,1)S(1)}, u32[]{:S(2)}, u32[]{:S(2)}) collective-permute-start(bf16[24,3584]{1,0:T(8,128)(2,1)S(1)} %get-tuple-element.32), channel_id=1, source_target_pairs={{0,2},{1,9},{2,0},{3,11},{4,6},{5,13},{6,4},{7,15},{8,10},{9,1},{1... | collective-permute-start | bytes 516104 | tf_op jit(solution)/shard_map/ppermute | solution.py:301
  32.6 6.4 %collective-permute-start.17 = (bf16[24,3584]{1,0:T(8,128)(2,1)S(1)}, bf16[24,3584]{1,0:T(8,128)(2,1)S(1)}, u32[]{:S(2)}, u32[]{:S(2)}) collective-permute-start(bf16[24,3584]{1,0:T(8,128)(2,1)S(1)} %get-tuple-element.33), channel_id=1, source_target_pairs={{0,6},{1,25},{2,4},{3,27},{4,2},{5,29},{6,0},{7,31},{8,14},{9,17},... | collective-permute-start | bytes 516104 | tf_op jit(solution)/shard_map/ppermute | solution.py:301
  33.2 8.4 %collective-permute-start.12 = (bf16[8,3584]{1,0:T(8,128)(2,1)S(1)}, bf16[8,3584]{1,0:T(8,128)(2,1)S(1)}, u32[]{:S(2)}, u32[]{:S(2)}) collective-permute-start(bf16[8,3584]{1,0:T(8,128)(2,1)S(1)} %get-tuple-element.27), channel_id=1, source_target_pairs={{0,4},{1,17},{2,6},{3,19},{4,0},{5,21},{6,2},{7,23},{8,12},{9,25},... | collective-permute-start | bytes 172040 | tf_op jit(solution)/shard_map/ppermute | solution.py:301
  34.6 9.0 %collective-permute-start.13 = (bf16[8,3584]{1,0:T(8,128)(2,1)S(1)}, bf16[8,3584]{1,0:T(8,128)(2,1)S(1)}, u32[]{:S(2)}, u32[]{:S(2)}) collective-permute-start(bf16[8,3584]{1,0:T(8,128)(2,1)S(1)} %get-tuple-element.28), channel_id=1, source_target_pairs={{0,2},{1,9},{2,0},{3,11},{4,6},{5,13},{6,4},{7,15},{8,10},{9,1},{1... | collective-permute-start | bytes 172040 | tf_op jit(solution)/shard_map/ppermute | solution.py:301
  36.1 7.5 %collective-permute-start.14 = (bf16[8,3584]{1,0:T(8,128)(2,1)S(1)}, bf16[8,3584]{1,0:T(8,128)(2,1)S(1)}, u32[]{:S(2)}, u32[]{:S(2)}) collective-permute-start(bf16[8,3584]{1,0:T(8,128)(2,1)S(1)} %get-tuple-element.29), channel_id=1, source_target_pairs={{0,6},{1,25},{2,4},{3,27},{4,2},{5,29},{6,0},{7,31},{8,14},{9,17},... | collective-permute-start | bytes 172040 | tf_op jit(solution)/shard_map/ppermute | solution.py:301
  39.1 6.0 %collective-permute-start.18 = (bf16[8,3584]{1,0:T(8,128)(2,1)S(1)}, bf16[8,3584]{1,0:T(8,128)(2,1)S(1)}, u32[]{:S(2)}, u32[]{:S(2)}) collective-permute-start(bf16[8,3584]{1,0:T(8,128)(2,1)S(1)} %get-tuple-element.34), channel_id=1, source_target_pairs={{0,24},{1,7},{2,26},{3,5},{4,28},{5,3},{6,30},{7,1},{8,16},{9,15},... | collective-permute-start | bytes 172040 | tf_op jit(solution)/shard_map/ppermute | solution.py:301
  41.6 5.6 %collective-permute-start.19 = (bf16[8,3584]{1,0:T(8,128)(2,1)S(1)}, bf16[8,3584]{1,0:T(8,128)(2,1)S(1)}, u32[]{:S(2)}, u32[]{:S(2)}) collective-permute-start(bf16[8,3584]{1,0:T(8,128)(2,1)S(1)} %get-tuple-element.35), channel_id=1, source_target_pairs={{0,16},{1,5},{2,18},{3,7},{4,20},{5,1},{6,22},{7,3},{8,24},{9,13},... | collective-permute-start | bytes 172040 | tf_op jit(solution)/shard_map/ppermute | solution.py:301
  41.6 5.6 %collective-permute-start.20 = (bf16[8,3584]{1,0:T(8,128)(2,1)S(1)}, bf16[8,3584]{1,0:T(8,128)(2,1)S(1)}, u32[]{:S(2)}, u32[]{:S(2)}) collective-permute-start(bf16[8,3584]{1,0:T(8,128)(2,1)S(1)} %get-tuple-element.36), channel_id=1, source_target_pairs={{0,8},{1,3},{2,10},{3,1},{4,12},{5,7},{6,14},{7,5},{8,0},{9,11},{1... | collective-permute-start | bytes 172040 | tf_op jit(solution)/shard_map/ppermute | solution.py:301

commit v8 on v7

--- a/solution.py
+++ b/solution.py
@@ -35,11 +35,11 @@
 
 
 def attend_kernel(
-    lengths_hbm, query_hbm, cache_hbm, gate_hbm, up_hbm, down_hbm, after_ref,
-    out_ref, gate_ref, up_ref, down_ref, token_ref, lengths_ref, query_ref, cache_ref, sems,
+    lengths_hbm, query_hbm, cache_hbm, gate_hbm, up_hbm, after_ref,
+    out_ref, gate_ref, up_ref, token_ref, lengths_ref, query_ref, cache_ref, sems,
 ):
     pairs = [(lengths_hbm, lengths_ref), (query_hbm, query_ref), (cache_hbm, cache_ref)]
-    for source, target in ((gate_hbm, gate_ref), (up_hbm, up_ref), (down_hbm, down_ref)):
+    for source, target in ((gate_hbm, gate_ref), (up_hbm, up_ref)):
         rows = source.shape[0] // FETCHES
         pairs += [(source.at[pl.ds(i * rows, rows)], target.at[pl.ds(i * rows, rows)]) for i in range(FETCHES)]
     copies = [pltpu.make_async_copy(s, t, sems.at[i]) for i, (s, t) in enumerate(pairs)]
@@ -78,13 +78,13 @@
             *(in_vmem(w.shape, w.dtype) for w in weights),
             in_vmem((8, LANES), jnp.float32),
         ),
-        in_specs=[HBM] * 6 + [ANY],
-        out_specs=(VMEM,) * 5,
+        in_specs=[HBM] * 5 + [ANY],
+        out_specs=(VMEM,) * 4,
         scratch_shapes=[
             pltpu.SMEM(cache_lengths.shape, jnp.int32),
             pltpu.VMEM(query.shape, query.dtype),
             pltpu.VMEM(cache.shape, cache.dtype),
-            pltpu.SemaphoreType.DMA((3 + 3 * FETCHES,)),
+            pltpu.SemaphoreType.DMA((3 + 2 * FETCHES,)),
         ],
         compiler_params=pltpu.CompilerParams(vmem_limit_bytes=12 << 20),
         cost_estimate=pl.CostEstimate(
@@ -182,7 +182,9 @@
 
 def expert_kernel(count, *refs):
     pieces = refs[:count]
-    gate_ref, up_ref, down_ref, mine_ref, other_ref, rows_ref, hidden_ref = refs[count:]
+    gate_ref, up_ref, down_hbm, mine_ref, other_ref, rows_ref, hidden_ref, down_ref, sem = refs[count:]
+    fetch = pltpu.make_async_copy(down_hbm, down_ref, sem)
+    fetch.start()
     total, _ = rows_ref.shape
     model_width, units = gate_ref.shape
     lanes = rows_ref.shape[1] - model_width
@@ -225,10 +227,12 @@
     step = 512
     if total == block:
         units_of(slice(0, block))
+        fetch.wait()
         for c in range(model_width // step):
             results_of(slice(c * step, (c + 1) * step))
     else:
         pl.loop(0, total // block)(lambda i: units_of(pl.ds(pl.multiple_of(i * block, block), block)))
+        fetch.wait()
         pl.loop(0, model_width // step)(lambda c: results_of(pl.ds(pl.multiple_of(c * step, step), step)))
 
 
@@ -239,16 +243,21 @@
     return pl.pallas_call(
         functools.partial(expert_kernel, len(pieces)),
         out_shape=(out, out),
-        in_specs=[VMEM] * (len(pieces) + 3),
+        in_specs=[VMEM] * (len(pieces) + 2) + [HBM],
         out_specs=(VMEM, VMEM),
-        scratch_shapes=[pltpu.VMEM((total, width), jnp.bfloat16), pltpu.VMEM((total, units), jnp.bfloat16)],
-        compiler_params=pltpu.CompilerParams(vmem_limit_bytes=(8 << 20) + 4 * total * units + 2 * total * width),
+        scratch_shapes=[
+            pltpu.VMEM((total, width), jnp.bfloat16),
+            pltpu.VMEM((total, units), jnp.bfloat16),
+            pltpu.VMEM(expert_down.shape, expert_down.dtype),
+            pltpu.SemaphoreType.DMA,
+        ],
+        compiler_params=pltpu.CompilerParams(vmem_limit_bytes=(8 << 20) + 4 * total * units + 2 * total * width + 2 * expert_down.size),
         cost_estimate=pl.CostEstimate(
             flops=6 * total * model_width * units,
             bytes_accessed=4 * total * width,
             transcendentals=total * units,
         ),
-    )(*(held(p) for p in pieces), *(held(w) for w in (expert_gate, expert_up, expert_down)))
+    )(*(held(p) for p in pieces), held(expert_gate), held(expert_up), stored(expert_down))
 
 
 def add_kernel(count, rows, sizes, *refs):
@@ -321,12 +330,12 @@
         query_latent,
         latent_cache,
         cache_lengths,
-        (expert_gate[0], expert_up[0], expert_down[0]),
+        (expert_gate[0], expert_up[0]),
         block,
     )
     pieces = [block] + [tie(far[k], token) for k in range(1, last)] + [join([ahead, far[last]], [token])]
     pieces += [over_cores(p) for p in pieces]
-    mine, other = expert_block(pieces, *weights)
+    mine, other = expert_block(pieces, *weights, expert_down[0])
 
     size = (outer - 1) * tok_rows
     kept, column, *parts = add([mine, over_cores(other)], [(0, mine.shape[0])] * 2, [tok_rows, size] * inner)

time: 48.1 us -> 48.9 us (1.017)
  starting transfers between devices: 25.2 us -> 24.2 us
  Pallas kernels: 10.6 us -> 11.5 us
  waiting for transfers between devices: 11.4 us -> 12.2 us
    pallas_call x1, Pallas kernels: 3.03 us -> 5.02 us  [expert_block(): pl.pallas_call(functools.partial(expert_kernel, len(pieces)), out_shape=(...]
    pallas_call x1, Pallas kernels: 5.58 us -> 4.52 us  [attend(): pl.pallas_call(attend_kernel, out_shape=(jax.ShapeDtypeStruct((rows, head...]
    ppermute x16, starting transfers between devices: 24.2 us -> 23.3 us  [swap(): return lax.ppermute(value, ('ep', 'sub'), pairs)]
    ppermute x16, waiting for transfers between devices: 7.67 us -> 8.36 us  [swap(): return lax.ppermute(value, ('ep', 'sub'), pairs)]
  transfers between devices with their start and end apart: 21 -> 21, of which waited for: 9 -> 11; matrix products, arithmetic and copies ran while one was open for 0% -> 0% of each run, Pallas kernels for 12% -> 10%
where the time goes in v8:
time: 48.9 us; the launch traced here: 48.7 us
  starting transfers between devices  24.2 us (49%)
  waiting for transfers between devices  12.2 us (25%)
  Pallas kernels  11.5 us (24%)
  between operations  0.72 us (1%)
    ppermute x16, starting transfers between devices, swap(): return lax.ppermute(value, ('ep', 'sub'), pairs)  23.3 us
    ppermute x16, waiting for transfers between devices, swap(): return lax.ppermute(value, ('ep', 'sub'), pairs)  8.36 us
    pallas_call x1, Pallas kernels, expert_block(): pl.pallas_call(functools.partial(expert_kernel, len(pieces)), out_shape=(...  5.02 us
    pallas_call x1, Pallas kernels, attend(): pl.pallas_call(attend_kernel, out_shape=(jax.ShapeDtypeStruct((rows, head...  4.52 us
    ppermute x5, waiting for transfers between devices, over_cores(): return lax.ppermute(value, 'sub', [(i, i ^ 1) for i in range(sub_count)])  3.86 us
  transfers between devices with their start and end apart: 21, of which 11 were waited for; matrix products, arithmetic and copies ran while one was open for 0% of the time, Pallas kernels for 10%

profile of v8, /device:TPU:0, one launch (start us, length us, event | category | flops | bytes accessed | tf_op | source)
XLA Modules:
  0.0 48.7 jit_solution(16182044403374229748)
XLA Ops:
  0.6 0.9 %shard_map.104.refs_0_ = bf16[8,3712]{1,0:T(8,128)(2,1)S(1)} custom-call(bf16[8,3584]{1,0:T(8,128)(2,1)} %hidden_ref.1, s32[8,8]{1,0:T(8,128)} %routes_ref.1, f32[8,8]{1,0:T(8,128)} %scores_ref.1), custom_call_target="tpu_custom_call" | custom-call | flops 65536 | bytes 114688 | tf_op jit(solution)/shard_map/pallas_call | solution.py:133
  1.6 5.1 %collective-permute-start.2 = (bf16[8,3712]{1,0:T(8,128)(2,1)S(1)}, bf16[8,3712]{1,0:T(8,128)(2,1)S(1)}, u32[]{:S(2)}, u32[]{:S(2)}) collective-permute-start(bf16[8,3712]{1,0:T(8,128)(2,1)S(1)} %shard_map.104.refs_0_), channel_id=1, source_target_pairs={{0,24},{1,7},{2,26},{3,5},{4,28},{5,3},{6,30},{7,1},{8,16},{9,15},... | collective-permute-start | bytes 178184 | tf_op jit(solution)/shard_map/ppermute | solution.py:310
  6.7 0.0 collective-permute-start.1
  6.7 0.6 %collective-permute-start = (bf16[8,3712]{1,0:T(8,128)(2,1)S(1)}, bf16[8,3712]{1,0:T(8,128)(2,1)S(1)}, u32[]{:S(2)}, u32[]{:S(2)}) collective-permute-start(bf16[8,3712]{1,0:T(8,128)(2,1)S(1)} %shard_map.104.refs_0_), channel_id=1, source_target_pairs={{0,8},{1,3},{2,10},{3,1},{4,12},{5,7},{6,14},{7,5},{8,0},{9,11},{1... | collective-permute-start | bytes 178184 | tf_op jit(solution)/shard_map/ppermute | solution.py:310
  7.3 2.6 %collective-permute-start.5 = (bf16[8,3712]{1,0:T(8,128)(2,1)S(1)}, bf16[8,3712]{1,0:T(8,128)(2,1)S(1)}, u32[]{:S(2)}, u32[]{:S(2)}) collective-permute-start(bf16[8,3712]{1,0:T(8,128)(2,1)S(1)} %shard_map.104.refs_0_), channel_id=1, source_target_pairs={{0,6},{1,25},{2,4},{3,27},{4,2},{5,29},{6,0},{7,31},{8,14},{9,17},... | collective-permute-start | bytes 178184 | tf_op jit(solution)/shard_map/ppermute | solution.py:310
  9.9 0.0 collective-permute-done.2.refs_3_.refs_2_
  9.9 2.1 %collective-permute-done.1.refs_2_.refs_1_ = bf16[8,3712]{1,0:T(8,128)(2,1)S(1)} collective-permute-done((bf16[8,3712]{1,0:T(8,128)(2,1)S(1)}, bf16[8,3712]{1,0:T(8,128)(2,1)S(1)}, u32[]{:S(2)}, u32[]{:S(2)}) %collective-permute-start.1) | collective-permute-done | bytes 59424 | tf_op jit(solution)/shard_map/ppermute | solution.py:310
  12.0 0.0 collective-permute-done.refs_1_.refs_0_
  12.0 1.6 %collective-permute-start.3 = (bf16[32,3712]{1,0:T(8,128)(2,1)S(1)}, bf16[32,3712]{1,0:T(8,128)(2,1)S(1)}, u32[]{:S(2)}, u32[]{:S(2)}) collective-permute-start(bf16[32,3712]{1,0:T(8,128)(2,1)S(1)} %shard_map.105.after_ref.refs_0_), channel_id=1, source_target_pairs={{0,2},{1,9},{2,0},{3,11},{4,6},{5,13},{6,4},{7,15},{8,10},{9,1},{1... | collective-permute-start | bytes 712712 | tf_op jit(solution)/shard_map/ppermute | solution.py:310
  13.6 1.5 %collective-permute-start.4 = (bf16[32,3712]{1,0:T(8,128)(2,1)S(1)}, bf16[32,3712]{1,0:T(8,128)(2,1)S(1)}, u32[]{:S(2)}, u32[]{:S(2)}) collective-permute-start(bf16[32,3712]{1,0:T(8,128)(2,1)S(1)} %shard_map.105.after_ref.refs_0_), channel_id=1, source_target_pairs={{0,4},{1,17},{2,6},{3,19},{4,0},{5,21},{6,2},{7,23},{8,12},{9,25},... | collective-permute-start | bytes 712712 | tf_op jit(solution)/shard_map/ppermute | solution.py:310
  15.1 0.0 collective-permute-done.5.refs_3_.refs_0_
  15.1 0.5 %collective-permute-start.6 = (bf16[24,3712]{1,0:T(8,128)(2,1)S(1)}, bf16[24,3712]{1,0:T(8,128)(2,1)S(1)}, u32[]{:S(2)}, u32[]{:S(2)}) collective-permute-start(bf16[24,3712]{1,0:T(8,128)(2,1)S(1)} %shard_map.109), channel_id=1, source_target_pairs={{0,6},{1,25},{2,4},{3,27},{4,2},{5,29},{6,0},{7,31},{8,14},{9,17},... | collective-permute-start | bytes 534536 | tf_op jit(solution)/shard_map/ppermute | solution.py:310
  15.7 0.0 collective-permute-start.7
  15.7 4.5 %shard_map.106 = (bf16[4,128,512]{2,1,0:T(8,128)(2,1)}, bf16[3584,512]{1,0:T(8,128)(2,1)S(1)}, bf16[3584,512]{1,0:T(8,128)(2,1)S(1)}, f32[8,128]{1,0:T(8,128)S(1)}) custom-call(s32[4]{0:T(128)} %lengths_hbm.1, bf16[4,576,128]{2,1,0:T(8,128)(2,1)} %bitcast.9, bf16[4,576,256]{2,1,0:T(8,128)(2,1)} %bitcast.8, bf16[3584,512]{1,0:T(8,128)(2,1)} %bitcast.5, ...), custom_call_target="tpu_custom_call" | custom-call | flops 301989888 | bytes 7340032 | tf_op jit(solution)/shard_map/pallas_call | solution.py:74
  20.2 1.4 %collective-permute-done.6.refs_1_ = bf16[24,3712]{1,0:T(8,128)(2,1)S(1)} collective-permute-done((bf16[24,3712]{1,0:T(8,128)(2,1)S(1)}, bf16[24,3712]{1,0:T(8,128)(2,1)S(1)}, u32[]{:S(2)}, u32[]{:S(2)}) %collective-permute-start.6) | collective-permute-done | bytes 178208 | tf_op jit(solution)/shard_map/ppermute | solution.py:310
  21.6 0.1 collective-permute-start.10
  21.7 0.0 collective-permute-done.3.value_ref
  21.7 0.5 collective-permute-start.8
  22.2 0.0 collective-permute-done.4.value_ref
  22.2 0.1 collective-permute-start.9
  22.3 0.0 collective-permute-done.7.refs_4_
  22.3 0.9 %collective-permute-done.10.refs_7_ = bf16[32,3712]{1,0:T(8,128)(2,1)S(1)} collective-permute-done((bf16[32,3712]{1,0:T(8,128)(2,1)S(1)}, bf16[32,3712]{1,0:T(8,128)(2,1)S(1)}, u32[]{:S(2)}, u32[]{:S(2)}) %collective-permute-start.10) | collective-permute-done | bytes 237600 | tf_op jit(solution)/shard_map/ppermute | solution.py:319
  23.2 0.3 collective-permute-done.8.refs_5_
  23.5 0.3 collective-permute-done.9.refs_6_
  23.9 5.0 %shard_map.111 = (bf16[128,3584]{1,0:T(8,128)(2,1)S(1)}, bf16[128,3584]{1,0:T(8,128)(2,1)S(1)}) custom-call(bf16[32,3712]{1,0:T(8,128)(2,1)S(1)} %shard_map.105.after_ref.refs_0_, bf16[32,3712]{1,0:T(8,128)(2,1)S(1)} %shard_map.107.refs_1_, bf16[32,3712]{1,0:T(8,128)(2,1)S(1)} %shard_map.108.refs_2_, bf16[32,3712]{1,0:T(8,128)(2,1)S(1)} %shard_map.110.refs_3_, ...), custom_call_target="tpu_custom_call" | custom-call | flops 2818572288 | bytes 3801088 | tf_op jit(solution)/shard_map/pallas_call | solution.py:243
  28.9 0.2 collective-permute-start.11
  29.2 2.3 %collective-permute-done.11.refs_1_ = bf16[128,3584]{1,0:T(8,128)(2,1)S(1)} collective-permute-done((bf16[128,3584]{1,0:T(8,128)(2,1)S(1)}, bf16[128,3584]{1,0:T(8,128)(2,1)S(1)}, u32[]{:S(2)}, u32[]{:S(2)}) %collective-permute-start.11) | collective-permute-done | bytes 917536 | tf_op jit(solution)/shard_map/ppermute | solution.py:319
  31.5 0.2 shard_map.112
  31.7 0.8 %collective-permute-start.15 = (bf16[24,3584]{1,0:T(8,128)(2,1)S(1)}, bf16[24,3584]{1,0:T(8,128)(2,1)S(1)}, u32[]{:S(2)}, u32[]{:S(2)}) collective-permute-start(bf16[24,3584]{1,0:T(8,128)(2,1)S(1)} %get-tuple-element.29), channel_id=1, source_target_pairs={{0,4},{1,17},{2,6},{3,19},{4,0},{5,21},{6,2},{7,23},{8,12},{9,25},... | collective-permute-start | bytes 516104 | tf_op jit(solution)/shard_map/ppermute | solution.py:310
  32.5 1.0 %collective-permute-start.16 = (bf16[24,3584]{1,0:T(8,128)(2,1)S(1)}, bf16[24,3584]{1,0:T(8,128)(2,1)S(1)}, u32[]{:S(2)}, u32[]{:S(2)}) collective-permute-start(bf16[24,3584]{1,0:T(8,128)(2,1)S(1)} %get-tuple-element.30), channel_id=1, source_target_pairs={{0,2},{1,9},{2,0},{3,11},{4,6},{5,13},{6,4},{7,15},{8,10},{9,1},{1... | collective-permute-start | bytes 516104 | tf_op jit(solution)/shard_map/ppermute | solution.py:310
  33.5 1.7 %collective-permute-start.17 = (bf16[24,3584]{1,0:T(8,128)(2,1)S(1)}, bf16[24,3584]{1,0:T(8,128)(2,1)S(1)}, u32[]{:S(2)}, u32[]{:S(2)}) collective-permute-start(bf16[24,3584]{1,0:T(8,128)(2,1)S(1)} %get-tuple-element.31), channel_id=1, source_target_pairs={{0,6},{1,25},{2,4},{3,27},{4,2},{5,29},{6,0},{7,31},{8,14},{9,17},... | collective-permute-start | bytes 516104 | tf_op jit(solution)/shard_map/ppermute | solution.py:310
  35.2 0.8 %collective-permute-start.12 = (bf16[8,3584]{1,0:T(8,128)(2,1)S(1)}, bf16[8,3584]{1,0:T(8,128)(2,1)S(1)}, u32[]{:S(2)}, u32[]{:S(2)}) collective-permute-start(bf16[8,3584]{1,0:T(8,128)(2,1)S(1)} %get-tuple-element.25), channel_id=1, source_target_pairs={{0,4},{1,17},{2,6},{3,19},{4,0},{5,21},{6,2},{7,23},{8,12},{9,25},... | collective-permute-start | bytes 172040 | tf_op jit(solution)/shard_map/ppermute | solution.py:310
  36.0 1.0 %collective-permute-start.13 = (bf16[8,3584]{1,0:T(8,128)(2,1)S(1)}, bf16[8,3584]{1,0:T(8,128)(2,1)S(1)}, u32[]{:S(2)}, u32[]{:S(2)}) collective-permute-start(bf16[8,3584]{1,0:T(8,128)(2,1)S(1)} %get-tuple-element.26), channel_id=1, source_target_pairs={{0,2},{1,9},{2,0},{3,11},{4,6},{5,13},{6,4},{7,15},{8,10},{9,1},{1... | collective-permute-start | bytes 172040 | tf_op jit(solution)/shard_map/ppermute | solution.py:310
  37.0 0.1 collective-permute-done.15.refs_1_
  37.1 1.6 %collective-permute-start.14 = (bf16[8,3584]{1,0:T(8,128)(2,1)S(1)}, bf16[8,3584]{1,0:T(8,128)(2,1)S(1)}, u32[]{:S(2)}, u32[]{:S(2)}) collective-permute-start(bf16[8,3584]{1,0:T(8,128)(2,1)S(1)} %get-tuple-element.27), channel_id=1, source_target_pairs={{0,6},{1,25},{2,4},{3,27},{4,2},{5,29},{6,0},{7,31},{8,14},{9,17},... | collective-permute-start | bytes 172040 | tf_op jit(solution)/shard_map/ppermute | solution.py:310
  38.7 0.0 collective-permute-done.16.refs_2_
  38.7 1.8 %collective-permute-done.17.refs_3_ = bf16[24,3584]{1,0:T(8,128)(2,1)S(1)} collective-permute-done((bf16[24,3584]{1,0:T(8,128)(2,1)S(1)}, bf16[24,3584]{1,0:T(8,128)(2,1)S(1)}, u32[]{:S(2)}, u32[]{:S(2)}) %collective-permute-start.17) | collective-permute-done | bytes 172064 | tf_op jit(solution)/shard_map/ppermute | solution.py:310
  40.5 0.1 shard_map.113
  40.6 1.9 %collective-permute-start.18 = (bf16[8,3584]{1,0:T(8,128)(2,1)S(1)}, bf16[8,3584]{1,0:T(8,128)(2,1)S(1)}, u32[]{:S(2)}, u32[]{:S(2)}) collective-permute-start(bf16[8,3584]{1,0:T(8,128)(2,1)S(1)} %get-tuple-element.32), channel_id=1, source_target_pairs={{0,24},{1,7},{2,26},{3,5},{4,28},{5,3},{6,30},{7,1},{8,16},{9,15},... | collective-permute-start | bytes 172040 | tf_op jit(solution)/shard_map/ppermute | solution.py:310
  42.5 0.7 %collective-permute-start.19 = (bf16[8,3584]{1,0:T(8,128)(2,1)S(1)}, bf16[8,3584]{1,0:T(8,128)(2,1)S(1)}, u32[]{:S(2)}, u32[]{:S(2)}) collective-permute-start(bf16[8,3584]{1,0:T(8,128)(2,1)S(1)} %get-tuple-element.33), channel_id=1, source_target_pairs={{0,16},{1,5},{2,18},{3,7},{4,20},{5,1},{6,22},{7,3},{8,24},{9,13},... | collective-permute-start | bytes 172040 | tf_op jit(solution)/shard_map/ppermute | solution.py:310
  43.2 0.0 collective-permute-done.12.refs_1_
  43.2 1.9 %collective-permute-start.20 = (bf16[8,3584]{1,0:T(8,128)(2,1)S(1)}, bf16[8,3584]{1,0:T(8,128)(2,1)S(1)}, u32[]{:S(2)}, u32[]{:S(2)}) collective-permute-start(bf16[8,3584]{1,0:T(8,128)(2,1)S(1)} %get-tuple-element.34), channel_id=1, source_target_pairs={{0,8},{1,3},{2,10},{3,1},{4,12},{5,7},{6,14},{7,5},{8,0},{9,11},{1... | collective-permute-start | bytes 172040 | tf_op jit(solution)/shard_map/ppermute | solution.py:310
  45.1 0.0 collective-permute-done.13.refs_2_
  45.1 0.0 collective-permute-done.14.refs_3_
  45.1 1.6 %collective-permute-done.18.refs_4_ = bf16[8,3584]{1,0:T(8,128)(2,1)S(1)} collective-permute-done((bf16[8,3584]{1,0:T(8,128)(2,1)S(1)}, bf16[8,3584]{1,0:T(8,128)(2,1)S(1)}, u32[]{:S(2)}, u32[]{:S(2)}) %collective-permute-start.18) | collective-permute-done | bytes 57376 | tf_op jit(solution)/shard_map/ppermute | solution.py:310
  46.7 1.0 %collective-permute-done.19.refs_5_ = bf16[8,3584]{1,0:T(8,128)(2,1)S(1)} collective-permute-done((bf16[8,3584]{1,0:T(8,128)(2,1)S(1)}, bf16[8,3584]{1,0:T(8,128)(2,1)S(1)}, u32[]{:S(2)}, u32[]{:S(2)}) %collective-permute-start.19) | collective-permute-done | bytes 57376 | tf_op jit(solution)/shard_map/ppermute | solution.py:310
  47.7 0.3 collective-permute-done.20.refs_6_
  48.0 0.7 %shard_map.114 = bf16[8,3584]{1,0:T(8,128)(2,1)} custom-call(bf16[8,3584]{1,0:T(8,128)(2,1)S(1)} %get-tuple-element.24.refs_0_, bf16[8,3584]{1,0:T(8,128)(2,1)S(1)} %collective-permute-done.12.refs_1_, bf16[8,3584]{1,0:T(8,128)(2,1)S(1)} %collective-permute-done.13.refs_2_, bf16[8,3584]{1,0:T(8,128)(2,1)S(1)} %collective-permute-done.14.refs_3_, ...), custom_call_target="tpu_custom_call" | custom-call | flops 200704 | bytes 401408 | tf_op jit(solution)/shard_map/pallas_call | solution.py:278
  (5 shorter events, 0.0 us)
Async XLA Ops:
  1.6 8.4 %collective-permute-start.2 = (bf16[8,3712]{1,0:T(8,128)(2,1)S(1)}, bf16[8,3712]{1,0:T(8,128)(2,1)S(1)}, u32[]{:S(2)}, u32[]{:S(2)}) collective-permute-start(bf16[8,3712]{1,0:T(8,128)(2,1)S(1)} %shard_map.104.refs_0_), channel_id=1, source_target_pairs={{0,24},{1,7},{2,26},{3,5},{4,28},{5,3},{6,30},{7,1},{8,16},{9,15},... | collective-permute-start | bytes 178184 | tf_op jit(solution)/shard_map/ppermute | solution.py:310
  6.7 5.3 %collective-permute-start.1 = (bf16[8,3712]{1,0:T(8,128)(2,1)S(1)}, bf16[8,3712]{1,0:T(8,128)(2,1)S(1)}, u32[]{:S(2)}, u32[]{:S(2)}) collective-permute-start(bf16[8,3712]{1,0:T(8,128)(2,1)S(1)} %shard_map.104.refs_0_), channel_id=1, source_target_pairs={{0,16},{1,5},{2,18},{3,7},{4,20},{5,1},{6,22},{7,3},{8,24},{9,13},... | collective-permute-start | bytes 178184 | tf_op jit(solution)/shard_map/ppermute | solution.py:310
  6.7 5.3 %collective-permute-start = (bf16[8,3712]{1,0:T(8,128)(2,1)S(1)}, bf16[8,3712]{1,0:T(8,128)(2,1)S(1)}, u32[]{:S(2)}, u32[]{:S(2)}) collective-permute-start(bf16[8,3712]{1,0:T(8,128)(2,1)S(1)} %shard_map.104.refs_0_), channel_id=1, source_target_pairs={{0,8},{1,3},{2,10},{3,1},{4,12},{5,7},{6,14},{7,5},{8,0},{9,11},{1... | collective-permute-start | bytes 178184 | tf_op jit(solution)/shard_map/ppermute | solution.py:310
  7.3 7.8 %collective-permute-start.5 = (bf16[8,3712]{1,0:T(8,128)(2,1)S(1)}, bf16[8,3712]{1,0:T(8,128)(2,1)S(1)}, u32[]{:S(2)}, u32[]{:S(2)}) collective-permute-start(bf16[8,3712]{1,0:T(8,128)(2,1)S(1)} %shard_map.104.refs_0_), channel_id=1, source_target_pairs={{0,6},{1,25},{2,4},{3,27},{4,2},{5,29},{6,0},{7,31},{8,14},{9,17},... | collective-permute-start | bytes 178184 | tf_op jit(solution)/shard_map/ppermute | solution.py:310
  12.0 9.7 %collective-permute-start.3 = (bf16[32,3712]{1,0:T(8,128)(2,1)S(1)}, bf16[32,3712]{1,0:T(8,128)(2,1)S(1)}, u32[]{:S(2)}, u32[]{:S(2)}) collective-permute-start(bf16[32,3712]{1,0:T(8,128)(2,1)S(1)} %shard_map.105.after_ref.refs_0_), channel_id=1, source_target_pairs={{0,2},{1,9},{2,0},{3,11},{4,6},{5,13},{6,4},{7,15},{8,10},{9,1},{1... | collective-permute-start | bytes 712712 | tf_op jit(solution)/shard_map/ppermute | solution.py:310
  13.6 8.6 %collective-permute-start.4 = (bf16[32,3712]{1,0:T(8,128)(2,1)S(1)}, bf16[32,3712]{1,0:T(8,128)(2,1)S(1)}, u32[]{:S(2)}, u32[]{:S(2)}) collective-permute-start(bf16[32,3712]{1,0:T(8,128)(2,1)S(1)} %shard_map.105.after_ref.refs_0_), channel_id=1, source_target_pairs={{0,4},{1,17},{2,6},{3,19},{4,0},{5,21},{6,2},{7,23},{8,12},{9,25},... | collective-permute-start | bytes 712712 | tf_op jit(solution)/shard_map/ppermute | solution.py:310
  15.1 6.5 %collective-permute-start.6 = (bf16[24,3712]{1,0:T(8,128)(2,1)S(1)}, bf16[24,3712]{1,0:T(8,128)(2,1)S(1)}, u32[]{:S(2)}, u32[]{:S(2)}) collective-permute-start(bf16[24,3712]{1,0:T(8,128)(2,1)S(1)} %shard_map.109), channel_id=1, source_target_pairs={{0,6},{1,25},{2,4},{3,27},{4,2},{5,29},{6,0},{7,31},{8,14},{9,17},... | collective-permute-start | bytes 534536 | tf_op jit(solution)/shard_map/ppermute | solution.py:310
  15.7 6.6 %collective-permute-start.7 = (bf16[32,3712]{1,0:T(8,128)(2,1)S(1)}, bf16[32,3712]{1,0:T(8,128)(2,1)S(1)}, u32[]{:S(2)}, u32[]{:S(2)}) collective-permute-start(bf16[32,3712]{1,0:T(8,128)(2,1)S(1)} %shard_map.105.after_ref.refs_0_), channel_id=1, source_target_pairs={{0,1},{1,0},{2,3},{3,2},{4,5},{5,4},{6,7},{7,6},{8,9},{9,8},{10,11... | collective-permute-start | bytes 712712 | tf_op jit(solution)/shard_map/ppermute | solution.py:319
  21.6 1.6 %collective-permute-start.10 = (bf16[32,3712]{1,0:T(8,128)(2,1)S(1)}, bf16[32,3712]{1,0:T(8,128)(2,1)S(1)}, u32[]{:S(2)}, u32[]{:S(2)}) collective-permute-start(bf16[32,3712]{1,0:T(8,128)(2,1)S(1)} %shard_map.110.refs_3_), channel_id=1, source_target_pairs={{0,1},{1,0},{2,3},{3,2},{4,5},{5,4},{6,7},{7,6},{8,9},{9,8},{10,11... | collective-permute-start | bytes 712712 | tf_op jit(solution)/shard_map/ppermute | solution.py:319
  21.7 1.8 %collective-permute-start.8 = (bf16[32,3712]{1,0:T(8,128)(2,1)S(1)}, bf16[32,3712]{1,0:T(8,128)(2,1)S(1)}, u32[]{:S(2)}, u32[]{:S(2)}) collective-permute-start(bf16[32,3712]{1,0:T(8,128)(2,1)S(1)} %shard_map.107.refs_1_), channel_id=1, source_target_pairs={{0,1},{1,0},{2,3},{3,2},{4,5},{5,4},{6,7},{7,6},{8,9},{9,8},{10,11... | collective-permute-start | bytes 712712 | tf_op jit(solution)/shard_map/ppermute | solution.py:319
  22.2 1.7 %collective-permute-start.9 = (bf16[32,3712]{1,0:T(8,128)(2,1)S(1)}, bf16[32,3712]{1,0:T(8,128)(2,1)S(1)}, u32[]{:S(2)}, u32[]{:S(2)}) collective-permute-start(bf16[32,3712]{1,0:T(8,128)(2,1)S(1)} %shard_map.108.refs_2_), channel_id=1, source_target_pairs={{0,1},{1,0},{2,3},{3,2},{4,5},{5,4},{6,7},{7,6},{8,9},{9,8},{10,11... | collective-permute-start | bytes 712712 | tf_op jit(solution)/shard_map/ppermute | solution.py:319
  28.9 2.5 %collective-permute-start.11 = (bf16[128,3584]{1,0:T(8,128)(2,1)S(1)}, bf16[128,3584]{1,0:T(8,128)(2,1)S(1)}, u32[]{:S(2)}, u32[]{:S(2)}) collective-permute-start(bf16[128,3584]{1,0:T(8,128)(2,1)S(1)} %get-tuple-element.23), channel_id=1, source_target_pairs={{0,1},{1,0},{2,3},{3,2},{4,5},{5,4},{6,7},{7,6},{8,9},{9,8},{10,11... | collective-permute-start | bytes 2752520 | tf_op jit(solution)/shard_map/ppermute | solution.py:319
  31.7 5.5 %collective-permute-start.15 = (bf16[24,3584]{1,0:T(8,128)(2,1)S(1)}, bf16[24,3584]{1,0:T(8,128)(2,1)S(1)}, u32[]{:S(2)}, u32[]{:S(2)}) collective-permute-start(bf16[24,3584]{1,0:T(8,128)(2,1)S(1)} %get-tuple-element.29), channel_id=1, source_target_pairs={{0,4},{1,17},{2,6},{3,19},{4,0},{5,21},{6,2},{7,23},{8,12},{9,25},... | collective-permute-start | bytes 516104 | tf_op jit(solution)/shard_map/ppermute | solution.py:310
  32.5 6.2 %collective-permute-start.16 = (bf16[24,3584]{1,0:T(8,128)(2,1)S(1)}, bf16[24,3584]{1,0:T(8,128)(2,1)S(1)}, u32[]{:S(2)}, u32[]{:S(2)}) collective-permute-start(bf16[24,3584]{1,0:T(8,128)(2,1)S(1)} %get-tuple-element.30), channel_id=1, source_target_pairs={{0,2},{1,9},{2,0},{3,11},{4,6},{5,13},{6,4},{7,15},{8,10},{9,1},{1... | collective-permute-start | bytes 516104 | tf_op jit(solution)/shard_map/ppermute | solution.py:310
  33.5 7.0 %collective-permute-start.17 = (bf16[24,3584]{1,0:T(8,128)(2,1)S(1)}, bf16[24,3584]{1,0:T(8,128)(2,1)S(1)}, u32[]{:S(2)}, u32[]{:S(2)}) collective-permute-start(bf16[24,3584]{1,0:T(8,128)(2,1)S(1)} %get-tuple-element.31), channel_id=1, source_target_pairs={{0,6},{1,25},{2,4},{3,27},{4,2},{5,29},{6,0},{7,31},{8,14},{9,17},... | collective-permute-start | bytes 516104 | tf_op jit(solution)/shard_map/ppermute | solution.py:310
  35.2 8.0 %collective-permute-start.12 = (bf16[8,3584]{1,0:T(8,128)(2,1)S(1)}, bf16[8,3584]{1,0:T(8,128)(2,1)S(1)}, u32[]{:S(2)}, u32[]{:S(2)}) collective-permute-start(bf16[8,3584]{1,0:T(8,128)(2,1)S(1)} %get-tuple-element.25), channel_id=1, source_target_pairs={{0,4},{1,17},{2,6},{3,19},{4,0},{5,21},{6,2},{7,23},{8,12},{9,25},... | collective-permute-start | bytes 172040 | tf_op jit(solution)/shard_map/ppermute | solution.py:310
  36.0 9.1 %collective-permute-start.13 = (bf16[8,3584]{1,0:T(8,128)(2,1)S(1)}, bf16[8,3584]{1,0:T(8,128)(2,1)S(1)}, u32[]{:S(2)}, u32[]{:S(2)}) collective-permute-start(bf16[8,3584]{1,0:T(8,128)(2,1)S(1)} %get-tuple-element.26), channel_id=1, source_target_pairs={{0,2},{1,9},{2,0},{3,11},{4,6},{5,13},{6,4},{7,15},{8,10},{9,1},{1... | collective-permute-start | bytes 172040 | tf_op jit(solution)/shard_map/ppermute | solution.py:310
  37.1 8.0 %collective-permute-start.14 = (bf16[8,3584]{1,0:T(8,128)(2,1)S(1)}, bf16[8,3584]{1,0:T(8,128)(2,1)S(1)}, u32[]{:S(2)}, u32[]{:S(2)}) collective-permute-start(bf16[8,3584]{1,0:T(8,128)(2,1)S(1)} %get-tuple-element.27), channel_id=1, source_target_pairs={{0,6},{1,25},{2,4},{3,27},{4,2},{5,29},{6,0},{7,31},{8,14},{9,17},... | collective-permute-start | bytes 172040 | tf_op jit(solution)/shard_map/ppermute | solution.py:310
  40.6 6.0 %collective-permute-start.18 = (bf16[8,3584]{1,0:T(8,128)(2,1)S(1)}, bf16[8,3584]{1,0:T(8,128)(2,1)S(1)}, u32[]{:S(2)}, u32[]{:S(2)}) collective-permute-start(bf16[8,3584]{1,0:T(8,128)(2,1)S(1)} %get-tuple-element.32), channel_id=1, source_target_pairs={{0,24},{1,7},{2,26},{3,5},{4,28},{5,3},{6,30},{7,1},{8,16},{9,15},... | collective-permute-start | bytes 172040 | tf_op jit(solution)/shard_map/ppermute | solution.py:310
  42.5 5.2 %collective-permute-start.19 = (bf16[8,3584]{1,0:T(8,128)(2,1)S(1)}, bf16[8,3584]{1,0:T(8,128)(2,1)S(1)}, u32[]{:S(2)}, u32[]{:S(2)}) collective-permute-start(bf16[8,3584]{1,0:T(8,128)(2,1)S(1)} %get-tuple-element.33), channel_id=1, source_target_pairs={{0,16},{1,5},{2,18},{3,7},{4,20},{5,1},{6,22},{7,3},{8,24},{9,13},... | collective-permute-start | bytes 172040 | tf_op jit(solution)/shard_map/ppermute | solution.py:310
  43.2 4.8 %collective-permute-start.20 = (bf16[8,3584]{1,0:T(8,128)(2,1)S(1)}, bf16[8,3584]{1,0:T(8,128)(2,1)S(1)}, u32[]{:S(2)}, u32[]{:S(2)}) collective-permute-start(bf16[8,3584]{1,0:T(8,128)(2,1)S(1)} %get-tuple-element.34), channel_id=1, source_target_pairs={{0,8},{1,3},{2,10},{3,1},{4,12},{5,7},{6,14},{7,5},{8,0},{9,11},{1... | collective-permute-start | bytes 172040 | tf_op jit(solution)/shard_map/ppermute | solution.py:310

commit v9 on v5

--- a/solution.py
+++ b/solution.py
@@ -179,13 +179,12 @@
     )(held(value), held(after))
 
 
-def expert_kernel(count, *refs):
+def hidden_kernel(count, *refs):
     pieces = refs[:count]
-    gate_ref, up_ref, down_ref, mine_ref, other_ref, rows_ref, hidden_ref = refs[count:]
+    gate_ref, up_ref, hidden_ref, rows_ref = refs[count:]
     total, _ = rows_ref.shape
     model_width, units = gate_ref.shape
     lanes = rows_ref.shape[1] - model_width
-    half = total // 2
     me = lax.axis_index("ep")
     block = min(total, 256)
     chunk = 256
@@ -208,46 +207,63 @@
             value = gate_value / (1.0 + jnp.exp(-gate_value)) * up_value * weight
             hidden_ref[here, cols] = value.astype(jnp.bfloat16)
 
+    if total == block:
+        units_of(slice(0, block))
+    else:
+        pl.loop(0, total // block)(lambda i: units_of(pl.ds(pl.multiple_of(i * block, block), block)))
+
+
+def hidden_units(pieces, expert_gate, expert_up):
+    total, width = sum(p.shape[0] for p in pieces), pieces[0].shape[1]
+    model_width, units = expert_gate.shape
+    return pl.pallas_call(
+        functools.partial(hidden_kernel, len(pieces)),
+        out_shape=in_vmem((total, units), jnp.bfloat16),
+        in_specs=[VMEM] * (len(pieces) + 2),
+        out_specs=VMEM,
+        scratch_shapes=[pltpu.VMEM((total, width), jnp.bfloat16)],
+        compiler_params=pltpu.CompilerParams(vmem_limit_bytes=(8 << 20) + 4 * total * width),
+        cost_estimate=pl.CostEstimate(
+            flops=4 * total * model_width * units,
+            bytes_accessed=4 * model_width * units + 2 * total * width,
+            transcendentals=total * units,
+        ),
+    )(*(held(v) for v in (*pieces, expert_gate, expert_up)))
+
+
+def down_kernel(hidden_ref, down_ref, out_ref):
+    total, model_width = out_ref.shape
+    block = min(total, 256)
+    step = 512
+
     def results_of(cols):
         for i in range(total // block):
-            low, high = i * block, (i + 1) * block
-            value = jnp.dot(hidden_ref[low:high, :], down_ref[:, cols], preferred_element_type=jnp.float32)
-            value = value.astype(jnp.bfloat16)
-            if high <= half:
-                mine_ref[low:high, cols] = value
-            elif low >= half:
-                other_ref[low - half : high - half, cols] = value
-            else:
-                mine_ref[low:half, cols] = value[: half - low]
-                other_ref[: high - half, cols] = value[half - low :]
-
-    step = 512
+            rows = slice(i * block, (i + 1) * block)
+            value = jnp.dot(hidden_ref[rows, :], down_ref[:, cols], preferred_element_type=jnp.float32)
+            out_ref[rows, cols] = value.astype(jnp.bfloat16)
+
     if total == block:
-        units_of(slice(0, block))
         for c in range(model_width // step):
             results_of(slice(c * step, (c + 1) * step))
     else:
-        pl.loop(0, total // block)(lambda i: units_of(pl.ds(pl.multiple_of(i * block, block), block)))
         pl.loop(0, model_width // step)(lambda c: results_of(pl.ds(pl.multiple_of(c * step, step), step)))
 
 
-def expert_block(pieces, expert_gate, expert_up, expert_down):
-    total, width = sum(p.shape[0] for p in pieces), pieces[0].shape[1]
-    model_width, units = expert_gate.shape
-    out = in_vmem((total // 2, model_width), jnp.bfloat16)
-    return pl.pallas_call(
-        functools.partial(expert_kernel, len(pieces)),
-        out_shape=(out, out),
-        in_specs=[VMEM] * (len(pieces) + 3),
-        out_specs=(VMEM, VMEM),
-        scratch_shapes=[pltpu.VMEM((total, width), jnp.bfloat16), pltpu.VMEM((total, units), jnp.bfloat16)],
-        compiler_params=pltpu.CompilerParams(vmem_limit_bytes=(8 << 20) + 4 * total * units + 2 * total * width),
+def down(hidden, expert_down):
+    total, units = hidden.shape
+    model_width = expert_down.shape[1]
+    return pl.pallas_call(
+        down_kernel,
+        out_shape=in_vmem((total, model_width), jnp.bfloat16),
+        in_specs=[VMEM] * 2,
+        out_specs=VMEM,
+        compiler_params=pltpu.CompilerParams(vmem_limit_bytes=8 << 20),
         cost_estimate=pl.CostEstimate(
-            flops=6 * total * model_width * units,
-            bytes_accessed=4 * total * width,
-            transcendentals=total * units,
+            flops=2 * total * model_width * units,
+            bytes_accessed=2 * model_width * units + 2 * total * model_width,
+            transcendentals=0,
         ),
-    )(*(held(p) for p in pieces), *(held(w) for w in (expert_gate, expert_up, expert_down)))
+    )(held(hidden), held(expert_down))
 
 
 def add_kernel(count, rows, sizes, *refs):
@@ -321,8 +337,10 @@
         block,
     )
     pieces = [block] + [tie(far[k], token) for k in range(1, inner)]
-    pieces += [over_cores(p) for p in pieces]
-    mine, other = expert_block(pieces, *weights)
+    received = [over_cores(p) for p in pieces]
+    hidden = hidden_units(pieces, *weights[:2])
+    other = down(hidden_units(received, *weights[:2]), weights[2])
+    mine = down(hidden, weights[2])
 
     size = (outer - 1) * tok_rows
     kept, column, *parts = add([mine, over_cores(other)], [(0, mine.shape[0])] * 2, [tok_rows, size] * inner)

time: 47.3 us -> 46.1 us (0.975)
  waiting for transfers between devices: 13.3 us -> 11.4 us
  Pallas kernels: 10.5 us -> 11.3 us
    ppermute x5, waiting for transfers between devices: 3.62 us -> 1.71 us  [over_cores(): return lax.ppermute(value, 'sub', [(i, i ^ 1) for i in range(sub_count)])]
    pallas_call x1 -> x4, Pallas kernels: 3.03 us -> 3.76 us  [the longest x2 2.47 us: hidden_units(): pl.pallas_call(functools.partial(hidden_kernel, len(pieces)), out_shape=i...]
  transfers between devices with their start and end apart: 20 -> 20, of which waited for: 10 -> 10; matrix products, arithmetic and copies ran while one was open for 0% -> 0% of each run, Pallas kernels for 12% -> 16%
where the time goes in v9:
time: 46.1 us; the launch traced here: 45.9 us
  starting transfers between devices  22.5 us (49%)
  waiting for transfers between devices  11.4 us (25%)
  Pallas kernels  11.3 us (25%)
  between operations  0.73 us (2%)
    ppermute x15, starting transfers between devices, swap(): return lax.ppermute(value, ('ep', 'sub'), pairs)  21.2 us
    ppermute x15, waiting for transfers between devices, swap(): return lax.ppermute(value, ('ep', 'sub'), pairs)  9.68 us
    pallas_call x1, Pallas kernels, attend(): pl.pallas_call(attend_kernel, out_shape=(jax.ShapeDtypeStruct((rows, head...  5.58 us
    pallas_call x2, Pallas kernels, hidden_units(): pl.pallas_call(functools.partial(hidden_kernel, len(pieces)), out_shape=i...  2.47 us
    ppermute x5, waiting for transfers between devices, over_cores(): return lax.ppermute(value, 'sub', [(i, i ^ 1) for i in range(sub_count)])  1.71 us
    ppermute x5, starting transfers between devices, over_cores(): return lax.ppermute(value, 'sub', [(i, i ^ 1) for i in range(sub_count)])  1.33 us
    pallas_call x2, Pallas kernels, down(): pl.pallas_call(down_kernel, out_shape=in_vmem((total, model_width), jnp.b...  1.29 us
    pallas_call x3, Pallas kernels, add(): pl.pallas_call(functools.partial(add_kernel, len(values), rows, sizes), o...  0.98 us
  transfers between devices with their start and end apart: 20, of which 10 were waited for; matrix products, arithmetic and copies ran while one was open for 0% of the time, Pallas kernels for 16%

profile of v9, /device:TPU:0, one launch (start us, length us, event | category | flops | bytes accessed | tf_op | source)
XLA Modules:
  0.0 45.9 jit_solution(8675113752380630133)
XLA Ops:
  0.6 0.9 %shard_map.104.refs_0_ = bf16[8,3712]{1,0:T(8,128)(2,1)S(1)} custom-call(bf16[8,3584]{1,0:T(8,128)(2,1)} %hidden_ref.1, s32[8,8]{1,0:T(8,128)} %routes_ref.1, f32[8,8]{1,0:T(8,128)} %scores_ref.1), custom_call_target="tpu_custom_call" | custom-call | flops 65536 | bytes 114688 | tf_op jit(solution)/shard_map/pallas_call | solution.py:133
  1.6 5.1 %collective-permute-start.2 = (bf16[8,3712]{1,0:T(8,128)(2,1)S(1)}, bf16[8,3712]{1,0:T(8,128)(2,1)S(1)}, u32[]{:S(2)}, u32[]{:S(2)}) collective-permute-start(bf16[8,3712]{1,0:T(8,128)(2,1)S(1)} %shard_map.104.refs_0_), channel_id=1, source_target_pairs={{0,24},{1,7},{2,26},{3,5},{4,28},{5,3},{6,30},{7,1},{8,16},{9,15},... | collective-permute-start | bytes 178184 | tf_op jit(solution)/shard_map/ppermute | solution.py:316
  6.7 0.0 collective-permute-start.1
  6.7 0.6 %collective-permute-start = (bf16[8,3712]{1,0:T(8,128)(2,1)S(1)}, bf16[8,3712]{1,0:T(8,128)(2,1)S(1)}, u32[]{:S(2)}, u32[]{:S(2)}) collective-permute-start(bf16[8,3712]{1,0:T(8,128)(2,1)S(1)} %shard_map.104.refs_0_), channel_id=1, source_target_pairs={{0,8},{1,3},{2,10},{3,1},{4,12},{5,7},{6,14},{7,5},{8,0},{9,11},{1... | collective-permute-start | bytes 178184 | tf_op jit(solution)/shard_map/ppermute | solution.py:316
  7.3 1.6 %collective-permute-done.2.refs_3_ = bf16[8,3712]{1,0:T(8,128)(2,1)S(1)} collective-permute-done((bf16[8,3712]{1,0:T(8,128)(2,1)S(1)}, bf16[8,3712]{1,0:T(8,128)(2,1)S(1)}, u32[]{:S(2)}, u32[]{:S(2)}) %collective-permute-start.2) | collective-permute-done | bytes 59424 | tf_op jit(solution)/shard_map/ppermute | solution.py:316
  8.9 2.9 %collective-permute-done.1.refs_2_ = bf16[8,3712]{1,0:T(8,128)(2,1)S(1)} collective-permute-done((bf16[8,3712]{1,0:T(8,128)(2,1)S(1)}, bf16[8,3712]{1,0:T(8,128)(2,1)S(1)}, u32[]{:S(2)}, u32[]{:S(2)}) %collective-permute-start.1) | collective-permute-done | bytes 59424 | tf_op jit(solution)/shard_map/ppermute | solution.py:316
  11.8 0.0 collective-permute-done.refs_1_
  11.8 1.9 %collective-permute-start.3 = (bf16[32,3712]{1,0:T(8,128)(2,1)S(1)}, bf16[32,3712]{1,0:T(8,128)(2,1)S(1)}, u32[]{:S(2)}, u32[]{:S(2)}) collective-permute-start(bf16[32,3712]{1,0:T(8,128)(2,1)S(1)} %shard_map.105.after_ref.refs_0_), channel_id=1, source_target_pairs={{0,2},{1,9},{2,0},{3,11},{4,6},{5,13},{6,4},{7,15},{8,10},{9,1},{1... | collective-permute-start | bytes 712712 | tf_op jit(solution)/shard_map/ppermute | solution.py:316
  13.7 1.5 %collective-permute-start.4 = (bf16[32,3712]{1,0:T(8,128)(2,1)S(1)}, bf16[32,3712]{1,0:T(8,128)(2,1)S(1)}, u32[]{:S(2)}, u32[]{:S(2)}) collective-permute-start(bf16[32,3712]{1,0:T(8,128)(2,1)S(1)} %shard_map.105.after_ref.refs_0_), channel_id=1, source_target_pairs={{0,4},{1,17},{2,6},{3,19},{4,0},{5,21},{6,2},{7,23},{8,12},{9,25},... | collective-permute-start | bytes 712712 | tf_op jit(solution)/shard_map/ppermute | solution.py:316
  15.3 0.1 collective-permute-start.5
  15.4 0.0 collective-permute-start.6
  15.4 5.6 %shard_map.106 = (bf16[4,128,512]{2,1,0:T(8,128)(2,1)}, bf16[3584,512]{1,0:T(8,128)(2,1)S(1)}, bf16[3584,512]{1,0:T(8,128)(2,1)S(1)}, bf16[512,3584]{1,0:T(8,128)(2,1)S(1)}, f32[8,128]{1,0:T(8,128)S(1)}) custom-call(s32[4]{0:T(128)} %lengths_hbm.1, bf16[4,576,128]{2,1,0:T(8,128)(2,1)} %bitcast.9, bf16[4,576,256]{2,1,0:T(8,128)(2,1)} %bitcast.8, ...), custom_call_target="tpu_custom_call" | custom-call | flops 301989888 | bytes 11010048 | tf_op jit(solution)/shard_map/pallas_call | solution.py:74
  21.0 0.0 collective-permute-done.3.value_ref
  21.0 0.6 %collective-permute-start.7 = (bf16[32,3712]{1,0:T(8,128)(2,1)S(1)}, bf16[32,3712]{1,0:T(8,128)(2,1)S(1)}, u32[]{:S(2)}, u32[]{:S(2)}) collective-permute-start(bf16[32,3712]{1,0:T(8,128)(2,1)S(1)} %shard_map.107.refs_1_), channel_id=1, source_target_pairs={{0,1},{1,0},{2,3},{3,2},{4,5},{5,4},{6,7},{7,6},{8,9},{9,8},{10,11... | collective-permute-start | bytes 712712 | tf_op jit(solution)/shard_map/ppermute | solution.py:325
  21.6 0.8 %collective-permute-done.4.value_ref = bf16[32,3712]{1,0:T(8,128)(2,1)S(1)} collective-permute-done((bf16[32,3712]{1,0:T(8,128)(2,1)S(1)}, bf16[32,3712]{1,0:T(8,128)(2,1)S(1)}, u32[]{:S(2)}, u32[]{:S(2)}) %collective-permute-start.4) | collective-permute-done | bytes 237600 | tf_op jit(solution)/shard_map/ppermute | solution.py:316
  22.4 0.0 collective-permute-start.8
  22.4 0.0 collective-permute-done.5.value_ref
  22.4 0.5 %collective-permute-start.9 = (bf16[32,3712]{1,0:T(8,128)(2,1)S(1)}, bf16[32,3712]{1,0:T(8,128)(2,1)S(1)}, u32[]{:S(2)}, u32[]{:S(2)}) collective-permute-start(bf16[32,3712]{1,0:T(8,128)(2,1)S(1)} %shard_map.109.refs_3_), channel_id=1, source_target_pairs={{0,1},{1,0},{2,3},{3,2},{4,5},{5,4},{6,7},{7,6},{8,9},{9,8},{10,11... | collective-permute-start | bytes 712712 | tf_op jit(solution)/shard_map/ppermute | solution.py:325
  22.9 0.0 collective-permute-done.6.refs_0_
  22.9 0.0 collective-permute-done.7.refs_1_
  22.9 1.0 %collective-permute-done.8.refs_2_ = bf16[32,3712]{1,0:T(8,128)(2,1)S(1)} collective-permute-done((bf16[32,3712]{1,0:T(8,128)(2,1)S(1)}, bf16[32,3712]{1,0:T(8,128)(2,1)S(1)}, u32[]{:S(2)}, u32[]{:S(2)}) %collective-permute-start.8) | collective-permute-done | bytes 237600 | tf_op jit(solution)/shard_map/ppermute | solution.py:325
  23.9 0.3 collective-permute-done.9.refs_3_
  24.2 1.2 %shard_map.112.hidden_ref = bf16[128,512]{1,0:T(8,128)(2,1)S(1)} custom-call(bf16[32,3712]{1,0:T(8,128)(2,1)S(1)} %collective-permute-done.6.refs_0_, bf16[32,3712]{1,0:T(8,128)(2,1)S(1)} %collective-permute-done.7.refs_1_, bf16[32,3712]{1,0:T(8,128)(2,1)S(1)} %collective-permute-done.8.refs_2_, bf16[32,3712]{1,0:T(8,128)(2,1)S(1)} %collective-permute-done.9.refs_3_, ...), custom_call_target="tpu_custom_call" | custom-call | flops 939524096 | bytes 8290304 | tf_op jit(solution)/shard_map/pallas_call | solution.py:219
  25.5 0.6 %shard_map.113 = bf16[128,3584]{1,0:T(8,128)(2,1)S(1)} custom-call(bf16[128,512]{1,0:T(8,128)(2,1)S(1)} %shard_map.112.hidden_ref, bf16[512,3584]{1,0:T(8,128)(2,1)S(1)} %get-tuple-element.21.down_ref), custom_call_target="tpu_custom_call" | custom-call | flops 469762048 | bytes 4587520 | tf_op jit(solution)/shard_map/pallas_call | solution.py:255
  26.1 0.2 collective-permute-start.10
  26.4 1.2 %shard_map.110.hidden_ref = bf16[128,512]{1,0:T(8,128)(2,1)S(1)} custom-call(bf16[32,3712]{1,0:T(8,128)(2,1)S(1)} %shard_map.105.after_ref.refs_0_, bf16[32,3712]{1,0:T(8,128)(2,1)S(1)} %shard_map.107.refs_1_, bf16[32,3712]{1,0:T(8,128)(2,1)S(1)} %shard_map.108.refs_2_, bf16[32,3712]{1,0:T(8,128)(2,1)S(1)} %shard_map.109.refs_3_, ...), custom_call_target="tpu_custom_call" | custom-call | flops 939524096 | bytes 8290304 | tf_op jit(solution)/shard_map/pallas_call | solution.py:219
  27.6 0.6 %shard_map.111.refs_0_ = bf16[128,3584]{1,0:T(8,128)(2,1)S(1)} custom-call(bf16[128,512]{1,0:T(8,128)(2,1)S(1)} %shard_map.110.hidden_ref, bf16[512,3584]{1,0:T(8,128)(2,1)S(1)} %get-tuple-element.21.down_ref), custom_call_target="tpu_custom_call" | custom-call | flops 469762048 | bytes 4587520 | tf_op jit(solution)/shard_map/pallas_call | solution.py:255
  28.3 0.4 collective-permute-done.10.refs_1_
  28.7 0.2 shard_map.114
  28.9 1.6 %collective-permute-start.14 = (bf16[24,3584]{1,0:T(8,128)(2,1)S(1)}, bf16[24,3584]{1,0:T(8,128)(2,1)S(1)}, u32[]{:S(2)}, u32[]{:S(2)}) collective-permute-start(bf16[24,3584]{1,0:T(8,128)(2,1)S(1)} %get-tuple-element.27), channel_id=1, source_target_pairs={{0,4},{1,17},{2,6},{3,19},{4,0},{5,21},{6,2},{7,23},{8,12},{9,25},... | collective-permute-start | bytes 516104 | tf_op jit(solution)/shard_map/ppermute | solution.py:316
  30.5 1.0 %collective-permute-start.15 = (bf16[24,3584]{1,0:T(8,128)(2,1)S(1)}, bf16[24,3584]{1,0:T(8,128)(2,1)S(1)}, u32[]{:S(2)}, u32[]{:S(2)}) collective-permute-start(bf16[24,3584]{1,0:T(8,128)(2,1)S(1)} %get-tuple-element.28), channel_id=1, source_target_pairs={{0,2},{1,9},{2,0},{3,11},{4,6},{5,13},{6,4},{7,15},{8,10},{9,1},{1... | collective-permute-start | bytes 516104 | tf_op jit(solution)/shard_map/ppermute | solution.py:316
  31.5 0.9 %collective-permute-start.16 = (bf16[24,3584]{1,0:T(8,128)(2,1)S(1)}, bf16[24,3584]{1,0:T(8,128)(2,1)S(1)}, u32[]{:S(2)}, u32[]{:S(2)}) collective-permute-start(bf16[24,3584]{1,0:T(8,128)(2,1)S(1)} %get-tuple-element.29), channel_id=1, source_target_pairs={{0,6},{1,25},{2,4},{3,27},{4,2},{5,29},{6,0},{7,31},{8,14},{9,17},... | collective-permute-start | bytes 516104 | tf_op jit(solution)/shard_map/ppermute | solution.py:316
  32.4 1.5 %collective-permute-start.11 = (bf16[8,3584]{1,0:T(8,128)(2,1)S(1)}, bf16[8,3584]{1,0:T(8,128)(2,1)S(1)}, u32[]{:S(2)}, u32[]{:S(2)}) collective-permute-start(bf16[8,3584]{1,0:T(8,128)(2,1)S(1)} %get-tuple-element.23), channel_id=1, source_target_pairs={{0,4},{1,17},{2,6},{3,19},{4,0},{5,21},{6,2},{7,23},{8,12},{9,25},... | collective-permute-start | bytes 172040 | tf_op jit(solution)/shard_map/ppermute | solution.py:316
  34.0 1.0 %collective-permute-start.12 = (bf16[8,3584]{1,0:T(8,128)(2,1)S(1)}, bf16[8,3584]{1,0:T(8,128)(2,1)S(1)}, u32[]{:S(2)}, u32[]{:S(2)}) collective-permute-start(bf16[8,3584]{1,0:T(8,128)(2,1)S(1)} %get-tuple-element.24), channel_id=1, source_target_pairs={{0,2},{1,9},{2,0},{3,11},{4,6},{5,13},{6,4},{7,15},{8,10},{9,1},{1... | collective-permute-start | bytes 172040 | tf_op jit(solution)/shard_map/ppermute | solution.py:316
  35.0 0.0 collective-permute-done.14.refs_1_
  35.0 1.3 %collective-permute-start.13 = (bf16[8,3584]{1,0:T(8,128)(2,1)S(1)}, bf16[8,3584]{1,0:T(8,128)(2,1)S(1)}, u32[]{:S(2)}, u32[]{:S(2)}) collective-permute-start(bf16[8,3584]{1,0:T(8,128)(2,1)S(1)} %get-tuple-element.25), channel_id=1, source_target_pairs={{0,6},{1,25},{2,4},{3,27},{4,2},{5,29},{6,0},{7,31},{8,14},{9,17},... | collective-permute-start | bytes 172040 | tf_op jit(solution)/shard_map/ppermute | solution.py:316
  36.3 0.0 collective-permute-done.15.refs_2_
  36.3 1.6 %collective-permute-done.16.refs_3_ = bf16[24,3584]{1,0:T(8,128)(2,1)S(1)} collective-permute-done((bf16[24,3584]{1,0:T(8,128)(2,1)S(1)}, bf16[24,3584]{1,0:T(8,128)(2,1)S(1)}, u32[]{:S(2)}, u32[]{:S(2)}) %collective-permute-start.16) | collective-permute-done | bytes 172064 | tf_op jit(solution)/shard_map/ppermute | solution.py:316
  37.9 0.1 shard_map.115
  38.0 1.2 %collective-permute-start.17 = (bf16[8,3584]{1,0:T(8,128)(2,1)S(1)}, bf16[8,3584]{1,0:T(8,128)(2,1)S(1)}, u32[]{:S(2)}, u32[]{:S(2)}) collective-permute-start(bf16[8,3584]{1,0:T(8,128)(2,1)S(1)} %get-tuple-element.30), channel_id=1, source_target_pairs={{0,24},{1,7},{2,26},{3,5},{4,28},{5,3},{6,30},{7,1},{8,16},{9,15},... | collective-permute-start | bytes 172040 | tf_op jit(solution)/shard_map/ppermute | solution.py:316
  39.2 1.1 %collective-permute-start.18 = (bf16[8,3584]{1,0:T(8,128)(2,1)S(1)}, bf16[8,3584]{1,0:T(8,128)(2,1)S(1)}, u32[]{:S(2)}, u32[]{:S(2)}) collective-permute-start(bf16[8,3584]{1,0:T(8,128)(2,1)S(1)} %get-tuple-element.31), channel_id=1, source_target_pairs={{0,16},{1,5},{2,18},{3,7},{4,20},{5,1},{6,22},{7,3},{8,24},{9,13},... | collective-permute-start | bytes 172040 | tf_op jit(solution)/shard_map/ppermute | solution.py:316
  40.4 0.0 collective-permute-done.11.refs_1_
  40.4 2.1 %collective-permute-start.19 = (bf16[8,3584]{1,0:T(8,128)(2,1)S(1)}, bf16[8,3584]{1,0:T(8,128)(2,1)S(1)}, u32[]{:S(2)}, u32[]{:S(2)}) collective-permute-start(bf16[8,3584]{1,0:T(8,128)(2,1)S(1)} %get-tuple-element.32), channel_id=1, source_target_pairs={{0,8},{1,3},{2,10},{3,1},{4,12},{5,7},{6,14},{7,5},{8,0},{9,11},{1... | collective-permute-start | bytes 172040 | tf_op jit(solution)/shard_map/ppermute | solution.py:316
  42.4 0.0 collective-permute-done.12.refs_2_
  42.4 0.0 collective-permute-done.13.refs_3_
  42.5 1.6 %collective-permute-done.17.refs_4_ = bf16[8,3584]{1,0:T(8,128)(2,1)S(1)} collective-permute-done((bf16[8,3584]{1,0:T(8,128)(2,1)S(1)}, bf16[8,3584]{1,0:T(8,128)(2,1)S(1)}, u32[]{:S(2)}, u32[]{:S(2)}) %collective-permute-start.17) | collective-permute-done | bytes 57376 | tf_op jit(solution)/shard_map/ppermute | solution.py:316
  44.1 0.6 %collective-permute-done.18.refs_5_ = bf16[8,3584]{1,0:T(8,128)(2,1)S(1)} collective-permute-done((bf16[8,3584]{1,0:T(8,128)(2,1)S(1)}, bf16[8,3584]{1,0:T(8,128)(2,1)S(1)}, u32[]{:S(2)}, u32[]{:S(2)}) %collective-permute-start.18) | collective-permute-done | bytes 57376 | tf_op jit(solution)/shard_map/ppermute | solution.py:316
  44.7 0.5 %collective-permute-done.19.refs_6_ = bf16[8,3584]{1,0:T(8,128)(2,1)S(1)} collective-permute-done((bf16[8,3584]{1,0:T(8,128)(2,1)S(1)}, bf16[8,3584]{1,0:T(8,128)(2,1)S(1)}, u32[]{:S(2)}, u32[]{:S(2)}) %collective-permute-start.19) | collective-permute-done | bytes 57376 | tf_op jit(solution)/shard_map/ppermute | solution.py:316
  45.3 0.7 %shard_map.116 = bf16[8,3584]{1,0:T(8,128)(2,1)} custom-call(bf16[8,3584]{1,0:T(8,128)(2,1)S(1)} %get-tuple-element.22.refs_0_, bf16[8,3584]{1,0:T(8,128)(2,1)S(1)} %collective-permute-done.11.refs_1_, bf16[8,3584]{1,0:T(8,128)(2,1)S(1)} %collective-permute-done.12.refs_2_, bf16[8,3584]{1,0:T(8,128)(2,1)S(1)} %collective-permute-done.13.refs_3_, ...), custom_call_target="tpu_custom_call" | custom-call | flops 200704 | bytes 401408 | tf_op jit(solution)/shard_map/pallas_call | solution.py:284
  (4 shorter events, 0.0 us)
Async XLA Ops:
  1.6 7.4 %collective-permute-start.2 = (bf16[8,3712]{1,0:T(8,128)(2,1)S(1)}, bf16[8,3712]{1,0:T(8,128)(2,1)S(1)}, u32[]{:S(2)}, u32[]{:S(2)}) collective-permute-start(bf16[8,3712]{1,0:T(8,128)(2,1)S(1)} %shard_map.104.refs_0_), channel_id=1, source_target_pairs={{0,24},{1,7},{2,26},{3,5},{4,28},{5,3},{6,30},{7,1},{8,16},{9,15},... | collective-permute-start | bytes 178184 | tf_op jit(solution)/shard_map/ppermute | solution.py:316
  6.7 5.1 %collective-permute-start.1 = (bf16[8,3712]{1,0:T(8,128)(2,1)S(1)}, bf16[8,3712]{1,0:T(8,128)(2,1)S(1)}, u32[]{:S(2)}, u32[]{:S(2)}) collective-permute-start(bf16[8,3712]{1,0:T(8,128)(2,1)S(1)} %shard_map.104.refs_0_), channel_id=1, source_target_pairs={{0,16},{1,5},{2,18},{3,7},{4,20},{5,1},{6,22},{7,3},{8,24},{9,13},... | collective-permute-start | bytes 178184 | tf_op jit(solution)/shard_map/ppermute | solution.py:316
  6.7 5.1 %collective-permute-start = (bf16[8,3712]{1,0:T(8,128)(2,1)S(1)}, bf16[8,3712]{1,0:T(8,128)(2,1)S(1)}, u32[]{:S(2)}, u32[]{:S(2)}) collective-permute-start(bf16[8,3712]{1,0:T(8,128)(2,1)S(1)} %shard_map.104.refs_0_), channel_id=1, source_target_pairs={{0,8},{1,3},{2,10},{3,1},{4,12},{5,7},{6,14},{7,5},{8,0},{9,11},{1... | collective-permute-start | bytes 178184 | tf_op jit(solution)/shard_map/ppermute | solution.py:316
  11.8 9.2 %collective-permute-start.3 = (bf16[32,3712]{1,0:T(8,128)(2,1)S(1)}, bf16[32,3712]{1,0:T(8,128)(2,1)S(1)}, u32[]{:S(2)}, u32[]{:S(2)}) collective-permute-start(bf16[32,3712]{1,0:T(8,128)(2,1)S(1)} %shard_map.105.after_ref.refs_0_), channel_id=1, source_target_pairs={{0,2},{1,9},{2,0},{3,11},{4,6},{5,13},{6,4},{7,15},{8,10},{9,1},{1... | collective-permute-start | bytes 712712 | tf_op jit(solution)/shard_map/ppermute | solution.py:316
  13.7 8.7 %collective-permute-start.4 = (bf16[32,3712]{1,0:T(8,128)(2,1)S(1)}, bf16[32,3712]{1,0:T(8,128)(2,1)S(1)}, u32[]{:S(2)}, u32[]{:S(2)}) collective-permute-start(bf16[32,3712]{1,0:T(8,128)(2,1)S(1)} %shard_map.105.after_ref.refs_0_), channel_id=1, source_target_pairs={{0,4},{1,17},{2,6},{3,19},{4,0},{5,21},{6,2},{7,23},{8,12},{9,25},... | collective-permute-start | bytes 712712 | tf_op jit(solution)/shard_map/ppermute | solution.py:316
  15.3 7.1 %collective-permute-start.5 = (bf16[32,3712]{1,0:T(8,128)(2,1)S(1)}, bf16[32,3712]{1,0:T(8,128)(2,1)S(1)}, u32[]{:S(2)}, u32[]{:S(2)}) collective-permute-start(bf16[32,3712]{1,0:T(8,128)(2,1)S(1)} %shard_map.105.after_ref.refs_0_), channel_id=1, source_target_pairs={{0,6},{1,25},{2,4},{3,27},{4,2},{5,29},{6,0},{7,31},{8,14},{9,17},... | collective-permute-start | bytes 712712 | tf_op jit(solution)/shard_map/ppermute | solution.py:316
  15.4 7.5 %collective-permute-start.6 = (bf16[32,3712]{1,0:T(8,128)(2,1)S(1)}, bf16[32,3712]{1,0:T(8,128)(2,1)S(1)}, u32[]{:S(2)}, u32[]{:S(2)}) collective-permute-start(bf16[32,3712]{1,0:T(8,128)(2,1)S(1)} %shard_map.105.after_ref.refs_0_), channel_id=1, source_target_pairs={{0,1},{1,0},{2,3},{3,2},{4,5},{5,4},{6,7},{7,6},{8,9},{9,8},{10,11... | collective-permute-start | bytes 712712 | tf_op jit(solution)/shard_map/ppermute | solution.py:325
  21.0 1.9 %collective-permute-start.7 = (bf16[32,3712]{1,0:T(8,128)(2,1)S(1)}, bf16[32,3712]{1,0:T(8,128)(2,1)S(1)}, u32[]{:S(2)}, u32[]{:S(2)}) collective-permute-start(bf16[32,3712]{1,0:T(8,128)(2,1)S(1)} %shard_map.107.refs_1_), channel_id=1, source_target_pairs={{0,1},{1,0},{2,3},{3,2},{4,5},{5,4},{6,7},{7,6},{8,9},{9,8},{10,11... | collective-permute-start | bytes 712712 | tf_op jit(solution)/shard_map/ppermute | solution.py:325
  22.4 1.5 %collective-permute-start.8 = (bf16[32,3712]{1,0:T(8,128)(2,1)S(1)}, bf16[32,3712]{1,0:T(8,128)(2,1)S(1)}, u32[]{:S(2)}, u32[]{:S(2)}) collective-permute-start(bf16[32,3712]{1,0:T(8,128)(2,1)S(1)} %shard_map.108.refs_2_), channel_id=1, source_target_pairs={{0,1},{1,0},{2,3},{3,2},{4,5},{5,4},{6,7},{7,6},{8,9},{9,8},{10,11... | collective-permute-start | bytes 712712 | tf_op jit(solution)/shard_map/ppermute | solution.py:325
  22.4 1.8 %collective-permute-start.9 = (bf16[32,3712]{1,0:T(8,128)(2,1)S(1)}, bf16[32,3712]{1,0:T(8,128)(2,1)S(1)}, u32[]{:S(2)}, u32[]{:S(2)}) collective-permute-start(bf16[32,3712]{1,0:T(8,128)(2,1)S(1)} %shard_map.109.refs_3_), channel_id=1, source_target_pairs={{0,1},{1,0},{2,3},{3,2},{4,5},{5,4},{6,7},{7,6},{8,9},{9,8},{10,11... | collective-permute-start | bytes 712712 | tf_op jit(solution)/shard_map/ppermute | solution.py:325
  26.1 2.5 %collective-permute-start.10 = (bf16[128,3584]{1,0:T(8,128)(2,1)S(1)}, bf16[128,3584]{1,0:T(8,128)(2,1)S(1)}, u32[]{:S(2)}, u32[]{:S(2)}) collective-permute-start(bf16[128,3584]{1,0:T(8,128)(2,1)S(1)} %shard_map.113), channel_id=1, source_target_pairs={{0,1},{1,0},{2,3},{3,2},{4,5},{5,4},{6,7},{7,6},{8,9},{9,8},{10,11... | collective-permute-start | bytes 2752520 | tf_op jit(solution)/shard_map/ppermute | solution.py:325
  28.9 6.1 %collective-permute-start.14 = (bf16[24,3584]{1,0:T(8,128)(2,1)S(1)}, bf16[24,3584]{1,0:T(8,128)(2,1)S(1)}, u32[]{:S(2)}, u32[]{:S(2)}) collective-permute-start(bf16[24,3584]{1,0:T(8,128)(2,1)S(1)} %get-tuple-element.27), channel_id=1, source_target_pairs={{0,4},{1,17},{2,6},{3,19},{4,0},{5,21},{6,2},{7,23},{8,12},{9,25},... | collective-permute-start | bytes 516104 | tf_op jit(solution)/shard_map/ppermute | solution.py:316
  30.5 5.9 %collective-permute-start.15 = (bf16[24,3584]{1,0:T(8,128)(2,1)S(1)}, bf16[24,3584]{1,0:T(8,128)(2,1)S(1)}, u32[]{:S(2)}, u32[]{:S(2)}) collective-permute-start(bf16[24,3584]{1,0:T(8,128)(2,1)S(1)} %get-tuple-element.28), channel_id=1, source_target_pairs={{0,2},{1,9},{2,0},{3,11},{4,6},{5,13},{6,4},{7,15},{8,10},{9,1},{1... | collective-permute-start | bytes 516104 | tf_op jit(solution)/shard_map/ppermute | solution.py:316
  31.5 6.4 %collective-permute-start.16 = (bf16[24,3584]{1,0:T(8,128)(2,1)S(1)}, bf16[24,3584]{1,0:T(8,128)(2,1)S(1)}, u32[]{:S(2)}, u32[]{:S(2)}) collective-permute-start(bf16[24,3584]{1,0:T(8,128)(2,1)S(1)} %get-tuple-element.29), channel_id=1, source_target_pairs={{0,6},{1,25},{2,4},{3,27},{4,2},{5,29},{6,0},{7,31},{8,14},{9,17},... | collective-permute-start | bytes 516104 | tf_op jit(solution)/shard_map/ppermute | solution.py:316
  32.4 7.9 %collective-permute-start.11 = (bf16[8,3584]{1,0:T(8,128)(2,1)S(1)}, bf16[8,3584]{1,0:T(8,128)(2,1)S(1)}, u32[]{:S(2)}, u32[]{:S(2)}) collective-permute-start(bf16[8,3584]{1,0:T(8,128)(2,1)S(1)} %get-tuple-element.23), channel_id=1, source_target_pairs={{0,4},{1,17},{2,6},{3,19},{4,0},{5,21},{6,2},{7,23},{8,12},{9,25},... | collective-permute-start | bytes 172040 | tf_op jit(solution)/shard_map/ppermute | solution.py:316
  34.0 8.5 %collective-permute-start.12 = (bf16[8,3584]{1,0:T(8,128)(2,1)S(1)}, bf16[8,3584]{1,0:T(8,128)(2,1)S(1)}, u32[]{:S(2)}, u32[]{:S(2)}) collective-permute-start(bf16[8,3584]{1,0:T(8,128)(2,1)S(1)} %get-tuple-element.24), channel_id=1, source_target_pairs={{0,2},{1,9},{2,0},{3,11},{4,6},{5,13},{6,4},{7,15},{8,10},{9,1},{1... | collective-permute-start | bytes 172040 | tf_op jit(solution)/shard_map/ppermute | solution.py:316
  35.0 7.5 %collective-permute-start.13 = (bf16[8,3584]{1,0:T(8,128)(2,1)S(1)}, bf16[8,3584]{1,0:T(8,128)(2,1)S(1)}, u32[]{:S(2)}, u32[]{:S(2)}) collective-permute-start(bf16[8,3584]{1,0:T(8,128)(2,1)S(1)} %get-tuple-element.25), channel_id=1, source_target_pairs={{0,6},{1,25},{2,4},{3,27},{4,2},{5,29},{6,0},{7,31},{8,14},{9,17},... | collective-permute-start | bytes 172040 | tf_op jit(solution)/shard_map/ppermute | solution.py:316
  38.0 6.1 %collective-permute-start.17 = (bf16[8,3584]{1,0:T(8,128)(2,1)S(1)}, bf16[8,3584]{1,0:T(8,128)(2,1)S(1)}, u32[]{:S(2)}, u32[]{:S(2)}) collective-permute-start(bf16[8,3584]{1,0:T(8,128)(2,1)S(1)} %get-tuple-element.30), channel_id=1, source_target_pairs={{0,24},{1,7},{2,26},{3,5},{4,28},{5,3},{6,30},{7,1},{8,16},{9,15},... | collective-permute-start | bytes 172040 | tf_op jit(solution)/shard_map/ppermute | solution.py:316
  39.2 5.5 %collective-permute-start.18 = (bf16[8,3584]{1,0:T(8,128)(2,1)S(1)}, bf16[8,3584]{1,0:T(8,128)(2,1)S(1)}, u32[]{:S(2)}, u32[]{:S(2)}) collective-permute-start(bf16[8,3584]{1,0:T(8,128)(2,1)S(1)} %get-tuple-element.31), channel_id=1, source_target_pairs={{0,16},{1,5},{2,18},{3,7},{4,20},{5,1},{6,22},{7,3},{8,24},{9,13},... | collective-permute-start | bytes 172040 | tf_op jit(solution)/shard_map/ppermute | solution.py:316
  40.4 4.9 %collective-permute-start.19 = (bf16[8,3584]{1,0:T(8,128)(2,1)S(1)}, bf16[8,3584]{1,0:T(8,128)(2,1)S(1)}, u32[]{:S(2)}, u32[]{:S(2)}) collective-permute-start(bf16[8,3584]{1,0:T(8,128)(2,1)S(1)} %get-tuple-element.32), channel_id=1, source_target_pairs={{0,8},{1,3},{2,10},{3,1},{4,12},{5,7},{6,14},{7,5},{8,0},{9,11},{1... | collective-permute-start | bytes 172040 | tf_op jit(solution)/shard_map/ppermute | solution.py:316

commit v10 on v9

--- a/solution.py
+++ b/solution.py
@@ -35,11 +35,11 @@
 
 
 def attend_kernel(
-    lengths_hbm, query_hbm, cache_hbm, gate_hbm, up_hbm, down_hbm, after_ref,
-    out_ref, gate_ref, up_ref, down_ref, token_ref, lengths_ref, query_ref, cache_ref, sems,
+    lengths_hbm, query_hbm, cache_hbm, up_hbm, down_hbm, after_ref,
+    out_ref, up_ref, down_ref, token_ref, lengths_ref, query_ref, cache_ref, sems,
 ):
     pairs = [(lengths_hbm, lengths_ref), (query_hbm, query_ref), (cache_hbm, cache_ref)]
-    for source, target in ((gate_hbm, gate_ref), (up_hbm, up_ref), (down_hbm, down_ref)):
+    for source, target in ((up_hbm, up_ref), (down_hbm, down_ref)):
         rows = source.shape[0] // FETCHES
         pairs += [(source.at[pl.ds(i * rows, rows)], target.at[pl.ds(i * rows, rows)]) for i in range(FETCHES)]
     copies = [pltpu.make_async_copy(s, t, sems.at[i]) for i, (s, t) in enumerate(pairs)]
@@ -78,13 +78,13 @@
             *(in_vmem(w.shape, w.dtype) for w in weights),
             in_vmem((8, LANES), jnp.float32),
         ),
-        in_specs=[HBM] * 6 + [ANY],
-        out_specs=(VMEM,) * 5,
+        in_specs=[HBM] * 5 + [ANY],
+        out_specs=(VMEM,) * 4,
         scratch_shapes=[
             pltpu.SMEM(cache_lengths.shape, jnp.int32),
             pltpu.VMEM(query.shape, query.dtype),
             pltpu.VMEM(cache.shape, cache.dtype),
-            pltpu.SemaphoreType.DMA((3 + 3 * FETCHES,)),
+            pltpu.SemaphoreType.DMA((3 + 2 * FETCHES,)),
         ],
         compiler_params=pltpu.CompilerParams(vmem_limit_bytes=12 << 20),
         cost_estimate=pl.CostEstimate(
@@ -146,21 +146,49 @@
     )(stored(hidden_in), stored(expert_routes), stored(route_scores))
 
 
-def join_kernel(*refs):
-    value = jnp.concatenate([ref[...].astype(jnp.float32) for ref in refs[:-1]], axis=0)
+def join_kernel(count, *refs):
+    value = jnp.concatenate([ref[...].astype(jnp.float32) for ref in refs[:count]], axis=0)
     refs[-1][...] = value.astype(jnp.bfloat16)
 
 
-def join(pieces):
+def join(pieces, after=()):
     total, width = sum(p.shape[0] for p in pieces), pieces[0].shape[1]
-    return pl.pallas_call(
-        join_kernel,
+    operands = [*pieces, *after]
+    return pl.pallas_call(
+        functools.partial(join_kernel, len(pieces)),
         out_shape=in_vmem((total, width), jnp.bfloat16),
-        in_specs=[VMEM] * len(pieces),
+        in_specs=[VMEM] * len(operands),
         out_specs=VMEM,
         compiler_params=pltpu.CompilerParams(vmem_limit_bytes=(2 << 20) + 8 * total * width),
         cost_estimate=pl.CostEstimate(flops=total * width, bytes_accessed=4 * total * width, transcendentals=0),
-    )(*(held(p) for p in pieces))
+    )(*(held(p) for p in operands))
+
+
+def fetch_kernel(source_ref, target_ref, token_ref, sems):
+    rows = source_ref.shape[0] // FETCHES
+    copies = [
+        pltpu.make_async_copy(
+            source_ref.at[pl.ds(i * rows, rows)], target_ref.at[pl.ds(i * rows, rows)], sems.at[i]
+        )
+        for i in range(FETCHES)
+    ]
+    for copy in copies:
+        copy.start()
+    token_ref[...] = jnp.zeros_like(token_ref)
+    for copy in copies:
+        copy.wait()
+
+
+def fetch(value):
+    return pl.pallas_call(
+        fetch_kernel,
+        out_shape=(in_vmem(value.shape, value.dtype), in_vmem((8, LANES), jnp.float32)),
+        in_specs=[HBM],
+        out_specs=(VMEM, VMEM),
+        scratch_shapes=[pltpu.SemaphoreType.DMA((FETCHES,))],
+        compiler_params=pltpu.CompilerParams(vmem_limit_bytes=1 << 20),
+        cost_estimate=pl.CostEstimate(flops=0, bytes_accessed=2 * value.size, transcendentals=0),
+    )(stored(value))
 
 
 def tie_kernel(value_ref, after_ref, out_ref):
@@ -326,21 +354,22 @@
 
     own = pack(hidden_in, expert_routes, route_scores, ep_count)
     near = {k: first(own, k) for k in range(outer - 1, 0, -1)}
-    block = join([own] + [near[k] for k in range(1, outer)])
+    gate, fetched = fetch(expert_gate[0])
+    block = join([own] + [near[k] for k in range(1, outer)], [fetched])
     steps = [*range(inner - 2, 0, -1), inner - 1]
     far = {k: second(block, k) for k in steps}
-    attention_latent, *weights, token = attend(
+    attention_latent, up, down_rows, token = attend(
         query_latent,
         latent_cache,
         cache_lengths,
-        (expert_gate[0], expert_up[0], expert_down[0]),
+        (expert_up[0], expert_down[0]),
         block,
     )
     pieces = [block] + [tie(far[k], token) for k in range(1, inner)]
     received = [over_cores(p) for p in pieces]
-    hidden = hidden_units(pieces, *weights[:2])
-    other = down(hidden_units(received, *weights[:2]), weights[2])
-    mine = down(hidden, weights[2])
+    hidden = hidden_units(pieces, gate, up)
+    other = down(hidden_units(received, gate, up), down_rows)
+    mine = down(hidden, down_rows)
 
     size = (outer - 1) * tok_rows
     kept, column, *parts = add([mine, over_cores(other)], [(0, mine.shape[0])] * 2, [tok_rows, size] * inner)

time: 46.1 us -> 45.9 us (level)
  Pallas kernels: 11.3 us -> 12.3 us
  waiting for transfers between devices: 11.4 us -> 10.6 us
  starting transfers between devices: 22.5 us -> 22 us
    pallas_call x1 -> x2, Pallas kernels: 0.02 us -> 2.09 us  [the longest x1 2.07 us: fetch(): pl.pallas_call(fetch_kernel, out_shape=(in_vmem(value.shape, value.dtype)...]
    pallas_call x1, Pallas kernels: 5.58 us -> 4.52 us  [attend(): pl.pallas_call(attend_kernel, out_shape=(jax.ShapeDtypeStruct((rows, head...]
    ppermute x15, waiting for transfers between devices: 9.68 us -> 8.9 us  [swap(): return lax.ppermute(value, ('ep', 'sub'), pairs)]
    ppermute x15, starting transfers between devices: 21.2 us -> 20.7 us  [swap(): return lax.ppermute(value, ('ep', 'sub'), pairs)]
  transfers between devices with their start and end apart: 20 -> 20, of which waited for: 10 -> 10; matrix products, arithmetic and copies ran while one was open for 0% -> 0% of each run, Pallas kernels for 16% -> 19%
where the time goes in v10:
time: 45.9 us; the launch traced here: 45.7 us
  starting transfers between devices  22 us (48%)
  Pallas kernels  12.3 us (27%)
  waiting for transfers between devices  10.6 us (23%)
  between operations  0.74 us (2%)
    ppermute x15, starting transfers between devices, swap(): return lax.ppermute(value, ('ep', 'sub'), pairs)  20.7 us
    ppermute x15, waiting for transfers between devices, swap(): return lax.ppermute(value, ('ep', 'sub'), pairs)  8.9 us
    pallas_call x1, Pallas kernels, attend(): pl.pallas_call(attend_kernel, out_shape=(jax.ShapeDtypeStruct((rows, head...  4.52 us
    pallas_call x2, Pallas kernels, hidden_units(): pl.pallas_call(functools.partial(hidden_kernel, len(pieces)), out_shape=i...  2.47 us
    pallas_call x1, Pallas kernels, fetch(): pl.pallas_call(fetch_kernel, out_shape=(in_vmem(value.shape, value.dtype)...  2.07 us
    ppermute x5, waiting for transfers between devices, over_cores(): return lax.ppermute(value, 'sub', [(i, i ^ 1) for i in range(sub_count)])  1.71 us
    pallas_call x2, Pallas kernels, down(): pl.pallas_call(down_kernel, out_shape=in_vmem((total, model_width), jnp.b...  1.34 us
    ppermute x5, starting transfers between devices, over_cores(): return lax.ppermute(value, 'sub', [(i, i ^ 1) for i in range(sub_count)])  1.32 us
  transfers between devices with their start and end apart: 20, of which 10 were waited for; matrix products, arithmetic and copies ran while one was open for 0% of the time, Pallas kernels for 19%

profile of v10, /device:TPU:0, one launch (start us, length us, event | category | flops | bytes accessed | tf_op | source)
XLA Modules:
  0.0 45.7 jit_solution(17992439431166015299)
XLA Ops:
  0.6 0.9 %shard_map.104.refs_0_ = bf16[8,3712]{1,0:T(8,128)(2,1)S(1)} custom-call(bf16[8,3584]{1,0:T(8,128)(2,1)} %hidden_ref.1, s32[8,8]{1,0:T(8,128)} %routes_ref.1, f32[8,8]{1,0:T(8,128)} %scores_ref.1), custom_call_target="tpu_custom_call" | custom-call | flops 65536 | bytes 114688 | tf_op jit(solution)/shard_map/pallas_call | solution.py:133
  1.6 5.1 %collective-permute-start.2 = (bf16[8,3712]{1,0:T(8,128)(2,1)S(1)}, bf16[8,3712]{1,0:T(8,128)(2,1)S(1)}, u32[]{:S(2)}, u32[]{:S(2)}) collective-permute-start(bf16[8,3712]{1,0:T(8,128)(2,1)S(1)} %shard_map.104.refs_0_), channel_id=1, source_target_pairs={{0,24},{1,7},{2,26},{3,5},{4,28},{5,3},{6,30},{7,1},{8,16},{9,15},... | collective-permute-start | bytes 178184 | tf_op jit(solution)/shard_map/ppermute | solution.py:344
  6.7 0.0 collective-permute-start.1
  6.7 0.6 %collective-permute-start = (bf16[8,3712]{1,0:T(8,128)(2,1)S(1)}, bf16[8,3712]{1,0:T(8,128)(2,1)S(1)}, u32[]{:S(2)}, u32[]{:S(2)}) collective-permute-start(bf16[8,3712]{1,0:T(8,128)(2,1)S(1)} %shard_map.104.refs_0_), channel_id=1, source_target_pairs={{0,8},{1,3},{2,10},{3,1},{4,12},{5,7},{6,14},{7,5},{8,0},{9,11},{1... | collective-permute-start | bytes 178184 | tf_op jit(solution)/shard_map/ppermute | solution.py:344
  7.3 2.1 %shard_map.105 = (bf16[3584,512]{1,0:T(8,128)(2,1)S(1)}, f32[8,128]{1,0:T(8,128)S(1)}) custom-call(bf16[3584,512]{1,0:T(8,128)(2,1)} %bitcast.5), custom_call_target="tpu_custom_call" | custom-call | bytes 3670016 | tf_op jit(solution)/shard_map/pallas_call | solution.py:183
  9.4 0.0 collective-permute-done.2.refs_3_
  9.4 2.4 %collective-permute-done.1.refs_2_ = bf16[8,3712]{1,0:T(8,128)(2,1)S(1)} collective-permute-done((bf16[8,3712]{1,0:T(8,128)(2,1)S(1)}, bf16[8,3712]{1,0:T(8,128)(2,1)S(1)}, u32[]{:S(2)}, u32[]{:S(2)}) %collective-permute-start.1) | collective-permute-done | bytes 59424 | tf_op jit(solution)/shard_map/ppermute | solution.py:344
  11.8 0.0 collective-permute-done.refs_1_
  11.8 1.8 %collective-permute-start.3 = (bf16[32,3712]{1,0:T(8,128)(2,1)S(1)}, bf16[32,3712]{1,0:T(8,128)(2,1)S(1)}, u32[]{:S(2)}, u32[]{:S(2)}) collective-permute-start(bf16[32,3712]{1,0:T(8,128)(2,1)S(1)} %shard_map.106.after_ref.refs_0_), channel_id=1, source_target_pairs={{0,2},{1,9},{2,0},{3,11},{4,6},{5,13},{6,4},{7,15},{8,10},{9,1},{1... | collective-permute-start | bytes 712712 | tf_op jit(solution)/shard_map/ppermute | solution.py:344
  13.6 1.5 %collective-permute-start.4 = (bf16[32,3712]{1,0:T(8,128)(2,1)S(1)}, bf16[32,3712]{1,0:T(8,128)(2,1)S(1)}, u32[]{:S(2)}, u32[]{:S(2)}) collective-permute-start(bf16[32,3712]{1,0:T(8,128)(2,1)S(1)} %shard_map.106.after_ref.refs_0_), channel_id=1, source_target_pairs={{0,4},{1,17},{2,6},{3,19},{4,0},{5,21},{6,2},{7,23},{8,12},{9,25},... | collective-permute-start | bytes 712712 | tf_op jit(solution)/shard_map/ppermute | solution.py:344
  15.1 0.3 collective-permute-start.5
  15.4 0.0 collective-permute-start.6
  15.4 4.5 %shard_map.107 = (bf16[4,128,512]{2,1,0:T(8,128)(2,1)}, bf16[3584,512]{1,0:T(8,128)(2,1)S(1)}, bf16[512,3584]{1,0:T(8,128)(2,1)S(1)}, f32[8,128]{1,0:T(8,128)S(1)}) custom-call(s32[4]{0:T(128)} %lengths_hbm.1, bf16[4,576,128]{2,1,0:T(8,128)(2,1)} %bitcast.9, bf16[4,576,256]{2,1,0:T(8,128)(2,1)} %bitcast.8, bf16[3584,512]{1,0:T(8,128)(2,1)} %bitcast.6, ...), custom_call_target="tpu_custom_call" | custom-call | flops 301989888 | bytes 7340032 | tf_op jit(solution)/shard_map/pallas_call | solution.py:74
  19.9 0.0 collective-permute-done.3.value_ref
  20.0 0.6 %collective-permute-start.7 = (bf16[32,3712]{1,0:T(8,128)(2,1)S(1)}, bf16[32,3712]{1,0:T(8,128)(2,1)S(1)}, u32[]{:S(2)}, u32[]{:S(2)}) collective-permute-start(bf16[32,3712]{1,0:T(8,128)(2,1)S(1)} %shard_map.108.refs_1_), channel_id=1, source_target_pairs={{0,1},{1,0},{2,3},{3,2},{4,5},{5,4},{6,7},{7,6},{8,9},{9,8},{10,11... | collective-permute-start | bytes 712712 | tf_op jit(solution)/shard_map/ppermute | solution.py:353
  20.5 1.7 %collective-permute-done.4.value_ref = bf16[32,3712]{1,0:T(8,128)(2,1)S(1)} collective-permute-done((bf16[32,3712]{1,0:T(8,128)(2,1)S(1)}, bf16[32,3712]{1,0:T(8,128)(2,1)S(1)}, u32[]{:S(2)}, u32[]{:S(2)}) %collective-permute-start.4) | collective-permute-done | bytes 237600 | tf_op jit(solution)/shard_map/ppermute | solution.py:344
  22.3 0.0 collective-permute-start.8
  22.3 0.0 collective-permute-done.5.value_ref
  22.3 0.5 %collective-permute-start.9 = (bf16[32,3712]{1,0:T(8,128)(2,1)S(1)}, bf16[32,3712]{1,0:T(8,128)(2,1)S(1)}, u32[]{:S(2)}, u32[]{:S(2)}) collective-permute-start(bf16[32,3712]{1,0:T(8,128)(2,1)S(1)} %shard_map.110.refs_3_), channel_id=1, source_target_pairs={{0,1},{1,0},{2,3},{3,2},{4,5},{5,4},{6,7},{7,6},{8,9},{9,8},{10,11... | collective-permute-start | bytes 712712 | tf_op jit(solution)/shard_map/ppermute | solution.py:353
  22.8 0.0 collective-permute-done.6.refs_0_
  22.8 0.0 collective-permute-done.7.refs_1_
  22.8 1.0 %collective-permute-done.8.refs_2_ = bf16[32,3712]{1,0:T(8,128)(2,1)S(1)} collective-permute-done((bf16[32,3712]{1,0:T(8,128)(2,1)S(1)}, bf16[32,3712]{1,0:T(8,128)(2,1)S(1)}, u32[]{:S(2)}, u32[]{:S(2)}) %collective-permute-start.8) | collective-permute-done | bytes 237600 | tf_op jit(solution)/shard_map/ppermute | solution.py:353
  23.8 0.3 collective-permute-done.9.refs_3_
  24.1 1.2 %shard_map.113.hidden_ref = bf16[128,512]{1,0:T(8,128)(2,1)S(1)} custom-call(bf16[32,3712]{1,0:T(8,128)(2,1)S(1)} %collective-permute-done.6.refs_0_, bf16[32,3712]{1,0:T(8,128)(2,1)S(1)} %collective-permute-done.7.refs_1_, bf16[32,3712]{1,0:T(8,128)(2,1)S(1)} %collective-permute-done.8.refs_2_, bf16[32,3712]{1,0:T(8,128)(2,1)S(1)} %collective-permute-done.9.refs_3_, ...), custom_call_target="tpu_custom_call" | custom-call | flops 939524096 | bytes 8290304 | tf_op jit(solution)/shard_map/pallas_call | solution.py:247
  25.4 0.7 %shard_map.114 = bf16[128,3584]{1,0:T(8,128)(2,1)S(1)} custom-call(bf16[128,512]{1,0:T(8,128)(2,1)S(1)} %shard_map.113.hidden_ref, bf16[512,3584]{1,0:T(8,128)(2,1)S(1)} %get-tuple-element.23.down_ref), custom_call_target="tpu_custom_call" | custom-call | flops 469762048 | bytes 4587520 | tf_op jit(solution)/shard_map/pallas_call | solution.py:283
  26.0 0.2 collective-permute-start.10
  26.3 1.2 %shard_map.111.hidden_ref = bf16[128,512]{1,0:T(8,128)(2,1)S(1)} custom-call(bf16[32,3712]{1,0:T(8,128)(2,1)S(1)} %shard_map.106.after_ref.refs_0_, bf16[32,3712]{1,0:T(8,128)(2,1)S(1)} %shard_map.108.refs_1_, bf16[32,3712]{1,0:T(8,128)(2,1)S(1)} %shard_map.109.refs_2_, bf16[32,3712]{1,0:T(8,128)(2,1)S(1)} %shard_map.110.refs_3_, ...), custom_call_target="tpu_custom_call" | custom-call | flops 939524096 | bytes 8290304 | tf_op jit(solution)/shard_map/pallas_call | solution.py:247
  27.5 0.7 %shard_map.112.refs_0_ = bf16[128,3584]{1,0:T(8,128)(2,1)S(1)} custom-call(bf16[128,512]{1,0:T(8,128)(2,1)S(1)} %shard_map.111.hidden_ref, bf16[512,3584]{1,0:T(8,128)(2,1)S(1)} %get-tuple-element.23.down_ref), custom_call_target="tpu_custom_call" | custom-call | flops 469762048 | bytes 4587520 | tf_op jit(solution)/shard_map/pallas_call | solution.py:283
  28.2 0.4 collective-permute-done.10.refs_1_
  28.6 0.2 shard_map.115
  28.8 1.6 %collective-permute-start.14 = (bf16[24,3584]{1,0:T(8,128)(2,1)S(1)}, bf16[24,3584]{1,0:T(8,128)(2,1)S(1)}, u32[]{:S(2)}, u32[]{:S(2)}) collective-permute-start(bf16[24,3584]{1,0:T(8,128)(2,1)S(1)} %get-tuple-element.29), channel_id=1, source_target_pairs={{0,4},{1,17},{2,6},{3,19},{4,0},{5,21},{6,2},{7,23},{8,12},{9,25},... | collective-permute-start | bytes 516104 | tf_op jit(solution)/shard_map/ppermute | solution.py:344
  30.4 0.3 collective-permute-start.15
  30.7 1.7 %collective-permute-start.16 = (bf16[24,3584]{1,0:T(8,128)(2,1)S(1)}, bf16[24,3584]{1,0:T(8,128)(2,1)S(1)}, u32[]{:S(2)}, u32[]{:S(2)}) collective-permute-start(bf16[24,3584]{1,0:T(8,128)(2,1)S(1)} %get-tuple-element.31), channel_id=1, source_target_pairs={{0,6},{1,25},{2,4},{3,27},{4,2},{5,29},{6,0},{7,31},{8,14},{9,17},... | collective-permute-start | bytes 516104 | tf_op jit(solution)/shard_map/ppermute | solution.py:344
  32.4 1.5 %collective-permute-start.11 = (bf16[8,3584]{1,0:T(8,128)(2,1)S(1)}, bf16[8,3584]{1,0:T(8,128)(2,1)S(1)}, u32[]{:S(2)}, u32[]{:S(2)}) collective-permute-start(bf16[8,3584]{1,0:T(8,128)(2,1)S(1)} %get-tuple-element.25), channel_id=1, source_target_pairs={{0,4},{1,17},{2,6},{3,19},{4,0},{5,21},{6,2},{7,23},{8,12},{9,25},... | collective-permute-start | bytes 172040 | tf_op jit(solution)/shard_map/ppermute | solution.py:344
  33.9 0.3 collective-permute-start.12
  34.2 0.1 collective-permute-done.14.refs_1_
  34.3 1.6 %collective-permute-start.13 = (bf16[8,3584]{1,0:T(8,128)(2,1)S(1)}, bf16[8,3584]{1,0:T(8,128)(2,1)S(1)}, u32[]{:S(2)}, u32[]{:S(2)}) collective-permute-start(bf16[8,3584]{1,0:T(8,128)(2,1)S(1)} %get-tuple-element.27), channel_id=1, source_target_pairs={{0,6},{1,25},{2,4},{3,27},{4,2},{5,29},{6,0},{7,31},{8,14},{9,17},... | collective-permute-start | bytes 172040 | tf_op jit(solution)/shard_map/ppermute | solution.py:344
  35.8 0.0 collective-permute-done.15.refs_2_
  35.8 1.8 %collective-permute-done.16.refs_3_ = bf16[24,3584]{1,0:T(8,128)(2,1)S(1)} collective-permute-done((bf16[24,3584]{1,0:T(8,128)(2,1)S(1)}, bf16[24,3584]{1,0:T(8,128)(2,1)S(1)}, u32[]{:S(2)}, u32[]{:S(2)}) %collective-permute-start.16) | collective-permute-done | bytes 172064 | tf_op jit(solution)/shard_map/ppermute | solution.py:344
  37.7 0.1 shard_map.116
  37.8 1.4 %collective-permute-start.17 = (bf16[8,3584]{1,0:T(8,128)(2,1)S(1)}, bf16[8,3584]{1,0:T(8,128)(2,1)S(1)}, u32[]{:S(2)}, u32[]{:S(2)}) collective-permute-start(bf16[8,3584]{1,0:T(8,128)(2,1)S(1)} %get-tuple-element.32), channel_id=1, source_target_pairs={{0,24},{1,7},{2,26},{3,5},{4,28},{5,3},{6,30},{7,1},{8,16},{9,15},... | collective-permute-start | bytes 172040 | tf_op jit(solution)/shard_map/ppermute | solution.py:344
  39.2 1.2 %collective-permute-start.18 = (bf16[8,3584]{1,0:T(8,128)(2,1)S(1)}, bf16[8,3584]{1,0:T(8,128)(2,1)S(1)}, u32[]{:S(2)}, u32[]{:S(2)}) collective-permute-start(bf16[8,3584]{1,0:T(8,128)(2,1)S(1)} %get-tuple-element.33), channel_id=1, source_target_pairs={{0,16},{1,5},{2,18},{3,7},{4,20},{5,1},{6,22},{7,3},{8,24},{9,13},... | collective-permute-start | bytes 172040 | tf_op jit(solution)/shard_map/ppermute | solution.py:344
  40.4 0.0 collective-permute-done.11.refs_1_
  40.4 1.8 %collective-permute-start.19 = (bf16[8,3584]{1,0:T(8,128)(2,1)S(1)}, bf16[8,3584]{1,0:T(8,128)(2,1)S(1)}, u32[]{:S(2)}, u32[]{:S(2)}) collective-permute-start(bf16[8,3584]{1,0:T(8,128)(2,1)S(1)} %get-tuple-element.34), channel_id=1, source_target_pairs={{0,8},{1,3},{2,10},{3,1},{4,12},{5,7},{6,14},{7,5},{8,0},{9,11},{1... | collective-permute-start | bytes 172040 | tf_op jit(solution)/shard_map/ppermute | solution.py:344
  42.2 0.0 collective-permute-done.12.refs_2_
  42.2 0.0 collective-permute-done.13.refs_3_
  42.2 1.6 %collective-permute-done.17.refs_4_ = bf16[8,3584]{1,0:T(8,128)(2,1)S(1)} collective-permute-done((bf16[8,3584]{1,0:T(8,128)(2,1)S(1)}, bf16[8,3584]{1,0:T(8,128)(2,1)S(1)}, u32[]{:S(2)}, u32[]{:S(2)}) %collective-permute-start.17) | collective-permute-done | bytes 57376 | tf_op jit(solution)/shard_map/ppermute | solution.py:344
  43.8 0.7 %collective-permute-done.18.refs_5_ = bf16[8,3584]{1,0:T(8,128)(2,1)S(1)} collective-permute-done((bf16[8,3584]{1,0:T(8,128)(2,1)S(1)}, bf16[8,3584]{1,0:T(8,128)(2,1)S(1)}, u32[]{:S(2)}, u32[]{:S(2)}) %collective-permute-start.18) | collective-permute-done | bytes 57376 | tf_op jit(solution)/shard_map/ppermute | solution.py:344
  44.5 0.6 %collective-permute-done.19.refs_6_ = bf16[8,3584]{1,0:T(8,128)(2,1)S(1)} collective-permute-done((bf16[8,3584]{1,0:T(8,128)(2,1)S(1)}, bf16[8,3584]{1,0:T(8,128)(2,1)S(1)}, u32[]{:S(2)}, u32[]{:S(2)}) %collective-permute-start.19) | collective-permute-done | bytes 57376 | tf_op jit(solution)/shard_map/ppermute | solution.py:344
  45.0 0.7 %shard_map.117 = bf16[8,3584]{1,0:T(8,128)(2,1)} custom-call(bf16[8,3584]{1,0:T(8,128)(2,1)S(1)} %get-tuple-element.24.refs_0_, bf16[8,3584]{1,0:T(8,128)(2,1)S(1)} %collective-permute-done.11.refs_1_, bf16[8,3584]{1,0:T(8,128)(2,1)S(1)} %collective-permute-done.12.refs_2_, bf16[8,3584]{1,0:T(8,128)(2,1)S(1)} %collective-permute-done.13.refs_3_, ...), custom_call_target="tpu_custom_call" | custom-call | flops 200704 | bytes 401408 | tf_op jit(solution)/shard_map/pallas_call | solution.py:312
  (4 shorter events, 0.0 us)
Async XLA Ops:
  1.6 7.8 %collective-permute-start.2 = (bf16[8,3712]{1,0:T(8,128)(2,1)S(1)}, bf16[8,3712]{1,0:T(8,128)(2,1)S(1)}, u32[]{:S(2)}, u32[]{:S(2)}) collective-permute-start(bf16[8,3712]{1,0:T(8,128)(2,1)S(1)} %shard_map.104.refs_0_), channel_id=1, source_target_pairs={{0,24},{1,7},{2,26},{3,5},{4,28},{5,3},{6,30},{7,1},{8,16},{9,15},... | collective-permute-start | bytes 178184 | tf_op jit(solution)/shard_map/ppermute | solution.py:344
  6.7 5.1 %collective-permute-start.1 = (bf16[8,3712]{1,0:T(8,128)(2,1)S(1)}, bf16[8,3712]{1,0:T(8,128)(2,1)S(1)}, u32[]{:S(2)}, u32[]{:S(2)}) collective-permute-start(bf16[8,3712]{1,0:T(8,128)(2,1)S(1)} %shard_map.104.refs_0_), channel_id=1, source_target_pairs={{0,16},{1,5},{2,18},{3,7},{4,20},{5,1},{6,22},{7,3},{8,24},{9,13},... | collective-permute-start | bytes 178184 | tf_op jit(solution)/shard_map/ppermute | solution.py:344
  6.7 5.1 %collective-permute-start = (bf16[8,3712]{1,0:T(8,128)(2,1)S(1)}, bf16[8,3712]{1,0:T(8,128)(2,1)S(1)}, u32[]{:S(2)}, u32[]{:S(2)}) collective-permute-start(bf16[8,3712]{1,0:T(8,128)(2,1)S(1)} %shard_map.104.refs_0_), channel_id=1, source_target_pairs={{0,8},{1,3},{2,10},{3,1},{4,12},{5,7},{6,14},{7,5},{8,0},{9,11},{1... | collective-permute-start | bytes 178184 | tf_op jit(solution)/shard_map/ppermute | solution.py:344
  11.8 8.1 %collective-permute-start.3 = (bf16[32,3712]{1,0:T(8,128)(2,1)S(1)}, bf16[32,3712]{1,0:T(8,128)(2,1)S(1)}, u32[]{:S(2)}, u32[]{:S(2)}) collective-permute-start(bf16[32,3712]{1,0:T(8,128)(2,1)S(1)} %shard_map.106.after_ref.refs_0_), channel_id=1, source_target_pairs={{0,2},{1,9},{2,0},{3,11},{4,6},{5,13},{6,4},{7,15},{8,10},{9,1},{1... | collective-permute-start | bytes 712712 | tf_op jit(solution)/shard_map/ppermute | solution.py:344
  13.6 8.7 %collective-permute-start.4 = (bf16[32,3712]{1,0:T(8,128)(2,1)S(1)}, bf16[32,3712]{1,0:T(8,128)(2,1)S(1)}, u32[]{:S(2)}, u32[]{:S(2)}) collective-permute-start(bf16[32,3712]{1,0:T(8,128)(2,1)S(1)} %shard_map.106.after_ref.refs_0_), channel_id=1, source_target_pairs={{0,4},{1,17},{2,6},{3,19},{4,0},{5,21},{6,2},{7,23},{8,12},{9,25},... | collective-permute-start | bytes 712712 | tf_op jit(solution)/shard_map/ppermute | solution.py:344
  15.1 7.1 %collective-permute-start.5 = (bf16[32,3712]{1,0:T(8,128)(2,1)S(1)}, bf16[32,3712]{1,0:T(8,128)(2,1)S(1)}, u32[]{:S(2)}, u32[]{:S(2)}) collective-permute-start(bf16[32,3712]{1,0:T(8,128)(2,1)S(1)} %shard_map.106.after_ref.refs_0_), channel_id=1, source_target_pairs={{0,6},{1,25},{2,4},{3,27},{4,2},{5,29},{6,0},{7,31},{8,14},{9,17},... | collective-permute-start | bytes 712712 | tf_op jit(solution)/shard_map/ppermute | solution.py:344
  15.4 7.4 %collective-permute-start.6 = (bf16[32,3712]{1,0:T(8,128)(2,1)S(1)}, bf16[32,3712]{1,0:T(8,128)(2,1)S(1)}, u32[]{:S(2)}, u32[]{:S(2)}) collective-permute-start(bf16[32,3712]{1,0:T(8,128)(2,1)S(1)} %shard_map.106.after_ref.refs_0_), channel_id=1, source_target_pairs={{0,1},{1,0},{2,3},{3,2},{4,5},{5,4},{6,7},{7,6},{8,9},{9,8},{10,11... | collective-permute-start | bytes 712712 | tf_op jit(solution)/shard_map/ppermute | solution.py:353
  20.0 2.8 %collective-permute-start.7 = (bf16[32,3712]{1,0:T(8,128)(2,1)S(1)}, bf16[32,3712]{1,0:T(8,128)(2,1)S(1)}, u32[]{:S(2)}, u32[]{:S(2)}) collective-permute-start(bf16[32,3712]{1,0:T(8,128)(2,1)S(1)} %shard_map.108.refs_1_), channel_id=1, source_target_pairs={{0,1},{1,0},{2,3},{3,2},{4,5},{5,4},{6,7},{7,6},{8,9},{9,8},{10,11... | collective-permute-start | bytes 712712 | tf_op jit(solution)/shard_map/ppermute | solution.py:353
  22.3 1.5 %collective-permute-start.8 = (bf16[32,3712]{1,0:T(8,128)(2,1)S(1)}, bf16[32,3712]{1,0:T(8,128)(2,1)S(1)}, u32[]{:S(2)}, u32[]{:S(2)}) collective-permute-start(bf16[32,3712]{1,0:T(8,128)(2,1)S(1)} %shard_map.109.refs_2_), channel_id=1, source_target_pairs={{0,1},{1,0},{2,3},{3,2},{4,5},{5,4},{6,7},{7,6},{8,9},{9,8},{10,11... | collective-permute-start | bytes 712712 | tf_op jit(solution)/shard_map/ppermute | solution.py:353
  22.3 1.8 %collective-permute-start.9 = (bf16[32,3712]{1,0:T(8,128)(2,1)S(1)}, bf16[32,3712]{1,0:T(8,128)(2,1)S(1)}, u32[]{:S(2)}, u32[]{:S(2)}) collective-permute-start(bf16[32,3712]{1,0:T(8,128)(2,1)S(1)} %shard_map.110.refs_3_), channel_id=1, source_target_pairs={{0,1},{1,0},{2,3},{3,2},{4,5},{5,4},{6,7},{7,6},{8,9},{9,8},{10,11... | collective-permute-start | bytes 712712 | tf_op jit(solution)/shard_map/ppermute | solution.py:353
  26.0 2.5 %collective-permute-start.10 = (bf16[128,3584]{1,0:T(8,128)(2,1)S(1)}, bf16[128,3584]{1,0:T(8,128)(2,1)S(1)}, u32[]{:S(2)}, u32[]{:S(2)}) collective-permute-start(bf16[128,3584]{1,0:T(8,128)(2,1)S(1)} %shard_map.114), channel_id=1, source_target_pairs={{0,1},{1,0},{2,3},{3,2},{4,5},{5,4},{6,7},{7,6},{8,9},{9,8},{10,11... | collective-permute-start | bytes 2752520 | tf_op jit(solution)/shard_map/ppermute | solution.py:353
  28.8 5.5 %collective-permute-start.14 = (bf16[24,3584]{1,0:T(8,128)(2,1)S(1)}, bf16[24,3584]{1,0:T(8,128)(2,1)S(1)}, u32[]{:S(2)}, u32[]{:S(2)}) collective-permute-start(bf16[24,3584]{1,0:T(8,128)(2,1)S(1)} %get-tuple-element.29), channel_id=1, source_target_pairs={{0,4},{1,17},{2,6},{3,19},{4,0},{5,21},{6,2},{7,23},{8,12},{9,25},... | collective-permute-start | bytes 516104 | tf_op jit(solution)/shard_map/ppermute | solution.py:344
  30.4 5.5 %collective-permute-start.15 = (bf16[24,3584]{1,0:T(8,128)(2,1)S(1)}, bf16[24,3584]{1,0:T(8,128)(2,1)S(1)}, u32[]{:S(2)}, u32[]{:S(2)}) collective-permute-start(bf16[24,3584]{1,0:T(8,128)(2,1)S(1)} %get-tuple-element.30), channel_id=1, source_target_pairs={{0,2},{1,9},{2,0},{3,11},{4,6},{5,13},{6,4},{7,15},{8,10},{9,1},{1... | collective-permute-start | bytes 516104 | tf_op jit(solution)/shard_map/ppermute | solution.py:344
  30.7 7.0 %collective-permute-start.16 = (bf16[24,3584]{1,0:T(8,128)(2,1)S(1)}, bf16[24,3584]{1,0:T(8,128)(2,1)S(1)}, u32[]{:S(2)}, u32[]{:S(2)}) collective-permute-start(bf16[24,3584]{1,0:T(8,128)(2,1)S(1)} %get-tuple-element.31), channel_id=1, source_target_pairs={{0,6},{1,25},{2,4},{3,27},{4,2},{5,29},{6,0},{7,31},{8,14},{9,17},... | collective-permute-start | bytes 516104 | tf_op jit(solution)/shard_map/ppermute | solution.py:344
  32.4 8.0 %collective-permute-start.11 = (bf16[8,3584]{1,0:T(8,128)(2,1)S(1)}, bf16[8,3584]{1,0:T(8,128)(2,1)S(1)}, u32[]{:S(2)}, u32[]{:S(2)}) collective-permute-start(bf16[8,3584]{1,0:T(8,128)(2,1)S(1)} %get-tuple-element.25), channel_id=1, source_target_pairs={{0,4},{1,17},{2,6},{3,19},{4,0},{5,21},{6,2},{7,23},{8,12},{9,25},... | collective-permute-start | bytes 172040 | tf_op jit(solution)/shard_map/ppermute | solution.py:344
  33.9 8.4 %collective-permute-start.12 = (bf16[8,3584]{1,0:T(8,128)(2,1)S(1)}, bf16[8,3584]{1,0:T(8,128)(2,1)S(1)}, u32[]{:S(2)}, u32[]{:S(2)}) collective-permute-start(bf16[8,3584]{1,0:T(8,128)(2,1)S(1)} %get-tuple-element.26), channel_id=1, source_target_pairs={{0,2},{1,9},{2,0},{3,11},{4,6},{5,13},{6,4},{7,15},{8,10},{9,1},{1... | collective-permute-start | bytes 172040 | tf_op jit(solution)/shard_map/ppermute | solution.py:344
  34.3 8.0 %collective-permute-start.13 = (bf16[8,3584]{1,0:T(8,128)(2,1)S(1)}, bf16[8,3584]{1,0:T(8,128)(2,1)S(1)}, u32[]{:S(2)}, u32[]{:S(2)}) collective-permute-start(bf16[8,3584]{1,0:T(8,128)(2,1)S(1)} %get-tuple-element.27), channel_id=1, source_target_pairs={{0,6},{1,25},{2,4},{3,27},{4,2},{5,29},{6,0},{7,31},{8,14},{9,17},... | collective-permute-start | bytes 172040 | tf_op jit(solution)/shard_map/ppermute | solution.py:344
  37.8 6.1 %collective-permute-start.17 = (bf16[8,3584]{1,0:T(8,128)(2,1)S(1)}, bf16[8,3584]{1,0:T(8,128)(2,1)S(1)}, u32[]{:S(2)}, u32[]{:S(2)}) collective-permute-start(bf16[8,3584]{1,0:T(8,128)(2,1)S(1)} %get-tuple-element.32), channel_id=1, source_target_pairs={{0,24},{1,7},{2,26},{3,5},{4,28},{5,3},{6,30},{7,1},{8,16},{9,15},... | collective-permute-start | bytes 172040 | tf_op jit(solution)/shard_map/ppermute | solution.py:344
  39.2 5.3 %collective-permute-start.18 = (bf16[8,3584]{1,0:T(8,128)(2,1)S(1)}, bf16[8,3584]{1,0:T(8,128)(2,1)S(1)}, u32[]{:S(2)}, u32[]{:S(2)}) collective-permute-start(bf16[8,3584]{1,0:T(8,128)(2,1)S(1)} %get-tuple-element.33), channel_id=1, source_target_pairs={{0,16},{1,5},{2,18},{3,7},{4,20},{5,1},{6,22},{7,3},{8,24},{9,13},... | collective-permute-start | bytes 172040 | tf_op jit(solution)/shard_map/ppermute | solution.py:344
  40.4 4.6 %collective-permute-start.19 = (bf16[8,3584]{1,0:T(8,128)(2,1)S(1)}, bf16[8,3584]{1,0:T(8,128)(2,1)S(1)}, u32[]{:S(2)}, u32[]{:S(2)}) collective-permute-start(bf16[8,3584]{1,0:T(8,128)(2,1)S(1)} %get-tuple-element.34), channel_id=1, source_target_pairs={{0,8},{1,3},{2,10},{3,1},{4,12},{5,7},{6,14},{7,5},{8,0},{9,11},{1... | collective-permute-start | bytes 172040 | tf_op jit(solution)/shard_map/ppermute | solution.py:344

commit v11 on v10

--- a/solution.py
+++ b/solution.py
@@ -355,9 +355,12 @@
     own = pack(hidden_in, expert_routes, route_scores, ep_count)
     near = {k: first(own, k) for k in range(outer - 1, 0, -1)}
     gate, fetched = fetch(expert_gate[0])
-    block = join([own] + [near[k] for k in range(1, outer)], [fetched])
-    steps = [*range(inner - 2, 0, -1), inner - 1]
-    far = {k: second(block, k) for k in steps}
+    last = inner - 1
+    ahead = second(own, last)
+    received = [near[k] for k in range(1, outer)]
+    block, column = join([own, *received], [fetched]), join(received, [ahead])
+    steps = [*range(last - 1, 0, -1), last]
+    far = {k: second(column if k == last else block, k) for k in steps}
     attention_latent, up, down_rows, token = attend(
         query_latent,
         latent_cache,
@@ -365,7 +368,7 @@
         (expert_up[0], expert_down[0]),
         block,
     )
-    pieces = [block] + [tie(far[k], token) for k in range(1, inner)]
+    pieces = [block] + [tie(far[k], token) for k in range(1, last)] + [join([ahead, far[last]], [token])]
     received = [over_cores(p) for p in pieces]
     hidden = hidden_units(pieces, gate, up)
     other = down(hidden_units(received, gate, up), down_rows)

time: 45.9 us -> 47.1 us (1.026)
  starting transfers between devices: 22 us -> 24.3 us
  waiting for transfers between devices: 10.6 us -> 9.5 us
    ppermute x15 -> x16, starting transfers between devices: 20.7 us -> 23.4 us  [swap(): return lax.ppermute(value, ('ep', 'sub'), pairs)]
    ppermute x15 -> x16, waiting for transfers between devices: 8.9 us -> 7.56 us  [swap(): return lax.ppermute(value, ('ep', 'sub'), pairs)]
  transfers between devices with their start and end apart: 20 -> 21, of which waited for: 10 -> 10; matrix products, arithmetic and copies ran while one was open for 0% -> 0% of each run, Pallas kernels for 19% -> 18%
where the time goes in v11:
time: 47.1 us; the launch traced here: 46.9 us
  starting transfers between devices  24.3 us (52%)
  Pallas kernels  12.4 us (26%)
  waiting for transfers between devices  9.5 us (20%)
  between operations  0.77 us (2%)
    ppermute x16, starting transfers between devices, swap(): return lax.ppermute(value, ('ep', 'sub'), pairs)  23.4 us
    ppermute x16, waiting for transfers between devices, swap(): return lax.ppermute(value, ('ep', 'sub'), pairs)  7.56 us
    pallas_call x1, Pallas kernels, attend(): pl.pallas_call(attend_kernel, out_shape=(jax.ShapeDtypeStruct((rows, head...  4.52 us
    pallas_call x2, Pallas kernels, hidden_units(): pl.pallas_call(functools.partial(hidden_kernel, len(pieces)), out_shape=i...  2.47 us
    pallas_call x1, Pallas kernels, fetch(): pl.pallas_call(fetch_kernel, out_shape=(in_vmem(value.shape, value.dtype)...  2.07 us
    ppermute x5, waiting for transfers between devices, over_cores(): return lax.ppermute(value, 'sub', [(i, i ^ 1) for i in range(sub_count)])  1.94 us
    pallas_call x2, Pallas kernels, down(): pl.pallas_call(down_kernel, out_shape=in_vmem((total, model_width), jnp.b...  1.35 us
    pallas_call x3, Pallas kernels, add(): pl.pallas_call(functools.partial(add_kernel, len(values), rows, sizes), o...  0.98 us
  transfers between devices with their start and end apart: 21, of which 10 were waited for; matrix products, arithmetic and copies ran while one was open for 0% of the time, Pallas kernels for 18%

profile of v11, /device:TPU:0, one launch (start us, length us, event | category | flops | bytes accessed | tf_op | source)
XLA Modules:
  0.0 46.9 jit_solution(12528450295322966491)
XLA Ops:
  0.6 0.9 %shard_map.104.refs_0_ = bf16[8,3712]{1,0:T(8,128)(2,1)S(1)} custom-call(bf16[8,3584]{1,0:T(8,128)(2,1)} %hidden_ref.1, s32[8,8]{1,0:T(8,128)} %routes_ref.1, f32[8,8]{1,0:T(8,128)} %scores_ref.1), custom_call_target="tpu_custom_call" | custom-call | flops 65536 | bytes 114688 | tf_op jit(solution)/shard_map/pallas_call | solution.py:133
  1.6 5.1 %collective-permute-start.2 = (bf16[8,3712]{1,0:T(8,128)(2,1)S(1)}, bf16[8,3712]{1,0:T(8,128)(2,1)S(1)}, u32[]{:S(2)}, u32[]{:S(2)}) collective-permute-start(bf16[8,3712]{1,0:T(8,128)(2,1)S(1)} %shard_map.104.refs_0_), channel_id=1, source_target_pairs={{0,24},{1,7},{2,26},{3,5},{4,28},{5,3},{6,30},{7,1},{8,16},{9,15},... | collective-permute-start | bytes 178184 | tf_op jit(solution)/shard_map/ppermute | solution.py:344
  6.7 0.0 collective-permute-start.1
  6.7 0.6 %collective-permute-start = (bf16[8,3712]{1,0:T(8,128)(2,1)S(1)}, bf16[8,3712]{1,0:T(8,128)(2,1)S(1)}, u32[]{:S(2)}, u32[]{:S(2)}) collective-permute-start(bf16[8,3712]{1,0:T(8,128)(2,1)S(1)} %shard_map.104.refs_0_), channel_id=1, source_target_pairs={{0,8},{1,3},{2,10},{3,1},{4,12},{5,7},{6,14},{7,5},{8,0},{9,11},{1... | collective-permute-start | bytes 178184 | tf_op jit(solution)/shard_map/ppermute | solution.py:344
  7.3 2.6 %collective-permute-start.5 = (bf16[8,3712]{1,0:T(8,128)(2,1)S(1)}, bf16[8,3712]{1,0:T(8,128)(2,1)S(1)}, u32[]{:S(2)}, u32[]{:S(2)}) collective-permute-start(bf16[8,3712]{1,0:T(8,128)(2,1)S(1)} %shard_map.104.refs_0_), channel_id=1, source_target_pairs={{0,6},{1,25},{2,4},{3,27},{4,2},{5,29},{6,0},{7,31},{8,14},{9,17},... | collective-permute-start | bytes 178184 | tf_op jit(solution)/shard_map/ppermute | solution.py:344
  9.9 2.1 %shard_map.105 = (bf16[3584,512]{1,0:T(8,128)(2,1)S(1)}, f32[8,128]{1,0:T(8,128)S(1)}) custom-call(bf16[3584,512]{1,0:T(8,128)(2,1)} %bitcast.5), custom_call_target="tpu_custom_call" | custom-call | bytes 3670016 | tf_op jit(solution)/shard_map/pallas_call | solution.py:183
  12.0 0.0 collective-permute-done.2.refs_3_.refs_2_
  12.0 0.0 collective-permute-done.1.refs_2_.refs_1_
  12.0 0.0 collective-permute-done.refs_1_.refs_0_
  12.0 1.5 %collective-permute-start.3 = (bf16[32,3712]{1,0:T(8,128)(2,1)S(1)}, bf16[32,3712]{1,0:T(8,128)(2,1)S(1)}, u32[]{:S(2)}, u32[]{:S(2)}) collective-permute-start(bf16[32,3712]{1,0:T(8,128)(2,1)S(1)} %shard_map.106.after_ref.refs_0_), channel_id=1, source_target_pairs={{0,2},{1,9},{2,0},{3,11},{4,6},{5,13},{6,4},{7,15},{8,10},{9,1},{1... | collective-permute-start | bytes 712712 | tf_op jit(solution)/shard_map/ppermute | solution.py:344
  13.6 1.5 %collective-permute-start.4 = (bf16[32,3712]{1,0:T(8,128)(2,1)S(1)}, bf16[32,3712]{1,0:T(8,128)(2,1)S(1)}, u32[]{:S(2)}, u32[]{:S(2)}) collective-permute-start(bf16[32,3712]{1,0:T(8,128)(2,1)S(1)} %shard_map.106.after_ref.refs_0_), channel_id=1, source_target_pairs={{0,4},{1,17},{2,6},{3,19},{4,0},{5,21},{6,2},{7,23},{8,12},{9,25},... | collective-permute-start | bytes 712712 | tf_op jit(solution)/shard_map/ppermute | solution.py:344
  15.1 0.0 collective-permute-done.5.refs_3_.refs_0_
  15.1 0.6 %collective-permute-start.6 = (bf16[24,3712]{1,0:T(8,128)(2,1)S(1)}, bf16[24,3712]{1,0:T(8,128)(2,1)S(1)}, u32[]{:S(2)}, u32[]{:S(2)}) collective-permute-start(bf16[24,3712]{1,0:T(8,128)(2,1)S(1)} %shard_map.110), channel_id=1, source_target_pairs={{0,6},{1,25},{2,4},{3,27},{4,2},{5,29},{6,0},{7,31},{8,14},{9,17},... | collective-permute-start | bytes 534536 | tf_op jit(solution)/shard_map/ppermute | solution.py:344
  15.7 0.0 collective-permute-start.7
  15.7 4.5 %shard_map.107 = (bf16[4,128,512]{2,1,0:T(8,128)(2,1)}, bf16[3584,512]{1,0:T(8,128)(2,1)S(1)}, bf16[512,3584]{1,0:T(8,128)(2,1)S(1)}, f32[8,128]{1,0:T(8,128)S(1)}) custom-call(s32[4]{0:T(128)} %lengths_hbm.1, bf16[4,576,128]{2,1,0:T(8,128)(2,1)} %bitcast.9, bf16[4,576,256]{2,1,0:T(8,128)(2,1)} %bitcast.8, bf16[3584,512]{1,0:T(8,128)(2,1)} %bitcast.6, ...), custom_call_target="tpu_custom_call" | custom-call | flops 301989888 | bytes 7340032 | tf_op jit(solution)/shard_map/pallas_call | solution.py:74
  20.2 1.4 %collective-permute-done.6.refs_1_ = bf16[24,3712]{1,0:T(8,128)(2,1)S(1)} collective-permute-done((bf16[24,3712]{1,0:T(8,128)(2,1)S(1)}, bf16[24,3712]{1,0:T(8,128)(2,1)S(1)}, u32[]{:S(2)}, u32[]{:S(2)}) %collective-permute-start.6) | collective-permute-done | bytes 178208 | tf_op jit(solution)/shard_map/ppermute | solution.py:344
  21.6 0.1 collective-permute-start.10
  21.7 0.0 collective-permute-done.3.value_ref
  21.7 0.5 %collective-permute-start.8 = (bf16[32,3712]{1,0:T(8,128)(2,1)S(1)}, bf16[32,3712]{1,0:T(8,128)(2,1)S(1)}, u32[]{:S(2)}, u32[]{:S(2)}) collective-permute-start(bf16[32,3712]{1,0:T(8,128)(2,1)S(1)} %shard_map.108.refs_1_), channel_id=1, source_target_pairs={{0,1},{1,0},{2,3},{3,2},{4,5},{5,4},{6,7},{7,6},{8,9},{9,8},{10,11... | collective-permute-start | bytes 712712 | tf_op jit(solution)/shard_map/ppermute | solution.py:353
  22.2 0.0 collective-permute-done.4.value_ref
  22.2 0.1 collective-permute-start.9
  22.3 0.0 collective-permute-done.7.refs_0_
  22.3 0.9 %collective-permute-done.10.refs_3_ = bf16[32,3712]{1,0:T(8,128)(2,1)S(1)} collective-permute-done((bf16[32,3712]{1,0:T(8,128)(2,1)S(1)}, bf16[32,3712]{1,0:T(8,128)(2,1)S(1)}, u32[]{:S(2)}, u32[]{:S(2)}) %collective-permute-start.10) | collective-permute-done | bytes 237600 | tf_op jit(solution)/shard_map/ppermute | solution.py:353
  23.2 0.3 collective-permute-done.8.refs_1_
  23.5 0.3 collective-permute-done.9.refs_2_
  23.8 1.2 %shard_map.114.hidden_ref = bf16[128,512]{1,0:T(8,128)(2,1)S(1)} custom-call(bf16[32,3712]{1,0:T(8,128)(2,1)S(1)} %collective-permute-done.7.refs_0_, bf16[32,3712]{1,0:T(8,128)(2,1)S(1)} %collective-permute-done.8.refs_1_, bf16[32,3712]{1,0:T(8,128)(2,1)S(1)} %collective-permute-done.9.refs_2_, bf16[32,3712]{1,0:T(8,128)(2,1)S(1)} %collective-permute-done.10.refs_3_, ...), custom_call_target="tpu_custom_call" | custom-call | flops 939524096 | bytes 8290304 | tf_op jit(solution)/shard_map/pallas_call | solution.py:247
  25.1 0.7 %shard_map.115 = bf16[128,3584]{1,0:T(8,128)(2,1)S(1)} custom-call(bf16[128,512]{1,0:T(8,128)(2,1)S(1)} %shard_map.114.hidden_ref, bf16[512,3584]{1,0:T(8,128)(2,1)S(1)} %get-tuple-element.23.down_ref), custom_call_target="tpu_custom_call" | custom-call | flops 469762048 | bytes 4587520 | tf_op jit(solution)/shard_map/pallas_call | solution.py:283
  25.8 0.2 collective-permute-start.11
  26.0 1.2 %shard_map.112.hidden_ref = bf16[128,512]{1,0:T(8,128)(2,1)S(1)} custom-call(bf16[32,3712]{1,0:T(8,128)(2,1)S(1)} %shard_map.106.after_ref.refs_0_, bf16[32,3712]{1,0:T(8,128)(2,1)S(1)} %shard_map.108.refs_1_, bf16[32,3712]{1,0:T(8,128)(2,1)S(1)} %shard_map.109.refs_2_, bf16[32,3712]{1,0:T(8,128)(2,1)S(1)} %shard_map.111.refs_3_, ...), custom_call_target="tpu_custom_call" | custom-call | flops 939524096 | bytes 8290304 | tf_op jit(solution)/shard_map/pallas_call | solution.py:247
  27.2 0.7 %shard_map.113.refs_0_ = bf16[128,3584]{1,0:T(8,128)(2,1)S(1)} custom-call(bf16[128,512]{1,0:T(8,128)(2,1)S(1)} %shard_map.112.hidden_ref, bf16[512,3584]{1,0:T(8,128)(2,1)S(1)} %get-tuple-element.23.down_ref), custom_call_target="tpu_custom_call" | custom-call | flops 469762048 | bytes 4587520 | tf_op jit(solution)/shard_map/pallas_call | solution.py:283
  27.9 0.4 collective-permute-done.11.refs_1_
  28.3 0.2 shard_map.116
  28.5 0.8 %collective-permute-start.15 = (bf16[24,3584]{1,0:T(8,128)(2,1)S(1)}, bf16[24,3584]{1,0:T(8,128)(2,1)S(1)}, u32[]{:S(2)}, u32[]{:S(2)}) collective-permute-start(bf16[24,3584]{1,0:T(8,128)(2,1)S(1)} %get-tuple-element.29), channel_id=1, source_target_pairs={{0,4},{1,17},{2,6},{3,19},{4,0},{5,21},{6,2},{7,23},{8,12},{9,25},... | collective-permute-start | bytes 516104 | tf_op jit(solution)/shard_map/ppermute | solution.py:344
  29.3 1.1 %collective-permute-start.16 = (bf16[24,3584]{1,0:T(8,128)(2,1)S(1)}, bf16[24,3584]{1,0:T(8,128)(2,1)S(1)}, u32[]{:S(2)}, u32[]{:S(2)}) collective-permute-start(bf16[24,3584]{1,0:T(8,128)(2,1)S(1)} %get-tuple-element.30), channel_id=1, source_target_pairs={{0,2},{1,9},{2,0},{3,11},{4,6},{5,13},{6,4},{7,15},{8,10},{9,1},{1... | collective-permute-start | bytes 516104 | tf_op jit(solution)/shard_map/ppermute | solution.py:344
  30.4 1.7 %collective-permute-start.17 = (bf16[24,3584]{1,0:T(8,128)(2,1)S(1)}, bf16[24,3584]{1,0:T(8,128)(2,1)S(1)}, u32[]{:S(2)}, u32[]{:S(2)}) collective-permute-start(bf16[24,3584]{1,0:T(8,128)(2,1)S(1)} %get-tuple-element.31), channel_id=1, source_target_pairs={{0,6},{1,25},{2,4},{3,27},{4,2},{5,29},{6,0},{7,31},{8,14},{9,17},... | collective-permute-start | bytes 516104 | tf_op jit(solution)/shard_map/ppermute | solution.py:344
  32.1 0.8 %collective-permute-start.12 = (bf16[8,3584]{1,0:T(8,128)(2,1)S(1)}, bf16[8,3584]{1,0:T(8,128)(2,1)S(1)}, u32[]{:S(2)}, u32[]{:S(2)}) collective-permute-start(bf16[8,3584]{1,0:T(8,128)(2,1)S(1)} %get-tuple-element.25), channel_id=1, source_target_pairs={{0,4},{1,17},{2,6},{3,19},{4,0},{5,21},{6,2},{7,23},{8,12},{9,25},... | collective-permute-start | bytes 172040 | tf_op jit(solution)/shard_map/ppermute | solution.py:344
  32.8 1.1 %collective-permute-start.13 = (bf16[8,3584]{1,0:T(8,128)(2,1)S(1)}, bf16[8,3584]{1,0:T(8,128)(2,1)S(1)}, u32[]{:S(2)}, u32[]{:S(2)}) collective-permute-start(bf16[8,3584]{1,0:T(8,128)(2,1)S(1)} %get-tuple-element.26), channel_id=1, source_target_pairs={{0,2},{1,9},{2,0},{3,11},{4,6},{5,13},{6,4},{7,15},{8,10},{9,1},{1... | collective-permute-start | bytes 172040 | tf_op jit(solution)/shard_map/ppermute | solution.py:344
  33.9 0.1 collective-permute-done.15.refs_1_
  34.0 1.6 %collective-permute-start.14 = (bf16[8,3584]{1,0:T(8,128)(2,1)S(1)}, bf16[8,3584]{1,0:T(8,128)(2,1)S(1)}, u32[]{:S(2)}, u32[]{:S(2)}) collective-permute-start(bf16[8,3584]{1,0:T(8,128)(2,1)S(1)} %get-tuple-element.27), channel_id=1, source_target_pairs={{0,6},{1,25},{2,4},{3,27},{4,2},{5,29},{6,0},{7,31},{8,14},{9,17},... | collective-permute-start | bytes 172040 | tf_op jit(solution)/shard_map/ppermute | solution.py:344
  35.6 0.0 collective-permute-done.16.refs_2_
  35.6 1.8 %collective-permute-done.17.refs_3_ = bf16[24,3584]{1,0:T(8,128)(2,1)S(1)} collective-permute-done((bf16[24,3584]{1,0:T(8,128)(2,1)S(1)}, bf16[24,3584]{1,0:T(8,128)(2,1)S(1)}, u32[]{:S(2)}, u32[]{:S(2)}) %collective-permute-start.17) | collective-permute-done | bytes 172064 | tf_op jit(solution)/shard_map/ppermute | solution.py:344
  37.4 0.1 shard_map.117
  37.5 2.5 %collective-permute-start.18 = (bf16[8,3584]{1,0:T(8,128)(2,1)S(1)}, bf16[8,3584]{1,0:T(8,128)(2,1)S(1)}, u32[]{:S(2)}, u32[]{:S(2)}) collective-permute-start(bf16[8,3584]{1,0:T(8,128)(2,1)S(1)} %get-tuple-element.32), channel_id=1, source_target_pairs={{0,24},{1,7},{2,26},{3,5},{4,28},{5,3},{6,30},{7,1},{8,16},{9,15},... | collective-permute-start | bytes 172040 | tf_op jit(solution)/shard_map/ppermute | solution.py:344
  40.0 1.7 %collective-permute-start.19 = (bf16[8,3584]{1,0:T(8,128)(2,1)S(1)}, bf16[8,3584]{1,0:T(8,128)(2,1)S(1)}, u32[]{:S(2)}, u32[]{:S(2)}) collective-permute-start(bf16[8,3584]{1,0:T(8,128)(2,1)S(1)} %get-tuple-element.33), channel_id=1, source_target_pairs={{0,16},{1,5},{2,18},{3,7},{4,20},{5,1},{6,22},{7,3},{8,24},{9,13},... | collective-permute-start | bytes 172040 | tf_op jit(solution)/shard_map/ppermute | solution.py:344
  41.7 0.0 collective-permute-done.12.refs_1_
  41.7 0.2 collective-permute-start.20
  41.9 0.0 collective-permute-done.13.refs_2_
  42.0 0.0 collective-permute-done.14.refs_3_
  42.0 1.6 %collective-permute-done.18.refs_4_ = bf16[8,3584]{1,0:T(8,128)(2,1)S(1)} collective-permute-done((bf16[8,3584]{1,0:T(8,128)(2,1)S(1)}, bf16[8,3584]{1,0:T(8,128)(2,1)S(1)}, u32[]{:S(2)}, u32[]{:S(2)}) %collective-permute-start.18) | collective-permute-done | bytes 57376 | tf_op jit(solution)/shard_map/ppermute | solution.py:344
  43.6 2.2 %collective-permute-done.19.refs_5_ = bf16[8,3584]{1,0:T(8,128)(2,1)S(1)} collective-permute-done((bf16[8,3584]{1,0:T(8,128)(2,1)S(1)}, bf16[8,3584]{1,0:T(8,128)(2,1)S(1)}, u32[]{:S(2)}, u32[]{:S(2)}) %collective-permute-start.19) | collective-permute-done | bytes 57376 | tf_op jit(solution)/shard_map/ppermute | solution.py:344
  45.8 0.4 collective-permute-done.20.refs_6_
  46.2 0.7 %shard_map.118 = bf16[8,3584]{1,0:T(8,128)(2,1)} custom-call(bf16[8,3584]{1,0:T(8,128)(2,1)S(1)} %get-tuple-element.24.refs_0_, bf16[8,3584]{1,0:T(8,128)(2,1)S(1)} %collective-permute-done.12.refs_1_, bf16[8,3584]{1,0:T(8,128)(2,1)S(1)} %collective-permute-done.13.refs_2_, bf16[8,3584]{1,0:T(8,128)(2,1)S(1)} %collective-permute-done.14.refs_3_, ...), custom_call_target="tpu_custom_call" | custom-call | flops 200704 | bytes 401408 | tf_op jit(solution)/shard_map/pallas_call | solution.py:312
  (5 shorter events, 0.1 us)
Async XLA Ops:
  1.6 10.4 %collective-permute-start.2 = (bf16[8,3712]{1,0:T(8,128)(2,1)S(1)}, bf16[8,3712]{1,0:T(8,128)(2,1)S(1)}, u32[]{:S(2)}, u32[]{:S(2)}) collective-permute-start(bf16[8,3712]{1,0:T(8,128)(2,1)S(1)} %shard_map.104.refs_0_), channel_id=1, source_target_pairs={{0,24},{1,7},{2,26},{3,5},{4,28},{5,3},{6,30},{7,1},{8,16},{9,15},... | collective-permute-start | bytes 178184 | tf_op jit(solution)/shard_map/ppermute | solution.py:344
  6.7 5.3 %collective-permute-start.1 = (bf16[8,3712]{1,0:T(8,128)(2,1)S(1)}, bf16[8,3712]{1,0:T(8,128)(2,1)S(1)}, u32[]{:S(2)}, u32[]{:S(2)}) collective-permute-start(bf16[8,3712]{1,0:T(8,128)(2,1)S(1)} %shard_map.104.refs_0_), channel_id=1, source_target_pairs={{0,16},{1,5},{2,18},{3,7},{4,20},{5,1},{6,22},{7,3},{8,24},{9,13},... | collective-permute-start | bytes 178184 | tf_op jit(solution)/shard_map/ppermute | solution.py:344
  6.7 5.3 %collective-permute-start = (bf16[8,3712]{1,0:T(8,128)(2,1)S(1)}, bf16[8,3712]{1,0:T(8,128)(2,1)S(1)}, u32[]{:S(2)}, u32[]{:S(2)}) collective-permute-start(bf16[8,3712]{1,0:T(8,128)(2,1)S(1)} %shard_map.104.refs_0_), channel_id=1, source_target_pairs={{0,8},{1,3},{2,10},{3,1},{4,12},{5,7},{6,14},{7,5},{8,0},{9,11},{1... | collective-permute-start | bytes 178184 | tf_op jit(solution)/shard_map/ppermute | solution.py:344
  7.3 7.8 %collective-permute-start.5 = (bf16[8,3712]{1,0:T(8,128)(2,1)S(1)}, bf16[8,3712]{1,0:T(8,128)(2,1)S(1)}, u32[]{:S(2)}, u32[]{:S(2)}) collective-permute-start(bf16[8,3712]{1,0:T(8,128)(2,1)S(1)} %shard_map.104.refs_0_), channel_id=1, source_target_pairs={{0,6},{1,25},{2,4},{3,27},{4,2},{5,29},{6,0},{7,31},{8,14},{9,17},... | collective-permute-start | bytes 178184 | tf_op jit(solution)/shard_map/ppermute | solution.py:344
  12.0 9.6 %collective-permute-start.3 = (bf16[32,3712]{1,0:T(8,128)(2,1)S(1)}, bf16[32,3712]{1,0:T(8,128)(2,1)S(1)}, u32[]{:S(2)}, u32[]{:S(2)}) collective-permute-start(bf16[32,3712]{1,0:T(8,128)(2,1)S(1)} %shard_map.106.after_ref.refs_0_), channel_id=1, source_target_pairs={{0,2},{1,9},{2,0},{3,11},{4,6},{5,13},{6,4},{7,15},{8,10},{9,1},{1... | collective-permute-start | bytes 712712 | tf_op jit(solution)/shard_map/ppermute | solution.py:344
  13.6 8.6 %collective-permute-start.4 = (bf16[32,3712]{1,0:T(8,128)(2,1)S(1)}, bf16[32,3712]{1,0:T(8,128)(2,1)S(1)}, u32[]{:S(2)}, u32[]{:S(2)}) collective-permute-start(bf16[32,3712]{1,0:T(8,128)(2,1)S(1)} %shard_map.106.after_ref.refs_0_), channel_id=1, source_target_pairs={{0,4},{1,17},{2,6},{3,19},{4,0},{5,21},{6,2},{7,23},{8,12},{9,25},... | collective-permute-start | bytes 712712 | tf_op jit(solution)/shard_map/ppermute | solution.py:344
  15.1 6.5 %collective-permute-start.6 = (bf16[24,3712]{1,0:T(8,128)(2,1)S(1)}, bf16[24,3712]{1,0:T(8,128)(2,1)S(1)}, u32[]{:S(2)}, u32[]{:S(2)}) collective-permute-start(bf16[24,3712]{1,0:T(8,128)(2,1)S(1)} %shard_map.110), channel_id=1, source_target_pairs={{0,6},{1,25},{2,4},{3,27},{4,2},{5,29},{6,0},{7,31},{8,14},{9,17},... | collective-permute-start | bytes 534536 | tf_op jit(solution)/shard_map/ppermute | solution.py:344
  15.7 6.6 %collective-permute-start.7 = (bf16[32,3712]{1,0:T(8,128)(2,1)S(1)}, bf16[32,3712]{1,0:T(8,128)(2,1)S(1)}, u32[]{:S(2)}, u32[]{:S(2)}) collective-permute-start(bf16[32,3712]{1,0:T(8,128)(2,1)S(1)} %shard_map.106.after_ref.refs_0_), channel_id=1, source_target_pairs={{0,1},{1,0},{2,3},{3,2},{4,5},{5,4},{6,7},{7,6},{8,9},{9,8},{10,11... | collective-permute-start | bytes 712712 | tf_op jit(solution)/shard_map/ppermute | solution.py:353
  21.6 1.6 %collective-permute-start.10 = (bf16[32,3712]{1,0:T(8,128)(2,1)S(1)}, bf16[32,3712]{1,0:T(8,128)(2,1)S(1)}, u32[]{:S(2)}, u32[]{:S(2)}) collective-permute-start(bf16[32,3712]{1,0:T(8,128)(2,1)S(1)} %shard_map.111.refs_3_), channel_id=1, source_target_pairs={{0,1},{1,0},{2,3},{3,2},{4,5},{5,4},{6,7},{7,6},{8,9},{9,8},{10,11... | collective-permute-start | bytes 712712 | tf_op jit(solution)/shard_map/ppermute | solution.py:353
  21.7 1.8 %collective-permute-start.8 = (bf16[32,3712]{1,0:T(8,128)(2,1)S(1)}, bf16[32,3712]{1,0:T(8,128)(2,1)S(1)}, u32[]{:S(2)}, u32[]{:S(2)}) collective-permute-start(bf16[32,3712]{1,0:T(8,128)(2,1)S(1)} %shard_map.108.refs_1_), channel_id=1, source_target_pairs={{0,1},{1,0},{2,3},{3,2},{4,5},{5,4},{6,7},{7,6},{8,9},{9,8},{10,11... | collective-permute-start | bytes 712712 | tf_op jit(solution)/shard_map/ppermute | solution.py:353
  22.2 1.7 %collective-permute-start.9 = (bf16[32,3712]{1,0:T(8,128)(2,1)S(1)}, bf16[32,3712]{1,0:T(8,128)(2,1)S(1)}, u32[]{:S(2)}, u32[]{:S(2)}) collective-permute-start(bf16[32,3712]{1,0:T(8,128)(2,1)S(1)} %shard_map.109.refs_2_), channel_id=1, source_target_pairs={{0,1},{1,0},{2,3},{3,2},{4,5},{5,4},{6,7},{7,6},{8,9},{9,8},{10,11... | collective-permute-start | bytes 712712 | tf_op jit(solution)/shard_map/ppermute | solution.py:353
  25.8 2.5 %collective-permute-start.11 = (bf16[128,3584]{1,0:T(8,128)(2,1)S(1)}, bf16[128,3584]{1,0:T(8,128)(2,1)S(1)}, u32[]{:S(2)}, u32[]{:S(2)}) collective-permute-start(bf16[128,3584]{1,0:T(8,128)(2,1)S(1)} %shard_map.115), channel_id=1, source_target_pairs={{0,1},{1,0},{2,3},{3,2},{4,5},{5,4},{6,7},{7,6},{8,9},{9,8},{10,11... | collective-permute-start | bytes 2752520 | tf_op jit(solution)/shard_map/ppermute | solution.py:353
  28.5 5.5 %collective-permute-start.15 = (bf16[24,3584]{1,0:T(8,128)(2,1)S(1)}, bf16[24,3584]{1,0:T(8,128)(2,1)S(1)}, u32[]{:S(2)}, u32[]{:S(2)}) collective-permute-start(bf16[24,3584]{1,0:T(8,128)(2,1)S(1)} %get-tuple-element.29), channel_id=1, source_target_pairs={{0,4},{1,17},{2,6},{3,19},{4,0},{5,21},{6,2},{7,23},{8,12},{9,25},... | collective-permute-start | bytes 516104 | tf_op jit(solution)/shard_map/ppermute | solution.py:344
  29.3 6.2 %collective-permute-start.16 = (bf16[24,3584]{1,0:T(8,128)(2,1)S(1)}, bf16[24,3584]{1,0:T(8,128)(2,1)S(1)}, u32[]{:S(2)}, u32[]{:S(2)}) collective-permute-start(bf16[24,3584]{1,0:T(8,128)(2,1)S(1)} %get-tuple-element.30), channel_id=1, source_target_pairs={{0,2},{1,9},{2,0},{3,11},{4,6},{5,13},{6,4},{7,15},{8,10},{9,1},{1... | collective-permute-start | bytes 516104 | tf_op jit(solution)/shard_map/ppermute | solution.py:344
  30.4 7.0 %collective-permute-start.17 = (bf16[24,3584]{1,0:T(8,128)(2,1)S(1)}, bf16[24,3584]{1,0:T(8,128)(2,1)S(1)}, u32[]{:S(2)}, u32[]{:S(2)}) collective-permute-start(bf16[24,3584]{1,0:T(8,128)(2,1)S(1)} %get-tuple-element.31), channel_id=1, source_target_pairs={{0,6},{1,25},{2,4},{3,27},{4,2},{5,29},{6,0},{7,31},{8,14},{9,17},... | collective-permute-start | bytes 516104 | tf_op jit(solution)/shard_map/ppermute | solution.py:344
  32.1 9.6 %collective-permute-start.12 = (bf16[8,3584]{1,0:T(8,128)(2,1)S(1)}, bf16[8,3584]{1,0:T(8,128)(2,1)S(1)}, u32[]{:S(2)}, u32[]{:S(2)}) collective-permute-start(bf16[8,3584]{1,0:T(8,128)(2,1)S(1)} %get-tuple-element.25), channel_id=1, source_target_pairs={{0,4},{1,17},{2,6},{3,19},{4,0},{5,21},{6,2},{7,23},{8,12},{9,25},... | collective-permute-start | bytes 172040 | tf_op jit(solution)/shard_map/ppermute | solution.py:344
  32.8 9.1 %collective-permute-start.13 = (bf16[8,3584]{1,0:T(8,128)(2,1)S(1)}, bf16[8,3584]{1,0:T(8,128)(2,1)S(1)}, u32[]{:S(2)}, u32[]{:S(2)}) collective-permute-start(bf16[8,3584]{1,0:T(8,128)(2,1)S(1)} %get-tuple-element.26), channel_id=1, source_target_pairs={{0,2},{1,9},{2,0},{3,11},{4,6},{5,13},{6,4},{7,15},{8,10},{9,1},{1... | collective-permute-start | bytes 172040 | tf_op jit(solution)/shard_map/ppermute | solution.py:344
  34.0 8.0 %collective-permute-start.14 = (bf16[8,3584]{1,0:T(8,128)(2,1)S(1)}, bf16[8,3584]{1,0:T(8,128)(2,1)S(1)}, u32[]{:S(2)}, u32[]{:S(2)}) collective-permute-start(bf16[8,3584]{1,0:T(8,128)(2,1)S(1)} %get-tuple-element.27), channel_id=1, source_target_pairs={{0,6},{1,25},{2,4},{3,27},{4,2},{5,29},{6,0},{7,31},{8,14},{9,17},... | collective-permute-start | bytes 172040 | tf_op jit(solution)/shard_map/ppermute | solution.py:344
  37.5 6.1 %collective-permute-start.18 = (bf16[8,3584]{1,0:T(8,128)(2,1)S(1)}, bf16[8,3584]{1,0:T(8,128)(2,1)S(1)}, u32[]{:S(2)}, u32[]{:S(2)}) collective-permute-start(bf16[8,3584]{1,0:T(8,128)(2,1)S(1)} %get-tuple-element.32), channel_id=1, source_target_pairs={{0,24},{1,7},{2,26},{3,5},{4,28},{5,3},{6,30},{7,1},{8,16},{9,15},... | collective-permute-start | bytes 172040 | tf_op jit(solution)/shard_map/ppermute | solution.py:344
  40.0 5.8 %collective-permute-start.19 = (bf16[8,3584]{1,0:T(8,128)(2,1)S(1)}, bf16[8,3584]{1,0:T(8,128)(2,1)S(1)}, u32[]{:S(2)}, u32[]{:S(2)}) collective-permute-start(bf16[8,3584]{1,0:T(8,128)(2,1)S(1)} %get-tuple-element.33), channel_id=1, source_target_pairs={{0,16},{1,5},{2,18},{3,7},{4,20},{5,1},{6,22},{7,3},{8,24},{9,13},... | collective-permute-start | bytes 172040 | tf_op jit(solution)/shard_map/ppermute | solution.py:344
  41.7 4.5 %collective-permute-start.20 = (bf16[8,3584]{1,0:T(8,128)(2,1)S(1)}, bf16[8,3584]{1,0:T(8,128)(2,1)S(1)}, u32[]{:S(2)}, u32[]{:S(2)}) collective-permute-start(bf16[8,3584]{1,0:T(8,128)(2,1)S(1)} %get-tuple-element.34), channel_id=1, source_target_pairs={{0,8},{1,3},{2,10},{3,1},{4,12},{5,7},{6,14},{7,5},{8,0},{9,11},{1... | collective-permute-start | bytes 172040 | tf_op jit(solution)/shard_map/ppermute | solution.py:344

commit v12 on v10

--- a/solution.py
+++ b/solution.py
@@ -356,7 +356,7 @@
     near = {k: first(own, k) for k in range(outer - 1, 0, -1)}
     gate, fetched = fetch(expert_gate[0])
     block = join([own] + [near[k] for k in range(1, outer)], [fetched])
-    steps = [*range(inner - 2, 0, -1), inner - 1]
+    steps = [*range(2, inner), 1]
     far = {k: second(block, k) for k in steps}
     attention_latent, up, down_rows, token = attend(
         query_latent,

time: 45.9 us -> 45.8 us (level)
  starting transfers between devices: 22 us -> 21.4 us
  waiting for transfers between devices: 10.6 us -> 11.2 us
    ppermute x15, starting transfers between devices: 20.7 us -> 20.1 us  [swap(): return lax.ppermute(value, ('ep', 'sub'), pairs)]
    ppermute x15, waiting for transfers between devices: 8.9 us -> 9.51 us  [swap(): return lax.ppermute(value, ('ep', 'sub'), pairs)]
  transfers between devices with their start and end apart: 20 -> 20, of which waited for: 10 -> 11; matrix products, arithmetic and copies ran while one was open for 0% -> 0% of each run, Pallas kernels for 19% -> 19%
where the time goes in v12:
time: 45.8 us; the launch traced here: 45.7 us
  starting transfers between devices  21.4 us (47%)
  Pallas kernels  12.3 us (27%)
  waiting for transfers between devices  11.2 us (24%)
  between operations  0.74 us (2%)
    ppermute x15, starting transfers between devices, swap(): return lax.ppermute(value, ('ep', 'sub'), pairs)  20.1 us
    ppermute x15, waiting for transfers between devices, swap(): return lax.ppermute(value, ('ep', 'sub'), pairs)  9.51 us
    pallas_call x1, Pallas kernels, attend(): pl.pallas_call(attend_kernel, out_shape=(jax.ShapeDtypeStruct((rows, head...  4.52 us
    pallas_call x2, Pallas kernels, hidden_units(): pl.pallas_call(functools.partial(hidden_kernel, len(pieces)), out_shape=i...  2.47 us
    pallas_call x1, Pallas kernels, fetch(): pl.pallas_call(fetch_kernel, out_shape=(in_vmem(value.shape, value.dtype)...  2.07 us
    ppermute x5, waiting for transfers between devices, over_cores(): return lax.ppermute(value, 'sub', [(i, i ^ 1) for i in range(sub_count)])  1.71 us
    pallas_call x2, Pallas kernels, down(): pl.pallas_call(down_kernel, out_shape=in_vmem((total, model_width), jnp.b...  1.34 us
    ppermute x5, starting transfers between devices, over_cores(): return lax.ppermute(value, 'sub', [(i, i ^ 1) for i in range(sub_count)])  1.32 us
  transfers between devices with their start and end apart: 20, of which 11 were waited for; matrix products, arithmetic and copies ran while one was open for 0% of the time, Pallas kernels for 19%

profile of v12, /device:TPU:0, one launch (start us, length us, event | category | flops | bytes accessed | tf_op | source)
XLA Modules:
  0.0 45.7 jit_solution(4027497067133499865)
XLA Ops:
  0.6 0.9 %shard_map.104.refs_0_ = bf16[8,3712]{1,0:T(8,128)(2,1)S(1)} custom-call(bf16[8,3584]{1,0:T(8,128)(2,1)} %hidden_ref.1, s32[8,8]{1,0:T(8,128)} %routes_ref.1, f32[8,8]{1,0:T(8,128)} %scores_ref.1), custom_call_target="tpu_custom_call" | custom-call | flops 65536 | bytes 114688 | tf_op jit(solution)/shard_map/pallas_call | solution.py:133
  1.6 5.1 %collective-permute-start.2 = (bf16[8,3712]{1,0:T(8,128)(2,1)S(1)}, bf16[8,3712]{1,0:T(8,128)(2,1)S(1)}, u32[]{:S(2)}, u32[]{:S(2)}) collective-permute-start(bf16[8,3712]{1,0:T(8,128)(2,1)S(1)} %shard_map.104.refs_0_), channel_id=1, source_target_pairs={{0,24},{1,7},{2,26},{3,5},{4,28},{5,3},{6,30},{7,1},{8,16},{9,15},... | collective-permute-start | bytes 178184 | tf_op jit(solution)/shard_map/ppermute | solution.py:344
  6.7 0.0 collective-permute-start.1
  6.7 0.6 %collective-permute-start = (bf16[8,3712]{1,0:T(8,128)(2,1)S(1)}, bf16[8,3712]{1,0:T(8,128)(2,1)S(1)}, u32[]{:S(2)}, u32[]{:S(2)}) collective-permute-start(bf16[8,3712]{1,0:T(8,128)(2,1)S(1)} %shard_map.104.refs_0_), channel_id=1, source_target_pairs={{0,8},{1,3},{2,10},{3,1},{4,12},{5,7},{6,14},{7,5},{8,0},{9,11},{1... | collective-permute-start | bytes 178184 | tf_op jit(solution)/shard_map/ppermute | solution.py:344
  7.3 2.1 %shard_map.105 = (bf16[3584,512]{1,0:T(8,128)(2,1)S(1)}, f32[8,128]{1,0:T(8,128)S(1)}) custom-call(bf16[3584,512]{1,0:T(8,128)(2,1)} %bitcast.5), custom_call_target="tpu_custom_call" | custom-call | bytes 3670016 | tf_op jit(solution)/shard_map/pallas_call | solution.py:183
  9.4 0.0 collective-permute-done.2.refs_3_
  9.4 2.4 %collective-permute-done.1.refs_2_ = bf16[8,3712]{1,0:T(8,128)(2,1)S(1)} collective-permute-done((bf16[8,3712]{1,0:T(8,128)(2,1)S(1)}, bf16[8,3712]{1,0:T(8,128)(2,1)S(1)}, u32[]{:S(2)}, u32[]{:S(2)}) %collective-permute-start.1) | collective-permute-done | bytes 59424 | tf_op jit(solution)/shard_map/ppermute | solution.py:344
  11.8 0.0 collective-permute-done.refs_1_
  11.8 1.8 %collective-permute-start.3 = (bf16[32,3712]{1,0:T(8,128)(2,1)S(1)}, bf16[32,3712]{1,0:T(8,128)(2,1)S(1)}, u32[]{:S(2)}, u32[]{:S(2)}) collective-permute-start(bf16[32,3712]{1,0:T(8,128)(2,1)S(1)} %shard_map.106.after_ref.refs_0_), channel_id=1, source_target_pairs={{0,2},{1,9},{2,0},{3,11},{4,6},{5,13},{6,4},{7,15},{8,10},{9,1},{1... | collective-permute-start | bytes 712712 | tf_op jit(solution)/shard_map/ppermute | solution.py:344
  13.6 1.5 %collective-permute-start.4 = (bf16[32,3712]{1,0:T(8,128)(2,1)S(1)}, bf16[32,3712]{1,0:T(8,128)(2,1)S(1)}, u32[]{:S(2)}, u32[]{:S(2)}) collective-permute-start(bf16[32,3712]{1,0:T(8,128)(2,1)S(1)} %shard_map.106.after_ref.refs_0_), channel_id=1, source_target_pairs={{0,4},{1,17},{2,6},{3,19},{4,0},{5,21},{6,2},{7,23},{8,12},{9,25},... | collective-permute-start | bytes 712712 | tf_op jit(solution)/shard_map/ppermute | solution.py:344
  15.1 0.3 collective-permute-start.5
  15.4 0.0 collective-permute-start.6
  15.4 4.5 %shard_map.107 = (bf16[4,128,512]{2,1,0:T(8,128)(2,1)}, bf16[3584,512]{1,0:T(8,128)(2,1)S(1)}, bf16[512,3584]{1,0:T(8,128)(2,1)S(1)}, f32[8,128]{1,0:T(8,128)S(1)}) custom-call(s32[4]{0:T(128)} %lengths_hbm.1, bf16[4,576,128]{2,1,0:T(8,128)(2,1)} %bitcast.9, bf16[4,576,256]{2,1,0:T(8,128)(2,1)} %bitcast.8, bf16[3584,512]{1,0:T(8,128)(2,1)} %bitcast.6, ...), custom_call_target="tpu_custom_call" | custom-call | flops 301989888 | bytes 7340032 | tf_op jit(solution)/shard_map/pallas_call | solution.py:74
  19.9 0.0 collective-permute-done.3.value_ref
  20.0 0.6 %collective-permute-start.7 = (bf16[32,3712]{1,0:T(8,128)(2,1)S(1)}, bf16[32,3712]{1,0:T(8,128)(2,1)S(1)}, u32[]{:S(2)}, u32[]{:S(2)}) collective-permute-start(bf16[32,3712]{1,0:T(8,128)(2,1)S(1)} %shard_map.108.refs_1_), channel_id=1, source_target_pairs={{0,1},{1,0},{2,3},{3,2},{4,5},{5,4},{6,7},{7,6},{8,9},{9,8},{10,11... | collective-permute-start | bytes 712712 | tf_op jit(solution)/shard_map/ppermute | solution.py:353
  20.5 1.7 %collective-permute-done.4.value_ref = bf16[32,3712]{1,0:T(8,128)(2,1)S(1)} collective-permute-done((bf16[32,3712]{1,0:T(8,128)(2,1)S(1)}, bf16[32,3712]{1,0:T(8,128)(2,1)S(1)}, u32[]{:S(2)}, u32[]{:S(2)}) %collective-permute-start.4) | collective-permute-done | bytes 237600 | tf_op jit(solution)/shard_map/ppermute | solution.py:344
  22.3 0.0 collective-permute-start.8
  22.3 0.0 collective-permute-done.5.value_ref
  22.3 0.5 %collective-permute-start.9 = (bf16[32,3712]{1,0:T(8,128)(2,1)S(1)}, bf16[32,3712]{1,0:T(8,128)(2,1)S(1)}, u32[]{:S(2)}, u32[]{:S(2)}) collective-permute-start(bf16[32,3712]{1,0:T(8,128)(2,1)S(1)} %shard_map.110.refs_3_), channel_id=1, source_target_pairs={{0,1},{1,0},{2,3},{3,2},{4,5},{5,4},{6,7},{7,6},{8,9},{9,8},{10,11... | collective-permute-start | bytes 712712 | tf_op jit(solution)/shard_map/ppermute | solution.py:353
  22.8 0.0 collective-permute-done.6.refs_0_
  22.8 0.0 collective-permute-done.7.refs_1_
  22.8 1.0 %collective-permute-done.8.refs_2_ = bf16[32,3712]{1,0:T(8,128)(2,1)S(1)} collective-permute-done((bf16[32,3712]{1,0:T(8,128)(2,1)S(1)}, bf16[32,3712]{1,0:T(8,128)(2,1)S(1)}, u32[]{:S(2)}, u32[]{:S(2)}) %collective-permute-start.8) | collective-permute-done | bytes 237600 | tf_op jit(solution)/shard_map/ppermute | solution.py:353
  23.8 0.3 collective-permute-done.9.refs_3_
  24.1 1.2 %shard_map.113.hidden_ref = bf16[128,512]{1,0:T(8,128)(2,1)S(1)} custom-call(bf16[32,3712]{1,0:T(8,128)(2,1)S(1)} %collective-permute-done.6.refs_0_, bf16[32,3712]{1,0:T(8,128)(2,1)S(1)} %collective-permute-done.7.refs_1_, bf16[32,3712]{1,0:T(8,128)(2,1)S(1)} %collective-permute-done.8.refs_2_, bf16[32,3712]{1,0:T(8,128)(2,1)S(1)} %collective-permute-done.9.refs_3_, ...), custom_call_target="tpu_custom_call" | custom-call | flops 939524096 | bytes 8290304 | tf_op jit(solution)/shard_map/pallas_call | solution.py:247
  25.4 0.7 %shard_map.114 = bf16[128,3584]{1,0:T(8,128)(2,1)S(1)} custom-call(bf16[128,512]{1,0:T(8,128)(2,1)S(1)} %shard_map.113.hidden_ref, bf16[512,3584]{1,0:T(8,128)(2,1)S(1)} %get-tuple-element.23.down_ref), custom_call_target="tpu_custom_call" | custom-call | flops 469762048 | bytes 4587520 | tf_op jit(solution)/shard_map/pallas_call | solution.py:283
  26.0 0.2 collective-permute-start.10
  26.3 1.2 %shard_map.111.hidden_ref = bf16[128,512]{1,0:T(8,128)(2,1)S(1)} custom-call(bf16[32,3712]{1,0:T(8,128)(2,1)S(1)} %shard_map.106.after_ref.refs_0_, bf16[32,3712]{1,0:T(8,128)(2,1)S(1)} %shard_map.108.refs_1_, bf16[32,3712]{1,0:T(8,128)(2,1)S(1)} %shard_map.109.refs_2_, bf16[32,3712]{1,0:T(8,128)(2,1)S(1)} %shard_map.110.refs_3_, ...), custom_call_target="tpu_custom_call" | custom-call | flops 939524096 | bytes 8290304 | tf_op jit(solution)/shard_map/pallas_call | solution.py:247
  27.5 0.7 %shard_map.112.refs_0_ = bf16[128,3584]{1,0:T(8,128)(2,1)S(1)} custom-call(bf16[128,512]{1,0:T(8,128)(2,1)S(1)} %shard_map.111.hidden_ref, bf16[512,3584]{1,0:T(8,128)(2,1)S(1)} %get-tuple-element.23.down_ref), custom_call_target="tpu_custom_call" | custom-call | flops 469762048 | bytes 4587520 | tf_op jit(solution)/shard_map/pallas_call | solution.py:283
  28.2 0.4 collective-permute-done.10.refs_1_
  28.6 0.2 shard_map.115
  28.8 1.6 %collective-permute-start.14 = (bf16[24,3584]{1,0:T(8,128)(2,1)S(1)}, bf16[24,3584]{1,0:T(8,128)(2,1)S(1)}, u32[]{:S(2)}, u32[]{:S(2)}) collective-permute-start(bf16[24,3584]{1,0:T(8,128)(2,1)S(1)} %get-tuple-element.29), channel_id=1, source_target_pairs={{0,4},{1,17},{2,6},{3,19},{4,0},{5,21},{6,2},{7,23},{8,12},{9,25},... | collective-permute-start | bytes 516104 | tf_op jit(solution)/shard_map/ppermute | solution.py:344
  30.4 0.6 %collective-permute-start.15 = (bf16[24,3584]{1,0:T(8,128)(2,1)S(1)}, bf16[24,3584]{1,0:T(8,128)(2,1)S(1)}, u32[]{:S(2)}, u32[]{:S(2)}) collective-permute-start(bf16[24,3584]{1,0:T(8,128)(2,1)S(1)} %get-tuple-element.30), channel_id=1, source_target_pairs={{0,6},{1,25},{2,4},{3,27},{4,2},{5,29},{6,0},{7,31},{8,14},{9,17},... | collective-permute-start | bytes 516104 | tf_op jit(solution)/shard_map/ppermute | solution.py:344
  30.9 1.4 %collective-permute-start.16 = (bf16[24,3584]{1,0:T(8,128)(2,1)S(1)}, bf16[24,3584]{1,0:T(8,128)(2,1)S(1)}, u32[]{:S(2)}, u32[]{:S(2)}) collective-permute-start(bf16[24,3584]{1,0:T(8,128)(2,1)S(1)} %get-tuple-element.31), channel_id=1, source_target_pairs={{0,2},{1,9},{2,0},{3,11},{4,6},{5,13},{6,4},{7,15},{8,10},{9,1},{1... | collective-permute-start | bytes 516104 | tf_op jit(solution)/shard_map/ppermute | solution.py:344
  32.4 1.5 %collective-permute-start.11 = (bf16[8,3584]{1,0:T(8,128)(2,1)S(1)}, bf16[8,3584]{1,0:T(8,128)(2,1)S(1)}, u32[]{:S(2)}, u32[]{:S(2)}) collective-permute-start(bf16[8,3584]{1,0:T(8,128)(2,1)S(1)} %get-tuple-element.25), channel_id=1, source_target_pairs={{0,4},{1,17},{2,6},{3,19},{4,0},{5,21},{6,2},{7,23},{8,12},{9,25},... | collective-permute-start | bytes 172040 | tf_op jit(solution)/shard_map/ppermute | solution.py:344
  33.9 0.6 %collective-permute-start.12 = (bf16[8,3584]{1,0:T(8,128)(2,1)S(1)}, bf16[8,3584]{1,0:T(8,128)(2,1)S(1)}, u32[]{:S(2)}, u32[]{:S(2)}) collective-permute-start(bf16[8,3584]{1,0:T(8,128)(2,1)S(1)} %get-tuple-element.26), channel_id=1, source_target_pairs={{0,6},{1,25},{2,4},{3,27},{4,2},{5,29},{6,0},{7,31},{8,14},{9,17},... | collective-permute-start | bytes 172040 | tf_op jit(solution)/shard_map/ppermute | solution.py:344
  34.4 0.7 %collective-permute-done.14.refs_1_ = bf16[24,3584]{1,0:T(8,128)(2,1)S(1)} collective-permute-done((bf16[24,3584]{1,0:T(8,128)(2,1)S(1)}, bf16[24,3584]{1,0:T(8,128)(2,1)S(1)}, u32[]{:S(2)}, u32[]{:S(2)}) %collective-permute-start.14) | collective-permute-done | bytes 172064 | tf_op jit(solution)/shard_map/ppermute | solution.py:344
  35.2 0.7 %collective-permute-start.13 = (bf16[8,3584]{1,0:T(8,128)(2,1)S(1)}, bf16[8,3584]{1,0:T(8,128)(2,1)S(1)}, u32[]{:S(2)}, u32[]{:S(2)}) collective-permute-start(bf16[8,3584]{1,0:T(8,128)(2,1)S(1)} %get-tuple-element.27), channel_id=1, source_target_pairs={{0,2},{1,9},{2,0},{3,11},{4,6},{5,13},{6,4},{7,15},{8,10},{9,1},{1... | collective-permute-start | bytes 172040 | tf_op jit(solution)/shard_map/ppermute | solution.py:344
  35.8 0.9 %collective-permute-done.15.refs_2_ = bf16[24,3584]{1,0:T(8,128)(2,1)S(1)} collective-permute-done((bf16[24,3584]{1,0:T(8,128)(2,1)S(1)}, bf16[24,3584]{1,0:T(8,128)(2,1)S(1)}, u32[]{:S(2)}, u32[]{:S(2)}) %collective-permute-start.15) | collective-permute-done | bytes 172064 | tf_op jit(solution)/shard_map/ppermute | solution.py:344
  36.8 0.9 %collective-permute-done.16.refs_3_ = bf16[24,3584]{1,0:T(8,128)(2,1)S(1)} collective-permute-done((bf16[24,3584]{1,0:T(8,128)(2,1)S(1)}, bf16[24,3584]{1,0:T(8,128)(2,1)S(1)}, u32[]{:S(2)}, u32[]{:S(2)}) %collective-permute-start.16) | collective-permute-done | bytes 172064 | tf_op jit(solution)/shard_map/ppermute | solution.py:344
  37.6 0.1 shard_map.116
  37.7 1.4 %collective-permute-start.17 = (bf16[8,3584]{1,0:T(8,128)(2,1)S(1)}, bf16[8,3584]{1,0:T(8,128)(2,1)S(1)}, u32[]{:S(2)}, u32[]{:S(2)}) collective-permute-start(bf16[8,3584]{1,0:T(8,128)(2,1)S(1)} %get-tuple-element.32), channel_id=1, source_target_pairs={{0,24},{1,7},{2,26},{3,5},{4,28},{5,3},{6,30},{7,1},{8,16},{9,15},... | collective-permute-start | bytes 172040 | tf_op jit(solution)/shard_map/ppermute | solution.py:344
  39.1 1.2 %collective-permute-start.18 = (bf16[8,3584]{1,0:T(8,128)(2,1)S(1)}, bf16[8,3584]{1,0:T(8,128)(2,1)S(1)}, u32[]{:S(2)}, u32[]{:S(2)}) collective-permute-start(bf16[8,3584]{1,0:T(8,128)(2,1)S(1)} %get-tuple-element.33), channel_id=1, source_target_pairs={{0,16},{1,5},{2,18},{3,7},{4,20},{5,1},{6,22},{7,3},{8,24},{9,13},... | collective-permute-start | bytes 172040 | tf_op jit(solution)/shard_map/ppermute | solution.py:344
  40.3 0.0 collective-permute-done.11.refs_1_
  40.3 1.8 %collective-permute-start.19 = (bf16[8,3584]{1,0:T(8,128)(2,1)S(1)}, bf16[8,3584]{1,0:T(8,128)(2,1)S(1)}, u32[]{:S(2)}, u32[]{:S(2)}) collective-permute-start(bf16[8,3584]{1,0:T(8,128)(2,1)S(1)} %get-tuple-element.34), channel_id=1, source_target_pairs={{0,8},{1,3},{2,10},{3,1},{4,12},{5,7},{6,14},{7,5},{8,0},{9,11},{1... | collective-permute-start | bytes 172040 | tf_op jit(solution)/shard_map/ppermute | solution.py:344
  42.2 0.0 collective-permute-done.12.refs_2_
  42.2 0.0 collective-permute-done.13.refs_3_
  42.2 1.6 %collective-permute-done.17.refs_4_ = bf16[8,3584]{1,0:T(8,128)(2,1)S(1)} collective-permute-done((bf16[8,3584]{1,0:T(8,128)(2,1)S(1)}, bf16[8,3584]{1,0:T(8,128)(2,1)S(1)}, u32[]{:S(2)}, u32[]{:S(2)}) %collective-permute-start.17) | collective-permute-done | bytes 57376 | tf_op jit(solution)/shard_map/ppermute | solution.py:344
  43.8 0.7 %collective-permute-done.18.refs_5_ = bf16[8,3584]{1,0:T(8,128)(2,1)S(1)} collective-permute-done((bf16[8,3584]{1,0:T(8,128)(2,1)S(1)}, bf16[8,3584]{1,0:T(8,128)(2,1)S(1)}, u32[]{:S(2)}, u32[]{:S(2)}) %collective-permute-start.18) | collective-permute-done | bytes 57376 | tf_op jit(solution)/shard_map/ppermute | solution.py:344
  44.4 0.6 %collective-permute-done.19.refs_6_ = bf16[8,3584]{1,0:T(8,128)(2,1)S(1)} collective-permute-done((bf16[8,3584]{1,0:T(8,128)(2,1)S(1)}, bf16[8,3584]{1,0:T(8,128)(2,1)S(1)}, u32[]{:S(2)}, u32[]{:S(2)}) %collective-permute-start.19) | collective-permute-done | bytes 57376 | tf_op jit(solution)/shard_map/ppermute | solution.py:344
  45.0 0.7 %shard_map.117 = bf16[8,3584]{1,0:T(8,128)(2,1)} custom-call(bf16[8,3584]{1,0:T(8,128)(2,1)S(1)} %get-tuple-element.24.refs_0_, bf16[8,3584]{1,0:T(8,128)(2,1)S(1)} %collective-permute-done.11.refs_1_, bf16[8,3584]{1,0:T(8,128)(2,1)S(1)} %collective-permute-done.12.refs_2_, bf16[8,3584]{1,0:T(8,128)(2,1)S(1)} %collective-permute-done.13.refs_3_, ...), custom_call_target="tpu_custom_call" | custom-call | flops 200704 | bytes 401408 | tf_op jit(solution)/shard_map/pallas_call | solution.py:312
  (4 shorter events, 0.0 us)
Async XLA Ops:
  1.6 7.8 %collective-permute-start.2 = (bf16[8,3712]{1,0:T(8,128)(2,1)S(1)}, bf16[8,3712]{1,0:T(8,128)(2,1)S(1)}, u32[]{:S(2)}, u32[]{:S(2)}) collective-permute-start(bf16[8,3712]{1,0:T(8,128)(2,1)S(1)} %shard_map.104.refs_0_), channel_id=1, source_target_pairs={{0,24},{1,7},{2,26},{3,5},{4,28},{5,3},{6,30},{7,1},{8,16},{9,15},... | collective-permute-start | bytes 178184 | tf_op jit(solution)/shard_map/ppermute | solution.py:344
  6.7 5.1 %collective-permute-start.1 = (bf16[8,3712]{1,0:T(8,128)(2,1)S(1)}, bf16[8,3712]{1,0:T(8,128)(2,1)S(1)}, u32[]{:S(2)}, u32[]{:S(2)}) collective-permute-start(bf16[8,3712]{1,0:T(8,128)(2,1)S(1)} %shard_map.104.refs_0_), channel_id=1, source_target_pairs={{0,16},{1,5},{2,18},{3,7},{4,20},{5,1},{6,22},{7,3},{8,24},{9,13},... | collective-permute-start | bytes 178184 | tf_op jit(solution)/shard_map/ppermute | solution.py:344
  6.7 5.1 %collective-permute-start = (bf16[8,3712]{1,0:T(8,128)(2,1)S(1)}, bf16[8,3712]{1,0:T(8,128)(2,1)S(1)}, u32[]{:S(2)}, u32[]{:S(2)}) collective-permute-start(bf16[8,3712]{1,0:T(8,128)(2,1)S(1)} %shard_map.104.refs_0_), channel_id=1, source_target_pairs={{0,8},{1,3},{2,10},{3,1},{4,12},{5,7},{6,14},{7,5},{8,0},{9,11},{1... | collective-permute-start | bytes 178184 | tf_op jit(solution)/shard_map/ppermute | solution.py:344
  11.8 8.1 %collective-permute-start.3 = (bf16[32,3712]{1,0:T(8,128)(2,1)S(1)}, bf16[32,3712]{1,0:T(8,128)(2,1)S(1)}, u32[]{:S(2)}, u32[]{:S(2)}) collective-permute-start(bf16[32,3712]{1,0:T(8,128)(2,1)S(1)} %shard_map.106.after_ref.refs_0_), channel_id=1, source_target_pairs={{0,2},{1,9},{2,0},{3,11},{4,6},{5,13},{6,4},{7,15},{8,10},{9,1},{1... | collective-permute-start | bytes 712712 | tf_op jit(solution)/shard_map/ppermute | solution.py:344
  13.6 8.7 %collective-permute-start.4 = (bf16[32,3712]{1,0:T(8,128)(2,1)S(1)}, bf16[32,3712]{1,0:T(8,128)(2,1)S(1)}, u32[]{:S(2)}, u32[]{:S(2)}) collective-permute-start(bf16[32,3712]{1,0:T(8,128)(2,1)S(1)} %shard_map.106.after_ref.refs_0_), channel_id=1, source_target_pairs={{0,4},{1,17},{2,6},{3,19},{4,0},{5,21},{6,2},{7,23},{8,12},{9,25},... | collective-permute-start | bytes 712712 | tf_op jit(solution)/shard_map/ppermute | solution.py:344
  15.1 7.1 %collective-permute-start.5 = (bf16[32,3712]{1,0:T(8,128)(2,1)S(1)}, bf16[32,3712]{1,0:T(8,128)(2,1)S(1)}, u32[]{:S(2)}, u32[]{:S(2)}) collective-permute-start(bf16[32,3712]{1,0:T(8,128)(2,1)S(1)} %shard_map.106.after_ref.refs_0_), channel_id=1, source_target_pairs={{0,6},{1,25},{2,4},{3,27},{4,2},{5,29},{6,0},{7,31},{8,14},{9,17},... | collective-permute-start | bytes 712712 | tf_op jit(solution)/shard_map/ppermute | solution.py:344
  15.4 7.4 %collective-permute-start.6 = (bf16[32,3712]{1,0:T(8,128)(2,1)S(1)}, bf16[32,3712]{1,0:T(8,128)(2,1)S(1)}, u32[]{:S(2)}, u32[]{:S(2)}) collective-permute-start(bf16[32,3712]{1,0:T(8,128)(2,1)S(1)} %shard_map.106.after_ref.refs_0_), channel_id=1, source_target_pairs={{0,1},{1,0},{2,3},{3,2},{4,5},{5,4},{6,7},{7,6},{8,9},{9,8},{10,11... | collective-permute-start | bytes 712712 | tf_op jit(solution)/shard_map/ppermute | solution.py:353
  20.0 2.8 %collective-permute-start.7 = (bf16[32,3712]{1,0:T(8,128)(2,1)S(1)}, bf16[32,3712]{1,0:T(8,128)(2,1)S(1)}, u32[]{:S(2)}, u32[]{:S(2)}) collective-permute-start(bf16[32,3712]{1,0:T(8,128)(2,1)S(1)} %shard_map.108.refs_1_), channel_id=1, source_target_pairs={{0,1},{1,0},{2,3},{3,2},{4,5},{5,4},{6,7},{7,6},{8,9},{9,8},{10,11... | collective-permute-start | bytes 712712 | tf_op jit(solution)/shard_map/ppermute | solution.py:353
  22.3 1.5 %collective-permute-start.8 = (bf16[32,3712]{1,0:T(8,128)(2,1)S(1)}, bf16[32,3712]{1,0:T(8,128)(2,1)S(1)}, u32[]{:S(2)}, u32[]{:S(2)}) collective-permute-start(bf16[32,3712]{1,0:T(8,128)(2,1)S(1)} %shard_map.109.refs_2_), channel_id=1, source_target_pairs={{0,1},{1,0},{2,3},{3,2},{4,5},{5,4},{6,7},{7,6},{8,9},{9,8},{10,11... | collective-permute-start | bytes 712712 | tf_op jit(solution)/shard_map/ppermute | solution.py:353
  22.3 1.8 %collective-permute-start.9 = (bf16[32,3712]{1,0:T(8,128)(2,1)S(1)}, bf16[32,3712]{1,0:T(8,128)(2,1)S(1)}, u32[]{:S(2)}, u32[]{:S(2)}) collective-permute-start(bf16[32,3712]{1,0:T(8,128)(2,1)S(1)} %shard_map.110.refs_3_), channel_id=1, source_target_pairs={{0,1},{1,0},{2,3},{3,2},{4,5},{5,4},{6,7},{7,6},{8,9},{9,8},{10,11... | collective-permute-start | bytes 712712 | tf_op jit(solution)/shard_map/ppermute | solution.py:353
  26.0 2.5 %collective-permute-start.10 = (bf16[128,3584]{1,0:T(8,128)(2,1)S(1)}, bf16[128,3584]{1,0:T(8,128)(2,1)S(1)}, u32[]{:S(2)}, u32[]{:S(2)}) collective-permute-start(bf16[128,3584]{1,0:T(8,128)(2,1)S(1)} %shard_map.114), channel_id=1, source_target_pairs={{0,1},{1,0},{2,3},{3,2},{4,5},{5,4},{6,7},{7,6},{8,9},{9,8},{10,11... | collective-permute-start | bytes 2752520 | tf_op jit(solution)/shard_map/ppermute | solution.py:353
  28.8 6.4 %collective-permute-start.14 = (bf16[24,3584]{1,0:T(8,128)(2,1)S(1)}, bf16[24,3584]{1,0:T(8,128)(2,1)S(1)}, u32[]{:S(2)}, u32[]{:S(2)}) collective-permute-start(bf16[24,3584]{1,0:T(8,128)(2,1)S(1)} %get-tuple-element.29), channel_id=1, source_target_pairs={{0,4},{1,17},{2,6},{3,19},{4,0},{5,21},{6,2},{7,23},{8,12},{9,25},... | collective-permute-start | bytes 516104 | tf_op jit(solution)/shard_map/ppermute | solution.py:344
  30.4 6.4 %collective-permute-start.15 = (bf16[24,3584]{1,0:T(8,128)(2,1)S(1)}, bf16[24,3584]{1,0:T(8,128)(2,1)S(1)}, u32[]{:S(2)}, u32[]{:S(2)}) collective-permute-start(bf16[24,3584]{1,0:T(8,128)(2,1)S(1)} %get-tuple-element.30), channel_id=1, source_target_pairs={{0,6},{1,25},{2,4},{3,27},{4,2},{5,29},{6,0},{7,31},{8,14},{9,17},... | collective-permute-start | bytes 516104 | tf_op jit(solution)/shard_map/ppermute | solution.py:344
  30.9 6.7 %collective-permute-start.16 = (bf16[24,3584]{1,0:T(8,128)(2,1)S(1)}, bf16[24,3584]{1,0:T(8,128)(2,1)S(1)}, u32[]{:S(2)}, u32[]{:S(2)}) collective-permute-start(bf16[24,3584]{1,0:T(8,128)(2,1)S(1)} %get-tuple-element.31), channel_id=1, source_target_pairs={{0,2},{1,9},{2,0},{3,11},{4,6},{5,13},{6,4},{7,15},{8,10},{9,1},{1... | collective-permute-start | bytes 516104 | tf_op jit(solution)/shard_map/ppermute | solution.py:344
  32.4 8.0 %collective-permute-start.11 = (bf16[8,3584]{1,0:T(8,128)(2,1)S(1)}, bf16[8,3584]{1,0:T(8,128)(2,1)S(1)}, u32[]{:S(2)}, u32[]{:S(2)}) collective-permute-start(bf16[8,3584]{1,0:T(8,128)(2,1)S(1)} %get-tuple-element.25), channel_id=1, source_target_pairs={{0,4},{1,17},{2,6},{3,19},{4,0},{5,21},{6,2},{7,23},{8,12},{9,25},... | collective-permute-start | bytes 172040 | tf_op jit(solution)/shard_map/ppermute | solution.py:344
  33.9 8.3 %collective-permute-start.12 = (bf16[8,3584]{1,0:T(8,128)(2,1)S(1)}, bf16[8,3584]{1,0:T(8,128)(2,1)S(1)}, u32[]{:S(2)}, u32[]{:S(2)}) collective-permute-start(bf16[8,3584]{1,0:T(8,128)(2,1)S(1)} %get-tuple-element.26), channel_id=1, source_target_pairs={{0,6},{1,25},{2,4},{3,27},{4,2},{5,29},{6,0},{7,31},{8,14},{9,17},... | collective-permute-start | bytes 172040 | tf_op jit(solution)/shard_map/ppermute | solution.py:344
  35.2 7.0 %collective-permute-start.13 = (bf16[8,3584]{1,0:T(8,128)(2,1)S(1)}, bf16[8,3584]{1,0:T(8,128)(2,1)S(1)}, u32[]{:S(2)}, u32[]{:S(2)}) collective-permute-start(bf16[8,3584]{1,0:T(8,128)(2,1)S(1)} %get-tuple-element.27), channel_id=1, source_target_pairs={{0,2},{1,9},{2,0},{3,11},{4,6},{5,13},{6,4},{7,15},{8,10},{9,1},{1... | collective-permute-start | bytes 172040 | tf_op jit(solution)/shard_map/ppermute | solution.py:344
  37.7 6.1 %collective-permute-start.17 = (bf16[8,3584]{1,0:T(8,128)(2,1)S(1)}, bf16[8,3584]{1,0:T(8,128)(2,1)S(1)}, u32[]{:S(2)}, u32[]{:S(2)}) collective-permute-start(bf16[8,3584]{1,0:T(8,128)(2,1)S(1)} %get-tuple-element.32), channel_id=1, source_target_pairs={{0,24},{1,7},{2,26},{3,5},{4,28},{5,3},{6,30},{7,1},{8,16},{9,15},... | collective-permute-start | bytes 172040 | tf_op jit(solution)/shard_map/ppermute | solution.py:344
  39.1 5.3 %collective-permute-start.18 = (bf16[8,3584]{1,0:T(8,128)(2,1)S(1)}, bf16[8,3584]{1,0:T(8,128)(2,1)S(1)}, u32[]{:S(2)}, u32[]{:S(2)}) collective-permute-start(bf16[8,3584]{1,0:T(8,128)(2,1)S(1)} %get-tuple-element.33), channel_id=1, source_target_pairs={{0,16},{1,5},{2,18},{3,7},{4,20},{5,1},{6,22},{7,3},{8,24},{9,13},... | collective-permute-start | bytes 172040 | tf_op jit(solution)/shard_map/ppermute | solution.py:344
  40.3 4.6 %collective-permute-start.19 = (bf16[8,3584]{1,0:T(8,128)(2,1)S(1)}, bf16[8,3584]{1,0:T(8,128)(2,1)S(1)}, u32[]{:S(2)}, u32[]{:S(2)}) collective-permute-start(bf16[8,3584]{1,0:T(8,128)(2,1)S(1)} %get-tuple-element.34), channel_id=1, source_target_pairs={{0,8},{1,3},{2,10},{3,1},{4,12},{5,7},{6,14},{7,5},{8,0},{9,11},{1... | collective-permute-start | bytes 172040 | tf_op jit(solution)/shard_map/ppermute | solution.py:344

commit v13 on v12

--- a/solution.py
+++ b/solution.py
@@ -259,39 +259,66 @@
     )(*(held(v) for v in (*pieces, expert_gate, expert_up)))
 
 
-def down_kernel(hidden_ref, down_ref, out_ref):
-    total, model_width = out_ref.shape
+def down_kernel(first, hidden_ref, down_ref, out_ref):
+    total, width = out_ref.shape
     block = min(total, 256)
     step = 512
 
-    def results_of(cols):
+    def results_of(source, cols):
         for i in range(total // block):
             rows = slice(i * block, (i + 1) * block)
-            value = jnp.dot(hidden_ref[rows, :], down_ref[:, cols], preferred_element_type=jnp.float32)
+            value = jnp.dot(hidden_ref[rows, :], down_ref[:, source], preferred_element_type=jnp.float32)
             out_ref[rows, cols] = value.astype(jnp.bfloat16)
 
     if total == block:
-        for c in range(model_width // step):
-            results_of(slice(c * step, (c + 1) * step))
+        for c in range(0, width, step):
+            results_of(slice(first + c, first + c + step), slice(c, c + step))
     else:
-        pl.loop(0, model_width // step)(lambda c: results_of(pl.ds(pl.multiple_of(c * step, step), step)))
-
-
-def down(hidden, expert_down):
+
+        @pl.loop(0, width // step)
+        def _(c):
+            at = pl.multiple_of(c * step, step)
+            results_of(pl.ds(pl.multiple_of(first + at, step), step), pl.ds(at, step))
+
+
+def down(hidden, expert_down, first, last):
     total, units = hidden.shape
-    model_width = expert_down.shape[1]
-    return pl.pallas_call(
-        down_kernel,
-        out_shape=in_vmem((total, model_width), jnp.bfloat16),
+    width = last - first
+    return pl.pallas_call(
+        functools.partial(down_kernel, first),
+        out_shape=in_vmem((total, width), jnp.bfloat16),
         in_specs=[VMEM] * 2,
         out_specs=VMEM,
         compiler_params=pltpu.CompilerParams(vmem_limit_bytes=8 << 20),
         cost_estimate=pl.CostEstimate(
-            flops=2 * total * model_width * units,
-            bytes_accessed=2 * model_width * units + 2 * total * model_width,
+            flops=2 * total * width * units,
+            bytes_accessed=2 * width * units + 2 * total * width,
             transcendentals=0,
         ),
     )(held(hidden), held(expert_down))
+
+
+def merge_kernel(count, sizes, mine_ref, *refs):
+    left = 0
+    for part_ref in refs[:count]:
+        width = part_ref.shape[1]
+        total = mine_ref[:, left : left + width].astype(jnp.float32) + part_ref[...].astype(jnp.float32)
+        low = 0
+        for out_ref, size in zip(refs[count:], sizes, strict=True):
+            out_ref[:, left : left + width] = total[low : low + size].astype(jnp.bfloat16)
+            low += size
+        left += width
+
+
+def merge(mine, parts, sizes):
+    return pl.pallas_call(
+        functools.partial(merge_kernel, len(parts), sizes),
+        out_shape=tuple(in_vmem((size, mine.shape[1]), jnp.bfloat16) for size in sizes),
+        in_specs=[VMEM] * (1 + len(parts)),
+        out_specs=(VMEM,) * len(sizes),
+        compiler_params=pltpu.CompilerParams(vmem_limit_bytes=(4 << 20) + 8 * mine.size),
+        cost_estimate=pl.CostEstimate(flops=mine.size, bytes_accessed=6 * mine.size, transcendentals=0),
+    )(held(mine), *(held(p) for p in parts))
 
 
 def add_kernel(count, rows, sizes, *refs):
@@ -368,11 +395,14 @@
     pieces = [block] + [tie(far[k], token) for k in range(1, inner)]
     received = [over_cores(p) for p in pieces]
     hidden = hidden_units(pieces, gate, up)
-    other = down(hidden_units(received, gate, up), down_rows)
-    mine = down(hidden, down_rows)
+    partner = hidden_units(received, gate, up)
+    cut = model_width // 1024 * 512
+    other = [down(partner, down_rows, first, last) for first, last in ((0, cut), (cut, model_width))]
+    other = [over_cores(part) for part in other]
+    mine = down(hidden, down_rows, 0, model_width)
 
     size = (outer - 1) * tok_rows
-    kept, column, *parts = add([mine, over_cores(other)], [(0, mine.shape[0])] * 2, [tok_rows, size] * inner)
+    kept, column, *parts = merge(mine, other, [tok_rows, size] * inner)
     far = [second(parts[2 * k - 1], k) for k in steps]
     side = [second(parts[2 * k - 2], k) for k in steps]
     near = add([column, *far], [(0, size)] * inner, [tok_rows] * (outer - 1))

time: 45.8 us -> 46.1 us (level)
    ppermute x5 -> x6, starting transfers between devices: 1.32 us -> 1.71 us  [over_cores(): return lax.ppermute(value, 'sub', [(i, i ^ 1) for i in range(sub_count)])]
    pallas_call x2 -> x4, Pallas kernels: 1.34 us -> 1.72 us  [the longest x3 1.51 us: down(): pl.pallas_call(functools.partial(down_kernel, first), out_shape=in_vmem((...]
    ppermute x5 -> x6, waiting for transfers between devices: 1.71 us -> 1.33 us  [over_cores(): return lax.ppermute(value, 'sub', [(i, i ^ 1) for i in range(sub_count)])]
    pallas_call x3 -> x2, Pallas kernels: 0.98 us -> 0.77 us  [add(): pl.pallas_call(functools.partial(add_kernel, len(values), rows, sizes), o...]
  transfers between devices with their start and end apart: 20 -> 21, of which waited for: 11 -> 10; matrix products, arithmetic and copies ran while one was open for 0% -> 0% of each run, Pallas kernels for 19% -> 20%
where the time goes in v13:
time: 46.1 us; the launch traced here: 45.9 us
  starting transfers between devices  21.8 us (47%)
  Pallas kernels  12.5 us (27%)
  waiting for transfers between devices  10.8 us (23%)
  between operations  0.77 us (2%)
    ppermute x15, starting transfers between devices, swap(): return lax.ppermute(value, ('ep', 'sub'), pairs)  20.1 us
    ppermute x15, waiting for transfers between devices, swap(): return lax.ppermute(value, ('ep', 'sub'), pairs)  9.51 us
    pallas_call x1, Pallas kernels, attend(): pl.pallas_call(attend_kernel, out_shape=(jax.ShapeDtypeStruct((rows, head...  4.52 us
    pallas_call x2, Pallas kernels, hidden_units(): pl.pallas_call(functools.partial(hidden_kernel, len(pieces)), out_shape=i...  2.47 us
    pallas_call x1, Pallas kernels, fetch(): pl.pallas_call(fetch_kernel, out_shape=(in_vmem(value.shape, value.dtype)...  2.07 us
    ppermute x6, starting transfers between devices, over_cores(): return lax.ppermute(value, 'sub', [(i, i ^ 1) for i in range(sub_count)])  1.71 us
    pallas_call x3, Pallas kernels, down(): pl.pallas_call(functools.partial(down_kernel, first), out_shape=in_vmem((...  1.51 us
    ppermute x6, waiting for transfers between devices, over_cores(): return lax.ppermute(value, 'sub', [(i, i ^ 1) for i in range(sub_count)])  1.33 us
  transfers between devices with their start and end apart: 21, of which 10 were waited for; matrix products, arithmetic and copies ran while one was open for 0% of the time, Pallas kernels for 20%

profile of v13, /device:TPU:0, one launch (start us, length us, event | category | flops | bytes accessed | tf_op | source)
XLA Modules:
  0.0 45.9 jit_solution(4786243388170815084)
XLA Ops:
  0.6 0.9 %shard_map.104.refs_0_ = bf16[8,3712]{1,0:T(8,128)(2,1)S(1)} custom-call(bf16[8,3584]{1,0:T(8,128)(2,1)} %hidden_ref.1, s32[8,8]{1,0:T(8,128)} %routes_ref.1, f32[8,8]{1,0:T(8,128)} %scores_ref.1), custom_call_target="tpu_custom_call" | custom-call | flops 65536 | bytes 114688 | tf_op jit(solution)/shard_map/pallas_call | solution.py:133
  1.6 5.1 %collective-permute-start.2 = (bf16[8,3712]{1,0:T(8,128)(2,1)S(1)}, bf16[8,3712]{1,0:T(8,128)(2,1)S(1)}, u32[]{:S(2)}, u32[]{:S(2)}) collective-permute-start(bf16[8,3712]{1,0:T(8,128)(2,1)S(1)} %shard_map.104.refs_0_), channel_id=1, source_target_pairs={{0,24},{1,7},{2,26},{3,5},{4,28},{5,3},{6,30},{7,1},{8,16},{9,15},... | collective-permute-start | bytes 178184 | tf_op jit(solution)/shard_map/ppermute | solution.py:371
  6.7 0.0 collective-permute-start.1
  6.7 0.6 %collective-permute-start = (bf16[8,3712]{1,0:T(8,128)(2,1)S(1)}, bf16[8,3712]{1,0:T(8,128)(2,1)S(1)}, u32[]{:S(2)}, u32[]{:S(2)}) collective-permute-start(bf16[8,3712]{1,0:T(8,128)(2,1)S(1)} %shard_map.104.refs_0_), channel_id=1, source_target_pairs={{0,8},{1,3},{2,10},{3,1},{4,12},{5,7},{6,14},{7,5},{8,0},{9,11},{1... | collective-permute-start | bytes 178184 | tf_op jit(solution)/shard_map/ppermute | solution.py:371
  7.3 2.1 %shard_map.105 = (bf16[3584,512]{1,0:T(8,128)(2,1)S(1)}, f32[8,128]{1,0:T(8,128)S(1)}) custom-call(bf16[3584,512]{1,0:T(8,128)(2,1)} %bitcast.5), custom_call_target="tpu_custom_call" | custom-call | bytes 3670016 | tf_op jit(solution)/shard_map/pallas_call | solution.py:183
  9.4 0.0 collective-permute-done.2.refs_3_
  9.4 2.4 %collective-permute-done.1.refs_2_ = bf16[8,3712]{1,0:T(8,128)(2,1)S(1)} collective-permute-done((bf16[8,3712]{1,0:T(8,128)(2,1)S(1)}, bf16[8,3712]{1,0:T(8,128)(2,1)S(1)}, u32[]{:S(2)}, u32[]{:S(2)}) %collective-permute-start.1) | collective-permute-done | bytes 59424 | tf_op jit(solution)/shard_map/ppermute | solution.py:371
  11.8 0.0 collective-permute-done.refs_1_
  11.8 1.8 %collective-permute-start.3 = (bf16[32,3712]{1,0:T(8,128)(2,1)S(1)}, bf16[32,3712]{1,0:T(8,128)(2,1)S(1)}, u32[]{:S(2)}, u32[]{:S(2)}) collective-permute-start(bf16[32,3712]{1,0:T(8,128)(2,1)S(1)} %shard_map.106.after_ref.refs_0_), channel_id=1, source_target_pairs={{0,2},{1,9},{2,0},{3,11},{4,6},{5,13},{6,4},{7,15},{8,10},{9,1},{1... | collective-permute-start | bytes 712712 | tf_op jit(solution)/shard_map/ppermute | solution.py:371
  13.6 1.5 %collective-permute-start.4 = (bf16[32,3712]{1,0:T(8,128)(2,1)S(1)}, bf16[32,3712]{1,0:T(8,128)(2,1)S(1)}, u32[]{:S(2)}, u32[]{:S(2)}) collective-permute-start(bf16[32,3712]{1,0:T(8,128)(2,1)S(1)} %shard_map.106.after_ref.refs_0_), channel_id=1, source_target_pairs={{0,4},{1,17},{2,6},{3,19},{4,0},{5,21},{6,2},{7,23},{8,12},{9,25},... | collective-permute-start | bytes 712712 | tf_op jit(solution)/shard_map/ppermute | solution.py:371
  15.1 0.3 collective-permute-start.5
  15.4 0.0 collective-permute-start.6
  15.4 4.5 %shard_map.107 = (bf16[4,128,512]{2,1,0:T(8,128)(2,1)}, bf16[3584,512]{1,0:T(8,128)(2,1)S(1)}, bf16[512,3584]{1,0:T(8,128)(2,1)S(1)}, f32[8,128]{1,0:T(8,128)S(1)}) custom-call(s32[4]{0:T(128)} %lengths_hbm.1, bf16[4,576,128]{2,1,0:T(8,128)(2,1)} %bitcast.9, bf16[4,576,256]{2,1,0:T(8,128)(2,1)} %bitcast.8, bf16[3584,512]{1,0:T(8,128)(2,1)} %bitcast.6, ...), custom_call_target="tpu_custom_call" | custom-call | flops 301989888 | bytes 7340032 | tf_op jit(solution)/shard_map/pallas_call | solution.py:74
  19.9 0.0 collective-permute-done.3.value_ref
  20.0 0.6 %collective-permute-start.7 = (bf16[32,3712]{1,0:T(8,128)(2,1)S(1)}, bf16[32,3712]{1,0:T(8,128)(2,1)S(1)}, u32[]{:S(2)}, u32[]{:S(2)}) collective-permute-start(bf16[32,3712]{1,0:T(8,128)(2,1)S(1)} %shard_map.108.refs_1_), channel_id=1, source_target_pairs={{0,1},{1,0},{2,3},{3,2},{4,5},{5,4},{6,7},{7,6},{8,9},{9,8},{10,11... | collective-permute-start | bytes 712712 | tf_op jit(solution)/shard_map/ppermute | solution.py:380
  20.5 1.7 %collective-permute-done.4.value_ref = bf16[32,3712]{1,0:T(8,128)(2,1)S(1)} collective-permute-done((bf16[32,3712]{1,0:T(8,128)(2,1)S(1)}, bf16[32,3712]{1,0:T(8,128)(2,1)S(1)}, u32[]{:S(2)}, u32[]{:S(2)}) %collective-permute-start.4) | collective-permute-done | bytes 237600 | tf_op jit(solution)/shard_map/ppermute | solution.py:371
  22.3 0.0 collective-permute-start.8
  22.3 0.0 collective-permute-done.5.value_ref
  22.3 0.5 %collective-permute-start.9 = (bf16[32,3712]{1,0:T(8,128)(2,1)S(1)}, bf16[32,3712]{1,0:T(8,128)(2,1)S(1)}, u32[]{:S(2)}, u32[]{:S(2)}) collective-permute-start(bf16[32,3712]{1,0:T(8,128)(2,1)S(1)} %shard_map.110.refs_3_), channel_id=1, source_target_pairs={{0,1},{1,0},{2,3},{3,2},{4,5},{5,4},{6,7},{7,6},{8,9},{9,8},{10,11... | collective-permute-start | bytes 712712 | tf_op jit(solution)/shard_map/ppermute | solution.py:380
  22.8 0.0 collective-permute-done.6.refs_0_
  22.8 0.0 collective-permute-done.7.refs_1_
  22.8 1.0 %collective-permute-done.8.refs_2_ = bf16[32,3712]{1,0:T(8,128)(2,1)S(1)} collective-permute-done((bf16[32,3712]{1,0:T(8,128)(2,1)S(1)}, bf16[32,3712]{1,0:T(8,128)(2,1)S(1)}, u32[]{:S(2)}, u32[]{:S(2)}) %collective-permute-start.8) | collective-permute-done | bytes 237600 | tf_op jit(solution)/shard_map/ppermute | solution.py:380
  23.8 0.3 collective-permute-done.9.refs_3_
  24.1 1.2 %shard_map.113.hidden_ref = bf16[128,512]{1,0:T(8,128)(2,1)S(1)} custom-call(bf16[32,3712]{1,0:T(8,128)(2,1)S(1)} %collective-permute-done.6.refs_0_, bf16[32,3712]{1,0:T(8,128)(2,1)S(1)} %collective-permute-done.7.refs_1_, bf16[32,3712]{1,0:T(8,128)(2,1)S(1)} %collective-permute-done.8.refs_2_, bf16[32,3712]{1,0:T(8,128)(2,1)S(1)} %collective-permute-done.9.refs_3_, ...), custom_call_target="tpu_custom_call" | custom-call | flops 939524096 | bytes 8290304 | tf_op jit(solution)/shard_map/pallas_call | solution.py:247
  25.4 0.5 shard_map.115
  25.8 0.2 collective-permute-start.11
  26.1 0.4 shard_map.114
  26.5 0.4 collective-permute-start.10
  26.8 1.2 %shard_map.111.hidden_ref = bf16[128,512]{1,0:T(8,128)(2,1)S(1)} custom-call(bf16[32,3712]{1,0:T(8,128)(2,1)S(1)} %shard_map.106.after_ref.refs_0_, bf16[32,3712]{1,0:T(8,128)(2,1)S(1)} %shard_map.108.refs_1_, bf16[32,3712]{1,0:T(8,128)(2,1)S(1)} %shard_map.109.refs_2_, bf16[32,3712]{1,0:T(8,128)(2,1)S(1)} %shard_map.110.refs_3_, ...), custom_call_target="tpu_custom_call" | custom-call | flops 939524096 | bytes 8290304 | tf_op jit(solution)/shard_map/pallas_call | solution.py:247
  28.1 0.7 %shard_map.112.mine_ref = bf16[128,3584]{1,0:T(8,128)(2,1)S(1)} custom-call(bf16[128,512]{1,0:T(8,128)(2,1)S(1)} %shard_map.111.hidden_ref, bf16[512,3584]{1,0:T(8,128)(2,1)S(1)} %get-tuple-element.23.down_ref), custom_call_target="tpu_custom_call" | custom-call | flops 469762048 | bytes 4587520 | tf_op jit(solution)/shard_map/pallas_call | solution.py:287
  28.8 0.0 collective-permute-done.10.refs_0_
  28.8 0.0 collective-permute-done.11.refs_1_
  28.8 0.2 shard_map.116
  29.0 1.6 %collective-permute-start.15 = (bf16[24,3584]{1,0:T(8,128)(2,1)S(1)}, bf16[24,3584]{1,0:T(8,128)(2,1)S(1)}, u32[]{:S(2)}, u32[]{:S(2)}) collective-permute-start(bf16[24,3584]{1,0:T(8,128)(2,1)S(1)} %get-tuple-element.29), channel_id=1, source_target_pairs={{0,4},{1,17},{2,6},{3,19},{4,0},{5,21},{6,2},{7,23},{8,12},{9,25},... | collective-permute-start | bytes 516104 | tf_op jit(solution)/shard_map/ppermute | solution.py:371
  30.6 0.6 %collective-permute-start.16 = (bf16[24,3584]{1,0:T(8,128)(2,1)S(1)}, bf16[24,3584]{1,0:T(8,128)(2,1)S(1)}, u32[]{:S(2)}, u32[]{:S(2)}) collective-permute-start(bf16[24,3584]{1,0:T(8,128)(2,1)S(1)} %get-tuple-element.30), channel_id=1, source_target_pairs={{0,6},{1,25},{2,4},{3,27},{4,2},{5,29},{6,0},{7,31},{8,14},{9,17},... | collective-permute-start | bytes 516104 | tf_op jit(solution)/shard_map/ppermute | solution.py:371
  31.2 1.4 %collective-permute-start.17 = (bf16[24,3584]{1,0:T(8,128)(2,1)S(1)}, bf16[24,3584]{1,0:T(8,128)(2,1)S(1)}, u32[]{:S(2)}, u32[]{:S(2)}) collective-permute-start(bf16[24,3584]{1,0:T(8,128)(2,1)S(1)} %get-tuple-element.31), channel_id=1, source_target_pairs={{0,2},{1,9},{2,0},{3,11},{4,6},{5,13},{6,4},{7,15},{8,10},{9,1},{1... | collective-permute-start | bytes 516104 | tf_op jit(solution)/shard_map/ppermute | solution.py:371
  32.6 1.5 %collective-permute-start.12 = (bf16[8,3584]{1,0:T(8,128)(2,1)S(1)}, bf16[8,3584]{1,0:T(8,128)(2,1)S(1)}, u32[]{:S(2)}, u32[]{:S(2)}) collective-permute-start(bf16[8,3584]{1,0:T(8,128)(2,1)S(1)} %get-tuple-element.25), channel_id=1, source_target_pairs={{0,4},{1,17},{2,6},{3,19},{4,0},{5,21},{6,2},{7,23},{8,12},{9,25},... | collective-permute-start | bytes 172040 | tf_op jit(solution)/shard_map/ppermute | solution.py:371
  34.1 0.6 %collective-permute-start.13 = (bf16[8,3584]{1,0:T(8,128)(2,1)S(1)}, bf16[8,3584]{1,0:T(8,128)(2,1)S(1)}, u32[]{:S(2)}, u32[]{:S(2)}) collective-permute-start(bf16[8,3584]{1,0:T(8,128)(2,1)S(1)} %get-tuple-element.26), channel_id=1, source_target_pairs={{0,6},{1,25},{2,4},{3,27},{4,2},{5,29},{6,0},{7,31},{8,14},{9,17},... | collective-permute-start | bytes 172040 | tf_op jit(solution)/shard_map/ppermute | solution.py:371
  34.6 0.8 %collective-permute-done.15.refs_1_ = bf16[24,3584]{1,0:T(8,128)(2,1)S(1)} collective-permute-done((bf16[24,3584]{1,0:T(8,128)(2,1)S(1)}, bf16[24,3584]{1,0:T(8,128)(2,1)S(1)}, u32[]{:S(2)}, u32[]{:S(2)}) %collective-permute-start.15) | collective-permute-done | bytes 172064 | tf_op jit(solution)/shard_map/ppermute | solution.py:371
  35.4 0.7 %collective-permute-start.14 = (bf16[8,3584]{1,0:T(8,128)(2,1)S(1)}, bf16[8,3584]{1,0:T(8,128)(2,1)S(1)}, u32[]{:S(2)}, u32[]{:S(2)}) collective-permute-start(bf16[8,3584]{1,0:T(8,128)(2,1)S(1)} %get-tuple-element.27), channel_id=1, source_target_pairs={{0,2},{1,9},{2,0},{3,11},{4,6},{5,13},{6,4},{7,15},{8,10},{9,1},{1... | collective-permute-start | bytes 172040 | tf_op jit(solution)/shard_map/ppermute | solution.py:371
  36.1 0.9 %collective-permute-done.16.refs_2_ = bf16[24,3584]{1,0:T(8,128)(2,1)S(1)} collective-permute-done((bf16[24,3584]{1,0:T(8,128)(2,1)S(1)}, bf16[24,3584]{1,0:T(8,128)(2,1)S(1)}, u32[]{:S(2)}, u32[]{:S(2)}) %collective-permute-start.16) | collective-permute-done | bytes 172064 | tf_op jit(solution)/shard_map/ppermute | solution.py:371
  37.0 0.8 %collective-permute-done.17.refs_3_ = bf16[24,3584]{1,0:T(8,128)(2,1)S(1)} collective-permute-done((bf16[24,3584]{1,0:T(8,128)(2,1)S(1)}, bf16[24,3584]{1,0:T(8,128)(2,1)S(1)}, u32[]{:S(2)}, u32[]{:S(2)}) %collective-permute-start.17) | collective-permute-done | bytes 172064 | tf_op jit(solution)/shard_map/ppermute | solution.py:371
  37.8 0.1 shard_map.117
  37.9 1.4 %collective-permute-start.18 = (bf16[8,3584]{1,0:T(8,128)(2,1)S(1)}, bf16[8,3584]{1,0:T(8,128)(2,1)S(1)}, u32[]{:S(2)}, u32[]{:S(2)}) collective-permute-start(bf16[8,3584]{1,0:T(8,128)(2,1)S(1)} %get-tuple-element.32), channel_id=1, source_target_pairs={{0,24},{1,7},{2,26},{3,5},{4,28},{5,3},{6,30},{7,1},{8,16},{9,15},... | collective-permute-start | bytes 172040 | tf_op jit(solution)/shard_map/ppermute | solution.py:371
  39.4 1.2 %collective-permute-start.19 = (bf16[8,3584]{1,0:T(8,128)(2,1)S(1)}, bf16[8,3584]{1,0:T(8,128)(2,1)S(1)}, u32[]{:S(2)}, u32[]{:S(2)}) collective-permute-start(bf16[8,3584]{1,0:T(8,128)(2,1)S(1)} %get-tuple-element.33), channel_id=1, source_target_pairs={{0,16},{1,5},{2,18},{3,7},{4,20},{5,1},{6,22},{7,3},{8,24},{9,13},... | collective-permute-start | bytes 172040 | tf_op jit(solution)/shard_map/ppermute | solution.py:371
  40.5 0.0 collective-permute-done.12.refs_1_
  40.5 1.8 %collective-permute-start.20 = (bf16[8,3584]{1,0:T(8,128)(2,1)S(1)}, bf16[8,3584]{1,0:T(8,128)(2,1)S(1)}, u32[]{:S(2)}, u32[]{:S(2)}) collective-permute-start(bf16[8,3584]{1,0:T(8,128)(2,1)S(1)} %get-tuple-element.34), channel_id=1, source_target_pairs={{0,8},{1,3},{2,10},{3,1},{4,12},{5,7},{6,14},{7,5},{8,0},{9,11},{1... | collective-permute-start | bytes 172040 | tf_op jit(solution)/shard_map/ppermute | solution.py:371
  42.4 0.0 collective-permute-done.13.refs_2_
  42.4 0.0 collective-permute-done.14.refs_3_
  42.4 1.6 %collective-permute-done.18.refs_4_ = bf16[8,3584]{1,0:T(8,128)(2,1)S(1)} collective-permute-done((bf16[8,3584]{1,0:T(8,128)(2,1)S(1)}, bf16[8,3584]{1,0:T(8,128)(2,1)S(1)}, u32[]{:S(2)}, u32[]{:S(2)}) %collective-permute-start.18) | collective-permute-done | bytes 57376 | tf_op jit(solution)/shard_map/ppermute | solution.py:371
  44.0 0.7 %collective-permute-done.19.refs_5_ = bf16[8,3584]{1,0:T(8,128)(2,1)S(1)} collective-permute-done((bf16[8,3584]{1,0:T(8,128)(2,1)S(1)}, bf16[8,3584]{1,0:T(8,128)(2,1)S(1)}, u32[]{:S(2)}, u32[]{:S(2)}) %collective-permute-start.19) | collective-permute-done | bytes 57376 | tf_op jit(solution)/shard_map/ppermute | solution.py:371
  44.6 0.6 %collective-permute-done.20.refs_6_ = bf16[8,3584]{1,0:T(8,128)(2,1)S(1)} collective-permute-done((bf16[8,3584]{1,0:T(8,128)(2,1)S(1)}, bf16[8,3584]{1,0:T(8,128)(2,1)S(1)}, u32[]{:S(2)}, u32[]{:S(2)}) %collective-permute-start.20) | collective-permute-done | bytes 57376 | tf_op jit(solution)/shard_map/ppermute | solution.py:371
  45.2 0.7 %shard_map.118 = bf16[8,3584]{1,0:T(8,128)(2,1)} custom-call(bf16[8,3584]{1,0:T(8,128)(2,1)S(1)} %get-tuple-element.24.refs_0_, bf16[8,3584]{1,0:T(8,128)(2,1)S(1)} %collective-permute-done.12.refs_1_, bf16[8,3584]{1,0:T(8,128)(2,1)S(1)} %collective-permute-done.13.refs_2_, bf16[8,3584]{1,0:T(8,128)(2,1)S(1)} %collective-permute-done.14.refs_3_, ...), custom_call_target="tpu_custom_call" | custom-call | flops 200704 | bytes 401408 | tf_op jit(solution)/shard_map/pallas_call | solution.py:339
  (4 shorter events, 0.0 us)
Async XLA Ops:
  1.6 7.8 %collective-permute-start.2 = (bf16[8,3712]{1,0:T(8,128)(2,1)S(1)}, bf16[8,3712]{1,0:T(8,128)(2,1)S(1)}, u32[]{:S(2)}, u32[]{:S(2)}) collective-permute-start(bf16[8,3712]{1,0:T(8,128)(2,1)S(1)} %shard_map.104.refs_0_), channel_id=1, source_target_pairs={{0,24},{1,7},{2,26},{3,5},{4,28},{5,3},{6,30},{7,1},{8,16},{9,15},... | collective-permute-start | bytes 178184 | tf_op jit(solution)/shard_map/ppermute | solution.py:371
  6.7 5.1 %collective-permute-start.1 = (bf16[8,3712]{1,0:T(8,128)(2,1)S(1)}, bf16[8,3712]{1,0:T(8,128)(2,1)S(1)}, u32[]{:S(2)}, u32[]{:S(2)}) collective-permute-start(bf16[8,3712]{1,0:T(8,128)(2,1)S(1)} %shard_map.104.refs_0_), channel_id=1, source_target_pairs={{0,16},{1,5},{2,18},{3,7},{4,20},{5,1},{6,22},{7,3},{8,24},{9,13},... | collective-permute-start | bytes 178184 | tf_op jit(solution)/shard_map/ppermute | solution.py:371
  6.7 5.1 %collective-permute-start = (bf16[8,3712]{1,0:T(8,128)(2,1)S(1)}, bf16[8,3712]{1,0:T(8,128)(2,1)S(1)}, u32[]{:S(2)}, u32[]{:S(2)}) collective-permute-start(bf16[8,3712]{1,0:T(8,128)(2,1)S(1)} %shard_map.104.refs_0_), channel_id=1, source_target_pairs={{0,8},{1,3},{2,10},{3,1},{4,12},{5,7},{6,14},{7,5},{8,0},{9,11},{1... | collective-permute-start | bytes 178184 | tf_op jit(solution)/shard_map/ppermute | solution.py:371
  11.8 8.1 %collective-permute-start.3 = (bf16[32,3712]{1,0:T(8,128)(2,1)S(1)}, bf16[32,3712]{1,0:T(8,128)(2,1)S(1)}, u32[]{:S(2)}, u32[]{:S(2)}) collective-permute-start(bf16[32,3712]{1,0:T(8,128)(2,1)S(1)} %shard_map.106.after_ref.refs_0_), channel_id=1, source_target_pairs={{0,2},{1,9},{2,0},{3,11},{4,6},{5,13},{6,4},{7,15},{8,10},{9,1},{1... | collective-permute-start | bytes 712712 | tf_op jit(solution)/shard_map/ppermute | solution.py:371
  13.6 8.7 %collective-permute-start.4 = (bf16[32,3712]{1,0:T(8,128)(2,1)S(1)}, bf16[32,3712]{1,0:T(8,128)(2,1)S(1)}, u32[]{:S(2)}, u32[]{:S(2)}) collective-permute-start(bf16[32,3712]{1,0:T(8,128)(2,1)S(1)} %shard_map.106.after_ref.refs_0_), channel_id=1, source_target_pairs={{0,4},{1,17},{2,6},{3,19},{4,0},{5,21},{6,2},{7,23},{8,12},{9,25},... | collective-permute-start | bytes 712712 | tf_op jit(solution)/shard_map/ppermute | solution.py:371
  15.1 7.1 %collective-permute-start.5 = (bf16[32,3712]{1,0:T(8,128)(2,1)S(1)}, bf16[32,3712]{1,0:T(8,128)(2,1)S(1)}, u32[]{:S(2)}, u32[]{:S(2)}) collective-permute-start(bf16[32,3712]{1,0:T(8,128)(2,1)S(1)} %shard_map.106.after_ref.refs_0_), channel_id=1, source_target_pairs={{0,6},{1,25},{2,4},{3,27},{4,2},{5,29},{6,0},{7,31},{8,14},{9,17},... | collective-permute-start | bytes 712712 | tf_op jit(solution)/shard_map/ppermute | solution.py:371
  15.4 7.4 %collective-permute-start.6 = (bf16[32,3712]{1,0:T(8,128)(2,1)S(1)}, bf16[32,3712]{1,0:T(8,128)(2,1)S(1)}, u32[]{:S(2)}, u32[]{:S(2)}) collective-permute-start(bf16[32,3712]{1,0:T(8,128)(2,1)S(1)} %shard_map.106.after_ref.refs_0_), channel_id=1, source_target_pairs={{0,1},{1,0},{2,3},{3,2},{4,5},{5,4},{6,7},{7,6},{8,9},{9,8},{10,11... | collective-permute-start | bytes 712712 | tf_op jit(solution)/shard_map/ppermute | solution.py:380
  20.0 2.8 %collective-permute-start.7 = (bf16[32,3712]{1,0:T(8,128)(2,1)S(1)}, bf16[32,3712]{1,0:T(8,128)(2,1)S(1)}, u32[]{:S(2)}, u32[]{:S(2)}) collective-permute-start(bf16[32,3712]{1,0:T(8,128)(2,1)S(1)} %shard_map.108.refs_1_), channel_id=1, source_target_pairs={{0,1},{1,0},{2,3},{3,2},{4,5},{5,4},{6,7},{7,6},{8,9},{9,8},{10,11... | collective-permute-start | bytes 712712 | tf_op jit(solution)/shard_map/ppermute | solution.py:380
  22.3 1.5 %collective-permute-start.8 = (bf16[32,3712]{1,0:T(8,128)(2,1)S(1)}, bf16[32,3712]{1,0:T(8,128)(2,1)S(1)}, u32[]{:S(2)}, u32[]{:S(2)}) collective-permute-start(bf16[32,3712]{1,0:T(8,128)(2,1)S(1)} %shard_map.109.refs_2_), channel_id=1, source_target_pairs={{0,1},{1,0},{2,3},{3,2},{4,5},{5,4},{6,7},{7,6},{8,9},{9,8},{10,11... | collective-permute-start | bytes 712712 | tf_op jit(solution)/shard_map/ppermute | solution.py:380
  22.3 1.8 %collective-permute-start.9 = (bf16[32,3712]{1,0:T(8,128)(2,1)S(1)}, bf16[32,3712]{1,0:T(8,128)(2,1)S(1)}, u32[]{:S(2)}, u32[]{:S(2)}) collective-permute-start(bf16[32,3712]{1,0:T(8,128)(2,1)S(1)} %shard_map.110.refs_3_), channel_id=1, source_target_pairs={{0,1},{1,0},{2,3},{3,2},{4,5},{5,4},{6,7},{7,6},{8,9},{9,8},{10,11... | collective-permute-start | bytes 712712 | tf_op jit(solution)/shard_map/ppermute | solution.py:380
  25.8 3.0 %collective-permute-start.11 = (bf16[128,2048]{1,0:T(8,128)(2,1)S(1)}, bf16[128,2048]{1,0:T(8,128)(2,1)S(1)}, u32[]{:S(2)}, u32[]{:S(2)}) collective-permute-start(bf16[128,2048]{1,0:T(8,128)(2,1)S(1)} %shard_map.115), channel_id=1, source_target_pairs={{0,1},{1,0},{2,3},{3,2},{4,5},{5,4},{6,7},{7,6},{8,9},{9,8},{10,11... | collective-permute-start | bytes 1572872 | tf_op jit(solution)/shard_map/ppermute | solution.py:380
  26.5 2.3 %collective-permute-start.10 = (bf16[128,1536]{1,0:T(8,128)(2,1)S(1)}, bf16[128,1536]{1,0:T(8,128)(2,1)S(1)}, u32[]{:S(2)}, u32[]{:S(2)}) collective-permute-start(bf16[128,1536]{1,0:T(8,128)(2,1)S(1)} %shard_map.114), channel_id=1, source_target_pairs={{0,1},{1,0},{2,3},{3,2},{4,5},{5,4},{6,7},{7,6},{8,9},{9,8},{10,11... | collective-permute-start | bytes 1179656 | tf_op jit(solution)/shard_map/ppermute | solution.py:380
  29.0 6.4 %collective-permute-start.15 = (bf16[24,3584]{1,0:T(8,128)(2,1)S(1)}, bf16[24,3584]{1,0:T(8,128)(2,1)S(1)}, u32[]{:S(2)}, u32[]{:S(2)}) collective-permute-start(bf16[24,3584]{1,0:T(8,128)(2,1)S(1)} %get-tuple-element.29), channel_id=1, source_target_pairs={{0,4},{1,17},{2,6},{3,19},{4,0},{5,21},{6,2},{7,23},{8,12},{9,25},... | collective-permute-start | bytes 516104 | tf_op jit(solution)/shard_map/ppermute | solution.py:371
  30.6 6.4 %collective-permute-start.16 = (bf16[24,3584]{1,0:T(8,128)(2,1)S(1)}, bf16[24,3584]{1,0:T(8,128)(2,1)S(1)}, u32[]{:S(2)}, u32[]{:S(2)}) collective-permute-start(bf16[24,3584]{1,0:T(8,128)(2,1)S(1)} %get-tuple-element.30), channel_id=1, source_target_pairs={{0,6},{1,25},{2,4},{3,27},{4,2},{5,29},{6,0},{7,31},{8,14},{9,17},... | collective-permute-start | bytes 516104 | tf_op jit(solution)/shard_map/ppermute | solution.py:371
  31.2 6.7 %collective-permute-start.17 = (bf16[24,3584]{1,0:T(8,128)(2,1)S(1)}, bf16[24,3584]{1,0:T(8,128)(2,1)S(1)}, u32[]{:S(2)}, u32[]{:S(2)}) collective-permute-start(bf16[24,3584]{1,0:T(8,128)(2,1)S(1)} %get-tuple-element.31), channel_id=1, source_target_pairs={{0,2},{1,9},{2,0},{3,11},{4,6},{5,13},{6,4},{7,15},{8,10},{9,1},{1... | collective-permute-start | bytes 516104 | tf_op jit(solution)/shard_map/ppermute | solution.py:371
  32.6 8.0 %collective-permute-start.12 = (bf16[8,3584]{1,0:T(8,128)(2,1)S(1)}, bf16[8,3584]{1,0:T(8,128)(2,1)S(1)}, u32[]{:S(2)}, u32[]{:S(2)}) collective-permute-start(bf16[8,3584]{1,0:T(8,128)(2,1)S(1)} %get-tuple-element.25), channel_id=1, source_target_pairs={{0,4},{1,17},{2,6},{3,19},{4,0},{5,21},{6,2},{7,23},{8,12},{9,25},... | collective-permute-start | bytes 172040 | tf_op jit(solution)/shard_map/ppermute | solution.py:371
  34.1 8.3 %collective-permute-start.13 = (bf16[8,3584]{1,0:T(8,128)(2,1)S(1)}, bf16[8,3584]{1,0:T(8,128)(2,1)S(1)}, u32[]{:S(2)}, u32[]{:S(2)}) collective-permute-start(bf16[8,3584]{1,0:T(8,128)(2,1)S(1)} %get-tuple-element.26), channel_id=1, source_target_pairs={{0,6},{1,25},{2,4},{3,27},{4,2},{5,29},{6,0},{7,31},{8,14},{9,17},... | collective-permute-start | bytes 172040 | tf_op jit(solution)/shard_map/ppermute | solution.py:371
  35.4 7.0 %collective-permute-start.14 = (bf16[8,3584]{1,0:T(8,128)(2,1)S(1)}, bf16[8,3584]{1,0:T(8,128)(2,1)S(1)}, u32[]{:S(2)}, u32[]{:S(2)}) collective-permute-start(bf16[8,3584]{1,0:T(8,128)(2,1)S(1)} %get-tuple-element.27), channel_id=1, source_target_pairs={{0,2},{1,9},{2,0},{3,11},{4,6},{5,13},{6,4},{7,15},{8,10},{9,1},{1... | collective-permute-start | bytes 172040 | tf_op jit(solution)/shard_map/ppermute | solution.py:371
  37.9 6.1 %collective-permute-start.18 = (bf16[8,3584]{1,0:T(8,128)(2,1)S(1)}, bf16[8,3584]{1,0:T(8,128)(2,1)S(1)}, u32[]{:S(2)}, u32[]{:S(2)}) collective-permute-start(bf16[8,3584]{1,0:T(8,128)(2,1)S(1)} %get-tuple-element.32), channel_id=1, source_target_pairs={{0,24},{1,7},{2,26},{3,5},{4,28},{5,3},{6,30},{7,1},{8,16},{9,15},... | collective-permute-start | bytes 172040 | tf_op jit(solution)/shard_map/ppermute | solution.py:371
  39.4 5.3 %collective-permute-start.19 = (bf16[8,3584]{1,0:T(8,128)(2,1)S(1)}, bf16[8,3584]{1,0:T(8,128)(2,1)S(1)}, u32[]{:S(2)}, u32[]{:S(2)}) collective-permute-start(bf16[8,3584]{1,0:T(8,128)(2,1)S(1)} %get-tuple-element.33), channel_id=1, source_target_pairs={{0,16},{1,5},{2,18},{3,7},{4,20},{5,1},{6,22},{7,3},{8,24},{9,13},... | collective-permute-start | bytes 172040 | tf_op jit(solution)/shard_map/ppermute | solution.py:371
  40.5 4.6 %collective-permute-start.20 = (bf16[8,3584]{1,0:T(8,128)(2,1)S(1)}, bf16[8,3584]{1,0:T(8,128)(2,1)S(1)}, u32[]{:S(2)}, u32[]{:S(2)}) collective-permute-start(bf16[8,3584]{1,0:T(8,128)(2,1)S(1)} %get-tuple-element.34), channel_id=1, source_target_pairs={{0,8},{1,3},{2,10},{3,1},{4,12},{5,7},{6,14},{7,5},{8,0},{9,11},{1... | collective-permute-start | bytes 172040 | tf_op jit(solution)/shard_map/ppermute | solution.py:371

commit v14 on v13

--- a/solution.py
+++ b/solution.py
@@ -209,7 +209,8 @@
 
 def hidden_kernel(count, *refs):
     pieces = refs[:count]
-    gate_ref, up_ref, hidden_ref, rows_ref = refs[count:]
+    gate_ref, up_ref = refs[count : count + 2]
+    hidden_ref, rows_ref = refs[-2:]
     total, _ = rows_ref.shape
     model_width, units = gate_ref.shape
     lanes = rows_ref.shape[1] - model_width
@@ -241,13 +242,13 @@
         pl.loop(0, total // block)(lambda i: units_of(pl.ds(pl.multiple_of(i * block, block), block)))
 
 
-def hidden_units(pieces, expert_gate, expert_up):
+def hidden_units(pieces, expert_gate, expert_up, after=()):
     total, width = sum(p.shape[0] for p in pieces), pieces[0].shape[1]
     model_width, units = expert_gate.shape
     return pl.pallas_call(
         functools.partial(hidden_kernel, len(pieces)),
         out_shape=in_vmem((total, units), jnp.bfloat16),
-        in_specs=[VMEM] * (len(pieces) + 2),
+        in_specs=[VMEM] * (len(pieces) + 2 + len(after)),
         out_specs=VMEM,
         scratch_shapes=[pltpu.VMEM((total, width), jnp.bfloat16)],
         compiler_params=pltpu.CompilerParams(vmem_limit_bytes=(8 << 20) + 4 * total * width),
@@ -256,7 +257,7 @@
             bytes_accessed=4 * model_width * units + 2 * total * width,
             transcendentals=total * units,
         ),
-    )(*(held(v) for v in (*pieces, expert_gate, expert_up)))
+    )(*(held(v) for v in (*pieces, expert_gate, expert_up, *after)))
 
 
 def down_kernel(first, hidden_ref, down_ref, out_ref):
@@ -395,7 +396,7 @@
     pieces = [block] + [tie(far[k], token) for k in range(1, inner)]
     received = [over_cores(p) for p in pieces]
     hidden = hidden_units(pieces, gate, up)
-    partner = hidden_units(received, gate, up)
+    partner = hidden_units(received, gate, up, [hidden])
     cut = model_width // 1024 * 512
     other = [down(partner, down_rows, first, last) for first, last in ((0, cut), (cut, model_width))]
     other = [over_cores(part) for part in other]

time: 46.1 us -> 46.7 us (1.013)
  starting transfers between devices: 21.8 us -> 22.9 us
  waiting for transfers between devices: 10.8 us -> 10.3 us
    ppermute x15, starting transfers between devices: 20.1 us -> 21.2 us  [swap(): return lax.ppermute(value, ('ep', 'sub'), pairs)]
  transfers between devices with their start and end apart: 21 -> 21, of which waited for: 10 -> 9; matrix products, arithmetic and copies ran while one was open for 0% -> 0% of each run, Pallas kernels for 20% -> 19%
where the time goes in v14:
time: 46.7 us; the launch traced here: 46.5 us
  starting transfers between devices  22.9 us (49%)
  Pallas kernels  12.5 us (27%)
  waiting for transfers between devices  10.3 us (22%)
  between operations  0.77 us (2%)
    ppermute x15, starting transfers between devices, swap(): return lax.ppermute(value, ('ep', 'sub'), pairs)  21.2 us
    ppermute x15, waiting for transfers between devices, swap(): return lax.ppermute(value, ('ep', 'sub'), pairs)  9.45 us
    pallas_call x1, Pallas kernels, attend(): pl.pallas_call(attend_kernel, out_shape=(jax.ShapeDtypeStruct((rows, head...  4.52 us
    pallas_call x2, Pallas kernels, hidden_units(): pl.pallas_call(functools.partial(hidden_kernel, len(pieces)), out_shape=i...  2.47 us
    pallas_call x1, Pallas kernels, fetch(): pl.pallas_call(fetch_kernel, out_shape=(in_vmem(value.shape, value.dtype)...  2.07 us
    ppermute x6, starting transfers between devices, over_cores(): return lax.ppermute(value, 'sub', [(i, i ^ 1) for i in range(sub_count)])  1.71 us
    pallas_call x3, Pallas kernels, down(): pl.pallas_call(functools.partial(down_kernel, first), out_shape=in_vmem((...  1.52 us
  transfers between devices with their start and end apart: 21, of which 9 were waited for; matrix products, arithmetic and copies ran while one was open for 0% of the time, Pallas kernels for 19%

profile of v14, /device:TPU:0, one launch (start us, length us, event | category | flops | bytes accessed | tf_op | source)
XLA Modules:
  0.0 46.5 jit_solution(2830036897200605336)
XLA Ops:
  0.6 0.9 %shard_map.104.refs_0_ = bf16[8,3712]{1,0:T(8,128)(2,1)S(1)} custom-call(bf16[8,3584]{1,0:T(8,128)(2,1)} %hidden_ref.1, s32[8,8]{1,0:T(8,128)} %routes_ref.1, f32[8,8]{1,0:T(8,128)} %scores_ref.1), custom_call_target="tpu_custom_call" | custom-call | flops 65536 | bytes 114688 | tf_op jit(solution)/shard_map/pallas_call | solution.py:133
  1.6 3.1 %collective-permute-start = (bf16[8,3712]{1,0:T(8,128)(2,1)S(1)}, bf16[8,3712]{1,0:T(8,128)(2,1)S(1)}, u32[]{:S(2)}, u32[]{:S(2)}) collective-permute-start(bf16[8,3712]{1,0:T(8,128)(2,1)S(1)} %shard_map.104.refs_0_), channel_id=1, source_target_pairs={{0,8},{1,3},{2,10},{3,1},{4,12},{5,7},{6,14},{7,5},{8,0},{9,11},{1... | collective-permute-start | bytes 178184 | tf_op jit(solution)/shard_map/ppermute | solution.py:372
  4.7 2.6 %collective-permute-start.1 = (bf16[8,3712]{1,0:T(8,128)(2,1)S(1)}, bf16[8,3712]{1,0:T(8,128)(2,1)S(1)}, u32[]{:S(2)}, u32[]{:S(2)}) collective-permute-start(bf16[8,3712]{1,0:T(8,128)(2,1)S(1)} %shard_map.104.refs_0_), channel_id=1, source_target_pairs={{0,16},{1,5},{2,18},{3,7},{4,20},{5,1},{6,22},{7,3},{8,24},{9,13},... | collective-permute-start | bytes 178184 | tf_op jit(solution)/shard_map/ppermute | solution.py:372
  7.2 0.0 collective-permute-start.2
  7.2 2.1 %shard_map.105 = (bf16[3584,512]{1,0:T(8,128)(2,1)S(1)}, f32[8,128]{1,0:T(8,128)S(1)}) custom-call(bf16[3584,512]{1,0:T(8,128)(2,1)} %bitcast.5), custom_call_target="tpu_custom_call" | custom-call | bytes 3670016 | tf_op jit(solution)/shard_map/pallas_call | solution.py:183
  9.3 0.0 collective-permute-done.refs_1_
  9.3 1.1 %collective-permute-done.1.refs_2_ = bf16[8,3712]{1,0:T(8,128)(2,1)S(1)} collective-permute-done((bf16[8,3712]{1,0:T(8,128)(2,1)S(1)}, bf16[8,3712]{1,0:T(8,128)(2,1)S(1)}, u32[]{:S(2)}, u32[]{:S(2)}) %collective-permute-start.1) | collective-permute-done | bytes 59424 | tf_op jit(solution)/shard_map/ppermute | solution.py:372
  10.4 2.9 %collective-permute-done.2.refs_3_ = bf16[8,3712]{1,0:T(8,128)(2,1)S(1)} collective-permute-done((bf16[8,3712]{1,0:T(8,128)(2,1)S(1)}, bf16[8,3712]{1,0:T(8,128)(2,1)S(1)}, u32[]{:S(2)}, u32[]{:S(2)}) %collective-permute-start.2) | collective-permute-done | bytes 59424 | tf_op jit(solution)/shard_map/ppermute | solution.py:372
  13.3 3.2 %collective-permute-start.5 = (bf16[32,3712]{1,0:T(8,128)(2,1)S(1)}, bf16[32,3712]{1,0:T(8,128)(2,1)S(1)}, u32[]{:S(2)}, u32[]{:S(2)}) collective-permute-start(bf16[32,3712]{1,0:T(8,128)(2,1)S(1)} %shard_map.106.after_ref.refs_0_), channel_id=1, source_target_pairs={{0,6},{1,25},{2,4},{3,27},{4,2},{5,29},{6,0},{7,31},{8,14},{9,17},... | collective-permute-start | bytes 712712 | tf_op jit(solution)/shard_map/ppermute | solution.py:372
  16.4 0.1 collective-permute-start.4
  16.5 0.6 %collective-permute-start.3 = (bf16[32,3712]{1,0:T(8,128)(2,1)S(1)}, bf16[32,3712]{1,0:T(8,128)(2,1)S(1)}, u32[]{:S(2)}, u32[]{:S(2)}) collective-permute-start(bf16[32,3712]{1,0:T(8,128)(2,1)S(1)} %shard_map.106.after_ref.refs_0_), channel_id=1, source_target_pairs={{0,2},{1,9},{2,0},{3,11},{4,6},{5,13},{6,4},{7,15},{8,10},{9,1},{1... | collective-permute-start | bytes 712712 | tf_op jit(solution)/shard_map/ppermute | solution.py:372
  17.1 0.0 collective-permute-start.6
  17.1 4.5 %shard_map.107 = (bf16[4,128,512]{2,1,0:T(8,128)(2,1)}, bf16[3584,512]{1,0:T(8,128)(2,1)S(1)}, bf16[512,3584]{1,0:T(8,128)(2,1)S(1)}, f32[8,128]{1,0:T(8,128)S(1)}) custom-call(s32[4]{0:T(128)} %lengths_hbm.1, bf16[4,576,128]{2,1,0:T(8,128)(2,1)} %bitcast.9, bf16[4,576,256]{2,1,0:T(8,128)(2,1)} %bitcast.8, bf16[3584,512]{1,0:T(8,128)(2,1)} %bitcast.6, ...), custom_call_target="tpu_custom_call" | custom-call | flops 301989888 | bytes 7340032 | tf_op jit(solution)/shard_map/pallas_call | solution.py:74
  21.6 0.0 collective-permute-done.5.value_ref
  21.6 0.6 %collective-permute-start.9 = (bf16[32,3712]{1,0:T(8,128)(2,1)S(1)}, bf16[32,3712]{1,0:T(8,128)(2,1)S(1)}, u32[]{:S(2)}, u32[]{:S(2)}) collective-permute-start(bf16[32,3712]{1,0:T(8,128)(2,1)S(1)} %shard_map.110.refs_3_), channel_id=1, source_target_pairs={{0,1},{1,0},{2,3},{3,2},{4,5},{5,4},{6,7},{7,6},{8,9},{9,8},{10,11... | collective-permute-start | bytes 712712 | tf_op jit(solution)/shard_map/ppermute | solution.py:381
  22.2 0.9 %collective-permute-done.4.value_ref = bf16[32,3712]{1,0:T(8,128)(2,1)S(1)} collective-permute-done((bf16[32,3712]{1,0:T(8,128)(2,1)S(1)}, bf16[32,3712]{1,0:T(8,128)(2,1)S(1)}, u32[]{:S(2)}, u32[]{:S(2)}) %collective-permute-start.4) | collective-permute-done | bytes 237600 | tf_op jit(solution)/shard_map/ppermute | solution.py:372
  23.1 0.2 collective-permute-start.8
  23.2 0.0 collective-permute-done.3.value_ref
  23.3 0.3 collective-permute-start.7
  23.6 1.2 %shard_map.111.hidden_ref.refs_6_ = bf16[128,512]{1,0:T(8,128)(2,1)S(1)} custom-call(bf16[32,3712]{1,0:T(8,128)(2,1)S(1)} %shard_map.106.after_ref.refs_0_, bf16[32,3712]{1,0:T(8,128)(2,1)S(1)} %shard_map.108.refs_1_, bf16[32,3712]{1,0:T(8,128)(2,1)S(1)} %shard_map.109.refs_2_, bf16[32,3712]{1,0:T(8,128)(2,1)S(1)} %shard_map.110.refs_3_, ...), custom_call_target="tpu_custom_call" | custom-call | flops 939524096 | bytes 8290304 | tf_op jit(solution)/shard_map/pallas_call | solution.py:248
  24.8 0.0 collective-permute-done.6.refs_0_
  24.8 0.0 collective-permute-done.9.refs_3_
  24.8 0.0 collective-permute-done.8.refs_2_
  24.9 0.1 collective-permute-done.7.refs_1_
  24.9 1.2 %shard_map.113.hidden_ref = bf16[128,512]{1,0:T(8,128)(2,1)S(1)} custom-call(bf16[32,3712]{1,0:T(8,128)(2,1)S(1)} %collective-permute-done.6.refs_0_, bf16[32,3712]{1,0:T(8,128)(2,1)S(1)} %collective-permute-done.7.refs_1_, bf16[32,3712]{1,0:T(8,128)(2,1)S(1)} %collective-permute-done.8.refs_2_, bf16[32,3712]{1,0:T(8,128)(2,1)S(1)} %collective-permute-done.9.refs_3_, ...), custom_call_target="tpu_custom_call" | custom-call | flops 939524096 | bytes 8290304 | tf_op jit(solution)/shard_map/pallas_call | solution.py:248
  26.2 0.5 shard_map.115
  26.6 0.2 collective-permute-start.11
  26.9 0.4 shard_map.114
  27.3 0.4 collective-permute-start.10
  27.6 0.7 %shard_map.112.mine_ref = bf16[128,3584]{1,0:T(8,128)(2,1)S(1)} custom-call(bf16[128,512]{1,0:T(8,128)(2,1)S(1)} %shard_map.111.hidden_ref.refs_6_, bf16[512,3584]{1,0:T(8,128)(2,1)S(1)} %get-tuple-element.23.down_ref), custom_call_target="tpu_custom_call" | custom-call | flops 469762048 | bytes 4587520 | tf_op jit(solution)/shard_map/pallas_call | solution.py:288
  28.3 0.8 %collective-permute-done.10.refs_0_ = bf16[128,1536]{1,0:T(8,128)(2,1)S(1)} collective-permute-done((bf16[128,1536]{1,0:T(8,128)(2,1)S(1)}, bf16[128,1536]{1,0:T(8,128)(2,1)S(1)}, u32[]{:S(2)}, u32[]{:S(2)}) %collective-permute-start.10) | collective-permute-done | bytes 393248 | tf_op jit(solution)/shard_map/ppermute | solution.py:381
  29.2 0.0 collective-permute-done.11.refs_1_
  29.2 0.2 shard_map.116
  29.4 1.7 %collective-permute-start.15 = (bf16[24,3584]{1,0:T(8,128)(2,1)S(1)}, bf16[24,3584]{1,0:T(8,128)(2,1)S(1)}, u32[]{:S(2)}, u32[]{:S(2)}) collective-permute-start(bf16[24,3584]{1,0:T(8,128)(2,1)S(1)} %get-tuple-element.29), channel_id=1, source_target_pairs={{0,4},{1,17},{2,6},{3,19},{4,0},{5,21},{6,2},{7,23},{8,12},{9,25},... | collective-permute-start | bytes 516104 | tf_op jit(solution)/shard_map/ppermute | solution.py:372
  31.0 1.6 %collective-permute-start.16 = (bf16[24,3584]{1,0:T(8,128)(2,1)S(1)}, bf16[24,3584]{1,0:T(8,128)(2,1)S(1)}, u32[]{:S(2)}, u32[]{:S(2)}) collective-permute-start(bf16[24,3584]{1,0:T(8,128)(2,1)S(1)} %get-tuple-element.30), channel_id=1, source_target_pairs={{0,6},{1,25},{2,4},{3,27},{4,2},{5,29},{6,0},{7,31},{8,14},{9,17},... | collective-permute-start | bytes 516104 | tf_op jit(solution)/shard_map/ppermute | solution.py:372
  32.6 0.3 collective-permute-start.17
  32.9 1.6 %collective-permute-start.12 = (bf16[8,3584]{1,0:T(8,128)(2,1)S(1)}, bf16[8,3584]{1,0:T(8,128)(2,1)S(1)}, u32[]{:S(2)}, u32[]{:S(2)}) collective-permute-start(bf16[8,3584]{1,0:T(8,128)(2,1)S(1)} %get-tuple-element.25), channel_id=1, source_target_pairs={{0,4},{1,17},{2,6},{3,19},{4,0},{5,21},{6,2},{7,23},{8,12},{9,25},... | collective-permute-start | bytes 172040 | tf_op jit(solution)/shard_map/ppermute | solution.py:372
  34.5 1.6 %collective-permute-start.13 = (bf16[8,3584]{1,0:T(8,128)(2,1)S(1)}, bf16[8,3584]{1,0:T(8,128)(2,1)S(1)}, u32[]{:S(2)}, u32[]{:S(2)}) collective-permute-start(bf16[8,3584]{1,0:T(8,128)(2,1)S(1)} %get-tuple-element.26), channel_id=1, source_target_pairs={{0,6},{1,25},{2,4},{3,27},{4,2},{5,29},{6,0},{7,31},{8,14},{9,17},... | collective-permute-start | bytes 172040 | tf_op jit(solution)/shard_map/ppermute | solution.py:372
  36.1 0.0 collective-permute-done.15.refs_1_
  36.1 0.5 collective-permute-start.14
  36.6 0.9 %collective-permute-done.16.refs_2_ = bf16[24,3584]{1,0:T(8,128)(2,1)S(1)} collective-permute-done((bf16[24,3584]{1,0:T(8,128)(2,1)S(1)}, bf16[24,3584]{1,0:T(8,128)(2,1)S(1)}, u32[]{:S(2)}, u32[]{:S(2)}) %collective-permute-start.16) | collective-permute-done | bytes 172064 | tf_op jit(solution)/shard_map/ppermute | solution.py:372
  37.4 0.8 %collective-permute-done.17.refs_3_ = bf16[24,3584]{1,0:T(8,128)(2,1)S(1)} collective-permute-done((bf16[24,3584]{1,0:T(8,128)(2,1)S(1)}, bf16[24,3584]{1,0:T(8,128)(2,1)S(1)}, u32[]{:S(2)}, u32[]{:S(2)}) %collective-permute-start.17) | collective-permute-done | bytes 172064 | tf_op jit(solution)/shard_map/ppermute | solution.py:372
  38.2 0.1 shard_map.117
  38.3 2.4 %collective-permute-start.18 = (bf16[8,3584]{1,0:T(8,128)(2,1)S(1)}, bf16[8,3584]{1,0:T(8,128)(2,1)S(1)}, u32[]{:S(2)}, u32[]{:S(2)}) collective-permute-start(bf16[8,3584]{1,0:T(8,128)(2,1)S(1)} %get-tuple-element.32), channel_id=1, source_target_pairs={{0,24},{1,7},{2,26},{3,5},{4,28},{5,3},{6,30},{7,1},{8,16},{9,15},... | collective-permute-start | bytes 172040 | tf_op jit(solution)/shard_map/ppermute | solution.py:372
  40.7 0.0 collective-permute-start.19
  40.7 0.0 collective-permute-done.12.refs_1_
  40.7 2.0 %collective-permute-start.20 = (bf16[8,3584]{1,0:T(8,128)(2,1)S(1)}, bf16[8,3584]{1,0:T(8,128)(2,1)S(1)}, u32[]{:S(2)}, u32[]{:S(2)}) collective-permute-start(bf16[8,3584]{1,0:T(8,128)(2,1)S(1)} %get-tuple-element.34), channel_id=1, source_target_pairs={{0,8},{1,3},{2,10},{3,1},{4,12},{5,7},{6,14},{7,5},{8,0},{9,11},{1... | collective-permute-start | bytes 172040 | tf_op jit(solution)/shard_map/ppermute | solution.py:372
  42.7 0.0 collective-permute-done.13.refs_2_
  42.7 0.0 collective-permute-done.14.refs_3_
  42.8 1.6 %collective-permute-done.18.refs_4_ = bf16[8,3584]{1,0:T(8,128)(2,1)S(1)} collective-permute-done((bf16[8,3584]{1,0:T(8,128)(2,1)S(1)}, bf16[8,3584]{1,0:T(8,128)(2,1)S(1)}, u32[]{:S(2)}, u32[]{:S(2)}) %collective-permute-start.18) | collective-permute-done | bytes 57376 | tf_op jit(solution)/shard_map/ppermute | solution.py:372
  44.3 1.5 %collective-permute-done.19.refs_5_ = bf16[8,3584]{1,0:T(8,128)(2,1)S(1)} collective-permute-done((bf16[8,3584]{1,0:T(8,128)(2,1)S(1)}, bf16[8,3584]{1,0:T(8,128)(2,1)S(1)}, u32[]{:S(2)}, u32[]{:S(2)}) %collective-permute-start.19) | collective-permute-done | bytes 57376 | tf_op jit(solution)/shard_map/ppermute | solution.py:372
  45.8 0.0 collective-permute-done.20.refs_6_
  45.8 0.7 %shard_map.118 = bf16[8,3584]{1,0:T(8,128)(2,1)} custom-call(bf16[8,3584]{1,0:T(8,128)(2,1)S(1)} %get-tuple-element.24.refs_0_, bf16[8,3584]{1,0:T(8,128)(2,1)S(1)} %collective-permute-done.12.refs_1_, bf16[8,3584]{1,0:T(8,128)(2,1)S(1)} %collective-permute-done.13.refs_2_, bf16[8,3584]{1,0:T(8,128)(2,1)S(1)} %collective-permute-done.14.refs_3_, ...), custom_call_target="tpu_custom_call" | custom-call | flops 200704 | bytes 401408 | tf_op jit(solution)/shard_map/pallas_call | solution.py:340
  (4 shorter events, 0.0 us)
Async XLA Ops:
  1.6 7.8 %collective-permute-start = (bf16[8,3712]{1,0:T(8,128)(2,1)S(1)}, bf16[8,3712]{1,0:T(8,128)(2,1)S(1)}, u32[]{:S(2)}, u32[]{:S(2)}) collective-permute-start(bf16[8,3712]{1,0:T(8,128)(2,1)S(1)} %shard_map.104.refs_0_), channel_id=1, source_target_pairs={{0,8},{1,3},{2,10},{3,1},{4,12},{5,7},{6,14},{7,5},{8,0},{9,11},{1... | collective-permute-start | bytes 178184 | tf_op jit(solution)/shard_map/ppermute | solution.py:372
  4.7 5.7 %collective-permute-start.1 = (bf16[8,3712]{1,0:T(8,128)(2,1)S(1)}, bf16[8,3712]{1,0:T(8,128)(2,1)S(1)}, u32[]{:S(2)}, u32[]{:S(2)}) collective-permute-start(bf16[8,3712]{1,0:T(8,128)(2,1)S(1)} %shard_map.104.refs_0_), channel_id=1, source_target_pairs={{0,16},{1,5},{2,18},{3,7},{4,20},{5,1},{6,22},{7,3},{8,24},{9,13},... | collective-permute-start | bytes 178184 | tf_op jit(solution)/shard_map/ppermute | solution.py:372
  7.2 6.0 %collective-permute-start.2 = (bf16[8,3712]{1,0:T(8,128)(2,1)S(1)}, bf16[8,3712]{1,0:T(8,128)(2,1)S(1)}, u32[]{:S(2)}, u32[]{:S(2)}) collective-permute-start(bf16[8,3712]{1,0:T(8,128)(2,1)S(1)} %shard_map.104.refs_0_), channel_id=1, source_target_pairs={{0,24},{1,7},{2,26},{3,5},{4,28},{5,3},{6,30},{7,1},{8,16},{9,15},... | collective-permute-start | bytes 178184 | tf_op jit(solution)/shard_map/ppermute | solution.py:372
  13.3 8.3 %collective-permute-start.5 = (bf16[32,3712]{1,0:T(8,128)(2,1)S(1)}, bf16[32,3712]{1,0:T(8,128)(2,1)S(1)}, u32[]{:S(2)}, u32[]{:S(2)}) collective-permute-start(bf16[32,3712]{1,0:T(8,128)(2,1)S(1)} %shard_map.106.after_ref.refs_0_), channel_id=1, source_target_pairs={{0,6},{1,25},{2,4},{3,27},{4,2},{5,29},{6,0},{7,31},{8,14},{9,17},... | collective-permute-start | bytes 712712 | tf_op jit(solution)/shard_map/ppermute | solution.py:372
  16.4 6.6 %collective-permute-start.4 = (bf16[32,3712]{1,0:T(8,128)(2,1)S(1)}, bf16[32,3712]{1,0:T(8,128)(2,1)S(1)}, u32[]{:S(2)}, u32[]{:S(2)}) collective-permute-start(bf16[32,3712]{1,0:T(8,128)(2,1)S(1)} %shard_map.106.after_ref.refs_0_), channel_id=1, source_target_pairs={{0,4},{1,17},{2,6},{3,19},{4,0},{5,21},{6,2},{7,23},{8,12},{9,25},... | collective-permute-start | bytes 712712 | tf_op jit(solution)/shard_map/ppermute | solution.py:372
  16.5 6.8 %collective-permute-start.3 = (bf16[32,3712]{1,0:T(8,128)(2,1)S(1)}, bf16[32,3712]{1,0:T(8,128)(2,1)S(1)}, u32[]{:S(2)}, u32[]{:S(2)}) collective-permute-start(bf16[32,3712]{1,0:T(8,128)(2,1)S(1)} %shard_map.106.after_ref.refs_0_), channel_id=1, source_target_pairs={{0,2},{1,9},{2,0},{3,11},{4,6},{5,13},{6,4},{7,15},{8,10},{9,1},{1... | collective-permute-start | bytes 712712 | tf_op jit(solution)/shard_map/ppermute | solution.py:372
  17.1 7.7 %collective-permute-start.6 = (bf16[32,3712]{1,0:T(8,128)(2,1)S(1)}, bf16[32,3712]{1,0:T(8,128)(2,1)S(1)}, u32[]{:S(2)}, u32[]{:S(2)}) collective-permute-start(bf16[32,3712]{1,0:T(8,128)(2,1)S(1)} %shard_map.106.after_ref.refs_0_), channel_id=1, source_target_pairs={{0,1},{1,0},{2,3},{3,2},{4,5},{5,4},{6,7},{7,6},{8,9},{9,8},{10,11... | collective-permute-start | bytes 712712 | tf_op jit(solution)/shard_map/ppermute | solution.py:381
  21.6 3.2 %collective-permute-start.9 = (bf16[32,3712]{1,0:T(8,128)(2,1)S(1)}, bf16[32,3712]{1,0:T(8,128)(2,1)S(1)}, u32[]{:S(2)}, u32[]{:S(2)}) collective-permute-start(bf16[32,3712]{1,0:T(8,128)(2,1)S(1)} %shard_map.110.refs_3_), channel_id=1, source_target_pairs={{0,1},{1,0},{2,3},{3,2},{4,5},{5,4},{6,7},{7,6},{8,9},{9,8},{10,11... | collective-permute-start | bytes 712712 | tf_op jit(solution)/shard_map/ppermute | solution.py:381
  23.1 1.8 %collective-permute-start.8 = (bf16[32,3712]{1,0:T(8,128)(2,1)S(1)}, bf16[32,3712]{1,0:T(8,128)(2,1)S(1)}, u32[]{:S(2)}, u32[]{:S(2)}) collective-permute-start(bf16[32,3712]{1,0:T(8,128)(2,1)S(1)} %shard_map.109.refs_2_), channel_id=1, source_target_pairs={{0,1},{1,0},{2,3},{3,2},{4,5},{5,4},{6,7},{7,6},{8,9},{9,8},{10,11... | collective-permute-start | bytes 712712 | tf_op jit(solution)/shard_map/ppermute | solution.py:381
  23.3 1.7 %collective-permute-start.7 = (bf16[32,3712]{1,0:T(8,128)(2,1)S(1)}, bf16[32,3712]{1,0:T(8,128)(2,1)S(1)}, u32[]{:S(2)}, u32[]{:S(2)}) collective-permute-start(bf16[32,3712]{1,0:T(8,128)(2,1)S(1)} %shard_map.108.refs_1_), channel_id=1, source_target_pairs={{0,1},{1,0},{2,3},{3,2},{4,5},{5,4},{6,7},{7,6},{8,9},{9,8},{10,11... | collective-permute-start | bytes 712712 | tf_op jit(solution)/shard_map/ppermute | solution.py:381
  26.6 2.5 %collective-permute-start.11 = (bf16[128,2048]{1,0:T(8,128)(2,1)S(1)}, bf16[128,2048]{1,0:T(8,128)(2,1)S(1)}, u32[]{:S(2)}, u32[]{:S(2)}) collective-permute-start(bf16[128,2048]{1,0:T(8,128)(2,1)S(1)} %shard_map.115), channel_id=1, source_target_pairs={{0,1},{1,0},{2,3},{3,2},{4,5},{5,4},{6,7},{7,6},{8,9},{9,8},{10,11... | collective-permute-start | bytes 1572872 | tf_op jit(solution)/shard_map/ppermute | solution.py:381
  27.3 1.9 %collective-permute-start.10 = (bf16[128,1536]{1,0:T(8,128)(2,1)S(1)}, bf16[128,1536]{1,0:T(8,128)(2,1)S(1)}, u32[]{:S(2)}, u32[]{:S(2)}) collective-permute-start(bf16[128,1536]{1,0:T(8,128)(2,1)S(1)} %shard_map.114), channel_id=1, source_target_pairs={{0,1},{1,0},{2,3},{3,2},{4,5},{5,4},{6,7},{7,6},{8,9},{9,8},{10,11... | collective-permute-start | bytes 1179656 | tf_op jit(solution)/shard_map/ppermute | solution.py:381
  29.4 6.8 %collective-permute-start.15 = (bf16[24,3584]{1,0:T(8,128)(2,1)S(1)}, bf16[24,3584]{1,0:T(8,128)(2,1)S(1)}, u32[]{:S(2)}, u32[]{:S(2)}) collective-permute-start(bf16[24,3584]{1,0:T(8,128)(2,1)S(1)} %get-tuple-element.29), channel_id=1, source_target_pairs={{0,4},{1,17},{2,6},{3,19},{4,0},{5,21},{6,2},{7,23},{8,12},{9,25},... | collective-permute-start | bytes 516104 | tf_op jit(solution)/shard_map/ppermute | solution.py:372
  31.0 6.4 %collective-permute-start.16 = (bf16[24,3584]{1,0:T(8,128)(2,1)S(1)}, bf16[24,3584]{1,0:T(8,128)(2,1)S(1)}, u32[]{:S(2)}, u32[]{:S(2)}) collective-permute-start(bf16[24,3584]{1,0:T(8,128)(2,1)S(1)} %get-tuple-element.30), channel_id=1, source_target_pairs={{0,6},{1,25},{2,4},{3,27},{4,2},{5,29},{6,0},{7,31},{8,14},{9,17},... | collective-permute-start | bytes 516104 | tf_op jit(solution)/shard_map/ppermute | solution.py:372
  32.6 5.6 %collective-permute-start.17 = (bf16[24,3584]{1,0:T(8,128)(2,1)S(1)}, bf16[24,3584]{1,0:T(8,128)(2,1)S(1)}, u32[]{:S(2)}, u32[]{:S(2)}) collective-permute-start(bf16[24,3584]{1,0:T(8,128)(2,1)S(1)} %get-tuple-element.31), channel_id=1, source_target_pairs={{0,2},{1,9},{2,0},{3,11},{4,6},{5,13},{6,4},{7,15},{8,10},{9,1},{1... | collective-permute-start | bytes 516104 | tf_op jit(solution)/shard_map/ppermute | solution.py:372
  32.9 7.8 %collective-permute-start.12 = (bf16[8,3584]{1,0:T(8,128)(2,1)S(1)}, bf16[8,3584]{1,0:T(8,128)(2,1)S(1)}, u32[]{:S(2)}, u32[]{:S(2)}) collective-permute-start(bf16[8,3584]{1,0:T(8,128)(2,1)S(1)} %get-tuple-element.25), channel_id=1, source_target_pairs={{0,4},{1,17},{2,6},{3,19},{4,0},{5,21},{6,2},{7,23},{8,12},{9,25},... | collective-permute-start | bytes 172040 | tf_op jit(solution)/shard_map/ppermute | solution.py:372
  34.5 8.2 %collective-permute-start.13 = (bf16[8,3584]{1,0:T(8,128)(2,1)S(1)}, bf16[8,3584]{1,0:T(8,128)(2,1)S(1)}, u32[]{:S(2)}, u32[]{:S(2)}) collective-permute-start(bf16[8,3584]{1,0:T(8,128)(2,1)S(1)} %get-tuple-element.26), channel_id=1, source_target_pairs={{0,6},{1,25},{2,4},{3,27},{4,2},{5,29},{6,0},{7,31},{8,14},{9,17},... | collective-permute-start | bytes 172040 | tf_op jit(solution)/shard_map/ppermute | solution.py:372
  36.1 6.6 %collective-permute-start.14 = (bf16[8,3584]{1,0:T(8,128)(2,1)S(1)}, bf16[8,3584]{1,0:T(8,128)(2,1)S(1)}, u32[]{:S(2)}, u32[]{:S(2)}) collective-permute-start(bf16[8,3584]{1,0:T(8,128)(2,1)S(1)} %get-tuple-element.27), channel_id=1, source_target_pairs={{0,2},{1,9},{2,0},{3,11},{4,6},{5,13},{6,4},{7,15},{8,10},{9,1},{1... | collective-permute-start | bytes 172040 | tf_op jit(solution)/shard_map/ppermute | solution.py:372
  38.3 6.0 %collective-permute-start.18 = (bf16[8,3584]{1,0:T(8,128)(2,1)S(1)}, bf16[8,3584]{1,0:T(8,128)(2,1)S(1)}, u32[]{:S(2)}, u32[]{:S(2)}) collective-permute-start(bf16[8,3584]{1,0:T(8,128)(2,1)S(1)} %get-tuple-element.32), channel_id=1, source_target_pairs={{0,24},{1,7},{2,26},{3,5},{4,28},{5,3},{6,30},{7,1},{8,16},{9,15},... | collective-permute-start | bytes 172040 | tf_op jit(solution)/shard_map/ppermute | solution.py:372
  40.7 5.1 %collective-permute-start.19 = (bf16[8,3584]{1,0:T(8,128)(2,1)S(1)}, bf16[8,3584]{1,0:T(8,128)(2,1)S(1)}, u32[]{:S(2)}, u32[]{:S(2)}) collective-permute-start(bf16[8,3584]{1,0:T(8,128)(2,1)S(1)} %get-tuple-element.33), channel_id=1, source_target_pairs={{0,16},{1,5},{2,18},{3,7},{4,20},{5,1},{6,22},{7,3},{8,24},{9,13},... | collective-permute-start | bytes 172040 | tf_op jit(solution)/shard_map/ppermute | solution.py:372
  40.7 5.1 %collective-permute-start.20 = (bf16[8,3584]{1,0:T(8,128)(2,1)S(1)}, bf16[8,3584]{1,0:T(8,128)(2,1)S(1)}, u32[]{:S(2)}, u32[]{:S(2)}) collective-permute-start(bf16[8,3584]{1,0:T(8,128)(2,1)S(1)} %get-tuple-element.34), channel_id=1, source_target_pairs={{0,8},{1,3},{2,10},{3,1},{4,12},{5,7},{6,14},{7,5},{8,0},{9,11},{1... | collective-permute-start | bytes 172040 | tf_op jit(solution)/shard_map/ppermute | solution.py:372

commit v15 on v14

--- a/solution.py
+++ b/solution.py
@@ -372,9 +372,11 @@
         return lax.ppermute(value, ("ep", "sub"), pairs)
 
     def first(value, k):
+        k = outer - k
         return swap(value, inner * k, k if inner == outer else inner * k)
 
     def second(value, k):
+        k = inner - k
         return swap(value, k, inner * k if inner == outer else k)
 
     def over_cores(value):
@@ -384,7 +386,7 @@
     near = {k: first(own, k) for k in range(outer - 1, 0, -1)}
     gate, fetched = fetch(expert_gate[0])
     block = join([own] + [near[k] for k in range(1, outer)], [fetched])
-    steps = [*range(2, inner), 1]
+    steps = [*range(inner - 2, 0, -1), inner - 1]
     far = {k: second(block, k) for k in steps}
     attention_latent, up, down_rows, token = attend(
         query_latent,
@@ -407,7 +409,7 @@
     far = [second(parts[2 * k - 1], k) for k in steps]
     side = [second(parts[2 * k - 2], k) for k in steps]
     near = add([column, *far], [(0, size)] * inner, [tok_rows] * (outer - 1))
-    near = [first(near[k - 1], k) for k in range(outer - 1, 0, -1)]
+    near = [first(near[k - 1], k) for k in range(1, outer)]
     (moe_output,) = add([kept, *side, *near], [(0, tok_rows)] * (1 + len(side) + len(near)), [tok_rows], last=True)
     return (moe_output, attention_latent)
 

time: 46.7 us -> 45.6 us (0.976)
  starting transfers between devices: 22.9 us -> 21.8 us
    ppermute x15, starting transfers between devices: 21.2 us -> 20.1 us  [swap(): return lax.ppermute(value, ('ep', 'sub'), pairs)]
  transfers between devices with their start and end apart: 21 -> 21, of which waited for: 9 -> 10; matrix products, arithmetic and copies ran while one was open for 0% -> 0% of each run, Pallas kernels for 19% -> 20%
where the time goes in v15:
time: 45.6 us; the launch traced here: 45.4 us
  starting transfers between devices  21.8 us (48%)
  Pallas kernels  12.5 us (27%)
  waiting for transfers between devices  10.4 us (23%)
  between operations  0.77 us (2%)
    ppermute x15, starting transfers between devices, swap(): return lax.ppermute(value, ('ep', 'sub'), pairs)  20.1 us
    ppermute x15, waiting for transfers between devices, swap(): return lax.ppermute(value, ('ep', 'sub'), pairs)  9.51 us
    pallas_call x1, Pallas kernels, attend(): pl.pallas_call(attend_kernel, out_shape=(jax.ShapeDtypeStruct((rows, head...  4.52 us
    pallas_call x2, Pallas kernels, hidden_units(): pl.pallas_call(functools.partial(hidden_kernel, len(pieces)), out_shape=i...  2.47 us
    pallas_call x1, Pallas kernels, fetch(): pl.pallas_call(fetch_kernel, out_shape=(in_vmem(value.shape, value.dtype)...  2.07 us
    ppermute x6, starting transfers between devices, over_cores(): return lax.ppermute(value, 'sub', [(i, i ^ 1) for i in range(sub_count)])  1.71 us
    pallas_call x3, Pallas kernels, down(): pl.pallas_call(functools.partial(down_kernel, first), out_shape=in_vmem((...  1.51 us
    pallas_call x1, Pallas kernels, pack(): pl.pallas_call(pack_kernel, out_shape=in_vmem((rows, model_width + lanes)...  0.93 us
  transfers between devices with their start and end apart: 21, of which 10 were waited for; matrix products, arithmetic and copies ran while one was open for 0% of the time, Pallas kernels for 20%

profile of v15, /device:TPU:0, one launch (start us, length us, event | category | flops | bytes accessed | tf_op | source)
XLA Modules:
  0.0 45.4 jit_solution(6576403914423467549)
XLA Ops:
  0.6 0.9 %shard_map.104.refs_0_ = bf16[8,3712]{1,0:T(8,128)(2,1)S(1)} custom-call(bf16[8,3584]{1,0:T(8,128)(2,1)} %hidden_ref.1, s32[8,8]{1,0:T(8,128)} %routes_ref.1, f32[8,8]{1,0:T(8,128)} %scores_ref.1), custom_call_target="tpu_custom_call" | custom-call | flops 65536 | bytes 114688 | tf_op jit(solution)/shard_map/pallas_call | solution.py:133
  1.6 5.1 %collective-permute-start = (bf16[8,3712]{1,0:T(8,128)(2,1)S(1)}, bf16[8,3712]{1,0:T(8,128)(2,1)S(1)}, u32[]{:S(2)}, u32[]{:S(2)}) collective-permute-start(bf16[8,3712]{1,0:T(8,128)(2,1)S(1)} %shard_map.104.refs_0_), channel_id=1, source_target_pairs={{0,24},{1,7},{2,26},{3,5},{4,28},{5,3},{6,30},{7,1},{8,16},{9,15},... | collective-permute-start | bytes 178184 | tf_op jit(solution)/shard_map/ppermute | solution.py:372
  6.7 0.0 collective-permute-start.1
  6.7 0.6 %collective-permute-start.2 = (bf16[8,3712]{1,0:T(8,128)(2,1)S(1)}, bf16[8,3712]{1,0:T(8,128)(2,1)S(1)}, u32[]{:S(2)}, u32[]{:S(2)}) collective-permute-start(bf16[8,3712]{1,0:T(8,128)(2,1)S(1)} %shard_map.104.refs_0_), channel_id=1, source_target_pairs={{0,8},{1,3},{2,10},{3,1},{4,12},{5,7},{6,14},{7,5},{8,0},{9,11},{1... | collective-permute-start | bytes 178184 | tf_op jit(solution)/shard_map/ppermute | solution.py:372
  7.3 2.1 %shard_map.105 = (bf16[3584,512]{1,0:T(8,128)(2,1)S(1)}, f32[8,128]{1,0:T(8,128)S(1)}) custom-call(bf16[3584,512]{1,0:T(8,128)(2,1)} %bitcast.5), custom_call_target="tpu_custom_call" | custom-call | bytes 3670016 | tf_op jit(solution)/shard_map/pallas_call | solution.py:183
  9.4 0.0 collective-permute-done.refs_1_
  9.4 2.4 %collective-permute-done.1.refs_2_ = bf16[8,3712]{1,0:T(8,128)(2,1)S(1)} collective-permute-done((bf16[8,3712]{1,0:T(8,128)(2,1)S(1)}, bf16[8,3712]{1,0:T(8,128)(2,1)S(1)}, u32[]{:S(2)}, u32[]{:S(2)}) %collective-permute-start.1) | collective-permute-done | bytes 59424 | tf_op jit(solution)/shard_map/ppermute | solution.py:372
  11.8 0.0 collective-permute-done.2.refs_3_
  11.8 1.8 %collective-permute-start.5 = (bf16[32,3712]{1,0:T(8,128)(2,1)S(1)}, bf16[32,3712]{1,0:T(8,128)(2,1)S(1)}, u32[]{:S(2)}, u32[]{:S(2)}) collective-permute-start(bf16[32,3712]{1,0:T(8,128)(2,1)S(1)} %shard_map.106.after_ref.refs_0_), channel_id=1, source_target_pairs={{0,2},{1,9},{2,0},{3,11},{4,6},{5,13},{6,4},{7,15},{8,10},{9,1},{1... | collective-permute-start | bytes 712712 | tf_op jit(solution)/shard_map/ppermute | solution.py:372
  13.6 1.5 %collective-permute-start.4 = (bf16[32,3712]{1,0:T(8,128)(2,1)S(1)}, bf16[32,3712]{1,0:T(8,128)(2,1)S(1)}, u32[]{:S(2)}, u32[]{:S(2)}) collective-permute-start(bf16[32,3712]{1,0:T(8,128)(2,1)S(1)} %shard_map.106.after_ref.refs_0_), channel_id=1, source_target_pairs={{0,4},{1,17},{2,6},{3,19},{4,0},{5,21},{6,2},{7,23},{8,12},{9,25},... | collective-permute-start | bytes 712712 | tf_op jit(solution)/shard_map/ppermute | solution.py:372
  15.1 0.3 collective-permute-start.3
  15.4 0.0 collective-permute-start.6
  15.4 4.5 %shard_map.107 = (bf16[4,128,512]{2,1,0:T(8,128)(2,1)}, bf16[3584,512]{1,0:T(8,128)(2,1)S(1)}, bf16[512,3584]{1,0:T(8,128)(2,1)S(1)}, f32[8,128]{1,0:T(8,128)S(1)}) custom-call(s32[4]{0:T(128)} %lengths_hbm.1, bf16[4,576,128]{2,1,0:T(8,128)(2,1)} %bitcast.9, bf16[4,576,256]{2,1,0:T(8,128)(2,1)} %bitcast.8, bf16[3584,512]{1,0:T(8,128)(2,1)} %bitcast.6, ...), custom_call_target="tpu_custom_call" | custom-call | flops 301989888 | bytes 7340032 | tf_op jit(solution)/shard_map/pallas_call | solution.py:74
  19.9 0.0 collective-permute-done.5.value_ref
  20.0 0.6 %collective-permute-start.9 = (bf16[32,3712]{1,0:T(8,128)(2,1)S(1)}, bf16[32,3712]{1,0:T(8,128)(2,1)S(1)}, u32[]{:S(2)}, u32[]{:S(2)}) collective-permute-start(bf16[32,3712]{1,0:T(8,128)(2,1)S(1)} %shard_map.110.refs_3_), channel_id=1, source_target_pairs={{0,1},{1,0},{2,3},{3,2},{4,5},{5,4},{6,7},{7,6},{8,9},{9,8},{10,11... | collective-permute-start | bytes 712712 | tf_op jit(solution)/shard_map/ppermute | solution.py:383
  20.5 1.7 %collective-permute-done.4.value_ref = bf16[32,3712]{1,0:T(8,128)(2,1)S(1)} collective-permute-done((bf16[32,3712]{1,0:T(8,128)(2,1)S(1)}, bf16[32,3712]{1,0:T(8,128)(2,1)S(1)}, u32[]{:S(2)}, u32[]{:S(2)}) %collective-permute-start.4) | collective-permute-done | bytes 237600 | tf_op jit(solution)/shard_map/ppermute | solution.py:372
  22.3 0.0 collective-permute-start.8
  22.3 0.0 collective-permute-done.3.value_ref
  22.3 0.5 %collective-permute-start.7 = (bf16[32,3712]{1,0:T(8,128)(2,1)S(1)}, bf16[32,3712]{1,0:T(8,128)(2,1)S(1)}, u32[]{:S(2)}, u32[]{:S(2)}) collective-permute-start(bf16[32,3712]{1,0:T(8,128)(2,1)S(1)} %shard_map.108.refs_1_), channel_id=1, source_target_pairs={{0,1},{1,0},{2,3},{3,2},{4,5},{5,4},{6,7},{7,6},{8,9},{9,8},{10,11... | collective-permute-start | bytes 712712 | tf_op jit(solution)/shard_map/ppermute | solution.py:383
  22.8 1.2 %shard_map.111.hidden_ref.refs_6_ = bf16[128,512]{1,0:T(8,128)(2,1)S(1)} custom-call(bf16[32,3712]{1,0:T(8,128)(2,1)S(1)} %shard_map.106.after_ref.refs_0_, bf16[32,3712]{1,0:T(8,128)(2,1)S(1)} %shard_map.108.refs_1_, bf16[32,3712]{1,0:T(8,128)(2,1)S(1)} %shard_map.109.refs_2_, bf16[32,3712]{1,0:T(8,128)(2,1)S(1)} %shard_map.110.refs_3_, ...), custom_call_target="tpu_custom_call" | custom-call | flops 939524096 | bytes 8290304 | tf_op jit(solution)/shard_map/pallas_call | solution.py:248
  24.0 0.0 collective-permute-done.6.refs_0_
  24.0 0.0 collective-permute-done.9.refs_3_
  24.1 0.0 collective-permute-done.8.refs_2_
  24.1 0.1 collective-permute-done.7.refs_1_
  24.1 1.2 %shard_map.113.hidden_ref = bf16[128,512]{1,0:T(8,128)(2,1)S(1)} custom-call(bf16[32,3712]{1,0:T(8,128)(2,1)S(1)} %collective-permute-done.6.refs_0_, bf16[32,3712]{1,0:T(8,128)(2,1)S(1)} %collective-permute-done.7.refs_1_, bf16[32,3712]{1,0:T(8,128)(2,1)S(1)} %collective-permute-done.8.refs_2_, bf16[32,3712]{1,0:T(8,128)(2,1)S(1)} %collective-permute-done.9.refs_3_, ...), custom_call_target="tpu_custom_call" | custom-call | flops 939524096 | bytes 8290304 | tf_op jit(solution)/shard_map/pallas_call | solution.py:248
  25.4 0.5 %shard_map.115 = bf16[128,2048]{1,0:T(8,128)(2,1)S(1)} custom-call(bf16[128,512]{1,0:T(8,128)(2,1)S(1)} %shard_map.113.hidden_ref, bf16[512,3584]{1,0:T(8,128)(2,1)S(1)} %get-tuple-element.23.down_ref), custom_call_target="tpu_custom_call" | custom-call | flops 268435456 | bytes 2621440 | tf_op jit(solution)/shard_map/pallas_call | solution.py:288
  25.8 0.2 collective-permute-start.11
  26.1 0.4 shard_map.114
  26.5 0.4 collective-permute-start.10
  26.8 0.7 %shard_map.112.mine_ref = bf16[128,3584]{1,0:T(8,128)(2,1)S(1)} custom-call(bf16[128,512]{1,0:T(8,128)(2,1)S(1)} %shard_map.111.hidden_ref.refs_6_, bf16[512,3584]{1,0:T(8,128)(2,1)S(1)} %get-tuple-element.23.down_ref), custom_call_target="tpu_custom_call" | custom-call | flops 469762048 | bytes 4587520 | tf_op jit(solution)/shard_map/pallas_call | solution.py:288
  27.5 0.8 %collective-permute-done.10.refs_0_ = bf16[128,1536]{1,0:T(8,128)(2,1)S(1)} collective-permute-done((bf16[128,1536]{1,0:T(8,128)(2,1)S(1)}, bf16[128,1536]{1,0:T(8,128)(2,1)S(1)}, u32[]{:S(2)}, u32[]{:S(2)}) %collective-permute-start.10) | collective-permute-done | bytes 393248 | tf_op jit(solution)/shard_map/ppermute | solution.py:383
  28.4 0.0 collective-permute-done.11.refs_1_
  28.4 0.2 shard_map.116
  28.6 1.6 %collective-permute-start.15 = (bf16[24,3584]{1,0:T(8,128)(2,1)S(1)}, bf16[24,3584]{1,0:T(8,128)(2,1)S(1)}, u32[]{:S(2)}, u32[]{:S(2)}) collective-permute-start(bf16[24,3584]{1,0:T(8,128)(2,1)S(1)} %get-tuple-element.29), channel_id=1, source_target_pairs={{0,4},{1,17},{2,6},{3,19},{4,0},{5,21},{6,2},{7,23},{8,12},{9,25},... | collective-permute-start | bytes 516104 | tf_op jit(solution)/shard_map/ppermute | solution.py:372
  30.2 0.6 %collective-permute-start.16 = (bf16[24,3584]{1,0:T(8,128)(2,1)S(1)}, bf16[24,3584]{1,0:T(8,128)(2,1)S(1)}, u32[]{:S(2)}, u32[]{:S(2)}) collective-permute-start(bf16[24,3584]{1,0:T(8,128)(2,1)S(1)} %get-tuple-element.30), channel_id=1, source_target_pairs={{0,6},{1,25},{2,4},{3,27},{4,2},{5,29},{6,0},{7,31},{8,14},{9,17},... | collective-permute-start | bytes 516104 | tf_op jit(solution)/shard_map/ppermute | solution.py:372
  30.7 1.4 %collective-permute-start.17 = (bf16[24,3584]{1,0:T(8,128)(2,1)S(1)}, bf16[24,3584]{1,0:T(8,128)(2,1)S(1)}, u32[]{:S(2)}, u32[]{:S(2)}) collective-permute-start(bf16[24,3584]{1,0:T(8,128)(2,1)S(1)} %get-tuple-element.31), channel_id=1, source_target_pairs={{0,2},{1,9},{2,0},{3,11},{4,6},{5,13},{6,4},{7,15},{8,10},{9,1},{1... | collective-permute-start | bytes 516104 | tf_op jit(solution)/shard_map/ppermute | solution.py:372
  32.1 1.5 %collective-permute-start.12 = (bf16[8,3584]{1,0:T(8,128)(2,1)S(1)}, bf16[8,3584]{1,0:T(8,128)(2,1)S(1)}, u32[]{:S(2)}, u32[]{:S(2)}) collective-permute-start(bf16[8,3584]{1,0:T(8,128)(2,1)S(1)} %get-tuple-element.25), channel_id=1, source_target_pairs={{0,4},{1,17},{2,6},{3,19},{4,0},{5,21},{6,2},{7,23},{8,12},{9,25},... | collective-permute-start | bytes 172040 | tf_op jit(solution)/shard_map/ppermute | solution.py:372
  33.7 0.6 %collective-permute-start.13 = (bf16[8,3584]{1,0:T(8,128)(2,1)S(1)}, bf16[8,3584]{1,0:T(8,128)(2,1)S(1)}, u32[]{:S(2)}, u32[]{:S(2)}) collective-permute-start(bf16[8,3584]{1,0:T(8,128)(2,1)S(1)} %get-tuple-element.26), channel_id=1, source_target_pairs={{0,6},{1,25},{2,4},{3,27},{4,2},{5,29},{6,0},{7,31},{8,14},{9,17},... | collective-permute-start | bytes 172040 | tf_op jit(solution)/shard_map/ppermute | solution.py:372
  34.2 0.7 %collective-permute-done.15.refs_1_ = bf16[24,3584]{1,0:T(8,128)(2,1)S(1)} collective-permute-done((bf16[24,3584]{1,0:T(8,128)(2,1)S(1)}, bf16[24,3584]{1,0:T(8,128)(2,1)S(1)}, u32[]{:S(2)}, u32[]{:S(2)}) %collective-permute-start.15) | collective-permute-done | bytes 172064 | tf_op jit(solution)/shard_map/ppermute | solution.py:372
  35.0 0.7 %collective-permute-start.14 = (bf16[8,3584]{1,0:T(8,128)(2,1)S(1)}, bf16[8,3584]{1,0:T(8,128)(2,1)S(1)}, u32[]{:S(2)}, u32[]{:S(2)}) collective-permute-start(bf16[8,3584]{1,0:T(8,128)(2,1)S(1)} %get-tuple-element.27), channel_id=1, source_target_pairs={{0,2},{1,9},{2,0},{3,11},{4,6},{5,13},{6,4},{7,15},{8,10},{9,1},{1... | collective-permute-start | bytes 172040 | tf_op jit(solution)/shard_map/ppermute | solution.py:372
  35.6 0.9 %collective-permute-done.16.refs_2_ = bf16[24,3584]{1,0:T(8,128)(2,1)S(1)} collective-permute-done((bf16[24,3584]{1,0:T(8,128)(2,1)S(1)}, bf16[24,3584]{1,0:T(8,128)(2,1)S(1)}, u32[]{:S(2)}, u32[]{:S(2)}) %collective-permute-start.16) | collective-permute-done | bytes 172064 | tf_op jit(solution)/shard_map/ppermute | solution.py:372
  36.6 0.9 %collective-permute-done.17.refs_3_ = bf16[24,3584]{1,0:T(8,128)(2,1)S(1)} collective-permute-done((bf16[24,3584]{1,0:T(8,128)(2,1)S(1)}, bf16[24,3584]{1,0:T(8,128)(2,1)S(1)}, u32[]{:S(2)}, u32[]{:S(2)}) %collective-permute-start.17) | collective-permute-done | bytes 172064 | tf_op jit(solution)/shard_map/ppermute | solution.py:372
  37.4 0.1 shard_map.117
  37.5 1.4 %collective-permute-start.18 = (bf16[8,3584]{1,0:T(8,128)(2,1)S(1)}, bf16[8,3584]{1,0:T(8,128)(2,1)S(1)}, u32[]{:S(2)}, u32[]{:S(2)}) collective-permute-start(bf16[8,3584]{1,0:T(8,128)(2,1)S(1)} %get-tuple-element.32), channel_id=1, source_target_pairs={{0,24},{1,7},{2,26},{3,5},{4,28},{5,3},{6,30},{7,1},{8,16},{9,15},... | collective-permute-start | bytes 172040 | tf_op jit(solution)/shard_map/ppermute | solution.py:372
  38.9 1.4 %collective-permute-start.19 = (bf16[8,3584]{1,0:T(8,128)(2,1)S(1)}, bf16[8,3584]{1,0:T(8,128)(2,1)S(1)}, u32[]{:S(2)}, u32[]{:S(2)}) collective-permute-start(bf16[8,3584]{1,0:T(8,128)(2,1)S(1)} %get-tuple-element.33), channel_id=1, source_target_pairs={{0,16},{1,5},{2,18},{3,7},{4,20},{5,1},{6,22},{7,3},{8,24},{9,13},... | collective-permute-start | bytes 172040 | tf_op jit(solution)/shard_map/ppermute | solution.py:372
  40.3 0.0 collective-permute-done.12.refs_1_
  40.3 1.7 %collective-permute-start.20 = (bf16[8,3584]{1,0:T(8,128)(2,1)S(1)}, bf16[8,3584]{1,0:T(8,128)(2,1)S(1)}, u32[]{:S(2)}, u32[]{:S(2)}) collective-permute-start(bf16[8,3584]{1,0:T(8,128)(2,1)S(1)} %get-tuple-element.34), channel_id=1, source_target_pairs={{0,8},{1,3},{2,10},{3,1},{4,12},{5,7},{6,14},{7,5},{8,0},{9,11},{1... | collective-permute-start | bytes 172040 | tf_op jit(solution)/shard_map/ppermute | solution.py:372
  42.0 0.0 collective-permute-done.13.refs_2_
  42.0 0.0 collective-permute-done.14.refs_3_
  42.0 1.6 %collective-permute-done.18.refs_4_ = bf16[8,3584]{1,0:T(8,128)(2,1)S(1)} collective-permute-done((bf16[8,3584]{1,0:T(8,128)(2,1)S(1)}, bf16[8,3584]{1,0:T(8,128)(2,1)S(1)}, u32[]{:S(2)}, u32[]{:S(2)}) %collective-permute-start.18) | collective-permute-done | bytes 57376 | tf_op jit(solution)/shard_map/ppermute | solution.py:372
  43.5 0.6 %collective-permute-done.19.refs_5_ = bf16[8,3584]{1,0:T(8,128)(2,1)S(1)} collective-permute-done((bf16[8,3584]{1,0:T(8,128)(2,1)S(1)}, bf16[8,3584]{1,0:T(8,128)(2,1)S(1)}, u32[]{:S(2)}, u32[]{:S(2)}) %collective-permute-start.19) | collective-permute-done | bytes 57376 | tf_op jit(solution)/shard_map/ppermute | solution.py:372
  44.2 0.6 %collective-permute-done.20.refs_6_ = bf16[8,3584]{1,0:T(8,128)(2,1)S(1)} collective-permute-done((bf16[8,3584]{1,0:T(8,128)(2,1)S(1)}, bf16[8,3584]{1,0:T(8,128)(2,1)S(1)}, u32[]{:S(2)}, u32[]{:S(2)}) %collective-permute-start.20) | collective-permute-done | bytes 57376 | tf_op jit(solution)/shard_map/ppermute | solution.py:372
  44.8 0.7 %shard_map.118 = bf16[8,3584]{1,0:T(8,128)(2,1)} custom-call(bf16[8,3584]{1,0:T(8,128)(2,1)S(1)} %get-tuple-element.24.refs_0_, bf16[8,3584]{1,0:T(8,128)(2,1)S(1)} %collective-permute-done.12.refs_1_, bf16[8,3584]{1,0:T(8,128)(2,1)S(1)} %collective-permute-done.13.refs_2_, bf16[8,3584]{1,0:T(8,128)(2,1)S(1)} %collective-permute-done.14.refs_3_, ...), custom_call_target="tpu_custom_call" | custom-call | flops 200704 | bytes 401408 | tf_op jit(solution)/shard_map/pallas_call | solution.py:340
  (4 shorter events, 0.0 us)
Async XLA Ops:
  1.6 7.8 %collective-permute-start = (bf16[8,3712]{1,0:T(8,128)(2,1)S(1)}, bf16[8,3712]{1,0:T(8,128)(2,1)S(1)}, u32[]{:S(2)}, u32[]{:S(2)}) collective-permute-start(bf16[8,3712]{1,0:T(8,128)(2,1)S(1)} %shard_map.104.refs_0_), channel_id=1, source_target_pairs={{0,24},{1,7},{2,26},{3,5},{4,28},{5,3},{6,30},{7,1},{8,16},{9,15},... | collective-permute-start | bytes 178184 | tf_op jit(solution)/shard_map/ppermute | solution.py:372
  6.7 5.1 %collective-permute-start.1 = (bf16[8,3712]{1,0:T(8,128)(2,1)S(1)}, bf16[8,3712]{1,0:T(8,128)(2,1)S(1)}, u32[]{:S(2)}, u32[]{:S(2)}) collective-permute-start(bf16[8,3712]{1,0:T(8,128)(2,1)S(1)} %shard_map.104.refs_0_), channel_id=1, source_target_pairs={{0,16},{1,5},{2,18},{3,7},{4,20},{5,1},{6,22},{7,3},{8,24},{9,13},... | collective-permute-start | bytes 178184 | tf_op jit(solution)/shard_map/ppermute | solution.py:372
  6.7 5.1 %collective-permute-start.2 = (bf16[8,3712]{1,0:T(8,128)(2,1)S(1)}, bf16[8,3712]{1,0:T(8,128)(2,1)S(1)}, u32[]{:S(2)}, u32[]{:S(2)}) collective-permute-start(bf16[8,3712]{1,0:T(8,128)(2,1)S(1)} %shard_map.104.refs_0_), channel_id=1, source_target_pairs={{0,8},{1,3},{2,10},{3,1},{4,12},{5,7},{6,14},{7,5},{8,0},{9,11},{1... | collective-permute-start | bytes 178184 | tf_op jit(solution)/shard_map/ppermute | solution.py:372
  11.8 8.1 %collective-permute-start.5 = (bf16[32,3712]{1,0:T(8,128)(2,1)S(1)}, bf16[32,3712]{1,0:T(8,128)(2,1)S(1)}, u32[]{:S(2)}, u32[]{:S(2)}) collective-permute-start(bf16[32,3712]{1,0:T(8,128)(2,1)S(1)} %shard_map.106.after_ref.refs_0_), channel_id=1, source_target_pairs={{0,2},{1,9},{2,0},{3,11},{4,6},{5,13},{6,4},{7,15},{8,10},{9,1},{1... | collective-permute-start | bytes 712712 | tf_op jit(solution)/shard_map/ppermute | solution.py:372
  13.6 8.7 %collective-permute-start.4 = (bf16[32,3712]{1,0:T(8,128)(2,1)S(1)}, bf16[32,3712]{1,0:T(8,128)(2,1)S(1)}, u32[]{:S(2)}, u32[]{:S(2)}) collective-permute-start(bf16[32,3712]{1,0:T(8,128)(2,1)S(1)} %shard_map.106.after_ref.refs_0_), channel_id=1, source_target_pairs={{0,4},{1,17},{2,6},{3,19},{4,0},{5,21},{6,2},{7,23},{8,12},{9,25},... | collective-permute-start | bytes 712712 | tf_op jit(solution)/shard_map/ppermute | solution.py:372
  15.1 7.1 %collective-permute-start.3 = (bf16[32,3712]{1,0:T(8,128)(2,1)S(1)}, bf16[32,3712]{1,0:T(8,128)(2,1)S(1)}, u32[]{:S(2)}, u32[]{:S(2)}) collective-permute-start(bf16[32,3712]{1,0:T(8,128)(2,1)S(1)} %shard_map.106.after_ref.refs_0_), channel_id=1, source_target_pairs={{0,6},{1,25},{2,4},{3,27},{4,2},{5,29},{6,0},{7,31},{8,14},{9,17},... | collective-permute-start | bytes 712712 | tf_op jit(solution)/shard_map/ppermute | solution.py:372
  15.4 8.6 %collective-permute-start.6 = (bf16[32,3712]{1,0:T(8,128)(2,1)S(1)}, bf16[32,3712]{1,0:T(8,128)(2,1)S(1)}, u32[]{:S(2)}, u32[]{:S(2)}) collective-permute-start(bf16[32,3712]{1,0:T(8,128)(2,1)S(1)} %shard_map.106.after_ref.refs_0_), channel_id=1, source_target_pairs={{0,1},{1,0},{2,3},{3,2},{4,5},{5,4},{6,7},{7,6},{8,9},{9,8},{10,11... | collective-permute-start | bytes 712712 | tf_op jit(solution)/shard_map/ppermute | solution.py:383
  20.0 4.1 %collective-permute-start.9 = (bf16[32,3712]{1,0:T(8,128)(2,1)S(1)}, bf16[32,3712]{1,0:T(8,128)(2,1)S(1)}, u32[]{:S(2)}, u32[]{:S(2)}) collective-permute-start(bf16[32,3712]{1,0:T(8,128)(2,1)S(1)} %shard_map.110.refs_3_), channel_id=1, source_target_pairs={{0,1},{1,0},{2,3},{3,2},{4,5},{5,4},{6,7},{7,6},{8,9},{9,8},{10,11... | collective-permute-start | bytes 712712 | tf_op jit(solution)/shard_map/ppermute | solution.py:383
  22.3 1.8 %collective-permute-start.8 = (bf16[32,3712]{1,0:T(8,128)(2,1)S(1)}, bf16[32,3712]{1,0:T(8,128)(2,1)S(1)}, u32[]{:S(2)}, u32[]{:S(2)}) collective-permute-start(bf16[32,3712]{1,0:T(8,128)(2,1)S(1)} %shard_map.109.refs_2_), channel_id=1, source_target_pairs={{0,1},{1,0},{2,3},{3,2},{4,5},{5,4},{6,7},{7,6},{8,9},{9,8},{10,11... | collective-permute-start | bytes 712712 | tf_op jit(solution)/shard_map/ppermute | solution.py:383
  22.3 1.8 %collective-permute-start.7 = (bf16[32,3712]{1,0:T(8,128)(2,1)S(1)}, bf16[32,3712]{1,0:T(8,128)(2,1)S(1)}, u32[]{:S(2)}, u32[]{:S(2)}) collective-permute-start(bf16[32,3712]{1,0:T(8,128)(2,1)S(1)} %shard_map.108.refs_1_), channel_id=1, source_target_pairs={{0,1},{1,0},{2,3},{3,2},{4,5},{5,4},{6,7},{7,6},{8,9},{9,8},{10,11... | collective-permute-start | bytes 712712 | tf_op jit(solution)/shard_map/ppermute | solution.py:383
  25.8 2.5 %collective-permute-start.11 = (bf16[128,2048]{1,0:T(8,128)(2,1)S(1)}, bf16[128,2048]{1,0:T(8,128)(2,1)S(1)}, u32[]{:S(2)}, u32[]{:S(2)}) collective-permute-start(bf16[128,2048]{1,0:T(8,128)(2,1)S(1)} %shard_map.115), channel_id=1, source_target_pairs={{0,1},{1,0},{2,3},{3,2},{4,5},{5,4},{6,7},{7,6},{8,9},{9,8},{10,11... | collective-permute-start | bytes 1572872 | tf_op jit(solution)/shard_map/ppermute | solution.py:383
  26.5 1.9 %collective-permute-start.10 = (bf16[128,1536]{1,0:T(8,128)(2,1)S(1)}, bf16[128,1536]{1,0:T(8,128)(2,1)S(1)}, u32[]{:S(2)}, u32[]{:S(2)}) collective-permute-start(bf16[128,1536]{1,0:T(8,128)(2,1)S(1)} %shard_map.114), channel_id=1, source_target_pairs={{0,1},{1,0},{2,3},{3,2},{4,5},{5,4},{6,7},{7,6},{8,9},{9,8},{10,11... | collective-permute-start | bytes 1179656 | tf_op jit(solution)/shard_map/ppermute | solution.py:383
  28.6 6.4 %collective-permute-start.15 = (bf16[24,3584]{1,0:T(8,128)(2,1)S(1)}, bf16[24,3584]{1,0:T(8,128)(2,1)S(1)}, u32[]{:S(2)}, u32[]{:S(2)}) collective-permute-start(bf16[24,3584]{1,0:T(8,128)(2,1)S(1)} %get-tuple-element.29), channel_id=1, source_target_pairs={{0,4},{1,17},{2,6},{3,19},{4,0},{5,21},{6,2},{7,23},{8,12},{9,25},... | collective-permute-start | bytes 516104 | tf_op jit(solution)/shard_map/ppermute | solution.py:372
  30.2 6.4 %collective-permute-start.16 = (bf16[24,3584]{1,0:T(8,128)(2,1)S(1)}, bf16[24,3584]{1,0:T(8,128)(2,1)S(1)}, u32[]{:S(2)}, u32[]{:S(2)}) collective-permute-start(bf16[24,3584]{1,0:T(8,128)(2,1)S(1)} %get-tuple-element.30), channel_id=1, source_target_pairs={{0,6},{1,25},{2,4},{3,27},{4,2},{5,29},{6,0},{7,31},{8,14},{9,17},... | collective-permute-start | bytes 516104 | tf_op jit(solution)/shard_map/ppermute | solution.py:372
  30.7 6.7 %collective-permute-start.17 = (bf16[24,3584]{1,0:T(8,128)(2,1)S(1)}, bf16[24,3584]{1,0:T(8,128)(2,1)S(1)}, u32[]{:S(2)}, u32[]{:S(2)}) collective-permute-start(bf16[24,3584]{1,0:T(8,128)(2,1)S(1)} %get-tuple-element.31), channel_id=1, source_target_pairs={{0,2},{1,9},{2,0},{3,11},{4,6},{5,13},{6,4},{7,15},{8,10},{9,1},{1... | collective-permute-start | bytes 516104 | tf_op jit(solution)/shard_map/ppermute | solution.py:372
  32.1 8.1 %collective-permute-start.12 = (bf16[8,3584]{1,0:T(8,128)(2,1)S(1)}, bf16[8,3584]{1,0:T(8,128)(2,1)S(1)}, u32[]{:S(2)}, u32[]{:S(2)}) collective-permute-start(bf16[8,3584]{1,0:T(8,128)(2,1)S(1)} %get-tuple-element.25), channel_id=1, source_target_pairs={{0,4},{1,17},{2,6},{3,19},{4,0},{5,21},{6,2},{7,23},{8,12},{9,25},... | collective-permute-start | bytes 172040 | tf_op jit(solution)/shard_map/ppermute | solution.py:372
  33.7 8.3 %collective-permute-start.13 = (bf16[8,3584]{1,0:T(8,128)(2,1)S(1)}, bf16[8,3584]{1,0:T(8,128)(2,1)S(1)}, u32[]{:S(2)}, u32[]{:S(2)}) collective-permute-start(bf16[8,3584]{1,0:T(8,128)(2,1)S(1)} %get-tuple-element.26), channel_id=1, source_target_pairs={{0,6},{1,25},{2,4},{3,27},{4,2},{5,29},{6,0},{7,31},{8,14},{9,17},... | collective-permute-start | bytes 172040 | tf_op jit(solution)/shard_map/ppermute | solution.py:372
  35.0 7.0 %collective-permute-start.14 = (bf16[8,3584]{1,0:T(8,128)(2,1)S(1)}, bf16[8,3584]{1,0:T(8,128)(2,1)S(1)}, u32[]{:S(2)}, u32[]{:S(2)}) collective-permute-start(bf16[8,3584]{1,0:T(8,128)(2,1)S(1)} %get-tuple-element.27), channel_id=1, source_target_pairs={{0,2},{1,9},{2,0},{3,11},{4,6},{5,13},{6,4},{7,15},{8,10},{9,1},{1... | collective-permute-start | bytes 172040 | tf_op jit(solution)/shard_map/ppermute | solution.py:372
  37.5 6.1 %collective-permute-start.18 = (bf16[8,3584]{1,0:T(8,128)(2,1)S(1)}, bf16[8,3584]{1,0:T(8,128)(2,1)S(1)}, u32[]{:S(2)}, u32[]{:S(2)}) collective-permute-start(bf16[8,3584]{1,0:T(8,128)(2,1)S(1)} %get-tuple-element.32), channel_id=1, source_target_pairs={{0,24},{1,7},{2,26},{3,5},{4,28},{5,3},{6,30},{7,1},{8,16},{9,15},... | collective-permute-start | bytes 172040 | tf_op jit(solution)/shard_map/ppermute | solution.py:372
  38.9 5.3 %collective-permute-start.19 = (bf16[8,3584]{1,0:T(8,128)(2,1)S(1)}, bf16[8,3584]{1,0:T(8,128)(2,1)S(1)}, u32[]{:S(2)}, u32[]{:S(2)}) collective-permute-start(bf16[8,3584]{1,0:T(8,128)(2,1)S(1)} %get-tuple-element.33), channel_id=1, source_target_pairs={{0,16},{1,5},{2,18},{3,7},{4,20},{5,1},{6,22},{7,3},{8,24},{9,13},... | collective-permute-start | bytes 172040 | tf_op jit(solution)/shard_map/ppermute | solution.py:372
  40.3 4.5 %collective-permute-start.20 = (bf16[8,3584]{1,0:T(8,128)(2,1)S(1)}, bf16[8,3584]{1,0:T(8,128)(2,1)S(1)}, u32[]{:S(2)}, u32[]{:S(2)}) collective-permute-start(bf16[8,3584]{1,0:T(8,128)(2,1)S(1)} %get-tuple-element.34), channel_id=1, source_target_pairs={{0,8},{1,3},{2,10},{3,1},{4,12},{5,7},{6,14},{7,5},{8,0},{9,11},{1... | collective-permute-start | bytes 172040 | tf_op jit(solution)/shard_map/ppermute | solution.py:372
